TPU v7x, 512 devices: a whole 4x4x16 slice. The times are simulated.
512 devices in a mesh: bulk: 32 (over z, x_hi), wide: 16 (over y, x_lo, core).
Axes of the slice: x: 4 (x_hi: 2, x_lo: 2; x = x_hi * 2 + x_lo), y: 4, z: 16, core: 2. Of those that a mesh axis runs over, the one named last changes fastest.
Arguments:
- seed_electric: float32 [3, 256, 256, 128], P(None, 'bulk', 'wide'), may hold values from -6 to 6
- seed_magnetic: float32 [3, 256, 256, 128], P(None, 'bulk', 'wide'), may hold values from -6 to 6
- saved_magnetic: bfloat16 [2, 3, 256, 256, 128], P(None, None, 'bulk', 'wide'), may hold values from -6 to 6
- material: int32 [256, 256, 128], P('bulk', 'wide'), may hold values from 0 to 7
- permittivity: float32 [8], replicated, may hold values from 1 to 12
- source_cells: int32 [64], replicated, may hold values from 0 to 8388607
- monitor_cells: int32 [64], replicated, may hold values from 0 to 8388607
- monitor_weights: float32 [2, 64, 3], replicated, may hold values from -24 to 24
- lift_weight: float32 [16, 3], replicated, may hold values from -3.5 to 3.5
- project_weight: float32 [3, 16], replicated, may hold values from -1.5 to 1.5
- mode_mix: bfloat16 [2, 48, 16, 16], replicated, may hold values from -1.5 to 1.5
- gain_first: float32 [16, 48], replicated, may hold values from 0.1 to 1.9
- gain_second: float32 [16, 48], replicated, may hold values from 0.1 to 1.9
Outputs:
- grad_electric: float32 [3, 256, 256, 128], P(None, 'bulk', 'wide')
- grad_magnetic: float32 [3, 256, 256, 128], P(None, 'bulk', 'wide')
- grad_permittivity: float32 [256, 256, 128], P('bulk', 'wide')
- grad_sources: float32 [2, 64, 3], replicated
All inputs are finite; a program needn't handle non-finite values.
Results may differ from a plain program's by a relative error of at most 0.02.
Values may be sent and summed in bfloat16 or wider, within the bound.
No kernel may reach another device: no remote copies, remote signals or barrier semaphores. Data moves between devices by JAX's collectives and lax.ppermute only.
A program may use at most 64 MiB of HBM per device.

v0:
```python
import math

import jax
import jax.numpy as jnp
from jax import lax
from jax.sharding import PartitionSpec as P

COURANT = 0.5


def passed_along(block, axis, distance):
    devices = range(lax.axis_size(axis))
    route = [(i - distance, i) for i in devices if i - distance in devices]
    return lax.ppermute(block, axis, route)


def waves(freqs, places, total):
    phase = freqs[:, None] * places[None, :] % total
    angle = phase.astype(jnp.float32) * (2.0 * math.pi / total)
    return (jnp.cos(angle), jnp.sin(angle))


def signed_modes(index, count):
    return jnp.where(index < count // 2, index, index - count)


def step_ahead(field, plane, axis):
    size = field.shape[axis]
    ahead = jnp.concatenate([lax.slice_in_dim(field, 1, size, axis=axis), plane], axis)
    return ahead - field


def step_behind(field, plane, axis):
    size = field.shape[axis]
    behind = jnp.concatenate([plane, lax.slice_in_dim(field, 0, size - 1, axis=axis)], axis)
    return field - behind


def curl_ahead(field):
    across_x = passed_along(field[1:3, 0:1], "bulk", -1)
    across_y = passed_along(jnp.stack([field[0, :, 0:1], field[2, :, 0:1]]), "wide", -1)
    zero_z = jnp.zeros_like(field[0, :, :, 0:1])
    first = step_ahead(field[2], across_y[1], 1) - step_ahead(field[1], zero_z, 2)
    second = step_ahead(field[0], zero_z, 2) - step_ahead(field[2], across_x[1], 0)
    third = step_ahead(field[1], across_x[0], 0) - step_ahead(field[0], across_y[0], 1)
    return jnp.stack([first, second, third])


def curl_behind(field):
    across_x = passed_along(field[1:3, -1:], "bulk", 1)
    across_y = passed_along(jnp.stack([field[0, :, -1:], field[2, :, -1:]]), "wide", 1)
    zero_z = jnp.zeros_like(field[0, :, :, 0:1])
    first = step_behind(field[2], across_y[1], 1) - step_behind(field[1], zero_z, 2)
    second = step_behind(field[0], zero_z, 2) - step_behind(field[2], across_x[1], 0)
    third = step_behind(field[1], across_x[0], 0) - step_behind(field[0], across_y[0], 1)
    return jnp.stack([first, second, third])


def body(
    seed_electric,
    seed_magnetic,
    saved_magnetic,
    material,
    permittivity,
    source_cells,
    monitor_cells,
    monitor_weights,
    lift_weight,
    project_weight,
    mode_mix,
    gain_first,
    gain_second,
):
    rows_x, rows_y, depth = (seed_electric.shape[1], seed_electric.shape[2], seed_electric.shape[3])
    bulk_count = lax.axis_size("bulk")
    wide_count = lax.axis_size("wide")
    total_x = rows_x * bulk_count
    total_y = rows_y * wide_count
    start_x = lax.axis_index("bulk") * rows_x
    start_y = lax.axis_index("wide") * rows_y
    modes = mode_mix.shape[1]
    channels = mode_mix.shape[2]
    modes_local = modes // wide_count
    levels = permittivity.shape[0]
    steps_total = saved_magnetic.shape[0]
    eps_cells = jnp.zeros(material.shape, jnp.float32)
    for level in range(levels):
        eps_cells = jnp.where(material == level, permittivity[level], eps_cells)

    def locate(flat):
        first = flat // (total_y * depth) - start_x
        second = flat // depth % total_y - start_y
        third = flat % depth
        owned = (first >= 0) & (first < rows_x) & (second >= 0) & (second < rows_y)
        return (jnp.clip(first, 0, rows_x - 1), jnp.clip(second, 0, rows_y - 1), third, owned)

    mon_x, mon_y, mon_z, mon_owned = locate(monitor_cells)
    src_x, src_y, src_z, src_owned = locate(source_cells)

    def inject(field, index):
        return field.at[:, mon_x, mon_y, mon_z].add(
            jnp.where(mon_owned[None, :], monitor_weights[index].T, 0.0)
        )

    mode_index = jnp.arange(modes, dtype=jnp.int32)
    cos_z, sin_z = waves(mode_index, jnp.arange(depth, dtype=jnp.int32), depth)
    table_z = (
        jnp.concatenate([cos_z, -sin_z]) * (1.0 / math.sqrt(total_x * total_y * depth))
    ).astype(jnp.bfloat16)
    back_scale = 1.0 / math.sqrt(modes**3)
    cos_back = (cos_z * back_scale).astype(jnp.bfloat16)
    sin_back = (sin_z * back_scale).astype(jnp.bfloat16)
    local_y = start_y + jnp.arange(rows_y, dtype=jnp.int32)
    f32 = jnp.float32

    def y_tables(freqs, places):
        cos_t, sin_t = waves(freqs, places, total_y)
        return (cos_t.astype(jnp.bfloat16), sin_t.astype(jnp.bfloat16))

    adjoint_e = inject(seed_electric, steps_total - 1)
    adjoint_h = seed_magnetic
    grad_eps = jnp.zeros(eps_cells.shape, f32)
    sources = [None] * steps_total
    for step in reversed(range(steps_total)):
        sources[step] = jnp.where(src_owned[:, None], adjoint_e[:, src_x, src_y, src_z].T, 0.0)
        scaled = COURANT / eps_cells * adjoint_e
        adjoint_h = adjoint_h + curl_ahead(scaled)
        saved_curl = curl_behind(saved_magnetic[step].astype(f32))
        grad_eps = grad_eps - jnp.sum(scaled / eps_cells * saved_curl, 0)
        updated = adjoint_e - COURANT * curl_behind(adjoint_h)
        if step % 2 == 1:
            lifted = jnp.einsum(
                "cd,dxyz->cxyz", lift_weight, adjoint_e, precision=lax.Precision.HIGHEST
            ).astype(jnp.bfloat16)
            along_z = jnp.einsum(
                "cxyz,mz->cxym", lifted, table_z, preferred_element_type=f32
            ).astype(jnp.bfloat16)
            lines = lax.all_to_all(along_z, "wide", split_axis=0, concat_axis=2, tiled=True)
            spectral_cos_t, spectral_sin_t = y_tables(
                signed_modes(mode_index, modes), jnp.arange(total_y, dtype=jnp.int32)
            )
            part_a = jnp.einsum("cxym,jy->jcxm", lines, spectral_cos_t, preferred_element_type=f32)
            part_b = jnp.einsum("cxym,jy->jcxm", lines, spectral_sin_t, preferred_element_type=f32)
            whole_modes = jnp.concatenate(
                [
                    part_a[..., :modes] + part_b[..., modes:],
                    part_a[..., modes:] - part_b[..., :modes],
                ],
                -1,
            ).astype(jnp.bfloat16)
            y_block = lax.all_to_all(whole_modes, "wide", split_axis=0, concat_axis=1, tiled=True)
            y_real = y_block[..., :modes]
            y_imag = y_block[..., modes:]
            mix_real = mode_mix[0]
            mix_imag = mode_mix[1]
            gain_rows = lax.dynamic_slice_in_dim(
                gain_second, lax.axis_index("wide") * modes_local, modes_local, 1
            ).T[:, :, None, None]
            spec = "jcxk,kco->jokx"
            p_real = (
                jnp.einsum(spec, y_real, mix_real, preferred_element_type=f32)
                - jnp.einsum(spec, y_imag, mix_imag, preferred_element_type=f32)
            ) * gain_rows
            p_imag = (
                jnp.einsum(spec, y_real, mix_imag, preferred_element_type=f32)
                + jnp.einsum(spec, y_imag, mix_real, preferred_element_type=f32)
            ) * gain_rows
            mixed = (
                jnp.stack([p_real, p_imag], 0)
                .astype(jnp.bfloat16)
                .reshape(2, modes_local, channels * modes, rows_x)
            )
            cos_x, sin_x = waves(
                signed_modes(mode_index, modes), jnp.arange(total_x, dtype=jnp.int32), total_x
            )
            cos_x, sin_x = (cos_x.astype(jnp.bfloat16), sin_x.astype(jnp.bfloat16))
            repeated_gain = jnp.repeat(gain_first, modes, axis=0)
            block = lax.all_to_all(mixed, "bulk", split_axis=2, concat_axis=3, tiled=True)
            block_rows = block.shape[2]
            gains = lax.dynamic_slice_in_dim(
                repeated_gain, lax.axis_index("bulk") * block_rows, block_rows, 0
            )[None, :, :]
            b_real = block[0]
            b_imag = block[1]
            fwd = "jrx,fx->jrf"
            x_real = jnp.einsum(fwd, b_real, cos_x, preferred_element_type=f32) + jnp.einsum(
                fwd, b_imag, sin_x, preferred_element_type=f32
            )
            x_imag = jnp.einsum(fwd, b_imag, cos_x, preferred_element_type=f32) - jnp.einsum(
                fwd, b_real, sin_x, preferred_element_type=f32
            )
            q_real = (gains * x_real).astype(jnp.bfloat16)
            q_imag = (gains * x_imag).astype(jnp.bfloat16)
            inv = "jrf,fx->jrx"
            r_real = jnp.einsum(inv, q_real, cos_x, preferred_element_type=f32) - jnp.einsum(
                inv, q_imag, sin_x, preferred_element_type=f32
            )
            r_imag = jnp.einsum(inv, q_real, sin_x, preferred_element_type=f32) + jnp.einsum(
                inv, q_imag, cos_x, preferred_element_type=f32
            )
            filtered = jnp.stack([r_real, r_imag], 0).astype(jnp.bfloat16)
            returned = lax.all_to_all(filtered, "bulk", split_axis=3, concat_axis=2, tiled=True)
            returned = returned.reshape(2, modes_local, channels, modes, rows_x)
            piece = lax.all_gather(returned, "wide", axis=1, tiled=True)
            count = piece.shape[1]
            spectral_freqs = signed_modes(jnp.arange(count, dtype=jnp.int32), modes)
            spectral_cos_t, spectral_sin_t = y_tables(spectral_freqs, local_y)
            piece_real = piece[0]
            piece_imag = piece[1]
            spec_y = "jokx,jy->okxy"
            w_real = jnp.einsum(
                spec_y, piece_real, spectral_cos_t, preferred_element_type=f32
            ) - jnp.einsum(spec_y, piece_imag, spectral_sin_t, preferred_element_type=f32)
            w_imag = jnp.einsum(
                spec_y, piece_real, spectral_sin_t, preferred_element_type=f32
            ) + jnp.einsum(spec_y, piece_imag, spectral_cos_t, preferred_element_type=f32)
            w_real, w_imag = (w_real, w_imag)
            values = jnp.einsum(
                "okxy,kz->oxyz", w_real.astype(jnp.bfloat16), cos_back, preferred_element_type=f32
            ) - jnp.einsum(
                "okxy,kz->oxyz", w_imag.astype(jnp.bfloat16), sin_back, preferred_element_type=f32
            )
            updated = updated + jnp.einsum(
                "do,oxyz->dxyz", project_weight, values, precision=lax.Precision.HIGHEST
            )
        adjoint_e = updated
        if step >= 1:
            adjoint_e = inject(adjoint_e, step - 1)
    grad_sources = lax.psum(jnp.stack(sources), ("bulk", "wide"))
    return (adjoint_e, adjoint_h, grad_eps, grad_sources)


def solution(mesh):
    placed = (
        P(None, "bulk", "wide", None),
        P(None, "bulk", "wide", None),
        P(None, None, "bulk", "wide", None),
        P("bulk", "wide", None),
        P(),
        P(),
        P(),
        P(),
        P(),
        P(),
        P(),
        P(),
        P(),
    )
    return jax.shard_map(
        body,
        mesh=mesh,
        in_specs=placed,
        out_specs=(
            P(None, "bulk", "wide", None),
            P(None, "bulk", "wide", None),
            P("bulk", "wide", None),
            P(),
        ),
        check_vma=False,
    )
```

profile of v0, /device:TPU:1, one launch (start us, length us, event | category | flops | bytes accessed | tf_op | source)
XLA Modules:
  0.0 352.1 jit_solution(10103388714135855080)
XLA Ops:
  8.2 4.5 %collective-permute-start.8 = (f32[2,8,1,128]{3,1,2,0:T(8,128)S(1)}, f32[2,8,1,128]{3,1,2,0:T(8,128)S(1)}, u32[]{:S(2)}, u32[]{:S(2)}) collective-permute-start(f32[2,8,1,128]{3,1,2,0:T(8,128)S(1)} %pad_maximum_fusion.7), channel_id=1, source_target_pairs={{0,1},{1,2},{2,3},{3,4},{4,5},{5,6},{6,7},{7,8},{8,9},{9,10},{10,1... | collective-permute-start | bytes 24584 | tf_op jit(solution)/shard_map/ppermute | solution.py:14
  15.3 4.9 %collective-permute-start.9 = (f32[2,1,16,128]{3,2,1,0:T(8,128)}, f32[2,1,16,128]{3,2,1,0:T(8,128)}, u32[]{:S(2)}, u32[]{:S(2)}) collective-permute-start(f32[2,1,16,128]{3,2,1,0:T(8,128)} %slice.653), channel_id=1, source_target_pairs={{0,16},{16,32},{32,48},{48,64},{64,80},{80,96},{96,112},{112,128},... | collective-permute-start | bytes 49160 | tf_op jit(solution)/shard_map/ppermute | solution.py:14
  20.8 3.8 %collective-permute-start.11 = (f32[2,1,16,128]{3,2,1,0:T(8,128)}, f32[2,1,16,128]{3,2,1,0:T(8,128)}, u32[]{:S(2)}, u32[]{:S(2)}) collective-permute-start(f32[2,1,16,128]{3,2,1,0:T(8,128)} %slice.669), channel_id=1, source_target_pairs={{0,16},{16,32},{32,48},{48,64},{64,80},{80,96},{96,112},{112,128},... | collective-permute-start | bytes 49160 | tf_op jit(solution)/shard_map/ppermute | solution.py:14
  25.7 5.7 %copy.253 = f32[3,8,16,128]{0,3,2,1:T(8,128)} copy(f32[3,8,16,128]{3,2,1,0:T(8,128)} %param.13) | data formatting | bytes 393216 | tf_op args[0]
  32.6 7.2 %scatter_fusion = f32[3,8,16,128]{0,3,2,1:T(8,128)} fusion(f32[3,8,16,128]{0,3,2,1:T(8,128)} %copy.253, s32[64]{0:T(128)S(1)} %fusion.174, f32[64,3]{1,0:T(8,128)S(1)} %get-tuple-element.126), kind=kCustom, calls=%fused_computation.2 | custom fusion | flops 192 | bytes 3072 | tf_op jit(solution)/shard_map/scatter-add | solution.py:101
  39.9 9.7 %fusion.8 = bf16[16,8,16,128]{3,0,2,1:T(8,128)(2,1)S(1)} fusion(f32[3,8,16,128]{0,3,2,1:T(8,128)} %scatter_fusion, f32[16,3]{0,1:T(4,128)S(1)} %copy-done.17), kind=kOutput, calls=%fused_computation.17 | convolution fusion | flops 9699328 | bytes 721088 | tf_op jit(solution)/shard_map/cd,dxyz->cxyz/dot_general | solution.py:132
  50.6 6.1 %all-to-all-start = ((bf16[16,8,16,96]{3,2,1,0:T(8,128)(2,1)}), bf16[16,8,16,96]{3,2,1,0:T(8,128)(2,1)S(1)}, u32[]{:S(2)}, u32[]{:S(2)}) async-start(bf16[16,8,16,96]{3,2,1,0:T(8,128)(2,1)} %convolution_convert_fusion.1), calls=%async_computation | async-start | bytes 1048576 | tf_op jit(solution)/shard_map/all_to_all | solution.py:138
  56.8 5.3 %copy.259 = f32[3,8,16,128]{3,2,1,0:T(8,128)S(1)} copy(f32[3,8,16,128]{0,3,2,1:T(8,128)} %scatter_fusion) | data formatting | bytes 393216 | tf_op jit(solution)/shard_map/scatter-add | solution.py:101
  62.8 5.1 %broadcast_divide_fusion = (f32[8,16,128]{2,1,0:T(8,128)S(1)}, f32[8,16,128]{2,1,0:T(8,128)S(1)}) fusion(f32[]{:T(128)} %bitcast.12, s32[8,16,128]{2,1,0:T(8,128)S(1)} %copy-done.8, f32[]{:T(128)} %bitcast.11, f32[]{:T(128)} %bitcast.10, f32[]{:T(128)} %bitcast.9, f32[]{:T(128)} %bitcast.8, f32[]{:T(128)} %bitcast.7, f32[]{:T(128)} %bitcast.6, f32[]{:T(128)} %bitcast.5), kind=kLoop, calls=%fused_computation.195 | loop fusion | flops 278528 | bytes 196640 | tf_op jit(solution)/shard_map/div | solution.py:126
  77.9 3.6 %collective-permute-done.1 = f32[2,1,16,128]{3,2,1,0:T(8,128)S(1)} collective-permute-done((f32[2,1,16,128]{3,2,1,0:T(8,128)S(1)}, f32[2,1,16,128]{3,2,1,0:T(8,128)S(1)}, u32[]{:S(2)}, u32[]{:S(2)}) %collective-permute-start.1) | collective-permute-done | bytes 16416 | tf_op jit(solution)/shard_map/ppermute | solution.py:14
  83.5 7.0 %all-to-all-start.1 = ((bf16[48,1,8,96]{3,2,1,0:T(8,128)(2,1)}), bf16[48,1,8,96]{3,2,1,0:T(8,128)(2,1)S(1)}, u32[]{:S(2)}, u32[]{:S(2)}) async-start(bf16[48,1,8,96]{3,2,1,0:T(8,128)(2,1)} %copy.265), calls=%async_computation.1 | async-start | bytes 196608 | tf_op jit(solution)/shard_map/all_to_all | solution.py:151
  90.5 5.8 %all-to-all-done.1 = bf16[48,1,8,96]{3,2,1,0:T(8,128)(2,1)S(1)} async-done(((bf16[48,1,8,96]{3,2,1,0:T(8,128)(2,1)}), bf16[48,1,8,96]{3,2,1,0:T(8,128)(2,1)S(1)}, u32[]{:S(2)}, u32[]{:S(2)}) %all-to-all-start.1) | async-done | bytes 73760 | tf_op jit(solution)/shard_map/all_to_all | solution.py:151
  103.5 17.8 %all-to-all-start.2 = ((bf16[32,2,576]{2,1,0:T(2,128)(2,1)}), bf16[32,2,576]{2,1,0:T(2,128)(2,1)S(1)}, u32[]{:S(2)}, u32[]{:S(2)}) async-start(bf16[32,2,576]{2,1,0:T(2,128)(2,1)} %reshape.204), calls=%async_computation.2 | async-start | bytes 163840 | tf_op jit(solution)/shard_map/all_to_all | solution.py:178
  121.9 2.3 collective-permute-start.2
  124.3 11.3 %all-to-all-done.2 = bf16[32,2,576]{2,1,0:T(2,128)(2,1)S(1)} async-done(((bf16[32,2,576]{2,1,0:T(2,128)(2,1)}), bf16[32,2,576]{2,1,0:T(2,128)(2,1)S(1)}, u32[]{:S(2)}, u32[]{:S(2)}) %all-to-all-start.2) | async-done | bytes 73760 | tf_op jit(solution)/shard_map/all_to_all | solution.py:178
  142.1 4.3 %all-to-all-start.3 = ((bf16[32,2,576]{2,1,0:T(2,128)(2,1)}), bf16[32,2,576]{2,1,0:T(2,128)(2,1)S(1)}, u32[]{:S(2)}, u32[]{:S(2)}) async-start(bf16[32,2,576]{2,1,0:T(2,128)(2,1)} %reshape.206), calls=%async_computation.3 | async-start | bytes 163840 | tf_op jit(solution)/shard_map/all_to_all | solution.py:202
  147.3 13.4 %all-to-all-done.3 = bf16[32,2,576]{2,1,0:T(2,128)(2,1)S(1)} async-done(((bf16[32,2,576]{2,1,0:T(2,128)(2,1)}), bf16[32,2,576]{2,1,0:T(2,128)(2,1)S(1)}, u32[]{:S(2)}, u32[]{:S(2)}) %all-to-all-start.3) | async-done | bytes 73760 | tf_op jit(solution)/shard_map/all_to_all | solution.py:202
  163.3 3.6 %collective-permute-start.3 = (f32[2,1,16,128]{3,2,1,0:T(8,128)S(1)}, f32[2,1,16,128]{3,2,1,0:T(8,128)S(1)}, u32[]{:S(2)}, u32[]{:S(2)}) collective-permute-start(f32[2,1,16,128]{3,2,1,0:T(8,128)S(1)} %slice.597), channel_id=1, source_target_pairs={{0,16},{16,32},{32,48},{48,64},{64,80},{80,96},{96,112},{112,128},... | collective-permute-start | bytes 49160 | tf_op jit(solution)/shard_map/ppermute | solution.py:14
  167.8 28.8 %all-gather.2.cloned.1.call-done = bf16[2,48,16,48,8]{3,4,2,0,1:T(8,128)(2,1)} async-done(((bf16[2,3,16,48,8]{3,4,2,0,1:T(8,128)(2,1)}), bf16[2,48,16,48,8]{3,4,2,0,1:T(8,128)(2,1)}) %all-gather.2.cloned.1.call-update) | async-done | bytes 1179664 | tf_op jit(solution)/shard_map/all_gather | solution.py:204
  204.9 4.7 %copy.290 = f32[3,8,16,128]{0,3,2,1:T(8,128)} copy(f32[3,8,16,128]{3,2,1,0:T(8,128)S(1)} %fusion.36) | data formatting | bytes 393216 | tf_op jit(solution)/shard_map/add | solution.py:223
  209.7 7.2 %scatter_fusion.1 = f32[3,8,16,128]{0,3,2,1:T(8,128)} fusion(f32[3,8,16,128]{0,3,2,1:T(8,128)} %copy.290, s32[64]{0:T(128)S(1)} %fusion.174, f32[64,3]{1,0:T(8,128)S(1)} %copy-done.7), kind=kCustom, calls=%fused_computation.3 | custom fusion | flops 192 | bytes 3072 | tf_op jit(solution)/shard_map/scatter-add | solution.py:101
  218.4 5.2 %copy.298 = f32[3,8,16,128]{3,2,1,0:T(8,128)S(1)} copy(f32[3,8,16,128]{0,3,2,1:T(8,128)} %scatter_fusion.1) | data formatting | bytes 393216 | tf_op jit(solution)/shard_map/scatter-add | solution.py:101
  228.8 107.9 %psum.7 = f32[2,64,3]{1,0,2:T(2,128)} all-reduce(f32[2,64,3]{1,0,2:T(2,128)S(1)} %pad_maximum_fusion.9), channel_id=1, replica_groups=mesh['bulk'=32,'wide'=16] {'bulk','wide'}, use_global_device_ids=true, to_apply=%region_4.5 | all-reduce | flops 384 | bytes 3072 | tf_op jit(solution)/shard_map/psum | solution.py:229
  339.2 4.3 %collective-permute-start.7 = (f32[2,1,16,128]{3,2,1,0:T(8,128)S(1)}, f32[2,1,16,128]{3,2,1,0:T(8,128)S(1)}, u32[]{:S(2)}, u32[]{:S(2)}) collective-permute-start(f32[2,1,16,128]{3,2,1,0:T(8,128)S(1)} %slice.637), channel_id=1, source_target_pairs={{0,16},{16,32},{32,48},{48,64},{64,80},{80,96},{96,112},{112,128},... | collective-permute-start | bytes 49160 | tf_op jit(solution)/shard_map/ppermute | solution.py:14
  (206 shorter events, 57.4 us)
Async XLA Ops:
  7.2 64.4 %copy-start = (f32[16,48]{1,0:T(8,128)S(1)}, f32[16,48]{1,0:T(8,128)}, u32[]{:S(2)}) copy-start(f32[16,48]{1,0:T(8,128)} %param.24) | copy-start | bytes 9220
  8.2 67.2 %collective-permute-start.8 = (f32[2,8,1,128]{3,1,2,0:T(8,128)S(1)}, f32[2,8,1,128]{3,1,2,0:T(8,128)S(1)}, u32[]{:S(2)}, u32[]{:S(2)}) collective-permute-start(f32[2,8,1,128]{3,1,2,0:T(8,128)S(1)} %pad_maximum_fusion.7), channel_id=1, source_target_pairs={{0,1},{1,2},{2,3},{3,4},{4,5},{5,6},{6,7},{7,8},{8,9},{9,10},{10,1... | collective-permute-start | bytes 24584 | tf_op jit(solution)/shard_map/ppermute | solution.py:14
  12.8 64.5 %collective-permute-start.10 = (f32[2,8,1,128]{3,1,2,0:T(8,128)S(1)}, f32[2,8,1,128]{3,1,2,0:T(8,128)S(1)}, u32[]{:S(2)}, u32[]{:S(2)}) collective-permute-start(f32[2,8,1,128]{3,1,2,0:T(8,128)S(1)} %pad_maximum_fusion.8), channel_id=1, source_target_pairs={{0,1},{1,2},{2,3},{3,4},{4,5},{5,6},{6,7},{7,8},{8,9},{9,10},{10,1... | collective-permute-start | bytes 24584 | tf_op jit(solution)/shard_map/ppermute | solution.py:14
  15.3 131.3 %collective-permute-start.9 = (f32[2,1,16,128]{3,2,1,0:T(8,128)}, f32[2,1,16,128]{3,2,1,0:T(8,128)}, u32[]{:S(2)}, u32[]{:S(2)}) collective-permute-start(f32[2,1,16,128]{3,2,1,0:T(8,128)} %slice.653), channel_id=1, source_target_pairs={{0,16},{16,32},{32,48},{48,64},{64,80},{80,96},{96,112},{112,128},... | collective-permute-start | bytes 49160 | tf_op jit(solution)/shard_map/ppermute | solution.py:14
  20.8 141.4 %collective-permute-start.11 = (f32[2,1,16,128]{3,2,1,0:T(8,128)}, f32[2,1,16,128]{3,2,1,0:T(8,128)}, u32[]{:S(2)}, u32[]{:S(2)}) collective-permute-start(f32[2,1,16,128]{3,2,1,0:T(8,128)} %slice.669), channel_id=1, source_target_pairs={{0,16},{16,32},{32,48},{48,64},{64,80},{80,96},{96,112},{112,128},... | collective-permute-start | bytes 49160 | tf_op jit(solution)/shard_map/ppermute | solution.py:14
  25.7 14.2 %copy-start.17 = (f32[16,3]{0,1:T(4,128)S(1)}, f32[16,3]{0,1:T(4,128)}, u32[]{:S(2)}) copy-start(f32[16,3]{0,1:T(4,128)} %param.21) | copy-start | bytes 580
  50.6 31.1 %all-to-all-start = ((bf16[16,8,16,96]{3,2,1,0:T(8,128)(2,1)}), bf16[16,8,16,96]{3,2,1,0:T(8,128)(2,1)S(1)}, u32[]{:S(2)}, u32[]{:S(2)}) async-start(bf16[16,8,16,96]{3,2,1,0:T(8,128)(2,1)} %convolution_convert_fusion.1), calls=%async_computation | async-start | bytes 1048576 | tf_op jit(solution)/shard_map/all_to_all | solution.py:138
  62.1 9.3 %copy-start.16 = (f32[16,48]{1,0:T(8,128)S(1)}, f32[16,48]{1,0:T(8,128)}, u32[]{:S(2)}) copy-start(f32[16,48]{1,0:T(8,128)} %param.25) | copy-start | bytes 9220
  68.0 9.9 %collective-permute-start = (f32[2,8,1,128]{3,2,1,0:T(1,128)S(1)}, f32[2,8,1,128]{3,2,1,0:T(1,128)S(1)}, u32[]{:S(2)}, u32[]{:S(2)}) collective-permute-start(f32[2,8,1,128]{3,2,1,0:T(1,128)S(1)} %pad_maximum_fusion.3), channel_id=1, source_target_pairs={{1,0},{2,1},{3,2},{4,3},{5,4},{6,5},{7,6},{8,7},{9,8},{10,9},{11,1... | collective-permute-start | bytes 24584 | tf_op jit(solution)/shard_map/ppermute | solution.py:14
  71.4 10.3 %copy-start.2 = (f32[3,8,16,128]{3,2,1,0:T(8,128)S(1)}, f32[3,8,16,128]{3,2,1,0:T(8,128)}, u32[]{:S(2)}) copy-start(f32[3,8,16,128]{3,2,1,0:T(8,128)} %param.14) | copy-start | bytes 589828
  75.4 6.1 %collective-permute-start.1 = (f32[2,1,16,128]{3,2,1,0:T(8,128)S(1)}, f32[2,1,16,128]{3,2,1,0:T(8,128)S(1)}, u32[]{:S(2)}, u32[]{:S(2)}) collective-permute-start(f32[2,1,16,128]{3,2,1,0:T(8,128)S(1)} %slice.582), channel_id=1, source_target_pairs={{16,0},{32,16},{48,32},{64,48},{80,64},{96,80},{112,96},{128,112},... | collective-permute-start | bytes 49160 | tf_op jit(solution)/shard_map/ppermute | solution.py:14
  83.5 12.8 %all-to-all-start.1 = ((bf16[48,1,8,96]{3,2,1,0:T(8,128)(2,1)}), bf16[48,1,8,96]{3,2,1,0:T(8,128)(2,1)S(1)}, u32[]{:S(2)}, u32[]{:S(2)}) async-start(bf16[48,1,8,96]{3,2,1,0:T(8,128)(2,1)} %copy.265), calls=%async_computation.1 | async-start | bytes 196608 | tf_op jit(solution)/shard_map/all_to_all | solution.py:151
  103.5 32.1 %all-to-all-start.2 = ((bf16[32,2,576]{2,1,0:T(2,128)(2,1)}), bf16[32,2,576]{2,1,0:T(2,128)(2,1)S(1)}, u32[]{:S(2)}, u32[]{:S(2)}) async-start(bf16[32,2,576]{2,1,0:T(2,128)(2,1)} %reshape.204), calls=%async_computation.2 | async-start | bytes 163840 | tf_op jit(solution)/shard_map/all_to_all | solution.py:178
  121.9 45.0 %collective-permute-start.2 = (f32[2,8,1,128]{3,1,2,0:T(8,128)}, f32[2,8,1,128]{3,1,2,0:T(8,128)}, u32[]{:S(2)}, u32[]{:S(2)}) collective-permute-start(f32[2,8,1,128]{3,1,2,0:T(8,128)} %pad_maximum_fusion.4), channel_id=1, source_target_pairs={{0,1},{1,2},{2,3},{3,4},{4,5},{5,6},{6,7},{7,8},{8,9},{9,10},{10,1... | collective-permute-start | bytes 24584 | tf_op jit(solution)/shard_map/ppermute | solution.py:14
  142.1 18.6 %all-to-all-start.3 = ((bf16[32,2,576]{2,1,0:T(2,128)(2,1)}), bf16[32,2,576]{2,1,0:T(2,128)(2,1)S(1)}, u32[]{:S(2)}, u32[]{:S(2)}) async-start(bf16[32,2,576]{2,1,0:T(2,128)(2,1)} %reshape.206), calls=%async_computation.3 | async-start | bytes 163840 | tf_op jit(solution)/shard_map/all_to_all | solution.py:202
  146.5 50.0 %all-gather.2.cloned.1.call-start = ((), (), s32[]{:S(2)}) async-start(), calls=%async_computation.4 | async-start | bytes 3342336 | tf_op jit(solution)/shard_map/all_gather | solution.py:204
  147.3 15.7 %copy-start.5 = (f32[1,7,16,128]{3,2,1,0:T(8,128)S(1)}, f32[1,7,16,128]{3,2,1,0:T(8,128)}, u32[]{:S(2)}) copy-start(f32[1,7,16,128]{3,2,1,0:T(8,128)} %get-tuple-element.61) | copy-start | bytes 172036
  147.3 15.7 %copy-start.13 = (f32[1,8,1,128]{3,1,2,0:T(8,128)S(1)}, f32[1,8,1,128]{3,1,2,0:T(8,128)}, u32[]{:S(2)}) copy-start(f32[1,8,1,128]{3,1,2,0:T(8,128)} %get-tuple-element.114) | copy-start | bytes 12292
  163.3 4.3 %collective-permute-start.3 = (f32[2,1,16,128]{3,2,1,0:T(8,128)S(1)}, f32[2,1,16,128]{3,2,1,0:T(8,128)S(1)}, u32[]{:S(2)}, u32[]{:S(2)}) collective-permute-start(f32[2,1,16,128]{3,2,1,0:T(8,128)S(1)} %slice.597), channel_id=1, source_target_pairs={{0,16},{16,32},{32,48},{48,64},{64,80},{80,96},{96,112},{112,128},... | collective-permute-start | bytes 49160 | tf_op jit(solution)/shard_map/ppermute | solution.py:14
  167.7 31.0 %copy-start.15 = (s32[16]{0:T(128)S(1)}, s32[16]{0:T(128)}, u32[]{:S(2)}) copy-start(s32[16]{0:T(128)} %iota_add_fusion) | copy-start | bytes 196
  224.6 112.0 %collective-permute-start.4 = (f32[2,8,1,128]{3,2,1,0:T(1,128)S(1)}, f32[2,8,1,128]{3,2,1,0:T(1,128)S(1)}, u32[]{:S(2)}, u32[]{:S(2)}) collective-permute-start(f32[2,8,1,128]{3,2,1,0:T(1,128)S(1)} %pad_maximum_fusion.5), channel_id=1, source_target_pairs={{1,0},{2,1},{3,2},{4,3},{5,4},{6,5},{7,6},{8,7},{9,8},{10,9},{11,1... | collective-permute-start | bytes 24584 | tf_op jit(solution)/shard_map/ppermute | solution.py:14
  226.8 109.8 %collective-permute-start.5 = (f32[2,1,16,128]{3,2,1,0:T(8,128)S(1)}, f32[2,1,16,128]{3,2,1,0:T(8,128)S(1)}, u32[]{:S(2)}, u32[]{:S(2)}) collective-permute-start(f32[2,1,16,128]{3,2,1,0:T(8,128)S(1)} %slice.622), channel_id=1, source_target_pairs={{16,0},{32,16},{48,32},{64,48},{80,64},{96,80},{112,96},{128,112},... | collective-permute-start | bytes 49160 | tf_op jit(solution)/shard_map/ppermute | solution.py:14
  337.0 6.6 %collective-permute-start.6 = (f32[2,8,1,128]{3,1,2,0:T(8,128)S(1)}, f32[2,8,1,128]{3,1,2,0:T(8,128)S(1)}, u32[]{:S(2)}, u32[]{:S(2)}) collective-permute-start(f32[2,8,1,128]{3,1,2,0:T(8,128)S(1)} %pad_maximum_fusion.6), channel_id=1, source_target_pairs={{0,1},{1,2},{2,3},{3,4},{4,5},{5,6},{6,7},{7,8},{8,9},{9,10},{10,1... | collective-permute-start | bytes 24584 | tf_op jit(solution)/shard_map/ppermute | solution.py:14
  339.2 5.2 %collective-permute-start.7 = (f32[2,1,16,128]{3,2,1,0:T(8,128)S(1)}, f32[2,1,16,128]{3,2,1,0:T(8,128)S(1)}, u32[]{:S(2)}, u32[]{:S(2)}) collective-permute-start(f32[2,1,16,128]{3,2,1,0:T(8,128)S(1)} %slice.637), channel_id=1, source_target_pairs={{0,16},{16,32},{32,48},{48,64},{64,80},{80,96},{96,112},{112,128},... | collective-permute-start | bytes 49160 | tf_op jit(solution)/shard_map/ppermute | solution.py:14
  (15 other events, 55.6 us)
Sparse Core Ops, SparseCore 0:
  162.3 34.1 all-gather.1
where the time goes:
time: 354 us; the launch traced here: 352 us
  blocking collectives  108 us (31%)
  starting transfers between devices  69.7 us (20%)
  waiting for transfers between devices  63.8 us (18%)
  local copies, waits for them, and re-layouts  46.4 us (13%)
  other arithmetic  25.7 us (7%)
  matrix products  23.6 us (7%)
  between operations  15 us (4%)
    psum x1, blocking collectives, body(): grad_sources = lax.psum(jnp.stack(sources), ('bulk', 'wide'))  108 us
    ppermute x12, starting transfers between devices, passed_along(): return lax.ppermute(block, axis, route)  34.3 us
    all_gather x1, waiting for transfers between devices, body(): piece = lax.all_gather(returned, 'wide', axis=1, tiled=True)  28.8 us
    all_to_all x1, starting transfers between devices, body(): lax.all_to_all(mixed, 'bulk', split_axis=2, concat_axis=3, tiled=True)  17.8 us
    scatter-add x2, other arithmetic, inject(): field.at[:, mon_x, mon_y, mon_z]  14.4 us
    all_to_all x1, waiting for transfers between devices, body(): lax.all_to_all(filtered, 'bulk', split_axis=3, concat_axis=2, tiled=True)  13.4 us
    unnamed x53, local copies, waits for them, and re-layouts  11.3 us
    all_to_all x1, waiting for transfers between devices, body(): lax.all_to_all(mixed, 'bulk', split_axis=2, concat_axis=3, tiled=True)  11.3 us
  transfers between devices with their start and end apart: 17, of which 6 were waited for; matrix products, arithmetic and copies ran while one was open for 19% of the time, Pallas kernels for 0%

commit v1 on v0

v1 whole, which is shorter than its diff:
```python
import functools
import math

import jax
import jax.numpy as jnp
import ml_dtypes
import numpy as np
from jax import lax
from jax.experimental import pallas as pl
from jax.experimental.pallas import tpu as pltpu
from jax.sharding import PartitionSpec as P

NX, NY, NZ = 256, 256, 128
K = 48
OWN = 3
WIDE, BULK = 16, 32
RX, RY = 8, 16
LANES = 128
F32, BF16 = jnp.float32, jnp.bfloat16
PARAMS = pltpu.CompilerParams(vmem_limit_bytes=40 * 1024 * 1024)


def waves(freqs, places, total):
    phase = np.mod(np.asarray(freqs)[:, None] * np.asarray(places)[None, :], total)
    angle = phase.astype(np.float32) * np.float32(2.0 * math.pi / total)
    return np.cos(angle).astype(np.float32), np.sin(angle).astype(np.float32)


def rounded(table):
    return np.asarray(table, np.float32).astype(ml_dtypes.bfloat16)


def make_tables():
    mode = np.arange(K)
    plane = np.where(mode < K // 2, mode, mode - K)
    cz, sz = waves(mode, np.arange(NZ), NZ)
    cx, sx = (rounded(t) for t in waves(plane, np.arange(NX), NX))
    cy, sy = (rounded(t) for t in waves(plane, np.arange(NY), NY))
    scale = np.float32(1.0 / math.sqrt(NX * NY * NZ))
    back = np.float32(1.0 / math.sqrt(K**3))
    fz, gz = rounded(cz * scale), rounded(-sz * scale)
    bz, hz = rounded(cz * back), rounded(sz * back)
    out = {}
    lift_z = np.zeros((LANES, LANES), ml_dtypes.bfloat16)
    back_z = np.zeros((LANES, LANES), ml_dtypes.bfloat16)
    for w in range(WIDE):
        for i in range(OWN):
            lift_z[:, w * 8 + i] = fz[w * OWN + i]
            lift_z[:, w * 8 + OWN + i] = gz[w * OWN + i]
            back_z[w * 8 + i] = bz[w * OWN + i]
            back_z[w * 8 + OWN + i] = -hz[w * OWN + i]
    out["lift_z"], out["back_z"] = lift_z, back_z

    lane = np.arange(LANES)
    y_of = np.concatenate([(h * 8 + lane % 8) * RY + lane // 8 for h in range(2)])
    fwd_y = np.zeros((512, 256), ml_dtypes.bfloat16)
    fwd_y[:256, :K] = cy[:, y_of].T
    fwd_y[256:, :K] = sy[:, y_of].T
    fwd_y[:256, 128 : 128 + K] = -sy[:, y_of].T
    fwd_y[256:, 128 : 128 + K] = cy[:, y_of].T
    out["fwd_y"] = fwd_y

    fwd_x = np.zeros((2, LANES, NX), ml_dtypes.bfloat16)
    fwd_x[0, :K], fwd_x[0, 64 : 64 + K] = cx, -sx
    fwd_x[1, :K], fwd_x[1, 64 : 64 + K] = sx, cx
    out["fwd_x"] = fwd_x

    inv_x = np.zeros((BULK, 16, LANES), ml_dtypes.bfloat16)
    for b in range(BULK):
        x_of = (b * RX + np.array([0, 1, 2, 3, 4, 5, 6, 7, 8, -1])) % NX
        inv_x[b, :10, :K] = cx[:, x_of].T
        inv_x[b, :10, 64 : 64 + K] = -sx[:, x_of].T
    out["inv_x"] = inv_x

    inv_y = np.zeros((LANES, 384), ml_dtypes.bfloat16)
    inv_y[:K, :256], inv_y[64 : 64 + K, :256] = cy, -sy
    for w in range(WIDE):
        for h, y in ((0, w * RY + RY), (7, w * RY - 1)):
            inv_y[:K, 256 + w * 8 + h] = cy[:, y % NY]
            inv_y[64 : 64 + K, 256 + w * 8 + h] = -sy[:, y % NY]
    out["inv_y"] = inv_y

    at_x = np.zeros((2, LANES, NX), ml_dtypes.bfloat16)
    at_x[0, :K], at_x[0, 64 : 64 + K] = cx, -sx
    at_x[1, :K], at_x[1, 64 : 64 + K] = sx, cx
    out["at_x"] = at_x
    out["at_y"] = np.stack([cy, sy])
    at_z = np.zeros((WIDE, 2, 8, NZ), ml_dtypes.bfloat16)
    for w in range(WIDE):
        at_z[w, 0, :OWN] = bz[w * OWN : (w + 1) * OWN]
        at_z[w, 1, :OWN] = hz[w * OWN : (w + 1) * OWN]
    out["at_z"] = at_z
    return out


TABLES = make_tables()


def iota(shape, axis):
    return lax.broadcasted_iota(jnp.int32, shape, axis)


def exchange(tiles, block, axis):
    tiles = list(tiles)
    shape = tiles[0].shape
    size = shape[axis]
    place = iota(shape, axis) // block
    step = 1
    while step < len(tiles):
        high = (place // step) % 2 == 1
        new = list(tiles)
        for low in range(len(tiles)):
            if low & step:
                continue
            u, v = tiles[low], tiles[low + step]
            new[low] = jnp.where(high, pltpu.roll(v, step * block, axis), u)
            new[low + step] = jnp.where(high, v, pltpu.roll(u, size - step * block, axis))
        tiles = new
        step *= 2
    return tiles


def z_ahead(v):
    axis = v.ndim - 1
    return jnp.where(iota(v.shape, axis) < NZ - 1, pltpu.roll(v, NZ - 1, axis), 0.0)


def z_behind(v):
    axis = v.ndim - 1
    return jnp.where(iota(v.shape, axis) > 0, pltpu.roll(v, 1, axis), 0.0)


def x_ahead(v):
    return jnp.concatenate([v[1:], v[:1]], 0)


def x_behind(v):
    return jnp.concatenate([v[-1:], v[:-1]], 0)


def y_ahead(v):
    return pltpu.roll(v, v.shape[1] - 1, 1)


def y_behind(v):
    return pltpu.roll(v, 1, 1)


def curl_ahead(fx, fy, fz):
    return (
        (y_ahead(fz) - fz) - (z_ahead(fy) - fy),
        (z_ahead(fx) - fx) - (x_ahead(fz) - fz),
        (x_ahead(fy) - fy) - (y_ahead(fx) - fx),
    )


def curl_behind(fx, fy, fz):
    return (
        (fz - y_behind(fz)) - (fy - z_behind(fy)),
        (fx - z_behind(fx)) - (fz - x_behind(fz)),
        (fy - x_behind(fy)) - (fx - y_behind(fx)),
    )


def place_of(flat):
    return flat >> 15, (flat >> 7) & (NY - 1), flat & (NZ - 1)


def lift_kernel(
    here, mon, src, weights, perm, electric, magnetic, material, table,
    out, taken, inverse, field, scaled, held,
):
    b, w = here[0], here[1]
    eps = jnp.zeros((RX, RY, NZ), F32)
    cells = material[...]
    for level in range(8):
        eps = jnp.where(cells == level, perm[level], eps)
    inv = 1.0 / eps
    inverse[...] = inv
    lane = iota((1, NZ), 1)
    field[...] = electric[...]

    def add(i, carry):
        x, y, z = place_of(mon[i])
        lx, ly = x - b * RX, y - w * RY

        @pl.when((lx >= 0) & (lx < RX) & (ly >= 0) & (ly < RY))
        def _():
            for c in range(3):
                row = field[c, lx, pl.ds(ly, 1), :]
                weight = weights[(64 + i) * 3 + c]
                field[c, lx, pl.ds(ly, 1), :] = row + jnp.where(lane == z, weight, 0.0)

        return carry

    lax.fori_loop(0, 64, add, 0)
    rows = field[...].reshape(3 * RX * RY, NZ).astype(BF16)
    modes = jnp.dot(rows, table[...], preferred_element_type=F32)
    modes = modes.reshape(3, RX, 2, 8, LANES)
    tiles = exchange([modes[:, x].reshape(6, 8, LANES) for x in range(RX)], 1, 1)
    tiles = [t.reshape(3, 2, 8, LANES) for t in tiles]
    tiles = exchange([tiles[y % 8][:, y // 8] for y in range(RY)], 8, 2)
    out[...] = jnp.concatenate([t.reshape(24, LANES) for t in tiles], 0).astype(BF16)

    zero = jnp.zeros((12, 32, NZ), F32)
    for c in range(3):
        scaled[c] = zero
        held[c] = zero
    for c in range(3):
        scaled[c, 2:10, 8:24, :] = 0.5 * inv * field[c]
        held[c, 2:10, 8:24, :] = magnetic[c]
    taken[...] = jnp.zeros((8, LANES), F32)
    spot_row, spot_lane = iota((8, LANES), 0), iota((8, LANES), 1)

    def take(i, carry):
        x, y, z = place_of(src[i])
        lx, ly = x - b * RX, y - w * RY

        @pl.when((lx >= -1) & (lx <= RX) & (ly >= -1) & (ly <= RY))
        def _():
            def a(c, dx, dy):
                return scaled[c, lx + 2 + dx, pl.ds(ly + 8 + dy, 1), :]

            def h(c, dx, dy):
                old = held[c, lx + 2 + dx, pl.ds(ly + 8 + dy, 1), :]
                if c == 0:
                    near = a(1, dx, dy)
                    turn = (a(2, dx, dy + 1) - a(2, dx, dy)) - (z_ahead(near) - near)
                elif c == 1:
                    near = a(0, dx, dy)
                    turn = (z_ahead(near) - near) - (a(2, dx + 1, dy) - a(2, dx, dy))
                else:
                    turn = (a(1, dx + 1, dy) - a(1, dx, dy)) - (a(0, dx, dy + 1) - a(0, dx, dy))
                return old + turn

            left = jnp.where(x > 0, 1.0, 0.0)
            down = jnp.where(y > 0, 1.0, 0.0)
            hx, hy, hz = h(0, 0, 0), h(1, 0, 0), h(2, 0, 0)
            hx_y, hz_y = down * h(0, 0, -1), down * h(2, 0, -1)
            hy_x, hz_x = left * h(1, -1, 0), left * h(2, -1, 0)
            curls = (
                (hz - hz_y) - (hy - z_behind(hy)),
                (hx - z_behind(hx)) - (hz - hz_x),
                (hy - hy_x) - (hx - hx_y),
            )
            mine = jnp.where((lx >= 0) & (lx < RX) & (ly >= 0) & (ly < RY), 1.0, 0.0)
            cx, cy = jnp.clip(lx, 0, RX - 1), jnp.clip(ly, 0, RY - 1)
            got = taken[...]
            for c in range(3):
                old = mine * field[c, cx, pl.ds(cy, 1), :]
                for n, row in ((0, old - 0.5 * curls[c]), (1, old)):
                    value = jnp.sum(jnp.where(lane == z, row, 0.0), axis=1, keepdims=True)
                    spot = (spot_row == n * 3 + c) & (spot_lane == i)
                    got = got + jnp.where(spot, value, 0.0)
            taken[...] = got

        return carry

    lax.fori_loop(0, 64, take, 0)


def middle_kernel(lines, taken, table, out):
    got = lines[...].astype(F32).reshape(WIDE, 24, LANES)
    halves = [exchange([got[h * 8 + i] for i in range(8)], 1, 1) for h in range(2)]
    rows = [
        jnp.concatenate([halves[0][k], halves[1][k], halves[0][OWN + k], halves[1][OWN + k]], 1)
        for k in range(OWN)
    ]
    lhs = jnp.concatenate(rows, 0).astype(BF16)
    found = jnp.dot(lhs, table[...], preferred_element_type=F32)
    lane = iota((8, LANES), 1)
    src = taken[...]
    high = src.astype(BF16).astype(F32)
    extra = (high, src - high)
    parts = []
    for part in range(2):
        tiles = [jnp.zeros((8, LANES), F32) for _ in range(4)]
        for d in range(3):
            for k in range(OWN):
                start = (d * OWN + k) * K
                tile, offset = start // LANES, start % LANES
                row = (k * 3 + d) * 8
                piece = found[row : row + 8, part * LANES : (part + 1) * LANES]
                if offset:
                    piece = pltpu.roll(piece, offset, 1)
                if offset + K <= LANES:
                    tiles[tile] = tiles[tile] + piece
                else:
                    tiles[tile] = tiles[tile] + jnp.where(lane >= offset, piece, 0.0)
                    tiles[tile + 1] = tiles[tile + 1] + jnp.where(lane < offset, piece, 0.0)
        tiles[3] = jnp.where(lane >= 64, pltpu.roll(extra[part], 64, 1), tiles[3])
        parts += tiles
    out[...] = jnp.concatenate(parts, 1).astype(BF16)


def phase_kernel(here, cells, at_x, at_y, at_z, phase_x, phase_yz):
    w = here[1]
    flat = cells[...]
    x, y, z = place_of(flat)
    first = iota((1, LANES), 1) < 64
    hot_x = jnp.where(iota((NX, LANES), 0) == x, 1.0, 0.0)
    real = jnp.where(first, hot_x, 0.0).astype(BF16)
    imag = jnp.where(first, 0.0, hot_x).astype(BF16)
    phase_x[...] = (
        jnp.dot(at_x[0], real, preferred_element_type=F32)
        + jnp.dot(at_x[1], imag, preferred_element_type=F32)
    ).astype(BF16)
    hot_y = jnp.where(iota((NY, LANES), 0) == y, 1.0, 0.0).astype(BF16)
    hot_z = jnp.where(iota((NZ, LANES), 0) == z, 1.0, 0.0).astype(BF16)
    cy = jnp.dot(at_y[0], hot_y, preferred_element_type=F32)
    sy = jnp.dot(at_y[1], hot_y, preferred_element_type=F32)
    cz = jnp.dot(at_z[w, 0].astype(F32).astype(BF16), hot_z, preferred_element_type=F32)
    sz = jnp.dot(at_z[w, 1].astype(F32).astype(BF16), hot_z, preferred_element_type=F32)
    for k in range(OWN):
        ck, sk = cz[k : k + 1], sz[k : k + 1]
        phase_yz[k * K : (k + 1) * K, :] = jnp.where(
            first, cy * ck - sy * sk, -(sy * ck + cy * sk)
        )


def filter_kernel(
    here, spectrum, coef_a, coef_b, fwd_x, inv_x, inv_y, phase_x, phase_yz, out, rows
):
    b = here[0]
    lane = iota((1, LANES), 1)
    got_r, got_i = spectrum[:, 0:512], spectrum[:, 512:1024]
    full = jnp.dot(fwd_x[0], got_r, preferred_element_type=F32) + jnp.dot(
        fwd_x[1], got_i, preferred_element_type=F32
    )
    full = full.T
    size = OWN * K
    field = [full[d * size : (d + 1) * size] for d in range(3)]
    turned = [pltpu.roll(f, 64, 1) for f in field]
    sign = jnp.where(lane < 64, 1.0, -1.0)
    gap = jnp.zeros((16, LANES), F32)
    right = []
    shares = []
    for e in range(3):
        q = jnp.zeros((size, LANES), F32)
        for d in range(3):
            at = (e * 3 + d) * size
            q = q + coef_a[at : at + size] * field[d] + coef_b[at : at + size] * turned[d]
        other = pltpu.roll(q, 64, 1) * sign
        for k in range(OWN):
            right += [q[k * K : (k + 1) * K], gap, other[k * K : (k + 1) * K], gap]
        for k in range(OWN):
            right += [other[k * K : (k + 1) * K], gap, -q[k * K : (k + 1) * K], gap]
        near = jnp.dot(q.astype(BF16), phase_x[...], preferred_element_type=F32)
        line = jnp.sum(near * phase_yz[...], axis=0, keepdims=True)
        shares.append(line + pltpu.roll(line, 64, 1))
    stacked = jnp.concatenate(right, 0).astype(BF16)
    at_b = inv_x[b]
    along = lax.dot_general(
        at_b, stacked, (((1,), (1,)), ((), ())), preferred_element_type=F32
    )
    rows[...] = jnp.zeros((32, 8, LANES), F32)
    for e in range(3):
        for m in range(6):
            tile = (e * 6 + m) * LANES
            for x in range(10):
                rows[e * 10 + x, m : m + 1, :] = along[x : x + 1, tile : tile + LANES]
    lhs = rows[...].reshape(256, LANES).astype(BF16)
    wide = jnp.dot(lhs, inv_y[...], preferred_element_type=F32).reshape(32, 8, 384)
    near = []
    for low in range(8):
        group = [wide[high * 8 + low, :, c * LANES : (c + 1) * LANES] for high in range(4) for c in range(2)]
        near.append(jnp.stack(group))
    near = exchange(near, 16, 2)
    edge = []
    for low in range(16):
        edge.append(jnp.stack([wide[high * 16 + low, :, 256:384] for high in range(2)]))
    edge = exchange(edge, 8, 2)

    extra_r = spectrum[:, 384:512].astype(F32).reshape(BULK, 8, LANES).sum(0)
    extra_i = spectrum[:, 896:1024].astype(F32).reshape(BULK, 8, LANES).sum(0)
    total = pltpu.roll(extra_r + extra_i, 64, 1)
    row = iota((8, LANES), 0)
    for e in range(3):
        total = total + jnp.where(row == e, shares[e], 0.0)
    total = jnp.where(lane < 64, total, 0.0)
    high = total.astype(BF16).astype(F32)
    last = high + pltpu.roll(total - high, 64, 1)
    blocks = []
    for w in range(WIDE):
        tiles = [near[w % 8][high_x * 2 + w // 8] for high_x in range(4)]
        tiles += [edge[w][high_x] for high_x in range(2)] + [last]
        blocks.append(jnp.concatenate(tiles, 1))
    out[...] = jnp.concatenate(blocks, 0).astype(BF16)


def first_kernel(
    here, mon, weights, electric, magnetic, inverse, saved, x_low, x_high, y_low, y_high,
    early, curled, factor, grad, ready, e_ext, h_ext, g_ext,
):
    b, w = here[0], here[1]
    lane = iota((1, NZ), 1)
    for c in range(7):
        to = e_ext.at[c] if c < 3 else (h_ext.at[c - 3] if c < 6 else g_ext)
        own = electric[c] if c < 3 else (magnetic[c - 3] if c < 6 else inverse[...])
        to[0:8, 0:16, :] = own
        to[8:10, 0:16, :] = x_high[c]
        to[10:12, 0:16, :] = x_low[c]
        low, high = y_low[c * 12 : (c + 1) * 12], y_high[c * 12 : (c + 1) * 12]
        to[:, 16:24, :] = jnp.concatenate([high, jnp.zeros((12, 4, NZ), F32), low], 1)

    def inject(ref, which):
        def add(i, carry):
            x, y, z = place_of(mon[i])
            lx, ly = x - b * RX, y - w * RY

            @pl.when((lx >= -2) & (lx < RX + 2) & (ly >= -2) & (ly < RY + 2))
            def _():
                px = jnp.where(lx < 0, lx + 12, lx)
                py = jnp.where(ly < 0, ly + 24, ly)
                for c in range(3):
                    row = ref[c, px, pl.ds(py, 1), :]
                    weight = weights[(which * 64 + i) * 3 + c]
                    ref[c, px, pl.ds(py, 1), :] = row + jnp.where(lane == z, weight, 0.0)

            return carry

        lax.fori_loop(0, 64, add, 0)

    inject(e_ext, 1)
    g = g_ext[...]
    half = 0.5 * g
    a = [half * e_ext[c] for c in range(3)]
    spot_x = iota((12, 24, 1), 0)
    spot_y = iota((12, 24, 1), 1)
    outside = ((spot_x >= 10) & (b == 0)) | ((spot_y >= 22) & (w == 0))
    inside = jnp.where(outside, 0.0, 1.0)
    turned = curl_ahead(*a)
    h = [h_ext[c] + inside * turned[c] for c in range(3)]
    back = curl_behind(*h)
    for c in range(3):
        e_ext[c] = e_ext[c] - 0.5 * back[c]
    inject(e_ext, 0)
    for c in range(3):
        early[c, 0:9] = e_ext[c, 0:9]
        early[c, 9:10] = e_ext[c, 11:12]
        curled[c, 0:9] = h[c][0:9]
        curled[c, 9:10] = h[c][11:12]
    factor[0:9] = half[0:9]
    factor[9:10] = half[11:12]

    near = inverse[...]
    for step in range(2):
        s = [saved[step, c].astype(F32) for c in range(3)]
        before_x = {c: jnp.concatenate([x_low[7 + step, c - 1 : c], s[c][:-1]], 0) for c in (1, 2)}
        at = 84 + step * 8
        before_y = {}
        for c in (0, 2):
            edge = y_low[at : at + 8, c // 2 : c // 2 + 1, :]
            first = iota((RX, RY, NZ), 1) == 0
            before_y[c] = jnp.where(first, edge, pltpu.roll(s[c], 1, 1))
        curls = (
            (s[2] - before_y[2]) - (s[1] - z_behind(s[1])),
            (s[0] - z_behind(s[0])) - (s[2] - before_x[2]),
            (s[1] - before_x[1]) - (s[0] - before_y[0]),
        )
        if step == 0:
            for c in range(3):
                ready[c] = near * curls[c]
        else:
            total = jnp.zeros((RX, RY, NZ), F32)
            for c in range(3):
                total = total + a[c][0:8, 0:16] * near * curls[c]
            grad[...] = -total


def second_kernel(
    here, lines, table, early, curled, factor, first_grad, ready, injected,
    grad_e, grad_h, grad_eps, sources,
):
    b, w = here[0], here[1]
    modes = lines[:, 0:768]
    back = lax.dot_general(
        modes, table[...], (((0,), (0,)), ((), ())), preferred_element_type=F32
    )
    main = back[0:512].reshape(32, 16, NZ)
    edge = back[512:768].reshape(32, 8, NZ)
    half = factor[...]
    e1 = []
    for c in range(3):
        at = slice(c * 10, c * 10 + 10)
        e1.append(early[c] + jnp.concatenate([main[at], edge[at]], 1))
    a = [half * e for e in e1]
    spot_x = iota((10, 24, 1), 0)
    spot_y = iota((10, 24, 1), 1)
    outside = ((spot_x == 9) & (b == 0)) | ((spot_y == 23) & (w == 0))
    inside = jnp.where(outside, 0.0, 1.0)
    turned = curl_ahead(*a)
    h = [curled[c] + inside * turned[c] for c in range(3)]
    backed = curl_behind(*h)
    total = first_grad[...]
    for c in range(3):
        grad_h[c] = h[c][0:8, 0:16]
        grad_e[c] = e1[c][0:8, 0:16] - 0.5 * backed[c][0:8, 0:16]
        total = total - a[c][0:8, 0:16] * ready[c]
    grad_eps[...] = total
    got = lines[:, 768:896].astype(F32).reshape(WIDE, 8, LANES).sum(0)
    got = got + pltpu.roll(got, 64, 1) + injected[...]
    columns = got.T
    sources[0] = columns[0:64, 0:3]
    sources[1] = columns[0:64, 3:6]


def call(kernel, outs, in_smem, count, scratch=(), flops=0, moved=0):
    smem, vmem = pl.BlockSpec(memory_space=pltpu.SMEM), pl.BlockSpec(memory_space=pltpu.VMEM)
    return pl.pallas_call(
        kernel,
        out_shape=outs,
        in_specs=[smem if i in in_smem else vmem for i in range(count)],
        out_specs=jax.tree.map(lambda _: vmem, outs),
        scratch_shapes=list(scratch),
        compiler_params=PARAMS,
        cost_estimate=pl.CostEstimate(flops=flops, bytes_accessed=moved, transcendentals=0),
    )


def shape(*dims, dtype=F32):
    return jax.ShapeDtypeStruct(dims, dtype)


def passed_along(block, axis, distance):
    devices = range(lax.axis_size(axis))
    route = [(i - distance, i) for i in devices if i - distance in devices]
    return lax.ppermute(block, axis, route)


def tables_of(name):
    return jnp.asarray(TABLES[name])


def body(
    seed_electric, seed_magnetic, saved_magnetic, material, permittivity, source_cells,
    monitor_cells, monitor_weights, lift_weight, project_weight, mode_mix, gain_first, gain_second,
):
    bulk, wide = lax.axis_index("bulk"), lax.axis_index("wide")
    here = jnp.stack([bulk, wide]).astype(jnp.int32)
    weights = monitor_weights.reshape(-1)

    payload, taken, inverse = call(
        lift_kernel,
        (shape(384, LANES, dtype=BF16), shape(8, LANES), shape(RX, RY, NZ)),
        range(5),
        9,
        [pltpu.VMEM((3, RX, RY, NZ), F32)] + [pltpu.VMEM((3, 12, 32, NZ), F32)] * 2,
        flops=13_000_000,
        moved=700_000,
    )(
        here, monitor_cells, source_cells, weights, permittivity,
        seed_electric, seed_magnetic, material, tables_of("lift_z"),
    )
    lines = lax.all_to_all(payload, "wide", split_axis=0, concat_axis=0, tiled=True)

    g = inverse[None]
    own = jnp.concatenate([seed_electric, seed_magnetic, g], 0)
    saved = saved_magnetic.astype(F32)
    x_low = passed_along(
        jnp.concatenate([own[:, 6:8], saved[:, 1:3, 7]], 0), "bulk", 1
    )
    x_high = passed_along(own[:, 0:2], "bulk", -1)
    block = jnp.concatenate([own, x_high, x_low[:7]], 1)
    lows = jnp.stack([saved[:, 0, :, 15], saved[:, 2, :, 15]], 2).reshape(16, 2, NZ)
    y_low = passed_along(
        jnp.concatenate([block[:, :, 14:16].reshape(84, 2, NZ), lows], 0), "wide", 1
    )
    y_high = passed_along(block[:, :, 0:2].reshape(84, 2, NZ), "wide", -1)

    spectrum = call(
        middle_kernel,
        shape(8, 1024, dtype=BF16),
        (),
        3,
        flops=20_000_000,
        moved=400_000,
    )(lines, taken, tables_of("fwd_y"))
    gathered = lax.all_gather(spectrum, "bulk", axis=0, tiled=True)

    cells = jnp.concatenate([source_cells, source_cells]).reshape(1, LANES)
    phase_x, phase_yz = call(
        phase_kernel,
        (shape(LANES, LANES, dtype=BF16), shape(OWN * K, LANES)),
        (0,),
        5,
        flops=20_000_000,
        moved=400_000,
    )(here, cells, tables_of("at_x"), tables_of("at_y"), tables_of("at_z"))

    mix = lax.dynamic_slice_in_dim(mode_mix, wide * OWN, OWN, 1).astype(F32)
    mixed = jnp.sum(
        lift_weight.T[None, None, :, :, None] * mix[:, :, None, :, :], axis=3
    )
    joint = (
        project_weight[None, :, None, None, None, :]
        * mixed.transpose(0, 2, 1, 3)[:, None, :, :, None, :]
        * gain_second.T[None, None, None, None, :, :]
    ).reshape(2, 9 * OWN * K, 16)
    blank = jnp.zeros((16, 16), F32)
    gain_a = jnp.concatenate([gain_first, blank, gain_first, blank], 1)
    gain_b = jnp.concatenate([-gain_first, blank, gain_first, blank], 1)
    coef_a = jnp.dot(joint[0], gain_a, precision=lax.Precision.HIGHEST)
    coef_b = jnp.dot(joint[1], gain_b, precision=lax.Precision.HIGHEST)
    injected = jnp.sum(
        jnp.where(
            source_cells[None, :, None] == monitor_cells[None, None, :],
            monitor_weights[0].T[:, None, :],
            0.0,
        ),
        axis=2,
    )
    injected = jnp.pad(injected, ((0, 5), (0, 64)))

    early, curled, factor, first_grad, ready = call(
        first_kernel,
        (
            shape(3, 10, 24, NZ), shape(3, 10, 24, NZ), shape(10, 24, NZ),
            shape(RX, RY, NZ), shape(3, RX, RY, NZ),
        ),
        range(3),
        11,
        [pltpu.VMEM((3, 12, 24, NZ), F32)] * 2 + [pltpu.VMEM((12, 24, NZ), F32)],
        flops=10_000_000,
        moved=3_000_000,
    )(
        here, monitor_cells, weights, seed_electric, seed_magnetic, inverse, saved_magnetic,
        x_low, x_high, y_low, y_high,
    )

    sent = call(
        filter_kernel,
        shape(128, 896, dtype=BF16),
        (0,),
        9,
        [pltpu.VMEM((32, 8, LANES), F32)],
        flops=200_000_000,
        moved=3_000_000,
    )(
        here, gathered, coef_a, coef_b, tables_of("fwd_x"), tables_of("inv_x"),
        tables_of("inv_y"), phase_x, phase_yz,
    )
    returned = lax.all_to_all(sent, "wide", split_axis=0, concat_axis=0, tiled=True)
    return call(
        second_kernel,
        (
            shape(3, RX, RY, NZ), shape(3, RX, RY, NZ), shape(RX, RY, NZ), shape(2, 64, 3),
        ),
        (0,),
        9,
        flops=40_000_000,
        moved=4_000_000,
    )(
        here, returned, tables_of("back_z"), early, curled, factor, first_grad, ready, injected
    )


def solution(mesh):
    field = P(None, "bulk", "wide", None)
    return jax.shard_map(
        body,
        mesh=mesh,
        in_specs=(
            field, field, P(None, None, "bulk", "wide", None), P("bulk", "wide", None),
            P(), P(), P(), P(), P(), P(), P(), P(), P(),
        ),
        out_specs=(field, field, P("bulk", "wide", None), P()),
        check_vma=False,
    )
```

time: 354 us -> 141 us (0.40)
  waiting for transfers between devices: 63.8 us -> 3.77 us
  local copies, waits for them, and re-layouts: 46.4 us -> 8.37 us
  blocking collectives: 108 us -> 71.7 us
  starting transfers between devices: 69.7 us -> 38.5 us
  other arithmetic: 25.7 us -> 1.65 us
  matrix products: 23.6 us -> 1.47 us
  between operations: 15 us -> 1.08 us
  Pallas kernels: 0 us -> 13.3 us
    psum x1 -> x0, blocking collectives: 108 us -> none  [body(): grad_sources = lax.psum(jnp.stack(sources), ('bulk', 'wide'))]
    all_gather x0 -> x1, blocking collectives: none -> 71.7 us  [body(): gathered = lax.all_gather(spectrum, 'bulk', axis=0, tiled=True)]
    all_to_all x4 -> x2, waiting for transfers between devices: 30.6 us -> 0.01 us  [the longest x1 0.01 us: body(): lax.all_to_all(sent, 'wide', split_axis=0, concat_axis=0, tiled=True)]
    all_gather x1 -> x0, waiting for transfers between devices: 28.8 us -> none  [body(): piece = lax.all_gather(returned, 'wide', axis=1, tiled=True)]
    ppermute x12 -> x4, starting transfers between devices: 34.3 us -> 8.05 us  [passed_along(): return lax.ppermute(block, axis, route)]
    dot_general x23 -> x2, matrix products: 23.6 us -> 1.47 us  [the longest x1 0.74 us: body(): coef_a = jnp.dot(joint[0], gain_a, precision=lax.Precision.HIGHEST)]
    scatter-add x2 -> x0, other arithmetic: 14.4 us -> none  [inject(): field.at[:, mon_x, mon_y, mon_z]]
    pallas_call x0 -> x6, Pallas kernels: none -> 13.3 us  [the longest x1 4.21 us: body(): call(lift_kernel, (shape(384, LANES, dtype=BF16), shape(8, LANES), shape(...]
  transfers between devices with their start and end apart: 17 -> 6, of which waited for: 6 -> 1; matrix products, arithmetic and copies ran while one was open for 19% -> 3% of each run, Pallas kernels for 0% -> 5%
where the time goes in v1:
time: 141 us; the launch traced here: 140 us
  blocking collectives  71.7 us (51%)
  starting transfers between devices  38.5 us (27%)
  Pallas kernels  13.3 us (9%)
  local copies, waits for them, and re-layouts  8.37 us (6%)
  waiting for transfers between devices  3.77 us (3%)
  other arithmetic  1.65 us (1%)
  matrix products  1.47 us (1%)
    all_gather x1, blocking collectives, body(): gathered = lax.all_gather(spectrum, 'bulk', axis=0, tiled=True)  71.7 us
    all_to_all x1, starting transfers between devices, body(): lax.all_to_all(sent, 'wide', split_axis=0, concat_axis=0, tiled=True)  20 us
    all_to_all x1, starting transfers between devices, body(): lax.all_to_all(payload, 'wide', split_axis=0, concat_axis=0, tiled=True)  10.5 us
    ppermute x4, starting transfers between devices, passed_along(): return lax.ppermute(block, axis, route)  8.05 us
    unnamed x51, local copies, waits for them, and re-layouts  7.19 us
    pallas_call x1, Pallas kernels, body(): call(lift_kernel, (shape(384, LANES, dtype=BF16), shape(8, LANES), shape(...  4.21 us
    ppermute x4, waiting for transfers between devices, passed_along(): return lax.ppermute(block, axis, route)  3.77 us
    pallas_call x1, Pallas kernels, body(): call(first_kernel, (shape(3, 10, 24, NZ), shape(3, 10, 24, NZ), shape(10,...  3.5 us
  transfers between devices with their start and end apart: 6, of which 1 were waited for; matrix products, arithmetic and copies ran while one was open for 3% of the time, Pallas kernels for 5%

profile of v1, /device:TPU:1, one launch (start us, length us, event | category | flops | bytes accessed | tf_op | source)
XLA Modules:
  0.0 139.8 jit_solution(12284521724505205735)
XLA Ops:
  0.7 0.8 copy.47
  1.8 0.9 copy-done.1
  2.7 0.9 copy-done.3
  3.6 0.8 copy-done.10
  4.5 0.8 copy-done.14
  5.2 0.7 copy-done.15
  5.9 0.7 copy-done.17
  7.2 4.2 %shard_map.237 = (bf16[384,128]{1,0:T(8,128)(2,1)}, f32[8,128]{1,0:T(8,128)S(1)}, f32[8,16,128]{2,1,0:T(8,128)S(1)}) custom-call(s32[2]{0:T(128)S(1)} %pad_add_fusion.here, s32[64]{0:T(128)S(1)} %copy-done.15, s32[64]{0:T(128)S(1)} %copy-done.17, f32[384]{0:T(512)S(1)} %reshape.79.weights, f32[8]{0:T(128)S(1)} %copy-done.19, ...), custom_call_target="tpu_custom_call" | custom-call | flops 13000000 | bytes 700000 | tf_op jit(solution)/shard_map/pallas_call | solution.py:543
  11.4 10.5 %all-to-all-start = ((bf16[16,24,128]{2,1,0:T(8,128)(2,1)}), bf16[16,24,128]{2,1,0:T(8,128)(2,1)S(1)}, u32[]{:S(2)}, u32[]{:S(2)}) async-start(bf16[16,24,128]{2,1,0:T(8,128)(2,1)} %bitcast.2), calls=%async_computation | async-start | bytes 196608 | tf_op jit(solution)/shard_map/all_to_all | solution.py:555
  21.9 1.0 copy_convert_fusion
  22.9 1.3 collective-permute-start
  24.3 1.3 collective-permute-start.1
  27.2 0.7 fusion.3.coef_a
  28.0 0.7 fusion.4.coef_b
  28.8 0.8 shard_map.239
  30.0 71.7 %all_gather.3.spectrum = bf16[256,1024]{1,0:T(8,128)(2,1)S(1)} all-gather(bf16[8,1024]{1,0:T(8,128)(2,1)S(1)} %shard_map.238), channel_id=1, replica_groups=mesh['bulk'=32,'wide'=16] {'bulk'}, dimensions={0}, use_global_device_ids=true | all-gather | bytes 540672 | tf_op jit(solution)/shard_map/all_gather | solution.py:579
  101.7 2.8 %shard_map.240 = bf16[128,896]{1,0:T(8,128)(2,1)} custom-call(s32[2]{0:T(128)S(1)} %pad_add_fusion.here, bf16[256,1024]{1,0:T(8,128)(2,1)S(1)} %all_gather.3.spectrum, f32[1296,128]{1,0:T(8,128)S(1)} %fusion.3.coef_a, f32[1296,128]{1,0:T(8,128)S(1)} %fusion.4.coef_b, bf16[2,128,256]{2,1,0:T(8,128)(2,1)S(1)} %copy-done.6, bf16[32,16,128]{2,1,0:T(8,128)(2,1)S(1)} %copy-done.8, ...), custom_call_target="tpu_custom_call" | custom-call | flops 200000000 | bytes 3000000 | tf_op jit(solution)/shard_map/pallas_call | solution.py:631
  104.5 20.0 %all-to-all-start.1 = ((bf16[16,8,896]{2,1,0:T(8,128)(2,1)}), bf16[16,8,896]{2,1,0:T(8,128)(2,1)S(1)}, u32[]{:S(2)}, u32[]{:S(2)}) async-start(bf16[16,8,896]{2,1,0:T(8,128)(2,1)} %bitcast.10), calls=%async_computation.1 | async-start | bytes 458752 | tf_op jit(solution)/shard_map/all_to_all | solution.py:643
  124.6 3.5 %collective-permute-start.2 = (f32[100,2,128]{2,1,0:T(2,128)S(1)}, f32[100,2,128]{2,1,0:T(2,128)S(1)}, u32[]{:S(2)}, u32[]{:S(2)}) collective-permute-start(f32[100,2,128]{2,1,0:T(2,128)S(1)} %maximum_maximum_fusion), channel_id=1, source_target_pairs={{0,1},{1,2},{2,3},{3,4},{4,5},{5,6},{6,7},{7,8},{8,9},{9,10},{10,1... | collective-permute-start | bytes 307208 | tf_op jit(solution)/shard_map/ppermute | solution.py:528
  128.1 1.9 %collective-permute-start.3 = (f32[84,2,128]{2,1,0:T(2,128)S(1)}, f32[84,2,128]{2,1,0:T(2,128)S(1)}, u32[]{:S(2)}, u32[]{:S(2)}) collective-permute-start(f32[84,2,128]{2,1,0:T(2,128)S(1)} %bitcast.35), channel_id=1, source_target_pairs={{1,0},{2,1},{3,2},{4,3},{5,4},{6,5},{7,6},{8,7},{9,8},{10,9},{11,1... | collective-permute-start | bytes 258056 | tf_op jit(solution)/shard_map/ppermute | solution.py:528
  130.2 3.8 %collective-permute-done.3.y_high = f32[84,2,128]{2,1,0:T(2,128)S(1)} collective-permute-done((f32[84,2,128]{2,1,0:T(2,128)S(1)}, f32[84,2,128]{2,1,0:T(2,128)S(1)}, u32[]{:S(2)}, u32[]{:S(2)}) %collective-permute-start.3) | collective-permute-done | bytes 86048 | tf_op jit(solution)/shard_map/ppermute | solution.py:528
  134.0 3.5 %shard_map.241 = (f32[3,10,24,128]{3,2,1,0:T(8,128)S(1)}, f32[3,10,24,128]{3,2,1,0:T(8,128)S(1)}, f32[10,24,128]{2,1,0:T(8,128)S(1)}, f32[8,16,128]{2,1,0:T(8,128)S(1)}, f32[3,8,16,128]{3,2,1,0:T(8,128)S(1)}) custom-call(s32[2]{0:T(128)S(1)} %pad_add_fusion.here, s32[64]{0:T(128)S(1)} %copy-done.16, f32[384]{0:T(512)S(1)} %reshape.79.weights, ...), custom_call_target="tpu_custom_call" | custom-call | flops 10000000 | bytes 3000000 | tf_op jit(solution)/shard_map/pallas_call | solution.py:615
  137.5 1.7 %shard_map.242 = (f32[3,8,16,128]{3,2,1,0:T(8,128)}, f32[3,8,16,128]{3,2,1,0:T(8,128)}, f32[8,16,128]{2,1,0:T(8,128)}, f32[2,64,3]{2,1,0:T(8,128)S(1)}) custom-call(s32[2]{0:T(128)S(1)} %pad_add_fusion.here, bf16[128,896]{1,0:T(8,128)(2,1)S(1)} %bitcast.30, bf16[128,128]{1,0:T(8,128)(2,1)S(1)} %copy-done.13, f32[3,10,24,128]{3,2,1,0:T(8,128)S(1)} %get-tuple-element.19.early, ...), custom_call_target="tpu_custom_call" | custom-call | flops 40000000 | bytes 4000000 | tf_op jit(solution)/shard_map/pallas_call | solution.py:644
  139.2 0.7 copy.54
  (77 shorter events, 3.3 us)
Async XLA Ops:
  0.6 25.1 %copy-start = (bf16[2,48,16,16]{1,3,2,0:T(8,128)(2,1)S(1)}, bf16[2,48,16,16]{1,3,2,0:T(8,128)(2,1)}, u32[]{:S(2)}) copy-start(bf16[2,48,16,16]{1,3,2,0:T(8,128)(2,1)} %param.32) | copy-start | bytes 147460
  1.5 24.1 %copy-start.16 = (s32[64]{0:T(128)S(1)}, s32[64]{0:T(128)}, u32[]{:S(2)}) copy-start(s32[64]{0:T(128)} %mon.3) | copy-start | bytes 772
  1.5 24.1 %copy-start.18 = (s32[64]{0:T(128)S(1)}, s32[64]{0:T(128)}, u32[]{:S(2)}) copy-start(s32[64]{0:T(128)} %src.1) | copy-start | bytes 772
  1.5 24.2 %copy-start.21 = (f32[16,48]{1,0:T(8,128)S(1)}, f32[16,48]{1,0:T(8,128)}, u32[]{:S(2)}) copy-start(f32[16,48]{1,0:T(8,128)} %param.34) | copy-start | bytes 9220
  1.8 0.9 copy-start.1
  2.7 0.9 copy-start.3
  7.2 15.7 %copy-start.2 = (f32[3,8,16,128]{3,2,1,0:T(8,128)S(1)}, f32[3,8,16,128]{3,2,1,0:T(8,128)}, u32[]{:S(2)}) copy-start(f32[3,8,16,128]{3,2,1,0:T(8,128)} %electric.3) | copy-start | bytes 589828
  7.2 15.7 %copy-start.4 = (f32[3,8,16,128]{3,2,1,0:T(8,128)S(1)}, f32[3,8,16,128]{3,2,1,0:T(8,128)}, u32[]{:S(2)}) copy-start(f32[3,8,16,128]{3,2,1,0:T(8,128)} %magnetic.3) | copy-start | bytes 589828
  11.4 14.8 %copy-start.22 = (f32[16,3]{0,1:T(4,128)S(1)}, f32[16,3]{0,1:T(4,128)}, u32[]{:S(2)}) copy-start(f32[16,3]{0,1:T(4,128)} %param.30) | copy-start | bytes 580
  11.4 14.9 %copy-start.23 = (f32[3,16]{1,0:T(4,128)S(1)}, f32[3,16]{1,0:T(4,128)}, u32[]{:S(2)}) copy-start(f32[3,16]{1,0:T(4,128)} %param.31) | copy-start | bytes 580
  11.4 18.2 %all-to-all-start = ((bf16[16,24,128]{2,1,0:T(8,128)(2,1)}), bf16[16,24,128]{2,1,0:T(8,128)(2,1)S(1)}, u32[]{:S(2)}, u32[]{:S(2)}) async-start(bf16[16,24,128]{2,1,0:T(8,128)(2,1)} %bitcast.2), calls=%async_computation | async-start | bytes 196608 | tf_op jit(solution)/shard_map/all_to_all | solution.py:555
  22.9 101.5 %collective-permute-start = (f32[9,2,16,128]{3,2,1,0:T(8,128)S(1)}, f32[9,2,16,128]{3,2,1,0:T(8,128)S(1)}, u32[]{:S(2)}, u32[]{:S(2)}) collective-permute-start(f32[9,2,16,128]{3,2,1,0:T(8,128)S(1)} %fusion), channel_id=1, source_target_pairs={{0,16},{16,32},{32,48},{48,64},{64,80},{80,96},{96,112},{112,128},... | collective-permute-start | bytes 442376 | tf_op jit(solution)/shard_map/ppermute | solution.py:528
  24.3 100.2 %collective-permute-start.1 = (f32[7,2,16,128]{3,2,1,0:T(8,128)S(1)}, f32[7,2,16,128]{3,2,1,0:T(8,128)S(1)}, u32[]{:S(2)}, u32[]{:S(2)}) collective-permute-start(f32[7,2,16,128]{3,2,1,0:T(8,128)S(1)} %pad_maximum_fusion.2), channel_id=1, source_target_pairs={{16,0},{32,16},{48,32},{64,48},{80,64},{96,80},{112,96},{128,112},... | collective-permute-start | bytes 344072 | tf_op jit(solution)/shard_map/ppermute | solution.py:528
  27.2 1.6 %copy-start.6 = (bf16[2,128,256]{2,1,0:T(8,128)(2,1)S(1)}, bf16[2,128,256]{2,1,0:T(8,128)(2,1)}, u32[]{:S(2)}) copy-start(bf16[2,128,256]{2,1,0:T(8,128)(2,1)} %constant.37.clone.at_x.fwd_x) | copy-start | bytes 393220
  27.2 1.6 %copy-start.11 = (bf16[16,2,8,128]{3,2,1,0:T(8,128)(2,1)S(1)}, bf16[16,2,8,128]{3,2,1,0:T(8,128)(2,1)}, u32[]{:S(2)}) copy-start(bf16[16,2,8,128]{3,2,1,0:T(8,128)(2,1)} %constant.39.clone.at_z) | copy-start | bytes 196612
  27.2 1.6 %copy-start.12 = (bf16[2,48,256]{2,1,0:T(8,128)(2,1)S(1)}, bf16[2,48,256]{2,1,0:T(8,128)(2,1)}, u32[]{:S(2)}) copy-start(bf16[2,48,256]{2,1,0:T(8,128)(2,1)} %constant.38.clone.at_y) | copy-start | bytes 147460
  27.2 2.4 %copy-start.7 = (bf16[512,256]{1,0:T(8,128)(2,1)S(1)}, bf16[512,256]{1,0:T(8,128)(2,1)}, u32[]{:S(2)}) copy-start(bf16[512,256]{1,0:T(8,128)(2,1)} %constant.36.clone.table) | copy-start | bytes 786436
  28.0 73.7 %copy-start.8 = (bf16[32,16,128]{2,1,0:T(8,128)(2,1)S(1)}, bf16[32,16,128]{2,1,0:T(8,128)(2,1)}, u32[]{:S(2)}) copy-start(bf16[32,16,128]{2,1,0:T(8,128)(2,1)} %constant.40.clone.inv_x) | copy-start | bytes 393220
  28.0 73.7 %copy-start.9 = (bf16[128,384]{1,0:T(8,128)(2,1)S(1)}, bf16[128,384]{1,0:T(8,128)(2,1)}, u32[]{:S(2)}) copy-start(bf16[128,384]{1,0:T(8,128)(2,1)} %constant.41.clone.inv_y) | copy-start | bytes 294916
  104.5 29.5 %copy-start.5 = (bf16[2,3,8,16,128]{4,3,2,1,0:T(8,128)(2,1)S(1)}, bf16[2,3,8,16,128]{4,3,2,1,0:T(8,128)(2,1)}, u32[]{:S(2)}) copy-start(bf16[2,3,8,16,128]{4,3,2,1,0:T(8,128)(2,1)} %saved.1) | copy-start | bytes 589828
  104.5 33.0 %all-to-all-start.1 = ((bf16[16,8,896]{2,1,0:T(8,128)(2,1)}), bf16[16,8,896]{2,1,0:T(8,128)(2,1)S(1)}, u32[]{:S(2)}, u32[]{:S(2)}) async-start(bf16[16,8,896]{2,1,0:T(8,128)(2,1)} %bitcast.10), calls=%async_computation.1 | async-start | bytes 458752 | tf_op jit(solution)/shard_map/all_to_all | solution.py:643
  124.4 13.1 %copy-start.13 = (bf16[128,128]{1,0:T(8,128)(2,1)S(1)}, bf16[128,128]{1,0:T(8,128)(2,1)}, u32[]{:S(2)}) copy-start(bf16[128,128]{1,0:T(8,128)(2,1)} %constant.42.clone.table) | copy-start | bytes 98308
  124.6 9.4 %collective-permute-start.2 = (f32[100,2,128]{2,1,0:T(2,128)S(1)}, f32[100,2,128]{2,1,0:T(2,128)S(1)}, u32[]{:S(2)}, u32[]{:S(2)}) collective-permute-start(f32[100,2,128]{2,1,0:T(2,128)S(1)} %maximum_maximum_fusion), channel_id=1, source_target_pairs={{0,1},{1,2},{2,3},{3,4},{4,5},{5,6},{6,7},{7,8},{8,9},{9,10},{10,1... | collective-permute-start | bytes 307208 | tf_op jit(solution)/shard_map/ppermute | solution.py:528
  128.1 5.8 %collective-permute-start.3 = (f32[84,2,128]{2,1,0:T(2,128)S(1)}, f32[84,2,128]{2,1,0:T(2,128)S(1)}, u32[]{:S(2)}, u32[]{:S(2)}) collective-permute-start(f32[84,2,128]{2,1,0:T(2,128)S(1)} %bitcast.35), channel_id=1, source_target_pairs={{1,0},{2,1},{3,2},{4,3},{5,4},{6,5},{7,6},{8,7},{9,8},{10,9},{11,1... | collective-permute-start | bytes 258056 | tf_op jit(solution)/shard_map/ppermute | solution.py:528
  (7 other events, 5.0 us)

commit v2 on v1

v2 whole, which is shorter than its diff:
```python
import functools
import math

import jax
import jax.numpy as jnp
import ml_dtypes
import numpy as np
from jax import lax
from jax.experimental import pallas as pl
from jax.experimental.pallas import tpu as pltpu
from jax.sharding import PartitionSpec as P

NX, NY, NZ = 256, 256, 128
K = 48
OWN = 3
WIDE, BULK = 16, 32
RX, RY = 8, 16
NEAR, FAR = 8, 4
SHARE = OWN * K // NEAR
LANES = 128
F32, BF16 = jnp.float32, jnp.bfloat16
PARAMS = pltpu.CompilerParams(vmem_limit_bytes=40 * 1024 * 1024)
HIGHEST = lax.Precision.HIGHEST


def waves(freqs, places, total):
    phase = np.mod(np.asarray(freqs)[:, None] * np.asarray(places)[None, :], total)
    angle = phase.astype(np.float32) * np.float32(2.0 * math.pi / total)
    return np.cos(angle).astype(np.float32), np.sin(angle).astype(np.float32)


def rounded(table):
    return np.asarray(table, np.float32).astype(ml_dtypes.bfloat16)


def make_tables():
    mode = np.arange(K)
    plane = np.where(mode < K // 2, mode, mode - K)
    cz, sz = waves(mode, np.arange(NZ), NZ)
    cx, sx = (rounded(t) for t in waves(plane, np.arange(NX), NX))
    cy, sy = (rounded(t) for t in waves(plane, np.arange(NY), NY))
    scale = np.float32(1.0 / math.sqrt(NX * NY * NZ))
    back = np.float32(1.0 / math.sqrt(K**3))
    fz, gz = rounded(cz * scale), rounded(-sz * scale)
    bz, hz = rounded(cz * back), rounded(sz * back)
    out = {}
    lift_z = np.zeros((LANES, LANES), ml_dtypes.bfloat16)
    back_z = np.zeros((LANES, LANES), ml_dtypes.bfloat16)
    for w in range(WIDE):
        for i in range(OWN):
            lift_z[:, w * 8 + i] = fz[w * OWN + i]
            lift_z[:, w * 8 + OWN + i] = gz[w * OWN + i]
            back_z[w * 8 + i] = bz[w * OWN + i]
            back_z[w * 8 + OWN + i] = -hz[w * OWN + i]
    out["lift_z"], out["back_z"] = lift_z, back_z

    lane = np.arange(LANES)
    y_of = np.concatenate([(h * 8 + lane % 8) * RY + lane // 8 for h in range(2)])
    fwd_y = np.zeros((512, 256), ml_dtypes.bfloat16)
    fwd_y[:256, :K] = cy[:, y_of].T
    fwd_y[256:, :K] = sy[:, y_of].T
    fwd_y[:256, 128 : 128 + K] = -sy[:, y_of].T
    fwd_y[256:, 128 : 128 + K] = cy[:, y_of].T
    out["fwd_y"] = fwd_y

    fwd_x = np.zeros((FAR, 2 * LANES, LANES), ml_dtypes.bfloat16)
    inv_x = np.zeros((FAR, LANES, LANES), ml_dtypes.bfloat16)
    for far in range(FAR):
        for n in range(NEAR):
            start = (far * NEAR + n) * RX
            here, at = slice(start, start + RX), slice(n * 16, n * 16 + RX)
            fwd_x[far, :K, at], fwd_x[far, 64 : 64 + K, at] = cx[:, here], -sx[:, here]
            fwd_x[far, 128 : 128 + K, at], fwd_x[far, 192 : 192 + K, at] = sx[:, here], cx[:, here]
            x_of = (start + np.array([0, 1, 2, 3, 4, 5, 6, 7, 8, -1])) % NX
            inv_x[far, n * 16 : n * 16 + 10, :K] = cx[:, x_of].T
            inv_x[far, n * 16 : n * 16 + 10, 64 : 64 + K] = -sx[:, x_of].T
    out["fwd_x"], out["inv_x"] = fwd_x, inv_x

    inv_y = np.zeros((LANES, 384), ml_dtypes.bfloat16)
    inv_y[:K, :256], inv_y[64 : 64 + K, :256] = cy, -sy
    for w in range(WIDE):
        for h, y in ((0, w * RY + RY), (7, w * RY - 1)):
            inv_y[:K, 256 + w * 8 + h] = cy[:, y % NY]
            inv_y[64 : 64 + K, 256 + w * 8 + h] = -sy[:, y % NY]
    out["inv_y"] = inv_y

    at_x = np.zeros((2, LANES, NX), ml_dtypes.bfloat16)
    at_x[0, :K], at_x[0, 64 : 64 + K] = cx, -sx
    at_x[1, :K], at_x[1, 64 : 64 + K] = sx, cx
    out["at_x"] = at_x
    at_y = np.zeros((NEAR, 2, 32, NY), ml_dtypes.bfloat16)
    for n in range(NEAR):
        j_of = np.arange(n * SHARE, (n + 1) * SHARE) % K
        at_y[n, 0, :SHARE], at_y[n, 1, :SHARE] = cy[j_of], sy[j_of]
    out["at_y"] = at_y
    at_z = np.zeros((WIDE, 2, 16, NZ), ml_dtypes.bfloat16)
    for w in range(WIDE):
        at_z[w, 0, :OWN] = bz[w * OWN : (w + 1) * OWN]
        at_z[w, 1, :OWN] = hz[w * OWN : (w + 1) * OWN]
    out["at_z"] = at_z
    return out


TABLES = make_tables()


def iota(shape, axis):
    return lax.broadcasted_iota(jnp.int32, shape, axis)


def exchange(tiles, block, axis):
    tiles = list(tiles)
    shape = tiles[0].shape
    size = shape[axis]
    place = iota(shape, axis) // block
    step = 1
    while step < len(tiles):
        high = (place // step) % 2 == 1
        new = list(tiles)
        for low in range(len(tiles)):
            if low & step:
                continue
            u, v = tiles[low], tiles[low + step]
            new[low] = jnp.where(high, pltpu.roll(v, step * block, axis), u)
            new[low + step] = jnp.where(high, v, pltpu.roll(u, size - step * block, axis))
        tiles = new
        step *= 2
    return tiles


def z_ahead(v):
    axis = v.ndim - 1
    return jnp.where(iota(v.shape, axis) < NZ - 1, pltpu.roll(v, NZ - 1, axis), 0.0)


def z_behind(v):
    axis = v.ndim - 1
    return jnp.where(iota(v.shape, axis) > 0, pltpu.roll(v, 1, axis), 0.0)


def x_ahead(v):
    return jnp.concatenate([v[1:], v[:1]], 0)


def x_behind(v):
    return jnp.concatenate([v[-1:], v[:-1]], 0)


def y_ahead(v):
    return pltpu.roll(v, v.shape[1] - 1, 1)


def y_behind(v):
    return pltpu.roll(v, 1, 1)


def curl_ahead(fx, fy, fz):
    return (
        (y_ahead(fz) - fz) - (z_ahead(fy) - fy),
        (z_ahead(fx) - fx) - (x_ahead(fz) - fz),
        (x_ahead(fy) - fy) - (y_ahead(fx) - fx),
    )


def curl_behind(fx, fy, fz):
    return (
        (fz - y_behind(fz)) - (fy - z_behind(fy)),
        (fx - z_behind(fx)) - (fz - x_behind(fz)),
        (fy - x_behind(fy)) - (fx - y_behind(fx)),
    )


def place_of(flat):
    return flat >> 15, (flat >> 7) & (NY - 1), flat & (NZ - 1)


def own_block():
    return lax.axis_index("bulk"), lax.axis_index("wide")


def fetch(pairs, sems):
    copies = [pltpu.make_async_copy(a, b, sems.at[i]) for i, (a, b) in enumerate(pairs)]
    for copy in copies:
        copy.start()
    return copies


def scan(cells, hit, act):
    def group(g, carry):
        found = [cells[g * 8 + i] for i in range(8)]
        hits = [hit(*place_of(f)) for f in found]
        some = functools.reduce(jnp.logical_or, hits)

        @pl.when(some)
        def _():
            for i in range(8):
                pl.when(hits[i])(functools.partial(act, g * 8 + i, found[i]))

        return carry

    lax.fori_loop(0, 8, group, 0)


def lift_kernel(mon_in, weights_in, electric, table_in, out, field, mon, weights, table, sems):
    b, w = own_block()
    copies = fetch(
        ((mon_in, mon), (electric, field), (weights_in, weights), (table_in, table)), sems
    )
    for copy in copies:
        copy.wait()
    lane = iota((1, NZ), 1)
    spot = iota((1, 64), 1)

    def hit(x, y, z):
        return ((x >> 3) == b) & ((y >> 4) == w)

    def add(i, flat):
        x, y, z = place_of(flat)
        lx, ly = x & (RX - 1), y & (RY - 1)
        for c in range(3):
            row = field[c, lx, pl.ds(ly, 1), :]
            given = jnp.where(spot == i, weights[c, 1:2, :], 0.0)
            weight = jnp.sum(given, axis=1, keepdims=True)
            field[c, lx, pl.ds(ly, 1), :] = row + jnp.where(lane == z, weight, 0.0)

    scan(mon, hit, add)
    rows = field[...].reshape(3 * RX * RY, NZ).astype(BF16)
    modes = jnp.dot(rows, table[...], preferred_element_type=F32)
    modes = modes.reshape(3, RX, 2, 8, LANES)
    tiles = exchange([modes[:, x].reshape(6, 8, LANES) for x in range(RX)], 1, 1)
    tiles = [t.reshape(3, 2, 8, LANES) for t in tiles]
    tiles = exchange([tiles[y % 8][:, y // 8] for y in range(RY)], 8, 2)
    out[...] = jnp.concatenate([t.reshape(24, LANES) for t in tiles], 0).astype(BF16)


def share_kernel(
    src_in, perm_in, field, magnetic_in, material_in, saved_in,
    taken, inverse, to_low, to_high,
    src, perm, magnetic, material, saved, scaled, held, sems,
):
    b, w = own_block()
    copies = fetch(
        (
            (src_in, src), (perm_in, perm), (magnetic_in, magnetic),
            (material_in, material), (saved_in, saved),
        ),
        sems,
    )
    zero = jnp.zeros((12, 32, NZ), F32)
    for c in range(3):
        scaled[c] = zero
        held[c] = zero
    for copy in copies:
        copy.wait()
    eps = jnp.zeros((RX, RY, NZ), F32)
    cells = material[...]
    for level in range(8):
        eps = jnp.where(cells == level, perm[level], eps)
    inv = 1.0 / eps
    inverse[...] = inv
    lane = iota((1, NZ), 1)
    for c in range(3):
        scaled[c, 2:10, 8:24, :] = 0.5 * inv * field[c]
        held[c, 2:10, 8:24, :] = magnetic[c]
        to_low[c], to_high[c] = field[c, 6:8], field[c, 0:2]
        to_low[3 + c], to_high[3 + c] = magnetic[c, 6:8], magnetic[c, 0:2]
    to_low[6], to_high[6] = inv[6:8], inv[0:2]
    for n in range(2):
        for c in range(2):
            to_low[7 + n, c] = saved[n, 1 + c, 7].astype(F32)
    taken[...] = jnp.zeros((8, LANES), F32)
    spot_row, spot_lane = iota((8, LANES), 0), iota((8, LANES), 1)

    def hit(x, y, z):
        lx, ly = x - b * RX, y - w * RY
        return (lx >= -1) & (lx <= RX) & (ly >= -1) & (ly <= RY)

    def take(i, flat):
        x, y, z = place_of(flat)
        lx, ly = x - b * RX, y - w * RY

        def a(c, dx, dy):
            return scaled[c, lx + 2 + dx, pl.ds(ly + 8 + dy, 1), :]

        def h(c, dx, dy):
            old = held[c, lx + 2 + dx, pl.ds(ly + 8 + dy, 1), :]
            if c == 0:
                near = a(1, dx, dy)
                turn = (a(2, dx, dy + 1) - a(2, dx, dy)) - (z_ahead(near) - near)
            elif c == 1:
                near = a(0, dx, dy)
                turn = (z_ahead(near) - near) - (a(2, dx + 1, dy) - a(2, dx, dy))
            else:
                turn = (a(1, dx + 1, dy) - a(1, dx, dy)) - (a(0, dx, dy + 1) - a(0, dx, dy))
            return old + turn

        left = jnp.where(x > 0, 1.0, 0.0)
        down = jnp.where(y > 0, 1.0, 0.0)
        hx, hy, hz = h(0, 0, 0), h(1, 0, 0), h(2, 0, 0)
        hx_y, hz_y = down * h(0, 0, -1), down * h(2, 0, -1)
        hy_x, hz_x = left * h(1, -1, 0), left * h(2, -1, 0)
        curls = (
            (hz - hz_y) - (hy - z_behind(hy)),
            (hx - z_behind(hx)) - (hz - hz_x),
            (hy - hy_x) - (hx - hx_y),
        )
        mine = jnp.where((lx >= 0) & (lx < RX) & (ly >= 0) & (ly < RY), 1.0, 0.0)
        cx, cy = jnp.clip(lx, 0, RX - 1), jnp.clip(ly, 0, RY - 1)
        got = taken[...]
        for c in range(3):
            old = mine * field[c, cx, pl.ds(cy, 1), :]
            for n, row in ((0, old - 0.5 * curls[c]), (1, old)):
                value = jnp.sum(jnp.where(lane == z, row, 0.0), axis=1, keepdims=True)
                spot = (spot_row == n * 3 + c) & (spot_lane == i)
                got = got + jnp.where(spot, value, 0.0)
        taken[...] = got

    scan(src, hit, take)


def middle_kernel(lines, taken, table, out):
    got = lines[...].astype(F32).reshape(WIDE, 24, LANES)
    halves = [exchange([got[h * 8 + i] for i in range(8)], 1, 1) for h in range(2)]
    rows = [
        jnp.concatenate([halves[0][k], halves[1][k], halves[0][OWN + k], halves[1][OWN + k]], 1)
        for k in range(OWN)
    ]
    lhs = jnp.concatenate(rows, 0).astype(BF16)
    found = jnp.dot(lhs, table[...], preferred_element_type=F32)
    lane = iota((8, LANES), 1)
    parts = [jnp.zeros((8, LANES), F32) for _ in range(NEAR)]
    for part in range(2):
        for d in range(3):
            piece = [
                found[(k * 3 + d) * 8 : (k * 3 + d) * 8 + 8, part * LANES : (part + 1) * LANES]
                for k in range(OWN)
            ]
            last = pltpu.roll(piece[2], 2 * K, 1)
            first = piece[0] + pltpu.roll(piece[1], K, 1) + jnp.where(lane >= 2 * K, last, 0.0)
            rest = jnp.where(lane < 16, last, 0.0)
            to = part * 64 + d * SHARE
            for n in range(NEAR):
                moved = pltpu.roll(first, (to - n * SHARE) % LANES, 1)
                if n == NEAR - 1:
                    moved = jnp.where(lane < to + 2, moved, pltpu.roll(rest, to + 2, 1))
                within = (lane >= to) & (lane < to + SHARE)
                parts[n] = parts[n] + jnp.where(within, moved, 0.0)
    src = taken[...]
    high = src.astype(BF16).astype(F32)
    extra = high + pltpu.roll(src - high, 64, 1)
    out[...] = jnp.concatenate([t for p in parts for t in (p, extra)], 0).astype(BF16)


def param_kernel(
    mon, weights, lift, cells, project, gain_x, gain_y, mix, at_x, at_y, at_z, after,
    coef_a, coef_b, phase_x, phase_yz, injected,
):
    b, w = own_block()
    n = b % NEAR
    flat = cells[...]
    x, y, z = place_of(flat)
    first = iota((1, LANES), 1) < 64
    hot_x = jnp.where(iota((NX, LANES), 0) == x, 1.0, 0.0)
    real = jnp.where(first, hot_x, 0.0).astype(BF16)
    imag = jnp.where(first, 0.0, hot_x).astype(BF16)
    phase_x[...] = (
        jnp.dot(at_x[0], real, preferred_element_type=F32)
        + jnp.dot(at_x[1], imag, preferred_element_type=F32)
    ).astype(BF16)
    hot_y = jnp.where(iota((NY, LANES), 0) == y, 1.0, 0.0).astype(BF16)
    hot_z = jnp.where(iota((NZ, LANES), 0) == z, 1.0, 0.0).astype(BF16)
    cy = jnp.dot(at_y[n, 0], hot_y, preferred_element_type=F32)[:24]
    sy = jnp.dot(at_y[n, 1], hot_y, preferred_element_type=F32)[:24]
    cz = jnp.dot(at_z[w, 0], hot_z, preferred_element_type=F32)
    sz = jnp.dot(at_z[w, 1], hot_z, preferred_element_type=F32)
    mode = n * SHARE + iota((24, 1), 0)
    ck = jnp.where(mode < K, cz[0:1], jnp.where(mode < 2 * K, cz[1:2], cz[2:3]))
    sk = jnp.where(mode < K, sz[0:1], jnp.where(mode < 2 * K, sz[1:2], sz[2:3]))
    phase_yz[...] = jnp.where(first, cy * ck - sy * sk, -(sy * ck + cy * sk))

    place = iota((K, 24), 1)
    mode = n * SHARE + place
    depth = jnp.where(mode < K, 0, jnp.where(mode < 2 * K, 1, 2))
    live = place < SHARE
    hot_j = jnp.where((iota((K, 24), 0) == mode - depth * K) & live, 1.0, 0.0)
    hot_k = jnp.where((iota((K, 24), 0) == w * OWN + depth) & live, 1.0, 0.0)
    gains = jnp.dot(gain_y[...], hot_j, precision=HIGHEST, preferred_element_type=F32)
    diagonal = iota((16, 16), 0) == iota((16, 16), 1)
    columns = [
        jnp.sum(jnp.where(diagonal, project[e : e + 1, :], 0.0), axis=1, keepdims=True)
        for e in range(3)
    ]
    blank = jnp.zeros((16, 16), F32)
    along = gain_x[...]
    for part, to in ((0, coef_a), (1, coef_b)):
        joined = []
        for d in range(3):
            total = jnp.zeros((16, K), F32)
            for c in range(16):
                total = total + lift[d, c] * mix[part, c].astype(F32)
            joined.append(
                gains * jnp.dot(total, hot_k, precision=HIGHEST, preferred_element_type=F32)
            )
        sign = 1.0 if part == 0 else -1.0
        right = jnp.concatenate([sign * along, blank, along, blank], 1)
        for e in range(3):
            for d in range(3):
                left = (columns[e] * joined[d]).T
                to[(e * 3 + d) * 24 : (e * 3 + d + 1) * 24, :] = jnp.dot(
                    left, right, precision=HIGHEST, preferred_element_type=F32
                )
    row = iota((8, LANES), 0)
    total = jnp.zeros((8, LANES), F32)
    for i in range(64):
        given = jnp.where(
            row == 0, weights[0, 0, i], jnp.where(row == 1, weights[1, 0, i], weights[2, 0, i])
        )
        total = total + jnp.where((flat == mon[i]) & (row < 3), given, 0.0)
    injected[...] = jnp.where(iota((8, LANES), 1) < 64, total, 0.0)


def filter_kernel(
    own, far_1, far_2, far_3, coef_a, coef_b, fwd_x, inv_x, phase_x, phase_yz, after, out, pre
):
    b, w = own_block()
    far = b // NEAR
    lane = iota((1, LANES), 1)
    both = jnp.zeros((2 * LANES, LANES), F32)
    total = jnp.zeros((8, LANES), F32)
    for t, ref in enumerate((own, far_1, far_2, far_3)):
        got = ref[...]
        both = both + jnp.dot(fwd_x[(far + FAR - t) % FAR], got, preferred_element_type=F32)
        total = total + got.astype(F32).reshape(NEAR, 2, 8, LANES)[:, 1].sum(0)
    pre[...] = jnp.where(lane < 64, total + pltpu.roll(total, 64, 1), 0.0)
    full = (both[:LANES] + pltpu.roll(both[LANES:], 64, 1)).T
    field = [full[d * SHARE : d * SHARE + 24] for d in range(3)]
    turned = [pltpu.roll(f, 64, 1) for f in field]
    sign = jnp.where(lane < 64, 1.0, -1.0)
    real = []
    for e in range(3):
        q = jnp.zeros((24, LANES), F32)
        for d in range(3):
            at = (e * 3 + d) * 24
            q = q + coef_a[at : at + 24] * field[d] + coef_b[at : at + 24] * turned[d]
        real.append(q)
    near = jnp.dot(
        jnp.concatenate(real, 0).astype(BF16), phase_x[...], preferred_element_type=F32
    )
    gap = jnp.zeros((10, LANES), F32)
    packed = jnp.concatenate([q[:SHARE] for q in real] + [gap], 0)
    right = jnp.concatenate([packed, pltpu.roll(packed, 64, 1) * sign], 0).astype(BF16)
    back = lax.dot_general(
        inv_x[far], right, (((1,), (1,)), ((), ())), preferred_element_type=F32
    ).reshape(NEAR, 2, 8, LANES)
    row = iota((8, LANES), 0)
    extra = jnp.zeros((8, LANES), F32)
    for e in range(3):
        line = jnp.sum(near[e * 24 : (e + 1) * 24] * phase_yz[...], axis=0, keepdims=True)
        line = line + pltpu.roll(line, 64, 1)
        high = line.astype(BF16).astype(F32)
        extra = extra + jnp.where(row == 2 + e, jnp.where(lane < 64, high, line - high), 0.0)
    tiles = []
    for n in range(NEAR):
        tiles += [back[n, 0], back[n, 1] + extra]
    out[...] = jnp.concatenate(tiles, 0).astype(BF16)


def spread_kernel(shares, pre, inv_y, out, rows):
    lane = iota((1, LANES), 1)
    got = shares[...].astype(F32).reshape(NEAR, 16, LANES)
    rows[...] = jnp.zeros((32, 8, LANES), F32)
    for e in range(3):
        flat = []
        for part in range(2):
            start = part * 64 + e * SHARE
            first, rest = jnp.zeros((16, LANES), F32), None
            for n in range(NEAR):
                moved = pltpu.roll(got[n], (n * SHARE - start) % LANES, 1)
                within = (lane >= n * SHARE) & (lane < (n + 1) * SHARE)
                first = first + jnp.where(within, moved, 0.0)
                if n == NEAR - 1:
                    rest = jnp.where(lane < 16, moved, 0.0)
            flat.append((first, rest))

        def mode_rows(part, k, to):
            first, rest = flat[part]
            moved = pltpu.roll(first, (to - k * K) % LANES, 1)
            if k < 2:
                return jnp.where((lane >= to) & (lane < to + K), moved, 0.0)
            tail = pltpu.roll(rest, to + 32, 1)
            return jnp.where((lane >= to) & (lane < to + 32), moved, 0.0) + jnp.where(
                (lane >= to + 32) & (lane < to + K), tail, 0.0
            )

        for k in range(OWN):
            real = mode_rows(0, k, 0) + mode_rows(1, k, 64)
            imag = mode_rows(1, k, 0) - mode_rows(0, k, 64)
            for x in range(10):
                rows[e * 10 + x, k : k + 1, :] = real[x : x + 1]
                rows[e * 10 + x, OWN + k : OWN + k + 1, :] = imag[x : x + 1]
    lhs = rows[...].reshape(256, LANES).astype(BF16)
    wide = jnp.dot(lhs, inv_y[...], preferred_element_type=F32).reshape(32, 8, 384)
    near = []
    for low in range(8):
        group = [wide[high * 8 + low, :, c * LANES : (c + 1) * LANES] for high in range(4) for c in range(2)]
        near.append(jnp.stack(group))
    near = exchange(near, 16, 2)
    edge = []
    for low in range(16):
        edge.append(jnp.stack([wide[high * 16 + low, :, 256:384] for high in range(2)]))
    edge = exchange(edge, 8, 2)
    row = iota((8, LANES), 0)
    spectral = pltpu.roll(got[:, 8:16].sum(0), 6, 0)
    spectral = jnp.where((row < 3) & (lane < 64), spectral + pltpu.roll(spectral, 64, 1), 0.0)
    total = pre[...] + spectral
    high = total.astype(BF16).astype(F32)
    last = high + pltpu.roll(total - high, 64, 1)
    blocks = []
    for w in range(WIDE):
        tiles = [near[w % 8][high_x * 2 + w // 8] for high_x in range(4)]
        tiles += [edge[w][high_x] for high_x in range(2)] + [last]
        blocks.append(jnp.concatenate(tiles, 1))
    out[...] = jnp.concatenate(blocks, 0).astype(BF16)


def corner_kernel(electric, magnetic, inverse, saved, x_low, x_high, after, to_low, to_high):
    for c in range(7):
        own = electric.at[c] if c < 3 else (magnetic.at[c - 3] if c < 6 else inverse)
        for to, rows in ((to_low, slice(14, 16)), (to_high, slice(0, 2))):
            to[c * 12 : c * 12 + 8] = own[:, rows, :]
            to[c * 12 + 8 : c * 12 + 10] = x_high[c, :, rows, :]
            to[c * 12 + 10 : c * 12 + 12] = x_low[c, :, rows, :]
    for n in range(2):
        for i, c in enumerate((0, 2)):
            edge = saved[n, c].astype(F32)[:, RY - 1 : RY, :]
            to_low[84 + n * 8 : 92 + n * 8, i : i + 1, :] = edge


def first_kernel(
    mon, weights, electric, magnetic, inverse, saved, x_low, x_high, y_low, y_high, after,
    early, curled, factor, grad, ready, e_ext, h_ext, g_ext,
):
    b, w = own_block()
    lane = iota((1, NZ), 1)
    for c in range(7):
        to = e_ext.at[c] if c < 3 else (h_ext.at[c - 3] if c < 6 else g_ext)
        own = electric[c] if c < 3 else (magnetic[c - 3] if c < 6 else inverse[...])
        to[0:8, 0:16, :] = own
        to[8:10, 0:16, :] = x_high[c]
        to[10:12, 0:16, :] = x_low[c]
        low, high = y_low[c * 12 : (c + 1) * 12], y_high[c * 12 : (c + 1) * 12]
        to[:, 16:24, :] = jnp.concatenate([high, jnp.zeros((12, 4, NZ), F32), low], 1)

    g = g_ext[...]
    half = 0.5 * g
    a = [half * e_ext[c] for c in range(3)]
    spot_x = iota((12, 24, 1), 0)
    spot_y = iota((12, 24, 1), 1)
    outside = ((spot_x >= 10) & (b == 0)) | ((spot_y >= 22) & (w == 0))
    inside = jnp.where(outside, 0.0, 1.0)
    turned = curl_ahead(*a)
    h = [h_ext[c] + inside * turned[c] for c in range(3)]
    back = curl_behind(*h)
    for c in range(3):
        e_ext[c] = e_ext[c] - 0.5 * back[c]

    def hit(x, y, z):
        lx, ly = x - b * RX, y - w * RY
        return (lx >= -2) & (lx < RX + 2) & (ly >= -2) & (ly < RY + 2)

    def add(i, flat):
        x, y, z = place_of(flat)
        lx, ly = x - b * RX, y - w * RY
        px = jnp.where(lx < 0, lx + 12, lx)
        py = jnp.where(ly < 0, ly + 24, ly)
        for c in range(3):
            row = e_ext[c, px, pl.ds(py, 1), :]
            e_ext[c, px, pl.ds(py, 1), :] = row + jnp.where(lane == z, weights[c, 0, i], 0.0)

    scan(mon, hit, add)
    for c in range(3):
        early[c, 0:9] = e_ext[c, 0:9]
        early[c, 9:10] = e_ext[c, 11:12]
        curled[c, 0:9] = h[c][0:9]
        curled[c, 9:10] = h[c][11:12]
    factor[0:9] = half[0:9]
    factor[9:10] = half[11:12]

    near = inverse[...]
    for step in range(2):
        s = [saved[step, c].astype(F32) for c in range(3)]
        before_x = {c: jnp.concatenate([x_low[7 + step, c - 1 : c], s[c][:-1]], 0) for c in (1, 2)}
        at = 84 + step * 8
        before_y = {}
        for c in (0, 2):
            edge = y_low[at : at + 8, c // 2 : c // 2 + 1, :]
            first = iota((RX, RY, NZ), 1) == 0
            before_y[c] = jnp.where(first, edge, pltpu.roll(s[c], 1, 1))
        curls = (
            (s[2] - before_y[2]) - (s[1] - z_behind(s[1])),
            (s[0] - z_behind(s[0])) - (s[2] - before_x[2]),
            (s[1] - before_x[1]) - (s[0] - before_y[0]),
        )
        if step == 0:
            for c in range(3):
                ready[c] = near * curls[c]
        else:
            total = jnp.zeros((RX, RY, NZ), F32)
            for c in range(3):
                total = total + a[c][0:8, 0:16] * near * curls[c]
            grad[...] = -total


def second_kernel(
    lines, table, early, curled, factor, first_grad, ready, injected,
    grad_e, grad_h, grad_eps, sources,
):
    b, w = own_block()
    modes = lines[:, 0:768]
    back = lax.dot_general(
        modes, table[...], (((0,), (0,)), ((), ())), preferred_element_type=F32
    )
    main = back[0:512].reshape(32, 16, NZ)
    edge = back[512:768].reshape(32, 8, NZ)
    half = factor[...]
    e1 = []
    for c in range(3):
        at = slice(c * 10, c * 10 + 10)
        e1.append(early[c] + jnp.concatenate([main[at], edge[at]], 1))
    a = [half * e for e in e1]
    spot_x = iota((10, 24, 1), 0)
    spot_y = iota((10, 24, 1), 1)
    outside = ((spot_x == 9) & (b == 0)) | ((spot_y == 23) & (w == 0))
    inside = jnp.where(outside, 0.0, 1.0)
    turned = curl_ahead(*a)
    h = [curled[c] + inside * turned[c] for c in range(3)]
    backed = curl_behind(*h)
    total = first_grad[...]
    for c in range(3):
        grad_h[c] = h[c][0:8, 0:16]
        grad_e[c] = e1[c][0:8, 0:16] - 0.5 * backed[c][0:8, 0:16]
        total = total - a[c][0:8, 0:16] * ready[c]
    grad_eps[...] = total
    got = lines[:, 768:896].astype(F32).reshape(WIDE, 8, LANES).sum(0)
    got = got + pltpu.roll(got, 64, 1) + injected[...]
    for n in range(2):
        for c in range(3):
            sources[c, n : n + 1, :] = got[n * 3 + c : n * 3 + c + 1, 0:64]


def call(kernel, outs, places, scratch=(), flops=0, moved=0, params=PARAMS):
    spaces = {"s": pltpu.SMEM, "v": pltpu.VMEM, "a": pl.ANY}
    return pl.pallas_call(
        kernel,
        out_shape=outs,
        in_specs=[pl.BlockSpec(memory_space=spaces[p]) for p in places],
        out_specs=jax.tree.map(lambda _: pl.BlockSpec(memory_space=pltpu.VMEM), outs),
        scratch_shapes=list(scratch),
        compiler_params=params,
        cost_estimate=pl.CostEstimate(flops=flops, bytes_accessed=moved, transcendentals=0),
    )


def shape(*dims, dtype=F32):
    return jax.ShapeDtypeStruct(dims, dtype)


def passed_along(block, axis, distance):
    devices = range(lax.axis_size(axis))
    route = [(i - distance, i) for i in devices if i - distance in devices]
    return lax.ppermute(block, axis, route)


def passed_far(block, distance):
    route = [(i, (i + distance * NEAR) % BULK) for i in range(BULK)]
    return lax.ppermute(block, "bulk", route)


def dealt_near(block):
    groups = [[f * NEAR + n for n in range(NEAR)] for f in range(FAR)]
    return lax.all_to_all(
        block, "bulk", split_axis=0, concat_axis=0, axis_index_groups=groups, tiled=True
    )


def tables_of(name):
    return jnp.asarray(TABLES[name])


def body(
    seed_electric, seed_magnetic, saved_magnetic, material, permittivity, source_cells,
    monitor_cells, monitor_weights, lift_weight, project_weight, mode_mix, gain_first, gain_second,
):
    weights = monitor_weights.transpose(2, 0, 1)
    big, dma = pltpu.CompilerParams(vmem_limit_bytes=56 * 1024 * 1024), pltpu.SemaphoreType.DMA
    block = (RX, RY, NZ)

    payload, field = call(
        lift_kernel,
        (shape(384, LANES, dtype=BF16), shape(3, *block)),
        "aaaa",
        [
            pltpu.SMEM((64,), jnp.int32), pltpu.VMEM((3, 2, 64), F32),
            pltpu.VMEM((LANES, LANES), BF16), dma((4,)),
        ],
        13_000_000,
        500_000,
        big,
    )(monitor_cells, weights, seed_electric, tables_of("lift_z"))
    lines = lax.all_to_all(payload, "wide", split_axis=0, concat_axis=0, tiled=True)

    taken, inverse, to_low, to_high = call(
        share_kernel,
        (shape(8, LANES), shape(*block), shape(9, 2, RY, NZ), shape(7, 2, RY, NZ)),
        "aavaaa",
        [
            pltpu.SMEM((64,), jnp.int32), pltpu.SMEM((8,), F32), pltpu.VMEM((3, *block), F32),
            pltpu.VMEM(block, jnp.int32), pltpu.VMEM((2, 3, *block), BF16),
            pltpu.VMEM((3, 12, 32, NZ), F32), pltpu.VMEM((3, 12, 32, NZ), F32), dma((5,)),
        ],
        3_000_000,
        1_500_000,
        big,
    )(source_cells, permittivity, field, seed_magnetic, material, saved_magnetic)
    x_low = passed_along(to_low, "bulk", 1)
    x_high = passed_along(to_high, "bulk", -1)

    dealt = call(
        middle_kernel, shape(LANES, LANES, dtype=BF16), "vvv", (), 20_000_000, 400_000
    )(lines, taken, tables_of("fwd_y"))
    own = dealt_near(dealt)

    cells = jnp.concatenate([source_cells, source_cells]).reshape(1, LANES)
    coef_a, coef_b, phase_x, phase_yz, injected = call(
        param_kernel,
        (
            shape(216, LANES), shape(216, LANES), shape(LANES, LANES, dtype=BF16),
            shape(24, LANES), shape(8, LANES),
        ),
        "sssvvvvvvvva",
        (),
        20_000_000,
        1_000_000,
    )(
        monitor_cells, weights, lift_weight.T, cells, project_weight, gain_first, gain_second,
        mode_mix.transpose(0, 2, 3, 1), tables_of("at_x"), tables_of("at_y"), tables_of("at_z"),
        dealt,
    )

    far = [passed_far(own, t) for t in (1, 2, 3)]
    low_part, high_part = call(
        corner_kernel, (shape(100, 2, NZ), shape(84, 2, NZ)), "vvvvvva", (), 0, 1_000_000
    )(field, seed_magnetic, inverse, saved_magnetic, x_low, x_high, own)
    y_low = passed_along(low_part, "wide", 1)
    y_high = passed_along(high_part, "wide", -1)

    shares, pre = call(
        filter_kernel,
        (shape(LANES, LANES, dtype=BF16), shape(8, LANES)),
        "vvvvvvvvvva",
        (),
        40_000_000,
        600_000,
    )(
        own, *far, coef_a, coef_b, tables_of("fwd_x"), tables_of("inv_x"), phase_x, phase_yz,
        low_part,
    )
    back = dealt_near(shares)

    early, curled, factor, first_grad, ready = call(
        first_kernel,
        (
            shape(3, 10, 24, NZ), shape(3, 10, 24, NZ), shape(10, 24, NZ), shape(*block),
            shape(3, *block),
        ),
        "ssvvvvvvvva",
        [pltpu.VMEM((3, 12, 24, NZ), F32)] * 2 + [pltpu.VMEM((12, 24, NZ), F32)],
        10_000_000,
        3_000_000,
    )(
        monitor_cells, weights, field, seed_magnetic, inverse, saved_magnetic,
        x_low, x_high, y_low, y_high, shares,
    )

    sent = call(
        spread_kernel,
        shape(128, 896, dtype=BF16),
        "vvv",
        [pltpu.VMEM((32, 8, LANES), F32)],
        40_000_000,
        600_000,
    )(back, pre, tables_of("inv_y"))
    returned = lax.all_to_all(sent, "wide", split_axis=0, concat_axis=0, tiled=True)
    grad_e, grad_h, grad_eps, sources = call(
        second_kernel,
        (shape(3, *block), shape(3, *block), shape(*block), shape(3, 2, 64)),
        "vvvvvvvv",
        (),
        40_000_000,
        4_000_000,
    )(returned, tables_of("back_z"), early, curled, factor, first_grad, ready, injected)
    return grad_e, grad_h, grad_eps, sources.transpose(1, 2, 0)


def solution(mesh):
    field = P(None, "bulk", "wide", None)
    return jax.shard_map(
        body,
        mesh=mesh,
        in_specs=(
            field, field, P(None, None, "bulk", "wide", None), P("bulk", "wide", None),
            P(), P(), P(), P(), P(), P(), P(), P(), P(),
        ),
        out_specs=(field, field, P("bulk", "wide", None), P()),
        check_vma=False,
    )
```

time: 141 us -> 94.7 us (0.67)
  blocking collectives: 71.7 us -> 11.6 us
  starting transfers between devices: 38.5 us -> 57.6 us
  local copies, waits for them, and re-layouts: 8.37 us -> 0.79 us
  waiting for transfers between devices: 3.77 us -> 9.27 us
  other arithmetic: 1.65 us -> 0.08 us
  matrix products: 1.47 us -> 0 us
    all_gather x1 -> x0, blocking collectives: 71.7 us -> none  [body(): gathered = lax.all_gather(spectrum, 'bulk', axis=0, tiled=True)]
    ppermute x0 -> x3, starting transfers between devices: none -> 23.9 us  [passed_far(): return lax.ppermute(block, 'bulk', route)]
    all_to_all x1, starting transfers between devices: 20 us -> 7.17 us  [body(): lax.all_to_all(sent, 'wide', split_axis=0, concat_axis=0, tiled=True)]
    all_to_all x0 -> x1, blocking collectives: none -> 11.6 us  [dealt_near(): lax.all_to_all(block, 'bulk', split_axis=0, concat_axis=0, axis_index_gro...]
    unnamed x51 -> x42, local copies, waits for them, and re-layouts: 7.19 us -> 0.79 us
    all_to_all x0 -> x1, starting transfers between devices: none -> 4.51 us  [dealt_near(): lax.all_to_all(block, 'bulk', split_axis=0, concat_axis=0, axis_index_gro...]
    ppermute x4, starting transfers between devices: 8.05 us -> 11.7 us  [passed_along(): return lax.ppermute(block, axis, route)]
    all_to_all x1, waiting for transfers between devices: 0.01 us -> 2.49 us  [body(): lax.all_to_all(payload, 'wide', split_axis=0, concat_axis=0, tiled=True)]
  transfers between devices with their start and end apart: 6 -> 10, of which waited for: 1 -> 4; matrix products, arithmetic and copies ran while one was open for 3% -> 0% of each run, Pallas kernels for 5% -> 7%
where the time goes in v2:
time: 94.7 us; the launch traced here: 93.9 us
  starting transfers between devices  57.6 us (61%)
  Pallas kernels  13.6 us (14%)
  blocking collectives  11.6 us (12%)
  waiting for transfers between devices  9.27 us (10%)
  between operations  0.96 us (1%)
    ppermute x3, starting transfers between devices, passed_far(): return lax.ppermute(block, 'bulk', route)  23.9 us
    ppermute x4, starting transfers between devices, passed_along(): return lax.ppermute(block, axis, route)  11.7 us
    all_to_all x1, blocking collectives, dealt_near(): lax.all_to_all(block, 'bulk', split_axis=0, concat_axis=0, axis_index_gro...  11.6 us
    all_to_all x1, starting transfers between devices, body(): lax.all_to_all(payload, 'wide', split_axis=0, concat_axis=0, tiled=True)  10.3 us
    all_to_all x1, starting transfers between devices, body(): lax.all_to_all(sent, 'wide', split_axis=0, concat_axis=0, tiled=True)  7.17 us
    all_to_all x1, starting transfers between devices, dealt_near(): lax.all_to_all(block, 'bulk', split_axis=0, concat_axis=0, axis_index_gro...  4.51 us
    ppermute x4, waiting for transfers between devices, passed_along(): return lax.ppermute(block, axis, route)  3.89 us
    pallas_call x1, Pallas kernels, body(): call(share_kernel, (shape(8, LANES), shape(*block), shape(9, 2, RY, NZ),...  3.36 us
  transfers between devices with their start and end apart: 10, of which 4 were waited for; matrix products, arithmetic and copies ran while one was open for 0% of the time, Pallas kernels for 7%

profile of v2, /device:TPU:1, one launch (start us, length us, event | category | flops | bytes accessed | tf_op | source)
XLA Modules:
  0.0 93.9 jit_solution(15193594028466478223)
XLA Ops:
  0.6 2.2 %shard_map.237 = (bf16[384,128]{1,0:T(8,128)(2,1)}, f32[3,8,16,128]{3,2,1,0:T(8,128)}) custom-call(s32[64]{0:T(128)} %mon.3, f32[3,2,64]{2,1,0:T(2,128)} %bitcast.24, f32[3,8,16,128]{3,2,1,0:T(8,128)} %electric.1, bf16[128,128]{1,0:T(8,128)(2,1)} %constant.18.clone.table_in), custom_call_target="tpu_custom_call" | custom-call | flops 13000000 | bytes 500000 | tf_op jit(solution)/shard_map/pallas_call | solution.py:698
  2.8 10.3 %all-to-all-start = ((bf16[16,24,128]{2,1,0:T(8,128)(2,1)}), bf16[16,24,128]{2,1,0:T(8,128)(2,1)S(1)}, u32[]{:S(2)}, u32[]{:S(2)}) async-start(bf16[16,24,128]{2,1,0:T(8,128)(2,1)} %bitcast.28), calls=%async_computation | async-start | bytes 196608 | tf_op jit(solution)/shard_map/all_to_all | solution.py:710
  13.1 3.4 %shard_map.238 = (f32[8,128]{1,0:T(8,128)}, f32[8,16,128]{2,1,0:T(8,128)}, f32[9,2,16,128]{3,2,1,0:T(8,128)}, f32[7,2,16,128]{3,2,1,0:T(8,128)}) custom-call(s32[64]{0:T(128)} %src_in.1, f32[8]{0:T(128)} %perm_in.1, f32[3,8,16,128]{3,2,1,0:T(8,128)} %get-tuple-element.29.field.electric, f32[3,8,16,128]{3,2,1,0:T(8,128)} %magnetic.3, ...), custom_call_target="tpu_custom_call" | custom-call | flops 3000000 | bytes 1500000 | tf_op jit(solution)/shard_map/pallas_call | solution.py:712
  16.5 2.5 %all-to-all-done = bf16[16,24,128]{2,1,0:T(8,128)(2,1)S(1)} async-done(((bf16[16,24,128]{2,1,0:T(8,128)(2,1)}), bf16[16,24,128]{2,1,0:T(8,128)(2,1)S(1)}, u32[]{:S(2)}, u32[]{:S(2)}) %all-to-all-start) | async-done | bytes 98336 | tf_op jit(solution)/shard_map/all_to_all | solution.py:710
  19.0 0.7 copy-done.17
  19.7 1.2 %shard_map.239.after = bf16[128,128]{1,0:T(8,128)(2,1)} custom-call(bf16[384,128]{1,0:T(8,128)(2,1)S(1)} %bitcast.15, f32[8,128]{1,0:T(8,128)S(1)} %copy-done.17, bf16[512,256]{1,0:T(8,128)(2,1)S(1)} %copy-done.4), custom_call_target="tpu_custom_call" | custom-call | flops 20000000 | bytes 400000 | tf_op jit(solution)/shard_map/pallas_call | solution.py:728
  20.9 4.5 %all-to-all-start.1 = ((bf16[8,16,128]{2,1,0:T(8,128)(2,1)}), bf16[8,16,128]{2,1,0:T(8,128)(2,1)S(1)}, u32[]{:S(2)}, u32[]{:S(2)}) async-start(bf16[8,16,128]{2,1,0:T(8,128)(2,1)} %bitcast.3), calls=%async_computation.1 | async-start | bytes 65536 | tf_op jit(solution)/shard_map/all_to_all | solution.py:681
  25.4 5.0 %collective-permute-start.3 = (f32[9,2,16,128]{3,2,1,0:T(8,128)}, f32[9,2,16,128]{3,2,1,0:T(8,128)S(1)}, u32[]{:S(2)}, u32[]{:S(2)}) collective-permute-start(f32[9,2,16,128]{3,2,1,0:T(8,128)} %get-tuple-element.36), channel_id=1, source_target_pairs={{0,16},{16,32},{32,48},{48,64},{64,80},{80,96},{96,112},{112,128},... | collective-permute-start | bytes 442376 | tf_op jit(solution)/shard_map/ppermute | solution.py:671
  30.4 1.3 %collective-permute-start.4 = (f32[7,2,16,128]{3,2,1,0:T(8,128)}, f32[7,2,16,128]{3,2,1,0:T(8,128)S(1)}, u32[]{:S(2)}, u32[]{:S(2)}) collective-permute-start(f32[7,2,16,128]{3,2,1,0:T(8,128)} %get-tuple-element.37), channel_id=1, source_target_pairs={{16,0},{32,16},{48,32},{64,48},{80,64},{96,80},{112,96},{128,112},... | collective-permute-start | bytes 344072 | tf_op jit(solution)/shard_map/ppermute | solution.py:671
  31.7 0.7 all-to-all-done.1
  32.4 10.8 %collective-permute-start = (bf16[128,128]{1,0:T(8,128)(2,1)S(1)}, bf16[128,128]{1,0:T(8,128)(2,1)S(1)}, u32[]{:S(2)}, u32[]{:S(2)}) collective-permute-start(bf16[128,128]{1,0:T(8,128)(2,1)S(1)} %bitcast.16), channel_id=1, source_target_pairs={{0,128},{16,144},{32,160},{48,176},{64,192},{80,208},{96,224},{112... | collective-permute-start | bytes 98312 | tf_op jit(solution)/shard_map/ppermute | solution.py:676
  43.3 8.9 %collective-permute-start.1 = (bf16[128,128]{1,0:T(8,128)(2,1)S(1)}, bf16[128,128]{1,0:T(8,128)(2,1)S(1)}, u32[]{:S(2)}, u32[]{:S(2)}) collective-permute-start(bf16[128,128]{1,0:T(8,128)(2,1)S(1)} %bitcast.17), channel_id=1, source_target_pairs={{0,256},{16,272},{32,288},{48,304},{64,320},{80,336},{96,352},{112... | collective-permute-start | bytes 98312 | tf_op jit(solution)/shard_map/ppermute | solution.py:676
  52.2 4.2 %collective-permute-start.2 = (bf16[128,128]{1,0:T(8,128)(2,1)S(1)}, bf16[128,128]{1,0:T(8,128)(2,1)S(1)}, u32[]{:S(2)}, u32[]{:S(2)}) collective-permute-start(bf16[128,128]{1,0:T(8,128)(2,1)S(1)} %bitcast.18), channel_id=1, source_target_pairs={{0,384},{16,400},{32,416},{48,432},{64,448},{80,464},{96,480},{112... | collective-permute-start | bytes 98312 | tf_op jit(solution)/shard_map/ppermute | solution.py:676
  56.5 1.9 %shard_map.240 = (f32[216,128]{1,0:T(8,128)S(1)}, f32[216,128]{1,0:T(8,128)S(1)}, bf16[128,128]{1,0:T(8,128)(2,1)S(1)}, f32[24,128]{1,0:T(8,128)S(1)}, f32[8,128]{1,0:T(8,128)S(1)}) custom-call(s32[64]{0:T(128)S(1)} %copy-done.16, f32[3,2,64]{2,1,0:T(2,128)S(1)} %bitcast.25, f32[3,16]{1,0:T(4,128)S(1)} %bitcast.27, s32[1,128]{1,0:T(1,128)S(1)} %add_bitcast_fusion.cells, ...), custom_call_target="tpu_custom_call" | custom-call | flops 20000000 | bytes 1000000 | tf_op jit(solution)/shard_map/pallas_call | solution.py:734
  58.7 2.2 %collective-permute-done.2.far_3 = bf16[128,128]{1,0:T(8,128)(2,1)S(1)} collective-permute-done((bf16[128,128]{1,0:T(8,128)(2,1)S(1)}, bf16[128,128]{1,0:T(8,128)(2,1)S(1)}, u32[]{:S(2)}, u32[]{:S(2)}) %collective-permute-start.2) | collective-permute-done | bytes 32800 | tf_op jit(solution)/shard_map/ppermute | solution.py:676
  60.8 0.7 shard_map.242
  61.5 11.6 %all_to_all.44 = bf16[8,16,128]{2,1,0:T(8,128)(2,1)S(1)} all-to-all(bf16[8,16,128]{2,1,0:T(8,128)(2,1)S(1)} %bitcast.21), channel_id=1, replica_groups={{0,16,32,48,64,80,96,112},{128,144,160,176,192,208,224,240},{256,272,28..., dimensions={0} | all-to-all | bytes 65536 | tf_op jit(solution)/shard_map/all_to_all | solution.py:681
  73.1 1.5 %shard_map.243 = bf16[128,896]{1,0:T(8,128)(2,1)} custom-call(bf16[128,128]{1,0:T(8,128)(2,1)S(1)} %bitcast.22, f32[8,128]{1,0:T(8,128)S(1)} %get-tuple-element.40.pre, bf16[128,384]{1,0:T(8,128)(2,1)S(1)} %copy-done.11), custom_call_target="tpu_custom_call" | custom-call | flops 40000000 | bytes 600000 | tf_op jit(solution)/shard_map/pallas_call | solution.py:785
  74.6 7.2 %all-to-all-start.3 = ((bf16[16,8,896]{2,1,0:T(8,128)(2,1)}), bf16[16,8,896]{2,1,0:T(8,128)(2,1)S(1)}, u32[]{:S(2)}, u32[]{:S(2)}) async-start(bf16[16,8,896]{2,1,0:T(8,128)(2,1)} %bitcast.10), calls=%async_computation.3 | async-start | bytes 458752 | tf_op jit(solution)/shard_map/all_to_all | solution.py:793
  81.8 3.5 %collective-permute-start.5 = (f32[100,2,128]{2,1,0:T(2,128)S(1)}, f32[100,2,128]{2,1,0:T(2,128)S(1)}, u32[]{:S(2)}, u32[]{:S(2)}) collective-permute-start(f32[100,2,128]{2,1,0:T(2,128)S(1)} %get-tuple-element.38.after), channel_id=1, source_target_pairs={{0,1},{1,2},{2,3},{3,4},{4,5},{5,6},{6,7},{7,8},{8,9},{9,10},{10,1... | collective-permute-start | bytes 307208 | tf_op jit(solution)/shard_map/ppermute | solution.py:671
  85.4 1.9 %collective-permute-start.6 = (f32[84,2,128]{2,1,0:T(2,128)S(1)}, f32[84,2,128]{2,1,0:T(2,128)S(1)}, u32[]{:S(2)}, u32[]{:S(2)}) collective-permute-start(f32[84,2,128]{2,1,0:T(2,128)S(1)} %get-tuple-element.41), channel_id=1, source_target_pairs={{1,0},{2,1},{3,2},{4,3},{5,4},{6,5},{7,6},{8,7},{9,8},{10,9},{11,1... | collective-permute-start | bytes 258056 | tf_op jit(solution)/shard_map/ppermute | solution.py:671
  87.3 3.9 %collective-permute-done.6.y_high = f32[84,2,128]{2,1,0:T(2,128)S(1)} collective-permute-done((f32[84,2,128]{2,1,0:T(2,128)S(1)}, f32[84,2,128]{2,1,0:T(2,128)S(1)}, u32[]{:S(2)}, u32[]{:S(2)}) %collective-permute-start.6) | collective-permute-done | bytes 86048 | tf_op jit(solution)/shard_map/ppermute | solution.py:671
  91.2 1.6 %shard_map.244 = (f32[3,10,24,128]{3,2,1,0:T(8,128)S(1)}, f32[3,10,24,128]{3,2,1,0:T(8,128)S(1)}, f32[10,24,128]{2,1,0:T(8,128)S(1)}, f32[8,16,128]{2,1,0:T(8,128)S(1)}, f32[3,8,16,128]{3,2,1,0:T(8,128)S(1)}) custom-call(s32[64]{0:T(128)S(1)} %copy-done.16, f32[3,2,64]{2,1,0:T(2,128)S(1)} %bitcast.26, f32[3,8,16,128]{3,2,1,0:T(8,128)S(1)} %copy-done.2, ...), custom_call_target="tpu_custom_call" | custom-call | flops 10000000 | bytes 3000000 | tf_op jit(solution)/shard_map/pallas_call | solution.py:770
  92.8 1.1 %shard_map.245 = (f32[3,8,16,128]{3,2,1,0:T(8,128)}, f32[3,8,16,128]{3,2,1,0:T(8,128)}, f32[8,16,128]{2,1,0:T(8,128)}, f32[3,2,64]{2,1,0:T(2,128)}) custom-call(bf16[128,896]{1,0:T(8,128)(2,1)S(1)} %bitcast.14, bf16[128,128]{1,0:T(8,128)(2,1)S(1)} %copy-done.12, f32[3,10,24,128]{3,2,1,0:T(8,128)S(1)} %get-tuple-element.42.early, ...), custom_call_target="tpu_custom_call" | custom-call | flops 40000000 | bytes 4000000 | tf_op jit(solution)/shard_map/pallas_call | solution.py:794
  (49 shorter events, 0.3 us)
Async XLA Ops:
  2.8 16.2 %all-to-all-start = ((bf16[16,24,128]{2,1,0:T(8,128)(2,1)}), bf16[16,24,128]{2,1,0:T(8,128)(2,1)S(1)}, u32[]{:S(2)}, u32[]{:S(2)}) async-start(bf16[16,24,128]{2,1,0:T(8,128)(2,1)} %bitcast.28), calls=%async_computation | async-start | bytes 196608 | tf_op jit(solution)/shard_map/all_to_all | solution.py:710
  13.1 5.9 %copy-start.4 = (bf16[512,256]{1,0:T(8,128)(2,1)S(1)}, bf16[512,256]{1,0:T(8,128)(2,1)}, u32[]{:S(2)}) copy-start(bf16[512,256]{1,0:T(8,128)(2,1)} %constant.19.clone.table) | copy-start | bytes 786436
  13.1 43.3 %copy-start.9 = (bf16[2,128,256]{2,1,0:T(8,128)(2,1)S(1)}, bf16[2,128,256]{2,1,0:T(8,128)(2,1)}, u32[]{:S(2)}) copy-start(bf16[2,128,256]{2,1,0:T(8,128)(2,1)} %constant.20.clone.at_x) | copy-start | bytes 393220
  13.1 43.3 %copy-start.10 = (bf16[16,2,16,128]{3,2,1,0:T(8,128)(2,1)S(1)}, bf16[16,2,16,128]{3,2,1,0:T(8,128)(2,1)}, u32[]{:S(2)}) copy-start(bf16[16,2,16,128]{3,2,1,0:T(8,128)(2,1)} %constant.22.clone.at_z) | copy-start | bytes 393220
  16.5 39.9 %copy-start.5 = (bf16[8,2,32,256]{3,2,1,0:T(8,128)(2,1)S(1)}, bf16[8,2,32,256]{3,2,1,0:T(8,128)(2,1)}, u32[]{:S(2)}) copy-start(bf16[8,2,32,256]{3,2,1,0:T(8,128)(2,1)} %constant.21.clone.at_y) | copy-start | bytes 786436
  19.7 36.7 %copy-start.8 = (bf16[2,48,16,16]{1,3,2,0:T(8,128)(2,1)S(1)}, bf16[2,48,16,16]{1,3,2,0:T(8,128)(2,1)}, u32[]{:S(2)}) copy-start(bf16[2,48,16,16]{1,3,2,0:T(8,128)(2,1)} %param.32) | copy-start | bytes 147460
  20.9 35.5 %copy-start.20 = (s32[64]{0:T(128)S(1)}, s32[64]{0:T(128)}, u32[]{:S(2)}) copy-start(s32[64]{0:T(128)} %src_in.1) | copy-start | bytes 772
  20.9 35.6 %copy-start.15 = (f32[16,48]{1,0:T(8,128)S(1)}, f32[16,48]{1,0:T(8,128)}, u32[]{:S(2)}) copy-start(f32[16,48]{1,0:T(8,128)} %gain_y.1) | copy-start | bytes 9220
  20.9 35.6 %copy-start.16 = (s32[64]{0:T(128)S(1)}, s32[64]{0:T(128)}, u32[]{:S(2)}) copy-start(s32[64]{0:T(128)} %mon.3) | copy-start | bytes 772
  20.9 35.6 %copy-start.18 = (f32[16,3]{0,1:T(4,128)S(1)}, f32[16,3]{0,1:T(4,128)}, u32[]{:S(2)}) copy-start(f32[16,3]{0,1:T(4,128)} %param.30) | copy-start | bytes 580
  20.9 35.6 %copy-start.19 = (f32[3,16]{1,0:T(4,128)S(1)}, f32[3,16]{1,0:T(4,128)}, u32[]{:S(2)}) copy-start(f32[3,16]{1,0:T(4,128)} %project.1) | copy-start | bytes 580
  20.9 11.6 %all-to-all-start.1 = ((bf16[8,16,128]{2,1,0:T(8,128)(2,1)}), bf16[8,16,128]{2,1,0:T(8,128)(2,1)S(1)}, u32[]{:S(2)}, u32[]{:S(2)}) async-start(bf16[8,16,128]{2,1,0:T(8,128)(2,1)} %bitcast.3), calls=%async_computation.1 | async-start | bytes 65536 | tf_op jit(solution)/shard_map/all_to_all | solution.py:681
  25.4 31.1 %copy-start.14 = (f32[16,48]{1,0:T(8,128)S(1)}, f32[16,48]{1,0:T(8,128)}, u32[]{:S(2)}) copy-start(f32[16,48]{1,0:T(8,128)} %gain_x.1) | copy-start | bytes 9220
  25.4 33.1 %collective-permute-start.3 = (f32[9,2,16,128]{3,2,1,0:T(8,128)}, f32[9,2,16,128]{3,2,1,0:T(8,128)S(1)}, u32[]{:S(2)}, u32[]{:S(2)}) collective-permute-start(f32[9,2,16,128]{3,2,1,0:T(8,128)} %get-tuple-element.36), channel_id=1, source_target_pairs={{0,16},{16,32},{32,48},{48,64},{64,80},{80,96},{96,112},{112,128},... | collective-permute-start | bytes 442376 | tf_op jit(solution)/shard_map/ppermute | solution.py:671
  30.4 28.1 %collective-permute-start.4 = (f32[7,2,16,128]{3,2,1,0:T(8,128)}, f32[7,2,16,128]{3,2,1,0:T(8,128)S(1)}, u32[]{:S(2)}, u32[]{:S(2)}) collective-permute-start(f32[7,2,16,128]{3,2,1,0:T(8,128)} %get-tuple-element.37), channel_id=1, source_target_pairs={{16,0},{32,16},{48,32},{64,48},{80,64},{96,80},{112,96},{128,112},... | collective-permute-start | bytes 344072 | tf_op jit(solution)/shard_map/ppermute | solution.py:671
  32.4 24.1 %copy-start.13 = (f32[2,64,3]{1,0,2:T(2,128)S(1)}, f32[2,64,3]{1,0,2:T(2,128)}, u32[]{:S(2)}) copy-start(f32[2,64,3]{1,0,2:T(2,128)} %param.29) | copy-start | bytes 4612
  32.4 26.2 %collective-permute-start = (bf16[128,128]{1,0:T(8,128)(2,1)S(1)}, bf16[128,128]{1,0:T(8,128)(2,1)S(1)}, u32[]{:S(2)}, u32[]{:S(2)}) collective-permute-start(bf16[128,128]{1,0:T(8,128)(2,1)S(1)} %bitcast.16), channel_id=1, source_target_pairs={{0,128},{16,144},{32,160},{48,176},{64,192},{80,208},{96,224},{112... | collective-permute-start | bytes 98312 | tf_op jit(solution)/shard_map/ppermute | solution.py:676
  43.3 15.4 %collective-permute-start.1 = (bf16[128,128]{1,0:T(8,128)(2,1)S(1)}, bf16[128,128]{1,0:T(8,128)(2,1)S(1)}, u32[]{:S(2)}, u32[]{:S(2)}) collective-permute-start(bf16[128,128]{1,0:T(8,128)(2,1)S(1)} %bitcast.17), channel_id=1, source_target_pairs={{0,256},{16,272},{32,288},{48,304},{64,320},{80,336},{96,352},{112... | collective-permute-start | bytes 98312 | tf_op jit(solution)/shard_map/ppermute | solution.py:676
  52.2 8.7 %collective-permute-start.2 = (bf16[128,128]{1,0:T(8,128)(2,1)S(1)}, bf16[128,128]{1,0:T(8,128)(2,1)S(1)}, u32[]{:S(2)}, u32[]{:S(2)}) collective-permute-start(bf16[128,128]{1,0:T(8,128)(2,1)S(1)} %bitcast.18), channel_id=1, source_target_pairs={{0,384},{16,400},{32,416},{48,432},{64,448},{80,464},{96,480},{112... | collective-permute-start | bytes 98312 | tf_op jit(solution)/shard_map/ppermute | solution.py:676
  58.5 2.3 %copy-start.3 = (bf16[4,256,128]{2,1,0:T(8,128)(2,1)S(1)}, bf16[4,256,128]{2,1,0:T(8,128)(2,1)}, u32[]{:S(2)}) copy-start(bf16[4,256,128]{2,1,0:T(8,128)(2,1)} %constant.23.clone.fwd_x) | copy-start | bytes 786436
  60.8 12.3 %copy-start.11 = (bf16[128,384]{1,0:T(8,128)(2,1)S(1)}, bf16[128,384]{1,0:T(8,128)(2,1)}, u32[]{:S(2)}) copy-start(bf16[128,384]{1,0:T(8,128)(2,1)} %constant.25.clone.inv_y) | copy-start | bytes 294916
  74.6 18.1 %all-to-all-start.3 = ((bf16[16,8,896]{2,1,0:T(8,128)(2,1)}), bf16[16,8,896]{2,1,0:T(8,128)(2,1)S(1)}, u32[]{:S(2)}, u32[]{:S(2)}) async-start(bf16[16,8,896]{2,1,0:T(8,128)(2,1)} %bitcast.10), calls=%async_computation.3 | async-start | bytes 458752 | tf_op jit(solution)/shard_map/all_to_all | solution.py:793
  81.8 9.3 %collective-permute-start.5 = (f32[100,2,128]{2,1,0:T(2,128)S(1)}, f32[100,2,128]{2,1,0:T(2,128)S(1)}, u32[]{:S(2)}, u32[]{:S(2)}) collective-permute-start(f32[100,2,128]{2,1,0:T(2,128)S(1)} %get-tuple-element.38.after), channel_id=1, source_target_pairs={{0,1},{1,2},{2,3},{3,4},{4,5},{5,6},{6,7},{7,8},{8,9},{9,10},{10,1... | collective-permute-start | bytes 307208 | tf_op jit(solution)/shard_map/ppermute | solution.py:671
  85.4 5.8 %collective-permute-start.6 = (f32[84,2,128]{2,1,0:T(2,128)S(1)}, f32[84,2,128]{2,1,0:T(2,128)S(1)}, u32[]{:S(2)}, u32[]{:S(2)}) collective-permute-start(f32[84,2,128]{2,1,0:T(2,128)S(1)} %get-tuple-element.41), channel_id=1, source_target_pairs={{1,0},{2,1},{3,2},{4,3},{5,4},{6,5},{7,6},{8,7},{9,8},{10,9},{11,1... | collective-permute-start | bytes 258056 | tf_op jit(solution)/shard_map/ppermute | solution.py:671
  (7 other events, 12.6 us)

commit v3 on v2

--- a/solution.py
+++ b/solution.py
@@ -63,14 +63,13 @@
     fwd_y[256:, 128 : 128 + K] = cy[:, y_of].T
     out["fwd_y"] = fwd_y
 
-    fwd_x = np.zeros((FAR, 2 * LANES, LANES), ml_dtypes.bfloat16)
+    fwd_x = np.zeros((2 * LANES, NX), ml_dtypes.bfloat16)
+    fwd_x[:K], fwd_x[64 : 64 + K] = cx, -sx
+    fwd_x[128 : 128 + K], fwd_x[192 : 192 + K] = sx, cx
     inv_x = np.zeros((FAR, LANES, LANES), ml_dtypes.bfloat16)
     for far in range(FAR):
         for n in range(NEAR):
             start = (far * NEAR + n) * RX
-            here, at = slice(start, start + RX), slice(n * 16, n * 16 + RX)
-            fwd_x[far, :K, at], fwd_x[far, 64 : 64 + K, at] = cx[:, here], -sx[:, here]
-            fwd_x[far, 128 : 128 + K, at], fwd_x[far, 192 : 192 + K, at] = sx[:, here], cx[:, here]
             x_of = (start + np.array([0, 1, 2, 3, 4, 5, 6, 7, 8, -1])) % NX
             inv_x[far, n * 16 : n * 16 + 10, :K] = cx[:, x_of].T
             inv_x[far, n * 16 : n * 16 + 10, 64 : 64 + K] = -sx[:, x_of].T
@@ -234,15 +233,15 @@
 
 
 def share_kernel(
-    src_in, perm_in, field, magnetic_in, material_in, saved_in,
-    taken, inverse, to_low, to_high,
-    src, perm, magnetic, material, saved, scaled, held, sems,
+    src_in, perm_in, field, magnetic_in, material_in,
+    taken, inverse,
+    src, perm, magnetic, material, scaled, held, sems,
 ):
     b, w = own_block()
     copies = fetch(
         (
             (src_in, src), (perm_in, perm), (magnetic_in, magnetic),
-            (material_in, material), (saved_in, saved),
+            (material_in, material),
         ),
         sems,
     )
@@ -262,12 +261,6 @@
     for c in range(3):
         scaled[c, 2:10, 8:24, :] = 0.5 * inv * field[c]
         held[c, 2:10, 8:24, :] = magnetic[c]
-        to_low[c], to_high[c] = field[c, 6:8], field[c, 0:2]
-        to_low[3 + c], to_high[3 + c] = magnetic[c, 6:8], magnetic[c, 0:2]
-    to_low[6], to_high[6] = inv[6:8], inv[0:2]
-    for n in range(2):
-        for c in range(2):
-            to_low[7 + n, c] = saved[n, 1 + c, 7].astype(F32)
     taken[...] = jnp.zeros((8, LANES), F32)
     spot_row, spot_lane = iota((8, LANES), 0), iota((8, LANES), 1)
 
@@ -345,10 +338,10 @@
                     moved = jnp.where(lane < to + 2, moved, pltpu.roll(rest, to + 2, 1))
                 within = (lane >= to) & (lane < to + SHARE)
                 parts[n] = parts[n] + jnp.where(within, moved, 0.0)
-    src = taken[...]
+    src = jnp.concatenate([taken[...], jnp.zeros((LANES - 8, LANES), F32)], 0).T
     high = src.astype(BF16).astype(F32)
-    extra = high + pltpu.roll(src - high, 64, 1)
-    out[...] = jnp.concatenate([t for p in parts for t in (p, extra)], 0).astype(BF16)
+    extra = pltpu.roll(high, 54, 1) + pltpu.roll(src - high, 118, 1)
+    out[...] = (jnp.concatenate(parts, 0) + extra[: NEAR * 8]).astype(BF16)
 
 
 def param_kernel(
@@ -420,18 +413,18 @@
 
 
 def filter_kernel(
-    own, far_1, far_2, far_3, coef_a, coef_b, fwd_x, inv_x, phase_x, phase_yz, after, out, pre
+    gathered, coef_a, coef_b, fwd_x, inv_x, phase_x, phase_yz, out
 ):
     b, w = own_block()
     far = b // NEAR
     lane = iota((1, LANES), 1)
-    both = jnp.zeros((2 * LANES, LANES), F32)
-    total = jnp.zeros((8, LANES), F32)
-    for t, ref in enumerate((own, far_1, far_2, far_3)):
-        got = ref[...]
-        both = both + jnp.dot(fwd_x[(far + FAR - t) % FAR], got, preferred_element_type=F32)
-        total = total + got.astype(F32).reshape(NEAR, 2, 8, LANES)[:, 1].sum(0)
-    pre[...] = jnp.where(lane < 64, total + pltpu.roll(total, 64, 1), 0.0)
+    got = gathered[...]
+    both = jnp.dot(fwd_x[...], got, preferred_element_type=F32)
+    total = got.astype(F32).reshape(BULK, 8, LANES).sum(0)
+    total = total + pltpu.roll(total, 64, 1)
+    total = jnp.where(lane < 6, pltpu.roll(total, LANES - 54, 1), 0.0)
+    total = jnp.concatenate([total, jnp.zeros((LANES - 8, LANES), F32)], 0).T[:8]
+    total = pltpu.roll(total, (b % NEAR) * 8, 1)
     full = (both[:LANES] + pltpu.roll(both[LANES:], 64, 1)).T
     field = [full[d * SHARE : d * SHARE + 24] for d in range(3)]
     turned = [pltpu.roll(f, 64, 1) for f in field]
@@ -453,19 +446,19 @@
         inv_x[far], right, (((1,), (1,)), ((), ())), preferred_element_type=F32
     ).reshape(NEAR, 2, 8, LANES)
     row = iota((8, LANES), 0)
-    extra = jnp.zeros((8, LANES), F32)
     for e in range(3):
         line = jnp.sum(near[e * 24 : (e + 1) * 24] * phase_yz[...], axis=0, keepdims=True)
         line = line + pltpu.roll(line, 64, 1)
-        high = line.astype(BF16).astype(F32)
-        extra = extra + jnp.where(row == 2 + e, jnp.where(lane < 64, high, line - high), 0.0)
+        total = total + jnp.where((row == e) & (lane < 64), line, 0.0)
+    high = total.astype(BF16).astype(F32)
+    extra = pltpu.roll(high + pltpu.roll(total - high, 64, 1), 2, 0)
     tiles = []
     for n in range(NEAR):
         tiles += [back[n, 0], back[n, 1] + extra]
     out[...] = jnp.concatenate(tiles, 0).astype(BF16)
 
 
-def spread_kernel(shares, pre, inv_y, out, rows):
+def spread_kernel(shares, inv_y, after, out, rows):
     lane = iota((1, LANES), 1)
     got = shares[...].astype(F32).reshape(NEAR, 16, LANES)
     rows[...] = jnp.zeros((32, 8, LANES), F32)
@@ -510,9 +503,8 @@
         edge.append(jnp.stack([wide[high * 16 + low, :, 256:384] for high in range(2)]))
     edge = exchange(edge, 8, 2)
     row = iota((8, LANES), 0)
-    spectral = pltpu.roll(got[:, 8:16].sum(0), 6, 0)
-    spectral = jnp.where((row < 3) & (lane < 64), spectral + pltpu.roll(spectral, 64, 1), 0.0)
-    total = pre[...] + spectral
+    total = pltpu.roll(got[:, 8:16].sum(0), 6, 0)
+    total = jnp.where((row < 6) & (lane < 64), total + pltpu.roll(total, 64, 1), 0.0)
     high = total.astype(BF16).astype(F32)
     last = high + pltpu.roll(total - high, 64, 1)
     blocks = []
@@ -521,6 +513,16 @@
         tiles += [edge[w][high_x] for high_x in range(2)] + [last]
         blocks.append(jnp.concatenate(tiles, 1))
     out[...] = jnp.concatenate(blocks, 0).astype(BF16)
+
+
+def edge_kernel(electric, magnetic, inverse, saved, after, to_low, to_high):
+    for c in range(3):
+        to_low[c], to_high[c] = electric[c, 6:8], electric[c, 0:2]
+        to_low[3 + c], to_high[3 + c] = magnetic[c, 6:8], magnetic[c, 0:2]
+    to_low[6], to_high[6] = inverse[6:8], inverse[0:2]
+    for n in range(2):
+        for c in range(2):
+            to_low[7 + n, c] = saved[n, 1 + c, 7].astype(F32)
 
 
 def corner_kernel(electric, magnetic, inverse, saved, x_low, x_high, after, to_low, to_high):
@@ -671,9 +673,12 @@
     return lax.ppermute(block, axis, route)
 
 
-def passed_far(block, distance):
-    route = [(i, (i + distance * NEAR) % BULK) for i in range(BULK)]
-    return lax.ppermute(block, "bulk", route)
+def joined_far(block):
+    groups = [[f * NEAR + n for f in range(FAR)] for n in range(NEAR)]
+    copies = jnp.concatenate([block] * FAR, 0)
+    return lax.all_to_all(
+        copies, "bulk", split_axis=0, concat_axis=0, axis_index_groups=groups, tiled=True
+    )
 
 
 def dealt_near(block):
@@ -709,24 +714,21 @@
     )(monitor_cells, weights, seed_electric, tables_of("lift_z"))
     lines = lax.all_to_all(payload, "wide", split_axis=0, concat_axis=0, tiled=True)
 
-    taken, inverse, to_low, to_high = call(
+    taken, inverse = call(
         share_kernel,
-        (shape(8, LANES), shape(*block), shape(9, 2, RY, NZ), shape(7, 2, RY, NZ)),
-        "aavaaa",
+        (shape(8, LANES), shape(*block)),
+        "aavaa",
         [
             pltpu.SMEM((64,), jnp.int32), pltpu.SMEM((8,), F32), pltpu.VMEM((3, *block), F32),
-            pltpu.VMEM(block, jnp.int32), pltpu.VMEM((2, 3, *block), BF16),
-            pltpu.VMEM((3, 12, 32, NZ), F32), pltpu.VMEM((3, 12, 32, NZ), F32), dma((5,)),
+            pltpu.VMEM(block, jnp.int32), pltpu.VMEM((3, 12, 32, NZ), F32),
+            pltpu.VMEM((3, 12, 32, NZ), F32), dma((4,)),
         ],
         3_000_000,
         1_500_000,
-        big,
-    )(source_cells, permittivity, field, seed_magnetic, material, saved_magnetic)
-    x_low = passed_along(to_low, "bulk", 1)
-    x_high = passed_along(to_high, "bulk", -1)
+    )(source_cells, permittivity, field, seed_magnetic, material)
 
     dealt = call(
-        middle_kernel, shape(LANES, LANES, dtype=BF16), "vvv", (), 20_000_000, 400_000
+        middle_kernel, shape(NEAR * 8, LANES, dtype=BF16), "vvv", (), 20_000_000, 400_000
     )(lines, taken, tables_of("fwd_y"))
     own = dealt_near(dealt)
 
@@ -747,25 +749,23 @@
         dealt,
     )
 
-    far = [passed_far(own, t) for t in (1, 2, 3)]
+    gathered = joined_far(own)
+    to_low, to_high = call(
+        edge_kernel, (shape(9, 2, RY, NZ), shape(7, 2, RY, NZ)), "vvvva", (), 0, 500_000
+    )(field, seed_magnetic, inverse, saved_magnetic, own)
+    x_low = passed_along(to_low, "bulk", 1)
+    x_high = passed_along(to_high, "bulk", -1)
+
+    shares = call(
+        filter_kernel, shape(LANES, LANES, dtype=BF16), "vvvvvvv", (), 40_000_000, 600_000
+    )(gathered, coef_a, coef_b, tables_of("fwd_x"), tables_of("inv_x"), phase_x, phase_yz)
+    back = dealt_near(shares)
+
     low_part, high_part = call(
         corner_kernel, (shape(100, 2, NZ), shape(84, 2, NZ)), "vvvvvva", (), 0, 1_000_000
-    )(field, seed_magnetic, inverse, saved_magnetic, x_low, x_high, own)
+    )(field, seed_magnetic, inverse, saved_magnetic, x_low, x_high, shares)
     y_low = passed_along(low_part, "wide", 1)
     y_high = passed_along(high_part, "wide", -1)
-
-    shares, pre = call(
-        filter_kernel,
-        (shape(LANES, LANES, dtype=BF16), shape(8, LANES)),
-        "vvvvvvvvvva",
-        (),
-        40_000_000,
-        600_000,
-    )(
-        own, *far, coef_a, coef_b, tables_of("fwd_x"), tables_of("inv_x"), phase_x, phase_yz,
-        low_part,
-    )
-    back = dealt_near(shares)
 
     early, curled, factor, first_grad, ready = call(
         first_kernel,
@@ -785,11 +785,11 @@
     sent = call(
         spread_kernel,
         shape(128, 896, dtype=BF16),
-        "vvv",
+        "vva",
         [pltpu.VMEM((32, 8, LANES), F32)],
         40_000_000,
         600_000,
-    )(back, pre, tables_of("inv_y"))
+    )(back, tables_of("inv_y"), factor)
     returned = lax.all_to_all(sent, "wide", split_axis=0, concat_axis=0, tiled=True)
     grad_e, grad_h, grad_eps, sources = call(
         second_kernel,

time: 94.7 us -> 88.7 us (0.937)
  starting transfers between devices: 57.6 us -> 36.9 us
  blocking collectives: 11.6 us -> 23.5 us
  waiting for transfers between devices: 9.27 us -> 13.5 us
  Pallas kernels: 13.6 us -> 10.9 us
    ppermute x3 -> x0, starting transfers between devices: 23.9 us -> none  [passed_far(): return lax.ppermute(block, 'bulk', route)]
    all_to_all x0 -> x1, blocking collectives: none -> 12.2 us  [body(): lax.all_to_all(sent, 'wide', split_axis=0, concat_axis=0, tiled=True)]
    all_to_all x1, waiting for transfers between devices: 0.01 us -> 5.53 us  [joined_far(): lax.all_to_all(copies, 'bulk', split_axis=0, concat_axis=0, axis_index_gr...]
    all_to_all x1, starting transfers between devices: 7.17 us -> 12.1 us  [joined_far(): lax.all_to_all(copies, 'bulk', split_axis=0, concat_axis=0, axis_index_gr...]
    pallas_call x4 -> x5, Pallas kernels: 6.72 us -> 3.94 us  [the longest x1 1.37 us: body(): call(filter_kernel, shape(LANES, LANES, dtype=BF16), 'vvvvvvv', (), 40000...]
    ppermute x3 -> x0, waiting for transfers between devices: 2.16 us -> none  [passed_far(): return lax.ppermute(block, 'bulk', route)]
    all_to_all x1, waiting for transfers between devices: 2.49 us -> 3.83 us  [body(): lax.all_to_all(payload, 'wide', split_axis=0, concat_axis=0, tiled=True)]
    ppermute x4, starting transfers between devices: 11.7 us -> 10.5 us  [passed_along(): return lax.ppermute(block, axis, route)]
  transfers between devices with their start and end apart: 10 -> 7, of which waited for: 4 -> 3; matrix products, arithmetic and copies ran while one was open for 0% -> 0% of each run, Pallas kernels for 7% -> 7%
where the time goes in v3:
time: 88.7 us; the launch traced here: 88 us
  starting transfers between devices  36.9 us (42%)
  blocking collectives  23.5 us (26%)
  waiting for transfers between devices  13.5 us (15%)
  Pallas kernels  10.9 us (12%)
  local copies, waits for them, and re-layouts  1.58 us (2%)
  between operations  0.95 us (1%)
    all_to_all x1, blocking collectives, body(): lax.all_to_all(sent, 'wide', split_axis=0, concat_axis=0, tiled=True)  12.2 us
    all_to_all x1, starting transfers between devices, joined_far(): lax.all_to_all(copies, 'bulk', split_axis=0, concat_axis=0, axis_index_gr...  12.1 us
    all_to_all x1, blocking collectives, dealt_near(): lax.all_to_all(block, 'bulk', split_axis=0, concat_axis=0, axis_index_gro...  11.3 us
    ppermute x4, starting transfers between devices, passed_along(): return lax.ppermute(block, axis, route)  10.5 us
    all_to_all x1, starting transfers between devices, body(): lax.all_to_all(payload, 'wide', split_axis=0, concat_axis=0, tiled=True)  10.4 us
    all_to_all x1, waiting for transfers between devices, joined_far(): lax.all_to_all(copies, 'bulk', split_axis=0, concat_axis=0, axis_index_gr...  5.53 us
    ppermute x4, waiting for transfers between devices, passed_along(): return lax.ppermute(block, axis, route)  4.12 us
    all_to_all x1, starting transfers between devices, dealt_near(): lax.all_to_all(block, 'bulk', split_axis=0, concat_axis=0, axis_index_gro...  3.91 us
  transfers between devices with their start and end apart: 7, of which 3 were waited for; matrix products, arithmetic and copies ran while one was open for 0% of the time, Pallas kernels for 7%

profile of v3, /device:TPU:1, one launch (start us, length us, event | category | flops | bytes accessed | tf_op | source)
XLA Modules:
  0.0 88.0 jit_solution(6627851006540266756)
XLA Ops:
  0.6 2.3 %shard_map.237 = (bf16[384,128]{1,0:T(8,128)(2,1)}, f32[3,8,16,128]{3,2,1,0:T(8,128)}) custom-call(s32[64]{0:T(128)} %mon.3, f32[3,2,64]{2,1,0:T(2,128)} %bitcast.25, f32[3,8,16,128]{3,2,1,0:T(8,128)} %electric.1, bf16[128,128]{1,0:T(8,128)(2,1)} %constant.18.clone.table_in), custom_call_target="tpu_custom_call" | custom-call | flops 13000000 | bytes 500000 | tf_op jit(solution)/shard_map/pallas_call | solution.py:703
  3.0 10.4 %all-to-all-start = ((bf16[16,24,128]{2,1,0:T(8,128)(2,1)}), bf16[16,24,128]{2,1,0:T(8,128)(2,1)S(1)}, u32[]{:S(2)}, u32[]{:S(2)}) async-start(bf16[16,24,128]{2,1,0:T(8,128)(2,1)} %bitcast.29), calls=%async_computation | async-start | bytes 196608 | tf_op jit(solution)/shard_map/all_to_all | solution.py:715
  13.4 0.9 copy-done.11
  14.3 1.1 %shard_map.238 = (f32[8,128]{1,0:T(8,128)S(1)}, f32[8,16,128]{2,1,0:T(8,128)S(1)}) custom-call(s32[64]{0:T(128)S(1)} %copy-done.20, f32[8]{0:T(128)S(1)} %copy-done.19, f32[3,8,16,128]{3,2,1,0:T(8,128)S(1)} %copy-done.1, f32[3,8,16,128]{3,2,1,0:T(8,128)S(1)} %copy-done, s32[8,16,128]{2,1,0:T(8,128)S(1)} %copy-done.11), custom_call_target="tpu_custom_call" | custom-call | flops 3000000 | bytes 1500000 | tf_op jit(solution)/shard_map/pallas_call | solution.py:717
  15.4 3.8 %all-to-all-done = bf16[16,24,128]{2,1,0:T(8,128)(2,1)S(1)} async-done(((bf16[16,24,128]{2,1,0:T(8,128)(2,1)}), bf16[16,24,128]{2,1,0:T(8,128)(2,1)S(1)}, u32[]{:S(2)}, u32[]{:S(2)}) %all-to-all-start) | async-done | bytes 98336 | tf_op jit(solution)/shard_map/all_to_all | solution.py:715
  19.3 0.6 shard_map.239.after
  19.9 11.3 %all_to_all.55 = bf16[8,8,128]{2,1,0:T(8,128)(2,1)S(1)} all-to-all(bf16[8,8,128]{2,1,0:T(8,128)(2,1)S(1)} %bitcast.20), channel_id=1, replica_groups={{0,16,32,48,64,80,96,112},{128,144,160,176,192,208,224,240},{256,272,28..., dimensions={0} | all-to-all | bytes 32768 | tf_op jit(solution)/shard_map/all_to_all | solution.py:686
  31.2 0.6 pad_maximum_fusion
  31.8 12.1 %all-to-all-start.2 = ((bf16[4,64,128]{2,1,0:T(8,128)(2,1)}), bf16[4,64,128]{2,1,0:T(8,128)(2,1)S(1)}, u32[]{:S(2)}, u32[]{:S(2)}) async-start(bf16[4,64,128]{2,1,0:T(8,128)(2,1)} %bitcast.5), calls=%async_computation.2 | async-start | bytes 131072 | tf_op jit(solution)/shard_map/all_to_all | solution.py:679
  44.0 2.6 %collective-permute-start = (f32[9,2,16,128]{3,2,1,0:T(8,128)S(1)}, f32[9,2,16,128]{3,2,1,0:T(8,128)S(1)}, u32[]{:S(2)}, u32[]{:S(2)}) collective-permute-start(f32[9,2,16,128]{3,2,1,0:T(8,128)S(1)} %get-tuple-element.34), channel_id=1, source_target_pairs={{0,16},{16,32},{32,48},{48,64},{64,80},{80,96},{96,112},{112,128},... | collective-permute-start | bytes 442376 | tf_op jit(solution)/shard_map/ppermute | solution.py:673
  46.6 1.3 %collective-permute-start.1 = (f32[7,2,16,128]{3,2,1,0:T(8,128)S(1)}, f32[7,2,16,128]{3,2,1,0:T(8,128)S(1)}, u32[]{:S(2)}, u32[]{:S(2)}) collective-permute-start(f32[7,2,16,128]{3,2,1,0:T(8,128)S(1)} %get-tuple-element.35), channel_id=1, source_target_pairs={{16,0},{32,16},{48,32},{64,48},{80,64},{96,80},{112,96},{128,112},... | collective-permute-start | bytes 344072 | tf_op jit(solution)/shard_map/ppermute | solution.py:673
  47.9 0.1 add_bitcast_fusion.cells
  48.0 0.6 copy-done.17
  48.7 1.9 %shard_map.240 = (f32[216,128]{1,0:T(8,128)S(1)}, f32[216,128]{1,0:T(8,128)S(1)}, bf16[128,128]{1,0:T(8,128)(2,1)S(1)}, f32[24,128]{1,0:T(8,128)S(1)}, f32[8,128]{1,0:T(8,128)S(1)}) custom-call(s32[64]{0:T(128)S(1)} %copy-done.16, f32[3,2,64]{2,1,0:T(2,128)S(1)} %bitcast.26, f32[3,16]{1,0:T(4,128)S(1)} %bitcast.28, s32[1,128]{1,0:T(1,128)S(1)} %add_bitcast_fusion.cells, ...), custom_call_target="tpu_custom_call" | custom-call | flops 20000000 | bytes 1000000 | tf_op jit(solution)/shard_map/pallas_call | solution.py:736
  50.6 5.5 %all-to-all-done.2 = bf16[4,64,128]{2,1,0:T(8,128)(2,1)S(1)} async-done(((bf16[4,64,128]{2,1,0:T(8,128)(2,1)}), bf16[4,64,128]{2,1,0:T(8,128)(2,1)S(1)}, u32[]{:S(2)}, u32[]{:S(2)}) %all-to-all-start.2) | async-done | bytes 65568 | tf_op jit(solution)/shard_map/all_to_all | solution.py:679
  56.1 1.4 %shard_map.241.after = bf16[128,128]{1,0:T(8,128)(2,1)} custom-call(bf16[256,128]{1,0:T(8,128)(2,1)S(1)} %bitcast.19, f32[216,128]{1,0:T(8,128)S(1)} %get-tuple-element.29.coef_a, f32[216,128]{1,0:T(8,128)S(1)} %get-tuple-element.30.coef_b, bf16[256,256]{1,0:T(8,128)(2,1)S(1)} %copy-done.5, bf16[4,128,128]{2,1,0:T(8,128)(2,1)S(1)} %copy-done.6, ...), custom_call_target="tpu_custom_call" | custom-call | flops 40000000 | bytes 600000 | tf_op jit(solution)/shard_map/pallas_call | solution.py:759
  57.5 3.9 %all-to-all-start.3 = ((bf16[8,16,128]{2,1,0:T(8,128)(2,1)}), bf16[8,16,128]{2,1,0:T(8,128)(2,1)S(1)}, u32[]{:S(2)}, u32[]{:S(2)}) async-start(bf16[8,16,128]{2,1,0:T(8,128)(2,1)} %bitcast.10), calls=%async_computation.3 | async-start | bytes 65536 | tf_op jit(solution)/shard_map/all_to_all | solution.py:686
  61.5 4.6 %collective-permute-start.2 = (f32[100,2,128]{2,1,0:T(2,128)S(1)}, f32[100,2,128]{2,1,0:T(2,128)S(1)}, u32[]{:S(2)}, u32[]{:S(2)}) collective-permute-start(f32[100,2,128]{2,1,0:T(2,128)S(1)} %get-tuple-element.36), channel_id=1, source_target_pairs={{0,1},{1,2},{2,3},{3,4},{4,5},{5,6},{6,7},{7,8},{8,9},{9,10},{10,1... | collective-permute-start | bytes 307208 | tf_op jit(solution)/shard_map/ppermute | solution.py:673
  66.1 2.1 %collective-permute-start.3 = (f32[84,2,128]{2,1,0:T(2,128)S(1)}, f32[84,2,128]{2,1,0:T(2,128)S(1)}, u32[]{:S(2)}, u32[]{:S(2)}) collective-permute-start(f32[84,2,128]{2,1,0:T(2,128)S(1)} %get-tuple-element.37), channel_id=1, source_target_pairs={{1,0},{2,1},{3,2},{4,3},{5,4},{6,5},{7,6},{8,7},{9,8},{10,9},{11,1... | collective-permute-start | bytes 258056 | tf_op jit(solution)/shard_map/ppermute | solution.py:673
  68.2 4.1 %collective-permute-done.3.y_high = f32[84,2,128]{2,1,0:T(2,128)S(1)} collective-permute-done((f32[84,2,128]{2,1,0:T(2,128)S(1)}, f32[84,2,128]{2,1,0:T(2,128)S(1)}, u32[]{:S(2)}, u32[]{:S(2)}) %collective-permute-start.3) | collective-permute-done | bytes 86048 | tf_op jit(solution)/shard_map/ppermute | solution.py:673
  72.3 1.6 %shard_map.244 = (f32[3,10,24,128]{3,2,1,0:T(8,128)S(1)}, f32[3,10,24,128]{3,2,1,0:T(8,128)S(1)}, f32[10,24,128]{2,1,0:T(8,128)S(1)}, f32[8,16,128]{2,1,0:T(8,128)S(1)}, f32[3,8,16,128]{3,2,1,0:T(8,128)S(1)}) custom-call(s32[64]{0:T(128)S(1)} %copy-done.16, f32[3,2,64]{2,1,0:T(2,128)S(1)} %bitcast.27, f32[3,8,16,128]{3,2,1,0:T(8,128)S(1)} %copy-done.1, ...), custom_call_target="tpu_custom_call" | custom-call | flops 10000000 | bytes 3000000 | tf_op jit(solution)/shard_map/pallas_call | solution.py:770
  73.9 0.8 shard_map.245
  74.8 12.2 %all_to_all.56 = bf16[16,8,896]{2,1,0:T(8,128)(2,1)S(1)} all-to-all(bf16[16,8,896]{2,1,0:T(8,128)(2,1)S(1)} %bitcast.16), channel_id=1, replica_groups=mesh['bulk'=32,'wide'=16] {'wide'}, dimensions={0} | all-to-all | bytes 458752 | tf_op jit(solution)/shard_map/all_to_all | solution.py:793
  86.9 1.1 %shard_map.246 = (f32[3,8,16,128]{3,2,1,0:T(8,128)}, f32[3,8,16,128]{3,2,1,0:T(8,128)}, f32[8,16,128]{2,1,0:T(8,128)}, f32[3,2,64]{2,1,0:T(2,128)}) custom-call(bf16[128,896]{1,0:T(8,128)(2,1)S(1)} %bitcast.17, bf16[128,128]{1,0:T(8,128)(2,1)S(1)} %copy-done.12, f32[3,10,24,128]{3,2,1,0:T(8,128)S(1)} %get-tuple-element.39.early, ...), custom_call_target="tpu_custom_call" | custom-call | flops 40000000 | bytes 4000000 | tf_op jit(solution)/shard_map/pallas_call | solution.py:794
  (46 shorter events, 0.2 us)
Async XLA Ops:
  0.6 12.7 %copy-start = (f32[3,8,16,128]{3,2,1,0:T(8,128)S(1)}, f32[3,8,16,128]{3,2,1,0:T(8,128)}, u32[]{:S(2)}) copy-start(f32[3,8,16,128]{3,2,1,0:T(8,128)} %magnetic.5) | copy-start | bytes 589828
  3.0 10.4 %copy-start.1 = (f32[3,8,16,128]{3,2,1,0:T(8,128)S(1)}, f32[3,8,16,128]{3,2,1,0:T(8,128)}, u32[]{:S(2)}) copy-start(f32[3,8,16,128]{3,2,1,0:T(8,128)} %get-tuple-element.27.field.electric) | copy-start | bytes 589828
  3.0 10.4 %copy-start.19 = (f32[8]{0:T(128)S(1)}, f32[8]{0:T(128)}, u32[]{:S(2)}) copy-start(f32[8]{0:T(128)} %perm_in.1) | copy-start | bytes 100
  3.0 10.4 %copy-start.20 = (s32[64]{0:T(128)S(1)}, s32[64]{0:T(128)}, u32[]{:S(2)}) copy-start(s32[64]{0:T(128)} %src_in.1) | copy-start | bytes 772
  3.0 16.3 %all-to-all-start = ((bf16[16,24,128]{2,1,0:T(8,128)(2,1)}), bf16[16,24,128]{2,1,0:T(8,128)(2,1)S(1)}, u32[]{:S(2)}, u32[]{:S(2)}) async-start(bf16[16,24,128]{2,1,0:T(8,128)(2,1)} %bitcast.29), calls=%async_computation | async-start | bytes 196608 | tf_op jit(solution)/shard_map/all_to_all | solution.py:715
  13.4 5.9 %copy-start.3 = (bf16[512,256]{1,0:T(8,128)(2,1)S(1)}, bf16[512,256]{1,0:T(8,128)(2,1)}, u32[]{:S(2)}) copy-start(bf16[512,256]{1,0:T(8,128)(2,1)} %constant.19.clone.table) | copy-start | bytes 786436
  19.8 24.0 %copy-start.2 = (bf16[2,3,8,16,128]{4,3,2,1,0:T(8,128)(2,1)S(1)}, bf16[2,3,8,16,128]{4,3,2,1,0:T(8,128)(2,1)}, u32[]{:S(2)}) copy-start(bf16[2,3,8,16,128]{4,3,2,1,0:T(8,128)(2,1)} %saved.5) | copy-start | bytes 589828
  31.8 24.3 %all-to-all-start.2 = ((bf16[4,64,128]{2,1,0:T(8,128)(2,1)}), bf16[4,64,128]{2,1,0:T(8,128)(2,1)S(1)}, u32[]{:S(2)}, u32[]{:S(2)}) async-start(bf16[4,64,128]{2,1,0:T(8,128)(2,1)} %bitcast.5), calls=%async_computation.2 | async-start | bytes 131072 | tf_op jit(solution)/shard_map/all_to_all | solution.py:679
  43.9 4.1 %copy-start.4 = (bf16[8,2,32,256]{3,2,1,0:T(8,128)(2,1)S(1)}, bf16[8,2,32,256]{3,2,1,0:T(8,128)(2,1)}, u32[]{:S(2)}) copy-start(bf16[8,2,32,256]{3,2,1,0:T(8,128)(2,1)} %constant.21.clone.at_y) | copy-start | bytes 786436
  43.9 4.1 %copy-start.7 = (bf16[2,48,16,16]{1,3,2,0:T(8,128)(2,1)S(1)}, bf16[2,48,16,16]{1,3,2,0:T(8,128)(2,1)}, u32[]{:S(2)}) copy-start(bf16[2,48,16,16]{1,3,2,0:T(8,128)(2,1)} %param.32) | copy-start | bytes 147460
  43.9 4.1 %copy-start.8 = (bf16[2,128,256]{2,1,0:T(8,128)(2,1)S(1)}, bf16[2,128,256]{2,1,0:T(8,128)(2,1)}, u32[]{:S(2)}) copy-start(bf16[2,128,256]{2,1,0:T(8,128)(2,1)} %constant.20.clone.at_x) | copy-start | bytes 393220
  43.9 4.1 %copy-start.9 = (bf16[16,2,16,128]{3,2,1,0:T(8,128)(2,1)S(1)}, bf16[16,2,16,128]{3,2,1,0:T(8,128)(2,1)}, u32[]{:S(2)}) copy-start(bf16[16,2,16,128]{3,2,1,0:T(8,128)(2,1)} %constant.22.clone.at_z) | copy-start | bytes 393220
  43.9 4.1 %copy-start.14 = (f32[16,48]{1,0:T(8,128)S(1)}, f32[16,48]{1,0:T(8,128)}, u32[]{:S(2)}) copy-start(f32[16,48]{1,0:T(8,128)} %gain_x.1) | copy-start | bytes 9220
  43.9 4.1 %copy-start.15 = (f32[16,48]{1,0:T(8,128)S(1)}, f32[16,48]{1,0:T(8,128)}, u32[]{:S(2)}) copy-start(f32[16,48]{1,0:T(8,128)} %gain_y.1) | copy-start | bytes 9220
  44.0 4.1 %copy-start.18 = (f32[3,16]{1,0:T(4,128)S(1)}, f32[3,16]{1,0:T(4,128)}, u32[]{:S(2)}) copy-start(f32[3,16]{1,0:T(4,128)} %project.1) | copy-start | bytes 580
  44.0 17.4 %collective-permute-start = (f32[9,2,16,128]{3,2,1,0:T(8,128)S(1)}, f32[9,2,16,128]{3,2,1,0:T(8,128)S(1)}, u32[]{:S(2)}, u32[]{:S(2)}) collective-permute-start(f32[9,2,16,128]{3,2,1,0:T(8,128)S(1)} %get-tuple-element.34), channel_id=1, source_target_pairs={{0,16},{16,32},{32,48},{48,64},{64,80},{80,96},{96,112},{112,128},... | collective-permute-start | bytes 442376 | tf_op jit(solution)/shard_map/ppermute | solution.py:673
  46.6 14.8 %collective-permute-start.1 = (f32[7,2,16,128]{3,2,1,0:T(8,128)S(1)}, f32[7,2,16,128]{3,2,1,0:T(8,128)S(1)}, u32[]{:S(2)}, u32[]{:S(2)}) collective-permute-start(f32[7,2,16,128]{3,2,1,0:T(8,128)S(1)} %get-tuple-element.35), channel_id=1, source_target_pairs={{16,0},{32,16},{48,32},{64,48},{80,64},{96,80},{112,96},{128,112},... | collective-permute-start | bytes 344072 | tf_op jit(solution)/shard_map/ppermute | solution.py:673
  48.7 7.5 %copy-start.5 = (bf16[256,256]{1,0:T(8,128)(2,1)S(1)}, bf16[256,256]{1,0:T(8,128)(2,1)}, u32[]{:S(2)}) copy-start(bf16[256,256]{1,0:T(8,128)(2,1)} %constant.23.clone.fwd_x) | copy-start | bytes 393220
  48.7 7.5 %copy-start.6 = (bf16[4,128,128]{2,1,0:T(8,128)(2,1)S(1)}, bf16[4,128,128]{2,1,0:T(8,128)(2,1)}, u32[]{:S(2)}) copy-start(bf16[4,128,128]{2,1,0:T(8,128)(2,1)} %constant.24.clone.inv_x) | copy-start | bytes 393220
  57.5 16.4 %all-to-all-start.3 = ((bf16[8,16,128]{2,1,0:T(8,128)(2,1)}), bf16[8,16,128]{2,1,0:T(8,128)(2,1)S(1)}, u32[]{:S(2)}, u32[]{:S(2)}) async-start(bf16[8,16,128]{2,1,0:T(8,128)(2,1)} %bitcast.10), calls=%async_computation.3 | async-start | bytes 65536 | tf_op jit(solution)/shard_map/all_to_all | solution.py:686
  61.5 10.8 %collective-permute-start.2 = (f32[100,2,128]{2,1,0:T(2,128)S(1)}, f32[100,2,128]{2,1,0:T(2,128)S(1)}, u32[]{:S(2)}, u32[]{:S(2)}) collective-permute-start(f32[100,2,128]{2,1,0:T(2,128)S(1)} %get-tuple-element.36), channel_id=1, source_target_pairs={{0,1},{1,2},{2,3},{3,4},{4,5},{5,6},{6,7},{7,8},{8,9},{9,10},{10,1... | collective-permute-start | bytes 307208 | tf_op jit(solution)/shard_map/ppermute | solution.py:673
  66.1 7.8 %copy-start.10 = (bf16[128,384]{1,0:T(8,128)(2,1)S(1)}, bf16[128,384]{1,0:T(8,128)(2,1)}, u32[]{:S(2)}) copy-start(bf16[128,384]{1,0:T(8,128)(2,1)} %constant.25.clone.inv_y) | copy-start | bytes 294916
  66.1 6.2 %collective-permute-start.3 = (f32[84,2,128]{2,1,0:T(2,128)S(1)}, f32[84,2,128]{2,1,0:T(2,128)S(1)}, u32[]{:S(2)}, u32[]{:S(2)}) collective-permute-start(f32[84,2,128]{2,1,0:T(2,128)S(1)} %get-tuple-element.37), channel_id=1, source_target_pairs={{1,0},{2,1},{3,2},{4,3},{5,4},{6,5},{7,6},{8,7},{9,8},{10,9},{11,1... | collective-permute-start | bytes 258056 | tf_op jit(solution)/shard_map/ppermute | solution.py:673
  74.7 12.2 %copy-start.12 = (bf16[128,128]{1,0:T(8,128)(2,1)S(1)}, bf16[128,128]{1,0:T(8,128)(2,1)}, u32[]{:S(2)}) copy-start(bf16[128,128]{1,0:T(8,128)(2,1)} %constant.26.clone.table) | copy-start | bytes 98308
  (4 other events, 3.7 us)

commit v4 on v3

--- a/solution.py
+++ b/solution.py
@@ -341,7 +341,9 @@
     src = jnp.concatenate([taken[...], jnp.zeros((LANES - 8, LANES), F32)], 0).T
     high = src.astype(BF16).astype(F32)
     extra = pltpu.roll(high, 54, 1) + pltpu.roll(src - high, 118, 1)
-    out[...] = (jnp.concatenate(parts, 0) + extra[: NEAR * 8]).astype(BF16)
+    deal = (jnp.concatenate(parts, 0) + extra[: NEAR * 8]).astype(BF16)
+    for f in range(FAR):
+        out[f * NEAR * 8 : (f + 1) * NEAR * 8, :] = deal
 
 
 def param_kernel(
@@ -413,7 +415,7 @@
 
 
 def filter_kernel(
-    gathered, coef_a, coef_b, fwd_x, inv_x, phase_x, phase_yz, out
+    gathered, coef_a, coef_b, fwd_x, inv_x, phase_x, phase_yz, after, out
 ):
     b, w = own_block()
     far = b // NEAR
@@ -458,7 +460,7 @@
     out[...] = jnp.concatenate(tiles, 0).astype(BF16)
 
 
-def spread_kernel(shares, inv_y, after, out, rows):
+def spread_kernel(shares, inv_y, after_low, after_high, out, rows):
     lane = iota((1, LANES), 1)
     got = shares[...].astype(F32).reshape(NEAR, 16, LANES)
     rows[...] = jnp.zeros((32, 8, LANES), F32)
@@ -673,14 +675,6 @@
     return lax.ppermute(block, axis, route)
 
 
-def joined_far(block):
-    groups = [[f * NEAR + n for f in range(FAR)] for n in range(NEAR)]
-    copies = jnp.concatenate([block] * FAR, 0)
-    return lax.all_to_all(
-        copies, "bulk", split_axis=0, concat_axis=0, axis_index_groups=groups, tiled=True
-    )
-
-
 def dealt_near(block):
     groups = [[f * NEAR + n for n in range(NEAR)] for f in range(FAR)]
     return lax.all_to_all(
@@ -728,9 +722,9 @@
     )(source_cells, permittivity, field, seed_magnetic, material)
 
     dealt = call(
-        middle_kernel, shape(NEAR * 8, LANES, dtype=BF16), "vvv", (), 20_000_000, 400_000
+        middle_kernel, shape(BULK * 8, LANES, dtype=BF16), "vvv", (), 20_000_000, 400_000
     )(lines, taken, tables_of("fwd_y"))
-    own = dealt_near(dealt)
+    gathered = lax.all_to_all(dealt, "bulk", split_axis=0, concat_axis=0, tiled=True)
 
     cells = jnp.concatenate([source_cells, source_cells]).reshape(1, LANES)
     coef_a, coef_b, phase_x, phase_yz, injected = call(
@@ -749,24 +743,35 @@
         dealt,
     )
 
-    gathered = joined_far(own)
     to_low, to_high = call(
         edge_kernel, (shape(9, 2, RY, NZ), shape(7, 2, RY, NZ)), "vvvva", (), 0, 500_000
-    )(field, seed_magnetic, inverse, saved_magnetic, own)
+    )(field, seed_magnetic, inverse, saved_magnetic, dealt)
     x_low = passed_along(to_low, "bulk", 1)
     x_high = passed_along(to_high, "bulk", -1)
 
-    shares = call(
-        filter_kernel, shape(LANES, LANES, dtype=BF16), "vvvvvvv", (), 40_000_000, 600_000
-    )(gathered, coef_a, coef_b, tables_of("fwd_x"), tables_of("inv_x"), phase_x, phase_yz)
-    back = dealt_near(shares)
-
     low_part, high_part = call(
         corner_kernel, (shape(100, 2, NZ), shape(84, 2, NZ)), "vvvvvva", (), 0, 1_000_000
-    )(field, seed_magnetic, inverse, saved_magnetic, x_low, x_high, shares)
+    )(field, seed_magnetic, inverse, saved_magnetic, x_low, x_high, coef_a)
+    shares = call(
+        filter_kernel, shape(LANES, LANES, dtype=BF16), "vvvvvvva", (), 40_000_000, 600_000
+    )(
+        gathered, coef_a, coef_b, tables_of("fwd_x"), tables_of("inv_x"), phase_x, phase_yz,
+        low_part,
+    )
+    back = dealt_near(shares)
+
     y_low = passed_along(low_part, "wide", 1)
     y_high = passed_along(high_part, "wide", -1)
 
+    sent = call(
+        spread_kernel,
+        shape(128, 896, dtype=BF16),
+        "vvaa",
+        [pltpu.VMEM((32, 8, LANES), F32)],
+        40_000_000,
+        600_000,
+    )(back, tables_of("inv_y"), y_low, y_high)
+    returned = lax.all_to_all(sent, "wide", split_axis=0, concat_axis=0, tiled=True)
     early, curled, factor, first_grad, ready = call(
         first_kernel,
         (
@@ -779,18 +784,9 @@
         3_000_000,
     )(
         monitor_cells, weights, field, seed_magnetic, inverse, saved_magnetic,
-        x_low, x_high, y_low, y_high, shares,
-    )
-
-    sent = call(
-        spread_kernel,
-        shape(128, 896, dtype=BF16),
-        "vva",
-        [pltpu.VMEM((32, 8, LANES), F32)],
-        40_000_000,
-        600_000,
-    )(back, tables_of("inv_y"), factor)
-    returned = lax.all_to_all(sent, "wide", split_axis=0, concat_axis=0, tiled=True)
+        x_low, x_high, y_low, y_high, sent,
+    )
+
     grad_e, grad_h, grad_eps, sources = call(
         second_kernel,
         (shape(3, *block), shape(3, *block), shape(*block), shape(3, 2, 64)),

time: 88.7 us -> 83.3 us (0.939)
  blocking collectives: 23.5 us -> 0 us
  starting transfers between devices: 36.9 us -> 49.4 us
  waiting for transfers between devices: 13.5 us -> 18.4 us
  Pallas kernels: 10.9 us -> 12.3 us
    all_to_all x2 -> x0, blocking collectives: 23.5 us -> none  [the longest x1 12.2 us: body(): lax.all_to_all(sent, 'wide', split_axis=0, concat_axis=0, tiled=True)]
    all_to_all x1 -> x2, starting transfers between devices: 12.1 us -> 19.4 us  [the longest x1 14 us: body(): lax.all_to_all(dealt, 'bulk', split_axis=0, concat_axis=0, tiled=True)]
    ppermute x4, waiting for transfers between devices: 4.12 us -> 7.65 us  [passed_along(): return lax.ppermute(block, axis, route)]
    all_to_all x1, starting transfers between devices: 3.91 us -> 7.32 us  [dealt_near(): lax.all_to_all(block, 'bulk', split_axis=0, concat_axis=0, axis_index_gro...]
    ppermute x4, starting transfers between devices: 10.5 us -> 12.3 us  [passed_along(): return lax.ppermute(block, axis, route)]
    all_to_all x1 -> x2, waiting for transfers between devices: 5.53 us -> 6.95 us  [the longest x1 5.31 us: body(): lax.all_to_all(sent, 'wide', split_axis=0, concat_axis=0, tiled=True)]
    pallas_call x3, Pallas kernels: 2.77 us -> 4.09 us  [the longest x1 1.51 us: body(): call(spread_kernel, shape(128, 896, dtype=BF16), 'vvaa', [pltpu.VMEM((32,...]
  transfers between devices with their start and end apart: 7 -> 8, of which waited for: 3 -> 5; matrix products, arithmetic and copies ran while one was open for 0% -> 0% of each run, Pallas kernels for 7% -> 6%
where the time goes in v4:
time: 83.3 us; the launch traced here: 82.7 us
  starting transfers between devices  49.4 us (59%)
  waiting for transfers between devices  18.4 us (22%)
  Pallas kernels  12.3 us (15%)
  local copies, waits for them, and re-layouts  1.58 us (2%)
  between operations  0.93 us (1%)
    all_to_all x1, starting transfers between devices, body(): lax.all_to_all(dealt, 'bulk', split_axis=0, concat_axis=0, tiled=True)  14 us
    ppermute x4, starting transfers between devices, passed_along(): return lax.ppermute(block, axis, route)  12.3 us
    all_to_all x1, starting transfers between devices, body(): lax.all_to_all(payload, 'wide', split_axis=0, concat_axis=0, tiled=True)  10.4 us
    ppermute x4, waiting for transfers between devices, passed_along(): return lax.ppermute(block, axis, route)  7.65 us
    all_to_all x1, starting transfers between devices, dealt_near(): lax.all_to_all(block, 'bulk', split_axis=0, concat_axis=0, axis_index_gro...  7.32 us
    all_to_all x1, starting transfers between devices, body(): lax.all_to_all(sent, 'wide', split_axis=0, concat_axis=0, tiled=True)  5.38 us
    all_to_all x1, waiting for transfers between devices, body(): lax.all_to_all(sent, 'wide', split_axis=0, concat_axis=0, tiled=True)  5.31 us
    all_to_all x1, waiting for transfers between devices, body(): lax.all_to_all(payload, 'wide', split_axis=0, concat_axis=0, tiled=True)  3.83 us
  transfers between devices with their start and end apart: 8, of which 5 were waited for; matrix products, arithmetic and copies ran while one was open for 0% of the time, Pallas kernels for 6%

profile of v4, /device:TPU:1, one launch (start us, length us, event | category | flops | bytes accessed | tf_op | source)
XLA Modules:
  0.0 82.7 jit_solution(7361079799189276622)
XLA Ops:
  0.6 2.3 %shard_map.237 = (bf16[384,128]{1,0:T(8,128)(2,1)}, f32[3,8,16,128]{3,2,1,0:T(8,128)}) custom-call(s32[64]{0:T(128)} %mon.3, f32[3,2,64]{2,1,0:T(2,128)} %bitcast.19, f32[3,8,16,128]{3,2,1,0:T(8,128)} %electric.1, bf16[128,128]{1,0:T(8,128)(2,1)} %constant.18.clone.table_in), custom_call_target="tpu_custom_call" | custom-call | flops 13000000 | bytes 500000 | tf_op jit(solution)/shard_map/pallas_call | solution.py:697
  3.0 10.4 %all-to-all-start = ((bf16[16,24,128]{2,1,0:T(8,128)(2,1)}), bf16[16,24,128]{2,1,0:T(8,128)(2,1)S(1)}, u32[]{:S(2)}, u32[]{:S(2)}) async-start(bf16[16,24,128]{2,1,0:T(8,128)(2,1)} %bitcast.23), calls=%async_computation | async-start | bytes 196608 | tf_op jit(solution)/shard_map/all_to_all | solution.py:709
  13.4 0.9 %copy-done.11 = s32[8,16,128]{2,1,0:T(8,128)S(1)} copy-done((s32[8,16,128]{2,1,0:T(8,128)S(1)}, s32[8,16,128]{2,1,0:T(8,128)}, u32[]{:S(2)}) %copy-start.11) | copy-done | bytes 65560
  14.3 1.1 %shard_map.238 = (f32[8,128]{1,0:T(8,128)S(1)}, f32[8,16,128]{2,1,0:T(8,128)S(1)}) custom-call(s32[64]{0:T(128)S(1)} %copy-done.20, f32[8]{0:T(128)S(1)} %copy-done.19, f32[3,8,16,128]{3,2,1,0:T(8,128)S(1)} %copy-done.1, f32[3,8,16,128]{3,2,1,0:T(8,128)S(1)} %copy-done, s32[8,16,128]{2,1,0:T(8,128)S(1)} %copy-done.11), custom_call_target="tpu_custom_call" | custom-call | flops 3000000 | bytes 1500000 | tf_op jit(solution)/shard_map/pallas_call | solution.py:711
  15.4 3.8 %all-to-all-done = bf16[16,24,128]{2,1,0:T(8,128)(2,1)S(1)} async-done(((bf16[16,24,128]{2,1,0:T(8,128)(2,1)}), bf16[16,24,128]{2,1,0:T(8,128)(2,1)S(1)}, u32[]{:S(2)}, u32[]{:S(2)}) %all-to-all-start) | async-done | bytes 98336 | tf_op jit(solution)/shard_map/all_to_all | solution.py:709
  19.3 1.2 %shard_map.239.after = bf16[256,128]{1,0:T(8,128)(2,1)} custom-call(bf16[384,128]{1,0:T(8,128)(2,1)S(1)} %bitcast.15, f32[8,128]{1,0:T(8,128)S(1)} %get-tuple-element.28.taken, bf16[512,256]{1,0:T(8,128)(2,1)S(1)} %copy-done.4), custom_call_target="tpu_custom_call" | custom-call | flops 20000000 | bytes 400000 | tf_op jit(solution)/shard_map/pallas_call | solution.py:724
  20.5 14.0 %all-to-all-start.1 = ((bf16[32,8,128]{2,1,0:T(8,128)(2,1)}), bf16[32,8,128]{2,1,0:T(8,128)(2,1)S(1)}, u32[]{:S(2)}, u32[]{:S(2)}) async-start(bf16[32,8,128]{2,1,0:T(8,128)(2,1)} %bitcast.3), calls=%async_computation.1 | async-start | bytes 131072 | tf_op jit(solution)/shard_map/all_to_all | solution.py:727
  34.7 4.8 %collective-permute-start = (f32[9,2,16,128]{3,2,1,0:T(8,128)S(1)}, f32[9,2,16,128]{3,2,1,0:T(8,128)S(1)}, u32[]{:S(2)}, u32[]{:S(2)}) collective-permute-start(f32[9,2,16,128]{3,2,1,0:T(8,128)S(1)} %get-tuple-element.34), channel_id=1, source_target_pairs={{0,16},{16,32},{32,48},{48,64},{64,80},{80,96},{96,112},{112,128},... | collective-permute-start | bytes 442376 | tf_op jit(solution)/shard_map/ppermute | solution.py:675
  39.5 1.3 %collective-permute-start.1 = (f32[7,2,16,128]{3,2,1,0:T(8,128)S(1)}, f32[7,2,16,128]{3,2,1,0:T(8,128)S(1)}, u32[]{:S(2)}, u32[]{:S(2)}) collective-permute-start(f32[7,2,16,128]{3,2,1,0:T(8,128)S(1)} %get-tuple-element.35), channel_id=1, source_target_pairs={{16,0},{32,16},{48,32},{64,48},{80,64},{96,80},{112,96},{128,112},... | collective-permute-start | bytes 344072 | tf_op jit(solution)/shard_map/ppermute | solution.py:675
  40.8 0.1 add_bitcast_fusion.cells
  40.9 0.6 copy-done.17
  41.5 1.9 %shard_map.240 = (f32[216,128]{1,0:T(8,128)S(1)}, f32[216,128]{1,0:T(8,128)S(1)}, bf16[128,128]{1,0:T(8,128)(2,1)S(1)}, f32[24,128]{1,0:T(8,128)S(1)}, f32[8,128]{1,0:T(8,128)S(1)}) custom-call(s32[64]{0:T(128)S(1)} %copy-done.16, f32[3,2,64]{2,1,0:T(2,128)S(1)} %bitcast.20, f32[3,16]{1,0:T(4,128)S(1)} %bitcast.22, s32[1,128]{1,0:T(1,128)S(1)} %add_bitcast_fusion.cells, ...), custom_call_target="tpu_custom_call" | custom-call | flops 20000000 | bytes 1000000 | tf_op jit(solution)/shard_map/pallas_call | solution.py:730
  43.4 3.5 %collective-permute-done.1.x_high = f32[7,2,16,128]{3,2,1,0:T(8,128)S(1)} collective-permute-done((f32[7,2,16,128]{3,2,1,0:T(8,128)S(1)}, f32[7,2,16,128]{3,2,1,0:T(8,128)S(1)}, u32[]{:S(2)}, u32[]{:S(2)}) %collective-permute-start.1) | collective-permute-done | bytes 114720 | tf_op jit(solution)/shard_map/ppermute | solution.py:675
  47.0 1.6 %all-to-all-done.1 = bf16[32,8,128]{2,1,0:T(8,128)(2,1)S(1)} async-done(((bf16[32,8,128]{2,1,0:T(8,128)(2,1)}), bf16[32,8,128]{2,1,0:T(8,128)(2,1)S(1)}, u32[]{:S(2)}, u32[]{:S(2)}) %all-to-all-start.1) | async-done | bytes 65568 | tf_op jit(solution)/shard_map/all_to_all | solution.py:727
  48.6 1.4 %shard_map.243 = bf16[128,128]{1,0:T(8,128)(2,1)} custom-call(bf16[256,128]{1,0:T(8,128)(2,1)S(1)} %bitcast.16, f32[216,128]{1,0:T(8,128)S(1)} %get-tuple-element.29.after.coef_a, f32[216,128]{1,0:T(8,128)S(1)} %get-tuple-element.30.coef_b, bf16[256,256]{1,0:T(8,128)(2,1)S(1)} %copy-done.6, bf16[4,128,128]{2,1,0:T(8,128)(2,1)S(1)} %copy-done.7, ...), custom_call_target="tpu_custom_call" | custom-call | flops 40000000 | bytes 600000 | tf_op jit(solution)/shard_map/pallas_call | solution.py:755
  50.0 7.3 %all-to-all-start.2 = ((bf16[8,16,128]{2,1,0:T(8,128)(2,1)}), bf16[8,16,128]{2,1,0:T(8,128)(2,1)S(1)}, u32[]{:S(2)}, u32[]{:S(2)}) async-start(bf16[8,16,128]{2,1,0:T(8,128)(2,1)} %bitcast.8), calls=%async_computation.2 | async-start | bytes 65536 | tf_op jit(solution)/shard_map/all_to_all | solution.py:680
  57.3 4.3 %collective-permute-start.2 = (f32[100,2,128]{2,1,0:T(2,128)S(1)}, f32[100,2,128]{2,1,0:T(2,128)S(1)}, u32[]{:S(2)}, u32[]{:S(2)}) collective-permute-start(f32[100,2,128]{2,1,0:T(2,128)S(1)} %get-tuple-element.36.after), channel_id=1, source_target_pairs={{0,1},{1,2},{2,3},{3,4},{4,5},{5,6},{6,7},{7,8},{8,9},{9,10},{10,1... | collective-permute-start | bytes 307208 | tf_op jit(solution)/shard_map/ppermute | solution.py:675
  61.6 1.9 %collective-permute-start.3 = (f32[84,2,128]{2,1,0:T(2,128)S(1)}, f32[84,2,128]{2,1,0:T(2,128)S(1)}, u32[]{:S(2)}, u32[]{:S(2)}) collective-permute-start(f32[84,2,128]{2,1,0:T(2,128)S(1)} %get-tuple-element.37), channel_id=1, source_target_pairs={{1,0},{2,1},{3,2},{4,3},{5,4},{6,5},{7,6},{8,7},{9,8},{10,9},{11,1... | collective-permute-start | bytes 258056 | tf_op jit(solution)/shard_map/ppermute | solution.py:675
  63.6 4.2 %collective-permute-done.3.after_high.y_high = f32[84,2,128]{2,1,0:T(2,128)S(1)} collective-permute-done((f32[84,2,128]{2,1,0:T(2,128)S(1)}, f32[84,2,128]{2,1,0:T(2,128)S(1)}, u32[]{:S(2)}, u32[]{:S(2)}) %collective-permute-start.3) | collective-permute-done | bytes 86048 | tf_op jit(solution)/shard_map/ppermute | solution.py:675
  67.8 1.5 %shard_map.244.after = bf16[128,896]{1,0:T(8,128)(2,1)} custom-call(bf16[128,128]{1,0:T(8,128)(2,1)S(1)} %bitcast.17, bf16[128,384]{1,0:T(8,128)(2,1)S(1)} %copy-done.10, f32[100,2,128]{2,1,0:T(2,128)S(1)} %collective-permute-done.2.after_low.y_low, f32[84,2,128]{2,1,0:T(2,128)S(1)} %collective-permute-done.3.after_high.y_high), custom_call_target="tpu_custom_call" | custom-call | flops 40000000 | bytes 600000 | tf_op jit(solution)/shard_map/pallas_call | solution.py:766
  69.3 5.4 %all-to-all-start.3 = ((bf16[16,8,896]{2,1,0:T(8,128)(2,1)}), bf16[16,8,896]{2,1,0:T(8,128)(2,1)S(1)}, u32[]{:S(2)}, u32[]{:S(2)}) async-start(bf16[16,8,896]{2,1,0:T(8,128)(2,1)} %bitcast.10), calls=%async_computation.3 | async-start | bytes 458752 | tf_op jit(solution)/shard_map/all_to_all | solution.py:774
  74.7 1.6 %shard_map.245 = (f32[3,10,24,128]{3,2,1,0:T(8,128)S(1)}, f32[3,10,24,128]{3,2,1,0:T(8,128)S(1)}, f32[10,24,128]{2,1,0:T(8,128)S(1)}, f32[8,16,128]{2,1,0:T(8,128)S(1)}, f32[3,8,16,128]{3,2,1,0:T(8,128)S(1)}) custom-call(s32[64]{0:T(128)S(1)} %copy-done.16, f32[3,2,64]{2,1,0:T(2,128)S(1)} %bitcast.21, f32[3,8,16,128]{3,2,1,0:T(8,128)S(1)} %copy-done.1, ...), custom_call_target="tpu_custom_call" | custom-call | flops 10000000 | bytes 3000000 | tf_op jit(solution)/shard_map/pallas_call | solution.py:775
  76.3 5.3 %all-to-all-done.3 = bf16[16,8,896]{2,1,0:T(8,128)(2,1)S(1)} async-done(((bf16[16,8,896]{2,1,0:T(8,128)(2,1)}), bf16[16,8,896]{2,1,0:T(8,128)(2,1)S(1)}, u32[]{:S(2)}, u32[]{:S(2)}) %all-to-all-start.3) | async-done | bytes 229408 | tf_op jit(solution)/shard_map/all_to_all | solution.py:774
  81.6 1.1 %shard_map.246 = (f32[3,8,16,128]{3,2,1,0:T(8,128)}, f32[3,8,16,128]{3,2,1,0:T(8,128)}, f32[8,16,128]{2,1,0:T(8,128)}, f32[3,2,64]{2,1,0:T(2,128)}) custom-call(bf16[128,896]{1,0:T(8,128)(2,1)S(1)} %bitcast.14, bf16[128,128]{1,0:T(8,128)(2,1)S(1)} %copy-done.12, f32[3,10,24,128]{3,2,1,0:T(8,128)S(1)} %get-tuple-element.38.early, ...), custom_call_target="tpu_custom_call" | custom-call | flops 40000000 | bytes 4000000 | tf_op jit(solution)/shard_map/pallas_call | solution.py:790
  (45 shorter events, 0.2 us)
Async XLA Ops:
  0.6 12.7 %copy-start = (f32[3,8,16,128]{3,2,1,0:T(8,128)S(1)}, f32[3,8,16,128]{3,2,1,0:T(8,128)}, u32[]{:S(2)}) copy-start(f32[3,8,16,128]{3,2,1,0:T(8,128)} %magnetic.5) | copy-start | bytes 589828
  3.0 10.4 %copy-start.1 = (f32[3,8,16,128]{3,2,1,0:T(8,128)S(1)}, f32[3,8,16,128]{3,2,1,0:T(8,128)}, u32[]{:S(2)}) copy-start(f32[3,8,16,128]{3,2,1,0:T(8,128)} %get-tuple-element.27.field.electric) | copy-start | bytes 589828
  3.0 10.4 %copy-start.19 = (f32[8]{0:T(128)S(1)}, f32[8]{0:T(128)}, u32[]{:S(2)}) copy-start(f32[8]{0:T(128)} %perm_in.1) | copy-start | bytes 100
  3.0 10.4 %copy-start.20 = (s32[64]{0:T(128)S(1)}, s32[64]{0:T(128)}, u32[]{:S(2)}) copy-start(s32[64]{0:T(128)} %src_in.1) | copy-start | bytes 772
  3.0 16.3 %all-to-all-start = ((bf16[16,24,128]{2,1,0:T(8,128)(2,1)}), bf16[16,24,128]{2,1,0:T(8,128)(2,1)S(1)}, u32[]{:S(2)}, u32[]{:S(2)}) async-start(bf16[16,24,128]{2,1,0:T(8,128)(2,1)} %bitcast.23), calls=%async_computation | async-start | bytes 196608 | tf_op jit(solution)/shard_map/all_to_all | solution.py:709
  13.4 5.9 %copy-start.4 = (bf16[512,256]{1,0:T(8,128)(2,1)S(1)}, bf16[512,256]{1,0:T(8,128)(2,1)}, u32[]{:S(2)}) copy-start(bf16[512,256]{1,0:T(8,128)(2,1)} %constant.19.clone.table) | copy-start | bytes 786436
  19.3 15.3 %copy-start.2 = (bf16[2,3,8,16,128]{4,3,2,1,0:T(8,128)(2,1)S(1)}, bf16[2,3,8,16,128]{4,3,2,1,0:T(8,128)(2,1)}, u32[]{:S(2)}) copy-start(bf16[2,3,8,16,128]{4,3,2,1,0:T(8,128)(2,1)} %saved.5) | copy-start | bytes 589828
  20.5 28.1 %all-to-all-start.1 = ((bf16[32,8,128]{2,1,0:T(8,128)(2,1)}), bf16[32,8,128]{2,1,0:T(8,128)(2,1)S(1)}, u32[]{:S(2)}, u32[]{:S(2)}) async-start(bf16[32,8,128]{2,1,0:T(8,128)(2,1)} %bitcast.3), calls=%async_computation.1 | async-start | bytes 131072 | tf_op jit(solution)/shard_map/all_to_all | solution.py:727
  34.5 6.3 %copy-start.3 = (bf16[8,2,32,256]{3,2,1,0:T(8,128)(2,1)S(1)}, bf16[8,2,32,256]{3,2,1,0:T(8,128)(2,1)}, u32[]{:S(2)}) copy-start(bf16[8,2,32,256]{3,2,1,0:T(8,128)(2,1)} %constant.21.clone.at_y) | copy-start | bytes 786436
  34.6 6.3 %copy-start.5 = (bf16[2,48,16,16]{1,3,2,0:T(8,128)(2,1)S(1)}, bf16[2,48,16,16]{1,3,2,0:T(8,128)(2,1)}, u32[]{:S(2)}) copy-start(bf16[2,48,16,16]{1,3,2,0:T(8,128)(2,1)} %param.32) | copy-start | bytes 147460
  34.6 6.3 %copy-start.8 = (bf16[2,128,256]{2,1,0:T(8,128)(2,1)S(1)}, bf16[2,128,256]{2,1,0:T(8,128)(2,1)}, u32[]{:S(2)}) copy-start(bf16[2,128,256]{2,1,0:T(8,128)(2,1)} %constant.20.clone.at_x) | copy-start | bytes 393220
  34.6 6.3 %copy-start.9 = (bf16[16,2,16,128]{3,2,1,0:T(8,128)(2,1)S(1)}, bf16[16,2,16,128]{3,2,1,0:T(8,128)(2,1)}, u32[]{:S(2)}) copy-start(bf16[16,2,16,128]{3,2,1,0:T(8,128)(2,1)} %constant.22.clone.at_z) | copy-start | bytes 393220
  34.6 6.3 %copy-start.14 = (f32[16,48]{1,0:T(8,128)S(1)}, f32[16,48]{1,0:T(8,128)}, u32[]{:S(2)}) copy-start(f32[16,48]{1,0:T(8,128)} %gain_x.1) | copy-start | bytes 9220
  34.6 6.3 %copy-start.15 = (f32[16,48]{1,0:T(8,128)S(1)}, f32[16,48]{1,0:T(8,128)}, u32[]{:S(2)}) copy-start(f32[16,48]{1,0:T(8,128)} %gain_y.1) | copy-start | bytes 9220
  34.6 6.3 %copy-start.18 = (f32[3,16]{1,0:T(4,128)S(1)}, f32[3,16]{1,0:T(4,128)}, u32[]{:S(2)}) copy-start(f32[3,16]{1,0:T(4,128)} %project.1) | copy-start | bytes 580
  34.7 12.2 %collective-permute-start = (f32[9,2,16,128]{3,2,1,0:T(8,128)S(1)}, f32[9,2,16,128]{3,2,1,0:T(8,128)S(1)}, u32[]{:S(2)}, u32[]{:S(2)}) collective-permute-start(f32[9,2,16,128]{3,2,1,0:T(8,128)S(1)} %get-tuple-element.34), channel_id=1, source_target_pairs={{0,16},{16,32},{32,48},{48,64},{64,80},{80,96},{96,112},{112,128},... | collective-permute-start | bytes 442376 | tf_op jit(solution)/shard_map/ppermute | solution.py:675
  39.5 7.4 %collective-permute-start.1 = (f32[7,2,16,128]{3,2,1,0:T(8,128)S(1)}, f32[7,2,16,128]{3,2,1,0:T(8,128)S(1)}, u32[]{:S(2)}, u32[]{:S(2)}) collective-permute-start(f32[7,2,16,128]{3,2,1,0:T(8,128)S(1)} %get-tuple-element.35), channel_id=1, source_target_pairs={{16,0},{32,16},{48,32},{64,48},{80,64},{96,80},{112,96},{128,112},... | collective-permute-start | bytes 344072 | tf_op jit(solution)/shard_map/ppermute | solution.py:675
  46.9 1.7 %copy-start.7 = (bf16[4,128,128]{2,1,0:T(8,128)(2,1)S(1)}, bf16[4,128,128]{2,1,0:T(8,128)(2,1)}, u32[]{:S(2)}) copy-start(bf16[4,128,128]{2,1,0:T(8,128)(2,1)} %constant.24.clone.inv_x) | copy-start | bytes 393220
  48.6 19.1 %copy-start.10 = (bf16[128,384]{1,0:T(8,128)(2,1)S(1)}, bf16[128,384]{1,0:T(8,128)(2,1)}, u32[]{:S(2)}) copy-start(bf16[128,384]{1,0:T(8,128)(2,1)} %constant.25.clone.inv_y) | copy-start | bytes 294916
  50.0 17.8 %all-to-all-start.2 = ((bf16[8,16,128]{2,1,0:T(8,128)(2,1)}), bf16[8,16,128]{2,1,0:T(8,128)(2,1)S(1)}, u32[]{:S(2)}, u32[]{:S(2)}) async-start(bf16[8,16,128]{2,1,0:T(8,128)(2,1)} %bitcast.8), calls=%async_computation.2 | async-start | bytes 65536 | tf_op jit(solution)/shard_map/all_to_all | solution.py:680
  57.3 10.4 %collective-permute-start.2 = (f32[100,2,128]{2,1,0:T(2,128)S(1)}, f32[100,2,128]{2,1,0:T(2,128)S(1)}, u32[]{:S(2)}, u32[]{:S(2)}) collective-permute-start(f32[100,2,128]{2,1,0:T(2,128)S(1)} %get-tuple-element.36.after), channel_id=1, source_target_pairs={{0,1},{1,2},{2,3},{3,4},{4,5},{5,6},{6,7},{7,8},{8,9},{9,10},{10,1... | collective-permute-start | bytes 307208 | tf_op jit(solution)/shard_map/ppermute | solution.py:675
  61.6 6.1 %collective-permute-start.3 = (f32[84,2,128]{2,1,0:T(2,128)S(1)}, f32[84,2,128]{2,1,0:T(2,128)S(1)}, u32[]{:S(2)}, u32[]{:S(2)}) collective-permute-start(f32[84,2,128]{2,1,0:T(2,128)S(1)} %get-tuple-element.37), channel_id=1, source_target_pairs={{1,0},{2,1},{3,2},{4,3},{5,4},{6,5},{7,6},{8,7},{9,8},{10,9},{11,1... | collective-permute-start | bytes 258056 | tf_op jit(solution)/shard_map/ppermute | solution.py:675
  69.3 12.3 %all-to-all-start.3 = ((bf16[16,8,896]{2,1,0:T(8,128)(2,1)}), bf16[16,8,896]{2,1,0:T(8,128)(2,1)S(1)}, u32[]{:S(2)}, u32[]{:S(2)}) async-start(bf16[16,8,896]{2,1,0:T(8,128)(2,1)} %bitcast.10), calls=%async_computation.3 | async-start | bytes 458752 | tf_op jit(solution)/shard_map/all_to_all | solution.py:774
  74.7 6.9 %copy-start.12 = (bf16[128,128]{1,0:T(8,128)(2,1)S(1)}, bf16[128,128]{1,0:T(8,128)(2,1)}, u32[]{:S(2)}) copy-start(bf16[128,128]{1,0:T(8,128)(2,1)} %constant.26.clone.table) | copy-start | bytes 98308
  (5 other events, 5.4 us)

commit v5 on v4

--- a/solution.py
+++ b/solution.py
@@ -78,10 +78,15 @@
     inv_y = np.zeros((LANES, 384), ml_dtypes.bfloat16)
     inv_y[:K, :256], inv_y[64 : 64 + K, :256] = cy, -sy
     for w in range(WIDE):
-        for h, y in ((0, w * RY + RY), (7, w * RY - 1)):
-            inv_y[:K, 256 + w * 8 + h] = cy[:, y % NY]
-            inv_y[64 : 64 + K, 256 + w * 8 + h] = -sy[:, y % NY]
+        for h, y in enumerate((w * RY + RY, w * RY - 1)):
+            inv_y[:K, 256 + w * 2 + h] = cy[:, y % NY]
+            inv_y[64 : 64 + K, 256 + w * 2 + h] = -sy[:, y % NY]
     out["inv_y"] = inv_y
+    apart = np.zeros((LANES, 256), ml_dtypes.bfloat16)
+    for cell in range(32):
+        apart[cell * 2, cell * 8] = 1
+        apart[cell * 2 + 1, cell * 8 + 7] = 1
+    out["apart"] = apart
 
     at_x = np.zeros((2, LANES, NX), ml_dtypes.bfloat16)
     at_x[0, :K], at_x[0, 64 : 64 + K] = cx, -sx
@@ -503,41 +508,80 @@
     edge = []
     for low in range(16):
         edge.append(jnp.stack([wide[high * 16 + low, :, 256:384] for high in range(2)]))
-    edge = exchange(edge, 8, 2)
+    edge = exchange(edge, 2, 2)
     row = iota((8, LANES), 0)
     total = pltpu.roll(got[:, 8:16].sum(0), 6, 0)
     total = jnp.where((row < 6) & (lane < 64), total + pltpu.roll(total, 64, 1), 0.0)
     high = total.astype(BF16).astype(F32)
-    last = high + pltpu.roll(total - high, 64, 1)
+    other = pltpu.roll(total - high, 64, 1)
+    moved = pltpu.roll(high, 64, 1)
+    low = total - high
+    extra = []
+    for t in range(3):
+        first = jnp.where(lane < 64, high[2 * t : 2 * t + 1], moved[2 * t + 1 : 2 * t + 2])
+        second = jnp.where(lane < 64, low[2 * t : 2 * t + 1], other[2 * t + 1 : 2 * t + 2])
+        extra.append(jnp.where(row == 6, first, jnp.where(row == 7, second, 0.0)))
     blocks = []
     for w in range(WIDE):
         tiles = [near[w % 8][high_x * 2 + w // 8] for high_x in range(4)]
-        tiles += [edge[w][high_x] for high_x in range(2)] + [last]
+        for t in range(3):
+            tiles[t] = tiles[t] + extra[t]
+        pair = jnp.where(lane < 32, edge[w], 0.0)
+        tiles.append(pair[0] + pltpu.roll(pair[1], 32, 1))
         blocks.append(jnp.concatenate(tiles, 1))
     out[...] = jnp.concatenate(blocks, 0).astype(BF16)
 
 
+def high_planes(across):
+    first, second = [c for c in range(3) if c != across]
+    planes = [(c, 0) for c in range(3)] + [(first, 1), (second, 1), (6, 0), (6, 1)]
+    return planes + [(3 + c, 0) for c in range(3)]
+
+
+def low_planes(across):
+    first, second = [c for c in range(3) if c != across]
+    planes = [(c, i) for i in range(2) for c in range(3)] + [(6, 0), (6, 1)]
+    return planes + [(3 + first, 0), (3 + second, 0)] + [(3 + c, 1) for c in range(3)]
+
+
 def edge_kernel(electric, magnetic, inverse, saved, after, to_low, to_high):
-    for c in range(3):
-        to_low[c], to_high[c] = electric[c, 6:8], electric[c, 0:2]
-        to_low[3 + c], to_high[3 + c] = magnetic[c, 6:8], magnetic[c, 0:2]
-    to_low[6], to_high[6] = inverse[6:8], inverse[0:2]
+    def own(f):
+        return electric.at[f] if f < 3 else (magnetic.at[f - 3] if f < 6 else inverse)
+
+    for p, (f, i) in enumerate(low_planes(0)):
+        to_low[p] = own(f)[6 + i].astype(BF16)
     for n in range(2):
         for c in range(2):
-            to_low[7 + n, c] = saved[n, 1 + c, 7].astype(F32)
-
-
-def corner_kernel(electric, magnetic, inverse, saved, x_low, x_high, after, to_low, to_high):
-    for c in range(7):
-        own = electric.at[c] if c < 3 else (magnetic.at[c - 3] if c < 6 else inverse)
-        for to, rows in ((to_low, slice(14, 16)), (to_high, slice(0, 2))):
-            to[c * 12 : c * 12 + 8] = own[:, rows, :]
-            to[c * 12 + 8 : c * 12 + 10] = x_high[c, :, rows, :]
-            to[c * 12 + 10 : c * 12 + 12] = x_low[c, :, rows, :]
+            to_low[13 + 2 * n + c] = saved[n, 1 + c, 7]
+    for p, (f, i) in enumerate(high_planes(0)):
+        to_high[p] = own(f)[i].astype(BF16)
+
+
+def corner_kernel(
+    electric, magnetic, inverse, saved, x_low, x_high, after, to_low, to_high, low, high
+):
+    x_of = [{}, {}]
+    for p, key in enumerate(low_planes(0)):
+        x_of[0][key] = x_low[p].astype(F32)
+    for p, key in enumerate(high_planes(0)):
+        x_of[1][key] = x_high[p].astype(F32)
+    low[...] = jnp.zeros(low.shape, F32)
+    high[...] = jnp.zeros(high.shape, F32)
+    for to, planes, start in ((low, low_planes(1), 14), (high, high_planes(1), 0)):
+        for p, (f, i) in enumerate(planes):
+            own = electric.at[f] if f < 3 else (magnetic.at[f - 3] if f < 6 else inverse)
+            row = start + i
+            to[p, 0:8, :] = own[:, row, :]
+            for side, at in ((1, 8), (0, 10)):
+                for layer in range(2):
+                    if (f, layer) in x_of[side]:
+                        got = x_of[side][(f, layer)]
+                        to[p, at + layer : at + layer + 1, :] = got[row : row + 1]
     for n in range(2):
         for i, c in enumerate((0, 2)):
-            edge = saved[n, c].astype(F32)[:, RY - 1 : RY, :]
-            to_low[84 + n * 8 : 92 + n * 8, i : i + 1, :] = edge
+            low[13 + 2 * n + i, 0:8, :] = saved[n, c].astype(F32)[:, RY - 1, :]
+    to_low[...] = low[...].astype(BF16)
+    to_high[...] = high[...].astype(BF16)
 
 
 def first_kernel(
@@ -546,14 +590,20 @@
 ):
     b, w = own_block()
     lane = iota((1, NZ), 1)
+    zero = jnp.zeros((12, 24, NZ), F32)
     for c in range(7):
         to = e_ext.at[c] if c < 3 else (h_ext.at[c - 3] if c < 6 else g_ext)
+        to[...] = zero
         own = electric[c] if c < 3 else (magnetic[c - 3] if c < 6 else inverse[...])
         to[0:8, 0:16, :] = own
-        to[8:10, 0:16, :] = x_high[c]
-        to[10:12, 0:16, :] = x_low[c]
-        low, high = y_low[c * 12 : (c + 1) * 12], y_high[c * 12 : (c + 1) * 12]
-        to[:, 16:24, :] = jnp.concatenate([high, jnp.zeros((12, 4, NZ), F32), low], 1)
+        for planes, ref, at in ((high_planes(0), x_high, 8), (low_planes(0), x_low, 10)):
+            for p, (f, i) in enumerate(planes):
+                if f == c:
+                    to[at + i, 0:16, :] = ref[p].astype(F32)
+        for planes, ref, at in ((high_planes(1), y_high, 16), (low_planes(1), y_low, 22)):
+            for p, (f, i) in enumerate(planes):
+                if f == c:
+                    to[:, at + i : at + i + 1, :] = ref[p].astype(F32)[0:12][:, None, :]
 
     g = g_ext[...]
     half = 0.5 * g
@@ -593,11 +643,10 @@
     near = inverse[...]
     for step in range(2):
         s = [saved[step, c].astype(F32) for c in range(3)]
-        before_x = {c: jnp.concatenate([x_low[7 + step, c - 1 : c], s[c][:-1]], 0) for c in (1, 2)}
-        at = 84 + step * 8
+        before_x = {c: jnp.concatenate([x_low[12 + 2 * step + c].astype(F32)[None], s[c][:-1]], 0) for c in (1, 2)}
         before_y = {}
         for c in (0, 2):
-            edge = y_low[at : at + 8, c // 2 : c // 2 + 1, :]
+            edge = y_low[13 + 2 * step + c // 2].astype(F32)[0:8][:, None, :]
             first = iota((RX, RY, NZ), 1) == 0
             before_y[c] = jnp.where(first, edge, pltpu.roll(s[c], 1, 1))
         curls = (
@@ -616,16 +665,16 @@
 
 
 def second_kernel(
-    lines, table, early, curled, factor, first_grad, ready, injected,
+    lines, table, apart, early, curled, factor, first_grad, ready, injected,
     grad_e, grad_h, grad_eps, sources,
 ):
     b, w = own_block()
-    modes = lines[:, 0:768]
-    back = lax.dot_general(
-        modes, table[...], (((0,), (0,)), ((), ())), preferred_element_type=F32
-    )
-    main = back[0:512].reshape(32, 16, NZ)
-    edge = back[512:768].reshape(32, 8, NZ)
+    turn = (((0,), (0,)), ((), ()))
+    main = lax.dot_general(lines[:, 0:512], table[...], turn, preferred_element_type=F32)
+    main = main.reshape(32, 16, NZ)
+    edge = jnp.dot(lines[:, 512:640], apart[...], preferred_element_type=F32).astype(BF16)
+    edge = lax.dot_general(edge, table[...], turn, preferred_element_type=F32)
+    edge = edge.reshape(32, 8, NZ)
     half = factor[...]
     e1 = []
     for c in range(3):
@@ -645,11 +694,17 @@
         grad_e[c] = e1[c][0:8, 0:16] - 0.5 * backed[c][0:8, 0:16]
         total = total - a[c][0:8, 0:16] * ready[c]
     grad_eps[...] = total
-    got = lines[:, 768:896].astype(F32).reshape(WIDE, 8, LANES).sum(0)
-    got = got + pltpu.roll(got, 64, 1) + injected[...]
+    got = lines[:, 0:384].astype(F32).reshape(WIDE, 8, 384).sum(0)
+    got = got[6:7] + got[7:8]
+    moved = pltpu.roll(got, 384 - 64, 1)
     for n in range(2):
         for c in range(3):
-            sources[c, n : n + 1, :] = got[n * 3 + c : n * 3 + c + 1, 0:64]
+            at = n * 3 + c
+            line = got if at % 2 == 0 else moved
+            line = line[:, at // 2 * LANES : (at // 2 + 1) * LANES]
+            if n == 0:
+                line = line + injected[c : c + 1, :]
+            sources[c, n : n + 1, :] = line[:, 0:64]
 
 
 def call(kernel, outs, places, scratch=(), flops=0, moved=0, params=PARAMS):
@@ -744,13 +799,23 @@
     )
 
     to_low, to_high = call(
-        edge_kernel, (shape(9, 2, RY, NZ), shape(7, 2, RY, NZ)), "vvvva", (), 0, 500_000
+        edge_kernel,
+        (shape(17, RY, NZ, dtype=BF16), shape(10, RY, NZ, dtype=BF16)),
+        "vvvva",
+        (),
+        0,
+        500_000,
     )(field, seed_magnetic, inverse, saved_magnetic, dealt)
     x_low = passed_along(to_low, "bulk", 1)
     x_high = passed_along(to_high, "bulk", -1)
 
     low_part, high_part = call(
-        corner_kernel, (shape(100, 2, NZ), shape(84, 2, NZ)), "vvvvvva", (), 0, 1_000_000
+        corner_kernel,
+        (shape(17, 16, NZ, dtype=BF16), shape(10, 16, NZ, dtype=BF16)),
+        "vvvvvva",
+        [pltpu.VMEM((17, 16, NZ), F32), pltpu.VMEM((10, 16, NZ), F32)],
+        0,
+        1_000_000,
     )(field, seed_magnetic, inverse, saved_magnetic, x_low, x_high, coef_a)
     shares = call(
         filter_kernel, shape(LANES, LANES, dtype=BF16), "vvvvvvva", (), 40_000_000, 600_000
@@ -765,7 +830,7 @@
 
     sent = call(
         spread_kernel,
-        shape(128, 896, dtype=BF16),
+        shape(128, 640, dtype=BF16),
         "vvaa",
         [pltpu.VMEM((32, 8, LANES), F32)],
         40_000_000,
@@ -790,11 +855,14 @@
     grad_e, grad_h, grad_eps, sources = call(
         second_kernel,
         (shape(3, *block), shape(3, *block), shape(*block), shape(3, 2, 64)),
-        "vvvvvvvv",
+        "vvvvvvvvv",
         (),
         40_000_000,
         4_000_000,
-    )(returned, tables_of("back_z"), early, curled, factor, first_grad, ready, injected)
+    )(
+        returned, tables_of("back_z"), tables_of("apart"), early, curled, factor, first_grad,
+        ready, injected,
+    )
     return grad_e, grad_h, grad_eps, sources.transpose(1, 2, 0)
 
 

time: 83.3 us -> 81.6 us (0.980)
  waiting for transfers between devices: 18.4 us -> 17.3 us
    ppermute x4, waiting for transfers between devices: 7.65 us -> 6.31 us  [passed_along(): return lax.ppermute(block, axis, route)]
    all_to_all x1, waiting for transfers between devices: 1.63 us -> 2.48 us  [body(): lax.all_to_all(dealt, 'bulk', split_axis=0, concat_axis=0, tiled=True)]
where the time goes in v5:
time: 81.6 us; the launch traced here: 81 us
  starting transfers between devices  48.6 us (60%)
  waiting for transfers between devices  17.3 us (21%)
  Pallas kernels  12.6 us (15%)
  local copies, waits for them, and re-layouts  1.59 us (2%)
  between operations  0.93 us (1%)
    all_to_all x1, starting transfers between devices, body(): lax.all_to_all(dealt, 'bulk', split_axis=0, concat_axis=0, tiled=True)  14 us
    ppermute x4, starting transfers between devices, passed_along(): return lax.ppermute(block, axis, route)  12.3 us
    all_to_all x1, starting transfers between devices, body(): lax.all_to_all(payload, 'wide', split_axis=0, concat_axis=0, tiled=True)  10.4 us
    all_to_all x1, starting transfers between devices, dealt_near(): lax.all_to_all(block, 'bulk', split_axis=0, concat_axis=0, axis_index_gro...  6.53 us
    ppermute x4, waiting for transfers between devices, passed_along(): return lax.ppermute(block, axis, route)  6.31 us
    all_to_all x1, starting transfers between devices, body(): lax.all_to_all(sent, 'wide', split_axis=0, concat_axis=0, tiled=True)  5.38 us
    all_to_all x1, waiting for transfers between devices, body(): lax.all_to_all(sent, 'wide', split_axis=0, concat_axis=0, tiled=True)  4.7 us
    all_to_all x1, waiting for transfers between devices, body(): lax.all_to_all(payload, 'wide', split_axis=0, concat_axis=0, tiled=True)  3.83 us
  transfers between devices with their start and end apart: 8, of which 5 were waited for; matrix products, arithmetic and copies ran while one was open for 0% of the time, Pallas kernels for 6%

profile of v5, /device:TPU:1, one launch (start us, length us, event | category | flops | bytes accessed | tf_op | source)
XLA Modules:
  0.0 81.0 jit_solution(2908334216442455050)
XLA Ops:
  0.6 2.3 %shard_map.246 = (bf16[384,128]{1,0:T(8,128)(2,1)}, f32[3,8,16,128]{3,2,1,0:T(8,128)}) custom-call(s32[64]{0:T(128)} %mon.3, f32[3,2,64]{2,1,0:T(2,128)} %bitcast.19, f32[3,8,16,128]{3,2,1,0:T(8,128)} %electric.1, bf16[128,128]{1,0:T(8,128)(2,1)} %constant.20.clone.table_in), custom_call_target="tpu_custom_call" | custom-call | flops 13000000 | bytes 500000 | tf_op jit(solution)/shard_map/pallas_call | solution.py:752
  3.0 10.4 %all-to-all-start = ((bf16[16,24,128]{2,1,0:T(8,128)(2,1)}), bf16[16,24,128]{2,1,0:T(8,128)(2,1)S(1)}, u32[]{:S(2)}, u32[]{:S(2)}) async-start(bf16[16,24,128]{2,1,0:T(8,128)(2,1)} %bitcast.23), calls=%async_computation | async-start | bytes 196608 | tf_op jit(solution)/shard_map/all_to_all | solution.py:764
  13.5 0.9 %copy-done.11 = s32[8,16,128]{2,1,0:T(8,128)S(1)} copy-done((s32[8,16,128]{2,1,0:T(8,128)S(1)}, s32[8,16,128]{2,1,0:T(8,128)}, u32[]{:S(2)}) %copy-start.11) | copy-done | bytes 65560
  14.3 1.1 %shard_map.247 = (f32[8,128]{1,0:T(8,128)S(1)}, f32[8,16,128]{2,1,0:T(8,128)S(1)}) custom-call(s32[64]{0:T(128)S(1)} %copy-done.21, f32[8]{0:T(128)S(1)} %copy-done.20, f32[3,8,16,128]{3,2,1,0:T(8,128)S(1)} %copy-done.1, f32[3,8,16,128]{3,2,1,0:T(8,128)S(1)} %copy-done, s32[8,16,128]{2,1,0:T(8,128)S(1)} %copy-done.11), custom_call_target="tpu_custom_call" | custom-call | flops 3000000 | bytes 1500000 | tf_op jit(solution)/shard_map/pallas_call | solution.py:766
  15.5 3.8 %all-to-all-done = bf16[16,24,128]{2,1,0:T(8,128)(2,1)S(1)} async-done(((bf16[16,24,128]{2,1,0:T(8,128)(2,1)}), bf16[16,24,128]{2,1,0:T(8,128)(2,1)S(1)}, u32[]{:S(2)}, u32[]{:S(2)}) %all-to-all-start) | async-done | bytes 98336 | tf_op jit(solution)/shard_map/all_to_all | solution.py:764
  19.3 1.2 %shard_map.248.after = bf16[256,128]{1,0:T(8,128)(2,1)} custom-call(bf16[384,128]{1,0:T(8,128)(2,1)S(1)} %bitcast.15, f32[8,128]{1,0:T(8,128)S(1)} %get-tuple-element.28.taken, bf16[512,256]{1,0:T(8,128)(2,1)S(1)} %copy-done.4), custom_call_target="tpu_custom_call" | custom-call | flops 20000000 | bytes 400000 | tf_op jit(solution)/shard_map/pallas_call | solution.py:779
  20.5 14.0 %all-to-all-start.1 = ((bf16[32,8,128]{2,1,0:T(8,128)(2,1)}), bf16[32,8,128]{2,1,0:T(8,128)(2,1)S(1)}, u32[]{:S(2)}, u32[]{:S(2)}) async-start(bf16[32,8,128]{2,1,0:T(8,128)(2,1)} %bitcast.3), calls=%async_computation.1 | async-start | bytes 131072 | tf_op jit(solution)/shard_map/all_to_all | solution.py:782
  34.6 4.8 %collective-permute-start = (bf16[17,16,128]{2,1,0:T(8,128)(2,1)S(1)}, bf16[17,16,128]{2,1,0:T(8,128)(2,1)S(1)}, u32[]{:S(2)}, u32[]{:S(2)}) collective-permute-start(bf16[17,16,128]{2,1,0:T(8,128)(2,1)S(1)} %get-tuple-element.34), channel_id=1, source_target_pairs={{0,16},{16,32},{32,48},{48,64},{64,80},{80,96},{96,112},{112,128},... | collective-permute-start | bytes 208904 | tf_op jit(solution)/shard_map/ppermute | solution.py:730
  39.4 1.3 %collective-permute-start.1 = (bf16[10,16,128]{2,1,0:T(8,128)(2,1)S(1)}, bf16[10,16,128]{2,1,0:T(8,128)(2,1)S(1)}, u32[]{:S(2)}, u32[]{:S(2)}) collective-permute-start(bf16[10,16,128]{2,1,0:T(8,128)(2,1)S(1)} %get-tuple-element.35), channel_id=1, source_target_pairs={{16,0},{32,16},{48,32},{64,48},{80,64},{96,80},{112,96},{128,112},... | collective-permute-start | bytes 122888 | tf_op jit(solution)/shard_map/ppermute | solution.py:730
  40.9 0.6 copy-done.18
  41.5 1.9 %shard_map.249 = (f32[216,128]{1,0:T(8,128)S(1)}, f32[216,128]{1,0:T(8,128)S(1)}, bf16[128,128]{1,0:T(8,128)(2,1)S(1)}, f32[24,128]{1,0:T(8,128)S(1)}, f32[8,128]{1,0:T(8,128)S(1)}) custom-call(s32[64]{0:T(128)S(1)} %copy-done.17, f32[3,2,64]{2,1,0:T(2,128)S(1)} %bitcast.20, f32[3,16]{1,0:T(4,128)S(1)} %bitcast.22, s32[1,128]{1,0:T(1,128)S(1)} %add_bitcast_fusion.cells, ...), custom_call_target="tpu_custom_call" | custom-call | flops 20000000 | bytes 1000000 | tf_op jit(solution)/shard_map/pallas_call | solution.py:785
  43.4 2.6 %collective-permute-done.1.x_high = bf16[10,16,128]{2,1,0:T(8,128)(2,1)S(1)} collective-permute-done((bf16[10,16,128]{2,1,0:T(8,128)(2,1)S(1)}, bf16[10,16,128]{2,1,0:T(8,128)(2,1)S(1)}, u32[]{:S(2)}, u32[]{:S(2)}) %collective-permute-start.1) | collective-permute-done | bytes 40992 | tf_op jit(solution)/shard_map/ppermute | solution.py:730
  46.0 0.1 shard_map.251
  46.1 2.5 %all-to-all-done.1 = bf16[32,8,128]{2,1,0:T(8,128)(2,1)S(1)} async-done(((bf16[32,8,128]{2,1,0:T(8,128)(2,1)}), bf16[32,8,128]{2,1,0:T(8,128)(2,1)S(1)}, u32[]{:S(2)}, u32[]{:S(2)}) %all-to-all-start.1) | async-done | bytes 65568 | tf_op jit(solution)/shard_map/all_to_all | solution.py:782
  48.6 1.4 %shard_map.252 = bf16[128,128]{1,0:T(8,128)(2,1)} custom-call(bf16[256,128]{1,0:T(8,128)(2,1)S(1)} %bitcast.16, f32[216,128]{1,0:T(8,128)S(1)} %get-tuple-element.29.after.coef_a, f32[216,128]{1,0:T(8,128)S(1)} %get-tuple-element.30.coef_b, bf16[256,256]{1,0:T(8,128)(2,1)S(1)} %copy-done.6, bf16[4,128,128]{2,1,0:T(8,128)(2,1)S(1)} %copy-done.7, ...), custom_call_target="tpu_custom_call" | custom-call | flops 40000000 | bytes 600000 | tf_op jit(solution)/shard_map/pallas_call | solution.py:820
  50.0 6.5 %all-to-all-start.2 = ((bf16[8,16,128]{2,1,0:T(8,128)(2,1)}), bf16[8,16,128]{2,1,0:T(8,128)(2,1)S(1)}, u32[]{:S(2)}, u32[]{:S(2)}) async-start(bf16[8,16,128]{2,1,0:T(8,128)(2,1)} %bitcast.8), calls=%async_computation.2 | async-start | bytes 65536 | tf_op jit(solution)/shard_map/all_to_all | solution.py:735
  56.5 4.3 %collective-permute-start.2 = (bf16[17,16,128]{2,1,0:T(8,128)(2,1)S(1)}, bf16[17,16,128]{2,1,0:T(8,128)(2,1)S(1)}, u32[]{:S(2)}, u32[]{:S(2)}) collective-permute-start(bf16[17,16,128]{2,1,0:T(8,128)(2,1)S(1)} %get-tuple-element.36.after), channel_id=1, source_target_pairs={{0,1},{1,2},{2,3},{3,4},{4,5},{5,6},{6,7},{7,8},{8,9},{9,10},{10,1... | collective-permute-start | bytes 208904 | tf_op jit(solution)/shard_map/ppermute | solution.py:730
  60.8 1.9 %collective-permute-start.3 = (bf16[10,16,128]{2,1,0:T(8,128)(2,1)S(1)}, bf16[10,16,128]{2,1,0:T(8,128)(2,1)S(1)}, u32[]{:S(2)}, u32[]{:S(2)}) collective-permute-start(bf16[10,16,128]{2,1,0:T(8,128)(2,1)S(1)} %get-tuple-element.37), channel_id=1, source_target_pairs={{1,0},{2,1},{3,2},{4,3},{5,4},{6,5},{7,6},{8,7},{9,8},{10,9},{11,1... | collective-permute-start | bytes 122888 | tf_op jit(solution)/shard_map/ppermute | solution.py:730
  62.7 3.7 %collective-permute-done.3.after_high.y_high = bf16[10,16,128]{2,1,0:T(8,128)(2,1)S(1)} collective-permute-done((bf16[10,16,128]{2,1,0:T(8,128)(2,1)S(1)}, bf16[10,16,128]{2,1,0:T(8,128)(2,1)S(1)}, u32[]{:S(2)}, u32[]{:S(2)}) %collective-permute-start.3) | collective-permute-done | bytes 40992 | tf_op jit(solution)/shard_map/ppermute | solution.py:730
  66.4 1.6 %shard_map.253.after = bf16[128,640]{1,0:T(8,128)(2,1)} custom-call(bf16[128,128]{1,0:T(8,128)(2,1)S(1)} %bitcast.17, bf16[128,384]{1,0:T(8,128)(2,1)S(1)} %copy-done.10, bf16[17,16,128]{2,1,0:T(8,128)(2,1)S(1)} %collective-permute-done.2.after_low.y_low, bf16[10,16,128]{2,1,0:T(8,128)(2,1)S(1)} %collective-permute-done.3.after_high.y_high), custom_call_target="tpu_custom_call" | custom-call | flops 40000000 | bytes 600000 | tf_op jit(solution)/shard_map/pallas_call | solution.py:831
  68.0 5.4 %all-to-all-start.3 = ((bf16[16,8,640]{2,1,0:T(8,128)(2,1)}), bf16[16,8,640]{2,1,0:T(8,128)(2,1)S(1)}, u32[]{:S(2)}, u32[]{:S(2)}) async-start(bf16[16,8,640]{2,1,0:T(8,128)(2,1)} %bitcast.10), calls=%async_computation.3 | async-start | bytes 327680 | tf_op jit(solution)/shard_map/all_to_all | solution.py:839
  73.4 1.7 %shard_map.254 = (f32[3,10,24,128]{3,2,1,0:T(8,128)S(1)}, f32[3,10,24,128]{3,2,1,0:T(8,128)S(1)}, f32[10,24,128]{2,1,0:T(8,128)S(1)}, f32[8,16,128]{2,1,0:T(8,128)S(1)}, f32[3,8,16,128]{3,2,1,0:T(8,128)S(1)}) custom-call(s32[64]{0:T(128)S(1)} %copy-done.17, f32[3,2,64]{2,1,0:T(2,128)S(1)} %bitcast.21, f32[3,8,16,128]{3,2,1,0:T(8,128)S(1)} %copy-done.1, ...), custom_call_target="tpu_custom_call" | custom-call | flops 10000000 | bytes 3000000 | tf_op jit(solution)/shard_map/pallas_call | solution.py:840
  75.2 4.7 %all-to-all-done.3 = bf16[16,8,640]{2,1,0:T(8,128)(2,1)S(1)} async-done(((bf16[16,8,640]{2,1,0:T(8,128)(2,1)}), bf16[16,8,640]{2,1,0:T(8,128)(2,1)S(1)}, u32[]{:S(2)}, u32[]{:S(2)}) %all-to-all-start.3) | async-done | bytes 163872 | tf_op jit(solution)/shard_map/all_to_all | solution.py:839
  79.9 1.2 %shard_map.255 = (f32[3,8,16,128]{3,2,1,0:T(8,128)}, f32[3,8,16,128]{3,2,1,0:T(8,128)}, f32[8,16,128]{2,1,0:T(8,128)}, f32[3,2,64]{2,1,0:T(2,128)}) custom-call(bf16[128,640]{1,0:T(8,128)(2,1)S(1)} %bitcast.14, bf16[128,128]{1,0:T(8,128)(2,1)S(1)} %copy-done.13, bf16[128,256]{1,0:T(8,128)(2,1)S(1)} %copy-done.12, ...), custom_call_target="tpu_custom_call" | custom-call | flops 40000000 | bytes 4000000 | tf_op jit(solution)/shard_map/pallas_call | solution.py:855
  (47 shorter events, 0.2 us)
Async XLA Ops:
  0.6 12.8 %copy-start = (f32[3,8,16,128]{3,2,1,0:T(8,128)S(1)}, f32[3,8,16,128]{3,2,1,0:T(8,128)}, u32[]{:S(2)}) copy-start(f32[3,8,16,128]{3,2,1,0:T(8,128)} %magnetic.5) | copy-start | bytes 589828
  3.0 10.5 %copy-start.1 = (f32[3,8,16,128]{3,2,1,0:T(8,128)S(1)}, f32[3,8,16,128]{3,2,1,0:T(8,128)}, u32[]{:S(2)}) copy-start(f32[3,8,16,128]{3,2,1,0:T(8,128)} %get-tuple-element.27.field.electric) | copy-start | bytes 589828
  3.0 10.5 %copy-start.20 = (f32[8]{0:T(128)S(1)}, f32[8]{0:T(128)}, u32[]{:S(2)}) copy-start(f32[8]{0:T(128)} %perm_in.1) | copy-start | bytes 100
  3.0 10.5 %copy-start.21 = (s32[64]{0:T(128)S(1)}, s32[64]{0:T(128)}, u32[]{:S(2)}) copy-start(s32[64]{0:T(128)} %src_in.1) | copy-start | bytes 772
  3.0 16.3 %all-to-all-start = ((bf16[16,24,128]{2,1,0:T(8,128)(2,1)}), bf16[16,24,128]{2,1,0:T(8,128)(2,1)S(1)}, u32[]{:S(2)}, u32[]{:S(2)}) async-start(bf16[16,24,128]{2,1,0:T(8,128)(2,1)} %bitcast.23), calls=%async_computation | async-start | bytes 196608 | tf_op jit(solution)/shard_map/all_to_all | solution.py:764
  13.4 5.9 %copy-start.4 = (bf16[512,256]{1,0:T(8,128)(2,1)S(1)}, bf16[512,256]{1,0:T(8,128)(2,1)}, u32[]{:S(2)}) copy-start(bf16[512,256]{1,0:T(8,128)(2,1)} %constant.21.clone.table) | copy-start | bytes 786436
  19.3 15.2 %copy-start.2 = (bf16[2,3,8,16,128]{4,3,2,1,0:T(8,128)(2,1)S(1)}, bf16[2,3,8,16,128]{4,3,2,1,0:T(8,128)(2,1)}, u32[]{:S(2)}) copy-start(bf16[2,3,8,16,128]{4,3,2,1,0:T(8,128)(2,1)} %saved.5) | copy-start | bytes 589828
  20.5 28.1 %all-to-all-start.1 = ((bf16[32,8,128]{2,1,0:T(8,128)(2,1)}), bf16[32,8,128]{2,1,0:T(8,128)(2,1)S(1)}, u32[]{:S(2)}, u32[]{:S(2)}) async-start(bf16[32,8,128]{2,1,0:T(8,128)(2,1)} %bitcast.3), calls=%async_computation.1 | async-start | bytes 131072 | tf_op jit(solution)/shard_map/all_to_all | solution.py:782
  34.5 6.3 %copy-start.3 = (bf16[8,2,32,256]{3,2,1,0:T(8,128)(2,1)S(1)}, bf16[8,2,32,256]{3,2,1,0:T(8,128)(2,1)}, u32[]{:S(2)}) copy-start(bf16[8,2,32,256]{3,2,1,0:T(8,128)(2,1)} %constant.23.clone.at_y) | copy-start | bytes 786436
  34.5 6.3 %copy-start.5 = (bf16[2,48,16,16]{1,3,2,0:T(8,128)(2,1)S(1)}, bf16[2,48,16,16]{1,3,2,0:T(8,128)(2,1)}, u32[]{:S(2)}) copy-start(bf16[2,48,16,16]{1,3,2,0:T(8,128)(2,1)} %param.33) | copy-start | bytes 147460
  34.5 6.3 %copy-start.8 = (bf16[2,128,256]{2,1,0:T(8,128)(2,1)S(1)}, bf16[2,128,256]{2,1,0:T(8,128)(2,1)}, u32[]{:S(2)}) copy-start(bf16[2,128,256]{2,1,0:T(8,128)(2,1)} %constant.22.clone.at_x) | copy-start | bytes 393220
  34.5 6.3 %copy-start.9 = (bf16[16,2,16,128]{3,2,1,0:T(8,128)(2,1)S(1)}, bf16[16,2,16,128]{3,2,1,0:T(8,128)(2,1)}, u32[]{:S(2)}) copy-start(bf16[16,2,16,128]{3,2,1,0:T(8,128)(2,1)} %constant.24.clone.at_z) | copy-start | bytes 393220
  34.6 6.3 %copy-start.15 = (f32[16,48]{1,0:T(8,128)S(1)}, f32[16,48]{1,0:T(8,128)}, u32[]{:S(2)}) copy-start(f32[16,48]{1,0:T(8,128)} %gain_x.1) | copy-start | bytes 9220
  34.6 6.3 %copy-start.16 = (f32[16,48]{1,0:T(8,128)S(1)}, f32[16,48]{1,0:T(8,128)}, u32[]{:S(2)}) copy-start(f32[16,48]{1,0:T(8,128)} %gain_y.1) | copy-start | bytes 9220
  34.6 6.3 %copy-start.19 = (f32[3,16]{1,0:T(4,128)S(1)}, f32[3,16]{1,0:T(4,128)}, u32[]{:S(2)}) copy-start(f32[3,16]{1,0:T(4,128)} %project.1) | copy-start | bytes 580
  34.6 11.4 %collective-permute-start = (bf16[17,16,128]{2,1,0:T(8,128)(2,1)S(1)}, bf16[17,16,128]{2,1,0:T(8,128)(2,1)S(1)}, u32[]{:S(2)}, u32[]{:S(2)}) collective-permute-start(bf16[17,16,128]{2,1,0:T(8,128)(2,1)S(1)} %get-tuple-element.34), channel_id=1, source_target_pairs={{0,16},{16,32},{32,48},{48,64},{64,80},{80,96},{96,112},{112,128},... | collective-permute-start | bytes 208904 | tf_op jit(solution)/shard_map/ppermute | solution.py:730
  39.4 6.6 %collective-permute-start.1 = (bf16[10,16,128]{2,1,0:T(8,128)(2,1)S(1)}, bf16[10,16,128]{2,1,0:T(8,128)(2,1)S(1)}, u32[]{:S(2)}, u32[]{:S(2)}) collective-permute-start(bf16[10,16,128]{2,1,0:T(8,128)(2,1)S(1)} %get-tuple-element.35), channel_id=1, source_target_pairs={{16,0},{32,16},{48,32},{64,48},{80,64},{96,80},{112,96},{128,112},... | collective-permute-start | bytes 122888 | tf_op jit(solution)/shard_map/ppermute | solution.py:730
  48.6 17.9 %copy-start.10 = (bf16[128,384]{1,0:T(8,128)(2,1)S(1)}, bf16[128,384]{1,0:T(8,128)(2,1)}, u32[]{:S(2)}) copy-start(bf16[128,384]{1,0:T(8,128)(2,1)} %constant.27.clone.inv_y) | copy-start | bytes 294916
  50.0 16.5 %all-to-all-start.2 = ((bf16[8,16,128]{2,1,0:T(8,128)(2,1)}), bf16[8,16,128]{2,1,0:T(8,128)(2,1)S(1)}, u32[]{:S(2)}, u32[]{:S(2)}) async-start(bf16[8,16,128]{2,1,0:T(8,128)(2,1)} %bitcast.8), calls=%async_computation.2 | async-start | bytes 65536 | tf_op jit(solution)/shard_map/all_to_all | solution.py:735
  56.5 9.9 %collective-permute-start.2 = (bf16[17,16,128]{2,1,0:T(8,128)(2,1)S(1)}, bf16[17,16,128]{2,1,0:T(8,128)(2,1)S(1)}, u32[]{:S(2)}, u32[]{:S(2)}) collective-permute-start(bf16[17,16,128]{2,1,0:T(8,128)(2,1)S(1)} %get-tuple-element.36.after), channel_id=1, source_target_pairs={{0,1},{1,2},{2,3},{3,4},{4,5},{5,6},{6,7},{7,8},{8,9},{9,10},{10,1... | collective-permute-start | bytes 208904 | tf_op jit(solution)/shard_map/ppermute | solution.py:730
  60.8 5.6 %collective-permute-start.3 = (bf16[10,16,128]{2,1,0:T(8,128)(2,1)S(1)}, bf16[10,16,128]{2,1,0:T(8,128)(2,1)S(1)}, u32[]{:S(2)}, u32[]{:S(2)}) collective-permute-start(bf16[10,16,128]{2,1,0:T(8,128)(2,1)S(1)} %get-tuple-element.37), channel_id=1, source_target_pairs={{1,0},{2,1},{3,2},{4,3},{5,4},{6,5},{7,6},{8,7},{9,8},{10,9},{11,1... | collective-permute-start | bytes 122888 | tf_op jit(solution)/shard_map/ppermute | solution.py:730
  68.0 11.8 %all-to-all-start.3 = ((bf16[16,8,640]{2,1,0:T(8,128)(2,1)}), bf16[16,8,640]{2,1,0:T(8,128)(2,1)S(1)}, u32[]{:S(2)}, u32[]{:S(2)}) async-start(bf16[16,8,640]{2,1,0:T(8,128)(2,1)} %bitcast.10), calls=%async_computation.3 | async-start | bytes 327680 | tf_op jit(solution)/shard_map/all_to_all | solution.py:839
  73.4 6.4 %copy-start.12 = (bf16[128,256]{1,0:T(8,128)(2,1)S(1)}, bf16[128,256]{1,0:T(8,128)(2,1)}, u32[]{:S(2)}) copy-start(bf16[128,256]{1,0:T(8,128)(2,1)} %constant.29.clone.apart) | copy-start | bytes 196612
  73.4 6.4 %copy-start.13 = (bf16[128,128]{1,0:T(8,128)(2,1)S(1)}, bf16[128,128]{1,0:T(8,128)(2,1)}, u32[]{:S(2)}) copy-start(bf16[128,128]{1,0:T(8,128)(2,1)} %constant.28.clone.table) | copy-start | bytes 98308
  (6 other events, 8.9 us)

commit v6 on v5

--- a/solution.py
+++ b/solution.py
@@ -15,8 +15,9 @@
 OWN = 3
 WIDE, BULK = 16, 32
 RX, RY = 8, 16
-NEAR, FAR = 8, 4
+NEAR, DEPTH, HALVES = 4, 16, 2
 SHARE = OWN * K // NEAR
+PAD = 40
 LANES = 128
 F32, BF16 = jnp.float32, jnp.bfloat16
 PARAMS = pltpu.CompilerParams(vmem_limit_bytes=40 * 1024 * 1024)
@@ -63,16 +64,19 @@
     fwd_y[256:, 128 : 128 + K] = cy[:, y_of].T
     out["fwd_y"] = fwd_y
 
-    fwd_x = np.zeros((2 * LANES, NX), ml_dtypes.bfloat16)
-    fwd_x[:K], fwd_x[64 : 64 + K] = cx, -sx
-    fwd_x[128 : 128 + K], fwd_x[192 : 192 + K] = sx, cx
-    inv_x = np.zeros((FAR, LANES, LANES), ml_dtypes.bfloat16)
-    for far in range(FAR):
-        for n in range(NEAR):
-            start = (far * NEAR + n) * RX
+    fwd_x = np.zeros((HALVES, 2 * LANES, DEPTH * RX), ml_dtypes.bfloat16)
+    inv_x = np.zeros((DEPTH // NEAR, HALVES, NEAR * 16, LANES), ml_dtypes.bfloat16)
+    for half in range(HALVES):
+        for z in range(DEPTH):
+            start = (z * HALVES + half) * RX
+            here, at = slice(start, start + RX), slice(z * RX, (z + 1) * RX)
+            fwd_x[half, :K, at], fwd_x[half, 64 : 64 + K, at] = cx[:, here], -sx[:, here]
+            fwd_x[half, 128 : 128 + K, at] = sx[:, here]
+            fwd_x[half, 192 : 192 + K, at] = cx[:, here]
             x_of = (start + np.array([0, 1, 2, 3, 4, 5, 6, 7, 8, -1])) % NX
-            inv_x[far, n * 16 : n * 16 + 10, :K] = cx[:, x_of].T
-            inv_x[far, n * 16 : n * 16 + 10, 64 : 64 + K] = -sx[:, x_of].T
+            at = slice(z % NEAR * 16, z % NEAR * 16 + 10)
+            inv_x[z // NEAR, half, at, :K] = cx[:, x_of].T
+            inv_x[z // NEAR, half, at, 64 : 64 + K] = -sx[:, x_of].T
     out["fwd_x"], out["inv_x"] = fwd_x, inv_x
 
     inv_y = np.zeros((LANES, 384), ml_dtypes.bfloat16)
@@ -92,7 +96,7 @@
     at_x[0, :K], at_x[0, 64 : 64 + K] = cx, -sx
     at_x[1, :K], at_x[1, 64 : 64 + K] = sx, cx
     out["at_x"] = at_x
-    at_y = np.zeros((NEAR, 2, 32, NY), ml_dtypes.bfloat16)
+    at_y = np.zeros((NEAR, 2, 48, NY), ml_dtypes.bfloat16)
     for n in range(NEAR):
         j_of = np.arange(n * SHARE, (n + 1) * SHARE) % K
         at_y[n, 0, :SHARE], at_y[n, 1, :SHARE] = cy[j_of], sy[j_of]
@@ -326,7 +330,8 @@
     lhs = jnp.concatenate(rows, 0).astype(BF16)
     found = jnp.dot(lhs, table[...], preferred_element_type=F32)
     lane = iota((8, LANES), 1)
-    parts = [jnp.zeros((8, LANES), F32) for _ in range(NEAR)]
+    parts = [[jnp.zeros((8, LANES), F32) for _ in range(2)] for _ in range(NEAR)]
+    split = LANES - (NEAR - 1) * SHARE
     for part in range(2):
         for d in range(3):
             piece = [
@@ -336,18 +341,29 @@
             last = pltpu.roll(piece[2], 2 * K, 1)
             first = piece[0] + pltpu.roll(piece[1], K, 1) + jnp.where(lane >= 2 * K, last, 0.0)
             rest = jnp.where(lane < 16, last, 0.0)
-            to = part * 64 + d * SHARE
+            to = d * SHARE
             for n in range(NEAR):
-                moved = pltpu.roll(first, (to - n * SHARE) % LANES, 1)
+                shift = (to - n * SHARE) % LANES
+                moved = pltpu.roll(first, shift, 1) if shift else first
                 if n == NEAR - 1:
-                    moved = jnp.where(lane < to + 2, moved, pltpu.roll(rest, to + 2, 1))
+                    moved = jnp.where(lane < to + split, moved, pltpu.roll(rest, to + split, 1))
                 within = (lane >= to) & (lane < to + SHARE)
-                parts[n] = parts[n] + jnp.where(within, moved, 0.0)
+                parts[n][part] = parts[n][part] + jnp.where(within, moved, 0.0)
     src = jnp.concatenate([taken[...], jnp.zeros((LANES - 8, LANES), F32)], 0).T
+    src = jnp.where(iota((LANES, LANES), 1) < 6, src, 0.0)
     high = src.astype(BF16).astype(F32)
-    extra = pltpu.roll(high, 54, 1) + pltpu.roll(src - high, 118, 1)
-    deal = (jnp.concatenate(parts, 0) + extra[: NEAR * 8]).astype(BF16)
-    for f in range(FAR):
+    at = 3 * SHARE
+    rows = []
+    for n in range(NEAR):
+        for part, value in enumerate((high, src - high)):
+            for i in range(2):
+                start = n * 16 + i * 8
+                parts[n][part] = parts[n][part] + pltpu.roll(
+                    value[start : start + 8], at + i * 6, 1
+                )
+        rows.append(jnp.concatenate(parts[n], 1))
+    deal = jnp.concatenate(rows, 0).astype(BF16)
+    for f in range(DEPTH // NEAR):
         out[f * NEAR * 8 : (f + 1) * NEAR * 8, :] = deal
 
 
@@ -356,7 +372,7 @@
     coef_a, coef_b, phase_x, phase_yz, injected,
 ):
     b, w = own_block()
-    n = b % NEAR
+    n = b // HALVES % NEAR
     flat = cells[...]
     x, y, z = place_of(flat)
     first = iota((1, LANES), 1) < 64
@@ -369,21 +385,21 @@
     ).astype(BF16)
     hot_y = jnp.where(iota((NY, LANES), 0) == y, 1.0, 0.0).astype(BF16)
     hot_z = jnp.where(iota((NZ, LANES), 0) == z, 1.0, 0.0).astype(BF16)
-    cy = jnp.dot(at_y[n, 0], hot_y, preferred_element_type=F32)[:24]
-    sy = jnp.dot(at_y[n, 1], hot_y, preferred_element_type=F32)[:24]
+    cy = jnp.dot(at_y[n, 0], hot_y, preferred_element_type=F32)[:PAD]
+    sy = jnp.dot(at_y[n, 1], hot_y, preferred_element_type=F32)[:PAD]
     cz = jnp.dot(at_z[w, 0], hot_z, preferred_element_type=F32)
     sz = jnp.dot(at_z[w, 1], hot_z, preferred_element_type=F32)
-    mode = n * SHARE + iota((24, 1), 0)
+    mode = n * SHARE + iota((PAD, 1), 0)
     ck = jnp.where(mode < K, cz[0:1], jnp.where(mode < 2 * K, cz[1:2], cz[2:3]))
     sk = jnp.where(mode < K, sz[0:1], jnp.where(mode < 2 * K, sz[1:2], sz[2:3]))
     phase_yz[...] = jnp.where(first, cy * ck - sy * sk, -(sy * ck + cy * sk))
 
-    place = iota((K, 24), 1)
+    place = iota((K, PAD), 1)
     mode = n * SHARE + place
     depth = jnp.where(mode < K, 0, jnp.where(mode < 2 * K, 1, 2))
     live = place < SHARE
-    hot_j = jnp.where((iota((K, 24), 0) == mode - depth * K) & live, 1.0, 0.0)
-    hot_k = jnp.where((iota((K, 24), 0) == w * OWN + depth) & live, 1.0, 0.0)
+    hot_j = jnp.where((iota((K, PAD), 0) == mode - depth * K) & live, 1.0, 0.0)
+    hot_k = jnp.where((iota((K, PAD), 0) == w * OWN + depth) & live, 1.0, 0.0)
     gains = jnp.dot(gain_y[...], hot_j, precision=HIGHEST, preferred_element_type=F32)
     diagonal = iota((16, 16), 0) == iota((16, 16), 1)
     columns = [
@@ -406,7 +422,7 @@
         for e in range(3):
             for d in range(3):
                 left = (columns[e] * joined[d]).T
-                to[(e * 3 + d) * 24 : (e * 3 + d + 1) * 24, :] = jnp.dot(
+                to[(e * 3 + d) * PAD : (e * 3 + d + 1) * PAD, :] = jnp.dot(
                     left, right, precision=HIGHEST, preferred_element_type=F32
                 )
     row = iota((8, LANES), 0)
@@ -420,45 +436,53 @@
 
 
 def filter_kernel(
-    gathered, coef_a, coef_b, fwd_x, inv_x, phase_x, phase_yz, after, out
+    own, other, coef_a, coef_b, fwd_x, inv_x, phase_x, phase_yz, after, out
 ):
     b, w = own_block()
-    far = b // NEAR
+    half, near = b % HALVES, b // HALVES % NEAR
     lane = iota((1, LANES), 1)
-    got = gathered[...]
-    both = jnp.dot(fwd_x[...], got, preferred_element_type=F32)
-    total = got.astype(F32).reshape(BULK, 8, LANES).sum(0)
-    total = total + pltpu.roll(total, 64, 1)
-    total = jnp.where(lane < 6, pltpu.roll(total, LANES - 54, 1), 0.0)
-    total = jnp.concatenate([total, jnp.zeros((LANES - 8, LANES), F32)], 0).T[:8]
-    total = pltpu.roll(total, (b % NEAR) * 8, 1)
-    full = (both[:LANES] + pltpu.roll(both[LANES:], 64, 1)).T
-    field = [full[d * SHARE : d * SHARE + 24] for d in range(3)]
+    mine, theirs = own[...], other[...]
+    both = jnp.dot(fwd_x[half], mine, preferred_element_type=F32) + jnp.dot(
+        fwd_x[1 - half], theirs, preferred_element_type=F32
+    )
+    full = (both[:LANES, :LANES] + both[LANES:, LANES:]).T
+    field = [full[d * SHARE : d * SHARE + PAD] for d in range(3)]
     turned = [pltpu.roll(f, 64, 1) for f in field]
     sign = jnp.where(lane < 64, 1.0, -1.0)
     real = []
     for e in range(3):
-        q = jnp.zeros((24, LANES), F32)
+        q = jnp.zeros((PAD, LANES), F32)
         for d in range(3):
-            at = (e * 3 + d) * 24
-            q = q + coef_a[at : at + 24] * field[d] + coef_b[at : at + 24] * turned[d]
+            at = (e * 3 + d) * PAD
+            q = q + coef_a[at : at + PAD] * field[d] + coef_b[at : at + PAD] * turned[d]
         real.append(q)
-    near = jnp.dot(
-        jnp.concatenate(real, 0).astype(BF16), phase_x[...], preferred_element_type=F32
-    )
-    gap = jnp.zeros((10, LANES), F32)
+    gap = jnp.zeros((LANES - 3 * SHARE, LANES), F32)
     packed = jnp.concatenate([q[:SHARE] for q in real] + [gap], 0)
     right = jnp.concatenate([packed, pltpu.roll(packed, 64, 1) * sign], 0).astype(BF16)
     back = lax.dot_general(
-        inv_x[far], right, (((1,), (1,)), ((), ())), preferred_element_type=F32
-    ).reshape(NEAR, 2, 8, LANES)
+        inv_x[b // (HALVES * NEAR), half], right, (((1,), (1,)), ((), ())),
+        preferred_element_type=F32,
+    ).reshape(NEAR, 2, 8, 2 * LANES)
+
+    total = mine.astype(F32).reshape(DEPTH, 8, 2 * LANES).sum(0)
+    total = total + theirs.astype(F32).reshape(DEPTH, 8, 2 * LANES).sum(0)
+    total = pltpu.roll(total[:, :LANES] + total[:, LANES:], LANES - 3 * SHARE, 1)
+    second = pltpu.roll(total, LANES - 6, 1)
+    gap = jnp.zeros((LANES - 16, LANES), F32)
+    total = jnp.concatenate([total, second, gap], 0)
+    total = jnp.where(iota((LANES, LANES), 1) < 6, total, 0.0).T[:8]
+    total = pltpu.roll(total, near * 16, 1)
+    near = jnp.dot(
+        jnp.concatenate(real, 0).astype(BF16), phase_x[...], preferred_element_type=F32
+    )
     row = iota((8, LANES), 0)
     for e in range(3):
-        line = jnp.sum(near[e * 24 : (e + 1) * 24] * phase_yz[...], axis=0, keepdims=True)
+        line = jnp.sum(near[e * PAD : (e + 1) * PAD] * phase_yz[...], axis=0, keepdims=True)
         line = line + pltpu.roll(line, 64, 1)
         total = total + jnp.where((row == e) & (lane < 64), line, 0.0)
     high = total.astype(BF16).astype(F32)
     extra = pltpu.roll(high + pltpu.roll(total - high, 64, 1), 2, 0)
+    extra = jnp.concatenate([extra, jnp.zeros((8, LANES), F32)], 1)
     tiles = []
     for n in range(NEAR):
         tiles += [back[n, 0], back[n, 1] + extra]
@@ -467,15 +491,17 @@
 
 def spread_kernel(shares, inv_y, after_low, after_high, out, rows):
     lane = iota((1, LANES), 1)
-    got = shares[...].astype(F32).reshape(NEAR, 16, LANES)
+    got = shares[...].astype(F32).reshape(NEAR, 16, 2 * LANES)
     rows[...] = jnp.zeros((32, 8, LANES), F32)
     for e in range(3):
         flat = []
         for part in range(2):
-            start = part * 64 + e * SHARE
+            start = e * SHARE
             first, rest = jnp.zeros((16, LANES), F32), None
             for n in range(NEAR):
-                moved = pltpu.roll(got[n], (n * SHARE - start) % LANES, 1)
+                moved = got[n][:, part * LANES : (part + 1) * LANES]
+                if n != e:
+                    moved = pltpu.roll(moved, (n * SHARE - start) % LANES, 1)
                 within = (lane >= n * SHARE) & (lane < (n + 1) * SHARE)
                 first = first + jnp.where(within, moved, 0.0)
                 if n == NEAR - 1:
@@ -510,7 +536,7 @@
         edge.append(jnp.stack([wide[high * 16 + low, :, 256:384] for high in range(2)]))
     edge = exchange(edge, 2, 2)
     row = iota((8, LANES), 0)
-    total = pltpu.roll(got[:, 8:16].sum(0), 6, 0)
+    total = pltpu.roll(got[:, 8:16, :LANES].sum(0), 6, 0)
     total = jnp.where((row < 6) & (lane < 64), total + pltpu.roll(total, 64, 1), 0.0)
     high = total.astype(BF16).astype(F32)
     other = pltpu.roll(total - high, 64, 1)
@@ -731,7 +757,18 @@
 
 
 def dealt_near(block):
-    groups = [[f * NEAR + n for n in range(NEAR)] for f in range(FAR)]
+    groups = [
+        [(f * NEAR + n) * HALVES + half for n in range(NEAR)]
+        for f in range(DEPTH // NEAR)
+        for half in range(HALVES)
+    ]
+    return lax.all_to_all(
+        block, "bulk", split_axis=0, concat_axis=0, axis_index_groups=groups, tiled=True
+    )
+
+
+def dealt_along(block):
+    groups = [[z * HALVES + half for z in range(DEPTH)] for half in range(HALVES)]
     return lax.all_to_all(
         block, "bulk", split_axis=0, concat_axis=0, axis_index_groups=groups, tiled=True
     )
@@ -777,16 +814,17 @@
     )(source_cells, permittivity, field, seed_magnetic, material)
 
     dealt = call(
-        middle_kernel, shape(BULK * 8, LANES, dtype=BF16), "vvv", (), 20_000_000, 400_000
+        middle_kernel, shape(DEPTH * 8, 2 * LANES, dtype=BF16), "vvv", (), 20_000_000, 400_000
     )(lines, taken, tables_of("fwd_y"))
-    gathered = lax.all_to_all(dealt, "bulk", split_axis=0, concat_axis=0, tiled=True)
+    mine = dealt_along(dealt)
+    theirs = lax.ppermute(mine, "bulk", [(i, i ^ 1) for i in range(BULK)])
 
     cells = jnp.concatenate([source_cells, source_cells]).reshape(1, LANES)
     coef_a, coef_b, phase_x, phase_yz, injected = call(
         param_kernel,
         (
-            shape(216, LANES), shape(216, LANES), shape(LANES, LANES, dtype=BF16),
-            shape(24, LANES), shape(8, LANES),
+            shape(9 * PAD, LANES), shape(9 * PAD, LANES), shape(LANES, LANES, dtype=BF16),
+            shape(PAD, LANES), shape(8, LANES),
         ),
         "sssvvvvvvvva",
         (),
@@ -818,9 +856,9 @@
         1_000_000,
     )(field, seed_magnetic, inverse, saved_magnetic, x_low, x_high, coef_a)
     shares = call(
-        filter_kernel, shape(LANES, LANES, dtype=BF16), "vvvvvvva", (), 40_000_000, 600_000
+        filter_kernel, shape(NEAR * 16, 2 * LANES, dtype=BF16), "vvvvvvvva", (), 40_000_000, 600_000
     )(
-        gathered, coef_a, coef_b, tables_of("fwd_x"), tables_of("inv_x"), phase_x, phase_yz,
+        mine, theirs, coef_a, coef_b, tables_of("fwd_x"), tables_of("inv_x"), phase_x, phase_yz,
         low_part,
     )
     back = dealt_near(shares)

time: 81.6 us -> 80.9 us (level)
  starting transfers between devices: 48.6 us -> 47.1 us
    ppermute x0 -> x1, starting transfers between devices: none -> 4.48 us  [body(): theirs = lax.ppermute(mine, 'bulk', [(i, i ^ 1) for i in range(BULK)])]
    all_to_all x1, starting transfers between devices: 6.53 us -> 3.26 us  [dealt_near(): lax.all_to_all(block, 'bulk', split_axis=0, concat_axis=0, axis_index_gro...]
    all_to_all x1, waiting for transfers between devices: 2.48 us -> 5.63 us  [dealt_along(): lax.all_to_all(block, 'bulk', split_axis=0, concat_axis=0, axis_index_gro...]
    ppermute x4, waiting for transfers between devices: 6.31 us -> 3.4 us  [passed_along(): return lax.ppermute(block, axis, route)]
    all_to_all x1, starting transfers between devices: 14 us -> 11.5 us  [dealt_along(): lax.all_to_all(block, 'bulk', split_axis=0, concat_axis=0, axis_index_gro...]
  transfers between devices with their start and end apart: 8 -> 9, of which waited for: 5 -> 4; matrix products, arithmetic and copies ran while one was open for 0% -> 0% of each run, Pallas kernels for 6% -> 6%
where the time goes in v6:
time: 80.9 us; the launch traced here: 80.3 us
  starting transfers between devices  47.1 us (58%)
  waiting for transfers between devices  17.6 us (22%)
  Pallas kernels  12.7 us (16%)
  local copies, waits for them, and re-layouts  1.82 us (2%)
  between operations  1 us (1%)
    ppermute x4, starting transfers between devices, passed_along(): return lax.ppermute(block, axis, route)  12.1 us
    all_to_all x1, starting transfers between devices, dealt_along(): lax.all_to_all(block, 'bulk', split_axis=0, concat_axis=0, axis_index_gro...  11.5 us
    all_to_all x1, starting transfers between devices, body(): lax.all_to_all(payload, 'wide', split_axis=0, concat_axis=0, tiled=True)  10.4 us
    all_to_all x1, waiting for transfers between devices, dealt_along(): lax.all_to_all(block, 'bulk', split_axis=0, concat_axis=0, axis_index_gro...  5.63 us
    all_to_all x1, starting transfers between devices, body(): lax.all_to_all(sent, 'wide', split_axis=0, concat_axis=0, tiled=True)  5.31 us
    all_to_all x1, waiting for transfers between devices, body(): lax.all_to_all(sent, 'wide', split_axis=0, concat_axis=0, tiled=True)  4.69 us
    ppermute x1, starting transfers between devices, body(): theirs = lax.ppermute(mine, 'bulk', [(i, i ^ 1) for i in range(BULK)])  4.48 us
    all_to_all x1, waiting for transfers between devices, body(): lax.all_to_all(payload, 'wide', split_axis=0, concat_axis=0, tiled=True)  3.83 us
  transfers between devices with their start and end apart: 9, of which 4 were waited for; matrix products, arithmetic and copies ran while one was open for 0% of the time, Pallas kernels for 6%

profile of v6, /device:TPU:1, one launch (start us, length us, event | category | flops | bytes accessed | tf_op | source)
XLA Modules:
  0.0 80.3 jit_solution(12599359057330532127)
XLA Ops:
  0.6 2.3 %shard_map.246 = (bf16[384,128]{1,0:T(8,128)(2,1)}, f32[3,8,16,128]{3,2,1,0:T(8,128)}) custom-call(s32[64]{0:T(128)} %mon.3, f32[3,2,64]{2,1,0:T(2,128)} %bitcast.20, f32[3,8,16,128]{3,2,1,0:T(8,128)} %electric.1, bf16[128,128]{1,0:T(8,128)(2,1)} %constant.20.clone.table_in), custom_call_target="tpu_custom_call" | custom-call | flops 13000000 | bytes 500000 | tf_op jit(solution)/shard_map/pallas_call | solution.py:789
  3.0 10.4 %all-to-all-start = ((bf16[16,24,128]{2,1,0:T(8,128)(2,1)}), bf16[16,24,128]{2,1,0:T(8,128)(2,1)S(1)}, u32[]{:S(2)}, u32[]{:S(2)}) async-start(bf16[16,24,128]{2,1,0:T(8,128)(2,1)} %bitcast.24), calls=%async_computation | async-start | bytes 196608 | tf_op jit(solution)/shard_map/all_to_all | solution.py:801
  13.5 0.9 %copy-done.11 = s32[8,16,128]{2,1,0:T(8,128)S(1)} copy-done((s32[8,16,128]{2,1,0:T(8,128)S(1)}, s32[8,16,128]{2,1,0:T(8,128)}, u32[]{:S(2)}) %copy-start.11) | copy-done | bytes 65560
  14.3 1.1 %shard_map.247 = (f32[8,128]{1,0:T(8,128)S(1)}, f32[8,16,128]{2,1,0:T(8,128)S(1)}) custom-call(s32[64]{0:T(128)S(1)} %copy-done.21, f32[8]{0:T(128)S(1)} %copy-done.20, f32[3,8,16,128]{3,2,1,0:T(8,128)S(1)} %copy-done.1, f32[3,8,16,128]{3,2,1,0:T(8,128)S(1)} %copy-done, s32[8,16,128]{2,1,0:T(8,128)S(1)} %copy-done.11), custom_call_target="tpu_custom_call" | custom-call | flops 3000000 | bytes 1500000 | tf_op jit(solution)/shard_map/pallas_call | solution.py:803
  15.5 3.8 %all-to-all-done = bf16[16,24,128]{2,1,0:T(8,128)(2,1)S(1)} async-done(((bf16[16,24,128]{2,1,0:T(8,128)(2,1)}), bf16[16,24,128]{2,1,0:T(8,128)(2,1)S(1)}, u32[]{:S(2)}, u32[]{:S(2)}) %all-to-all-start) | async-done | bytes 98336 | tf_op jit(solution)/shard_map/all_to_all | solution.py:801
  19.3 1.3 %shard_map.248.after = bf16[128,256]{1,0:T(8,128)(2,1)} custom-call(bf16[384,128]{1,0:T(8,128)(2,1)S(1)} %bitcast.15, f32[8,128]{1,0:T(8,128)S(1)} %get-tuple-element.28.taken, bf16[512,256]{1,0:T(8,128)(2,1)S(1)} %copy-done.3), custom_call_target="tpu_custom_call" | custom-call | flops 20000000 | bytes 400000 | tf_op jit(solution)/shard_map/pallas_call | solution.py:816
  20.6 11.5 %all-to-all-start.1 = ((bf16[16,8,256]{2,1,0:T(8,128)(2,1)}), bf16[16,8,256]{2,1,0:T(8,128)(2,1)S(1)}, u32[]{:S(2)}, u32[]{:S(2)}) async-start(bf16[16,8,256]{2,1,0:T(8,128)(2,1)} %bitcast.3), calls=%async_computation.1 | async-start | bytes 131072 | tf_op jit(solution)/shard_map/all_to_all | solution.py:772
  32.2 4.5 %collective-permute-start.1 = (bf16[17,16,128]{2,1,0:T(8,128)(2,1)S(1)}, bf16[17,16,128]{2,1,0:T(8,128)(2,1)S(1)}, u32[]{:S(2)}, u32[]{:S(2)}) collective-permute-start(bf16[17,16,128]{2,1,0:T(8,128)(2,1)S(1)} %get-tuple-element.34), channel_id=1, source_target_pairs={{0,16},{16,32},{32,48},{48,64},{64,80},{80,96},{96,112},{112,128},... | collective-permute-start | bytes 208904 | tf_op jit(solution)/shard_map/ppermute | solution.py:756
  36.7 1.3 %collective-permute-start.2 = (bf16[10,16,128]{2,1,0:T(8,128)(2,1)S(1)}, bf16[10,16,128]{2,1,0:T(8,128)(2,1)S(1)}, u32[]{:S(2)}, u32[]{:S(2)}) collective-permute-start(bf16[10,16,128]{2,1,0:T(8,128)(2,1)S(1)} %get-tuple-element.35), channel_id=1, source_target_pairs={{16,0},{32,16},{48,32},{64,48},{80,64},{96,80},{112,96},{128,112},... | collective-permute-start | bytes 122888 | tf_op jit(solution)/shard_map/ppermute | solution.py:756
  38.0 5.6 %all-to-all-done.1 = bf16[16,8,256]{2,1,0:T(8,128)(2,1)S(1)} async-done(((bf16[16,8,256]{2,1,0:T(8,128)(2,1)}), bf16[16,8,256]{2,1,0:T(8,128)(2,1)S(1)}, u32[]{:S(2)}, u32[]{:S(2)}) %all-to-all-start.1) | async-done | bytes 65568 | tf_op jit(solution)/shard_map/all_to_all | solution.py:772
  43.7 4.5 %collective-permute-start = (bf16[128,256]{1,0:T(8,128)(2,1)S(1)}, bf16[128,256]{1,0:T(8,128)(2,1)S(1)}, u32[]{:S(2)}, u32[]{:S(2)}) collective-permute-start(bf16[128,256]{1,0:T(8,128)(2,1)S(1)} %bitcast.16), channel_id=1, source_target_pairs={{0,16},{16,0},{32,48},{48,32},{64,80},{80,64},{96,112},{112,96},{1... | collective-permute-start | bytes 196616 | tf_op jit(solution)/shard_map/ppermute | solution.py:820
  48.3 2.1 %shard_map.249 = (f32[360,128]{1,0:T(8,128)S(1)}, f32[360,128]{1,0:T(8,128)S(1)}, bf16[128,128]{1,0:T(8,128)(2,1)S(1)}, f32[40,128]{1,0:T(8,128)S(1)}, f32[8,128]{1,0:T(8,128)S(1)}) custom-call(s32[64]{0:T(128)S(1)} %copy-done.17, f32[3,2,64]{2,1,0:T(2,128)S(1)} %bitcast.21, f32[3,16]{1,0:T(4,128)S(1)} %bitcast.23, s32[1,128]{1,0:T(1,128)S(1)} %add_bitcast_fusion.cells, ...), custom_call_target="tpu_custom_call" | custom-call | flops 20000000 | bytes 1000000 | tf_op jit(solution)/shard_map/pallas_call | solution.py:823
  50.5 0.1 shard_map.251
  50.6 0.8 copy-done.5
  51.4 1.4 %shard_map.252 = bf16[64,256]{1,0:T(8,128)(2,1)} custom-call(bf16[128,256]{1,0:T(8,128)(2,1)S(1)} %bitcast.17, bf16[128,256]{1,0:T(8,128)(2,1)S(1)} %collective-permute-done.other, f32[360,128]{1,0:T(8,128)S(1)} %get-tuple-element.29.after.coef_a, f32[360,128]{1,0:T(8,128)S(1)} %get-tuple-element.30.coef_b, bf16[2,256,128]{2,1,0:T(8,128)(2,1)S(1)} %copy-done.5, ...), custom_call_target="tpu_custom_call" | custom-call | flops 40000000 | bytes 600000 | tf_op jit(solution)/shard_map/pallas_call | solution.py:858
  52.8 3.3 %all-to-all-start.2 = ((bf16[4,16,256]{2,1,0:T(8,128)(2,1)}), bf16[4,16,256]{2,1,0:T(8,128)(2,1)S(1)}, u32[]{:S(2)}, u32[]{:S(2)}) async-start(bf16[4,16,256]{2,1,0:T(8,128)(2,1)} %bitcast.8), calls=%async_computation.2 | async-start | bytes 65536 | tf_op jit(solution)/shard_map/all_to_all | solution.py:765
  56.1 4.4 %collective-permute-start.3 = (bf16[17,16,128]{2,1,0:T(8,128)(2,1)S(1)}, bf16[17,16,128]{2,1,0:T(8,128)(2,1)S(1)}, u32[]{:S(2)}, u32[]{:S(2)}) collective-permute-start(bf16[17,16,128]{2,1,0:T(8,128)(2,1)S(1)} %get-tuple-element.36.after), channel_id=1, source_target_pairs={{0,1},{1,2},{2,3},{3,4},{4,5},{5,6},{6,7},{7,8},{8,9},{9,10},{10,1... | collective-permute-start | bytes 208904 | tf_op jit(solution)/shard_map/ppermute | solution.py:756
  60.5 1.9 %collective-permute-start.4 = (bf16[10,16,128]{2,1,0:T(8,128)(2,1)S(1)}, bf16[10,16,128]{2,1,0:T(8,128)(2,1)S(1)}, u32[]{:S(2)}, u32[]{:S(2)}) collective-permute-start(bf16[10,16,128]{2,1,0:T(8,128)(2,1)S(1)} %get-tuple-element.37), channel_id=1, source_target_pairs={{1,0},{2,1},{3,2},{4,3},{5,4},{6,5},{7,6},{8,7},{9,8},{10,9},{11,1... | collective-permute-start | bytes 122888 | tf_op jit(solution)/shard_map/ppermute | solution.py:756
  62.5 3.4 %collective-permute-done.4.after_high.y_high = bf16[10,16,128]{2,1,0:T(8,128)(2,1)S(1)} collective-permute-done((bf16[10,16,128]{2,1,0:T(8,128)(2,1)S(1)}, bf16[10,16,128]{2,1,0:T(8,128)(2,1)S(1)}, u32[]{:S(2)}, u32[]{:S(2)}) %collective-permute-start.4) | collective-permute-done | bytes 40992 | tf_op jit(solution)/shard_map/ppermute | solution.py:756
  65.9 1.5 %shard_map.253.after = bf16[128,640]{1,0:T(8,128)(2,1)} custom-call(bf16[64,256]{1,0:T(8,128)(2,1)S(1)} %bitcast.18, bf16[128,384]{1,0:T(8,128)(2,1)S(1)} %copy-done.10, bf16[17,16,128]{2,1,0:T(8,128)(2,1)S(1)} %collective-permute-done.3.after_low.y_low, bf16[10,16,128]{2,1,0:T(8,128)(2,1)S(1)} %collective-permute-done.4.after_high.y_high), custom_call_target="tpu_custom_call" | custom-call | flops 40000000 | bytes 600000 | tf_op jit(solution)/shard_map/pallas_call | solution.py:869
  67.4 5.3 %all-to-all-start.3 = ((bf16[16,8,640]{2,1,0:T(8,128)(2,1)}), bf16[16,8,640]{2,1,0:T(8,128)(2,1)S(1)}, u32[]{:S(2)}, u32[]{:S(2)}) async-start(bf16[16,8,640]{2,1,0:T(8,128)(2,1)} %bitcast.10), calls=%async_computation.3 | async-start | bytes 327680 | tf_op jit(solution)/shard_map/all_to_all | solution.py:877
  72.7 1.7 %shard_map.254 = (f32[3,10,24,128]{3,2,1,0:T(8,128)S(1)}, f32[3,10,24,128]{3,2,1,0:T(8,128)S(1)}, f32[10,24,128]{2,1,0:T(8,128)S(1)}, f32[8,16,128]{2,1,0:T(8,128)S(1)}, f32[3,8,16,128]{3,2,1,0:T(8,128)S(1)}) custom-call(s32[64]{0:T(128)S(1)} %copy-done.17, f32[3,2,64]{2,1,0:T(2,128)S(1)} %bitcast.22, f32[3,8,16,128]{3,2,1,0:T(8,128)S(1)} %copy-done.1, ...), custom_call_target="tpu_custom_call" | custom-call | flops 10000000 | bytes 3000000 | tf_op jit(solution)/shard_map/pallas_call | solution.py:878
  74.4 4.7 %all-to-all-done.3 = bf16[16,8,640]{2,1,0:T(8,128)(2,1)S(1)} async-done(((bf16[16,8,640]{2,1,0:T(8,128)(2,1)}), bf16[16,8,640]{2,1,0:T(8,128)(2,1)S(1)}, u32[]{:S(2)}, u32[]{:S(2)}) %all-to-all-start.3) | async-done | bytes 163872 | tf_op jit(solution)/shard_map/all_to_all | solution.py:877
  79.1 1.2 %shard_map.255 = (f32[3,8,16,128]{3,2,1,0:T(8,128)}, f32[3,8,16,128]{3,2,1,0:T(8,128)}, f32[8,16,128]{2,1,0:T(8,128)}, f32[3,2,64]{2,1,0:T(2,128)}) custom-call(bf16[128,640]{1,0:T(8,128)(2,1)S(1)} %bitcast.14, bf16[128,128]{1,0:T(8,128)(2,1)S(1)} %copy-done.13, bf16[128,256]{1,0:T(8,128)(2,1)S(1)} %copy-done.12, ...), custom_call_target="tpu_custom_call" | custom-call | flops 40000000 | bytes 4000000 | tf_op jit(solution)/shard_map/pallas_call | solution.py:893
  (49 shorter events, 0.3 us)
Async XLA Ops:
  0.6 12.8 %copy-start = (f32[3,8,16,128]{3,2,1,0:T(8,128)S(1)}, f32[3,8,16,128]{3,2,1,0:T(8,128)}, u32[]{:S(2)}) copy-start(f32[3,8,16,128]{3,2,1,0:T(8,128)} %magnetic.5) | copy-start | bytes 589828
  3.0 10.5 %copy-start.1 = (f32[3,8,16,128]{3,2,1,0:T(8,128)S(1)}, f32[3,8,16,128]{3,2,1,0:T(8,128)}, u32[]{:S(2)}) copy-start(f32[3,8,16,128]{3,2,1,0:T(8,128)} %get-tuple-element.27.field.electric) | copy-start | bytes 589828
  3.0 10.5 %copy-start.20 = (f32[8]{0:T(128)S(1)}, f32[8]{0:T(128)}, u32[]{:S(2)}) copy-start(f32[8]{0:T(128)} %perm_in.1) | copy-start | bytes 100
  3.0 10.4 %copy-start.21 = (s32[64]{0:T(128)S(1)}, s32[64]{0:T(128)}, u32[]{:S(2)}) copy-start(s32[64]{0:T(128)} %src_in.1) | copy-start | bytes 772
  3.0 16.3 %all-to-all-start = ((bf16[16,24,128]{2,1,0:T(8,128)(2,1)}), bf16[16,24,128]{2,1,0:T(8,128)(2,1)S(1)}, u32[]{:S(2)}, u32[]{:S(2)}) async-start(bf16[16,24,128]{2,1,0:T(8,128)(2,1)} %bitcast.24), calls=%async_computation | async-start | bytes 196608 | tf_op jit(solution)/shard_map/all_to_all | solution.py:801
  19.3 12.8 %copy-start.2 = (bf16[2,3,8,16,128]{4,3,2,1,0:T(8,128)(2,1)S(1)}, bf16[2,3,8,16,128]{4,3,2,1,0:T(8,128)(2,1)}, u32[]{:S(2)}) copy-start(bf16[2,3,8,16,128]{4,3,2,1,0:T(8,128)(2,1)} %saved.5) | copy-start | bytes 589828
  20.6 23.1 %all-to-all-start.1 = ((bf16[16,8,256]{2,1,0:T(8,128)(2,1)}), bf16[16,8,256]{2,1,0:T(8,128)(2,1)S(1)}, u32[]{:S(2)}, u32[]{:S(2)}) async-start(bf16[16,8,256]{2,1,0:T(8,128)(2,1)} %bitcast.3), calls=%async_computation.1 | async-start | bytes 131072 | tf_op jit(solution)/shard_map/all_to_all | solution.py:772
  32.1 16.1 %copy-start.4 = (bf16[4,2,48,256]{3,2,1,0:T(8,128)(2,1)S(1)}, bf16[4,2,48,256]{3,2,1,0:T(8,128)(2,1)}, u32[]{:S(2)}) copy-start(bf16[4,2,48,256]{3,2,1,0:T(8,128)(2,1)} %constant.23.clone.at_y) | copy-start | bytes 589828
  32.1 16.1 %copy-start.7 = (bf16[2,48,16,16]{1,3,2,0:T(8,128)(2,1)S(1)}, bf16[2,48,16,16]{1,3,2,0:T(8,128)(2,1)}, u32[]{:S(2)}) copy-start(bf16[2,48,16,16]{1,3,2,0:T(8,128)(2,1)} %param.33) | copy-start | bytes 147460
  32.1 16.1 %copy-start.8 = (bf16[2,128,256]{2,1,0:T(8,128)(2,1)S(1)}, bf16[2,128,256]{2,1,0:T(8,128)(2,1)}, u32[]{:S(2)}) copy-start(bf16[2,128,256]{2,1,0:T(8,128)(2,1)} %constant.22.clone.at_x) | copy-start | bytes 393220
  32.1 16.1 %copy-start.9 = (bf16[16,2,16,128]{3,2,1,0:T(8,128)(2,1)S(1)}, bf16[16,2,16,128]{3,2,1,0:T(8,128)(2,1)}, u32[]{:S(2)}) copy-start(bf16[16,2,16,128]{3,2,1,0:T(8,128)(2,1)} %constant.24.clone.at_z) | copy-start | bytes 393220
  32.2 16.1 %copy-start.16 = (f32[16,48]{1,0:T(8,128)S(1)}, f32[16,48]{1,0:T(8,128)}, u32[]{:S(2)}) copy-start(f32[16,48]{1,0:T(8,128)} %gain_y.1) | copy-start | bytes 9220
  32.2 16.1 %copy-start.17 = (s32[64]{0:T(128)S(1)}, s32[64]{0:T(128)}, u32[]{:S(2)}) copy-start(s32[64]{0:T(128)} %mon.3) | copy-start | bytes 772
  32.2 16.1 %copy-start.18 = (f32[16,3]{0,1:T(4,128)S(1)}, f32[16,3]{0,1:T(4,128)}, u32[]{:S(2)}) copy-start(f32[16,3]{0,1:T(4,128)} %param.31) | copy-start | bytes 580
  32.2 16.1 %copy-start.19 = (f32[3,16]{1,0:T(4,128)S(1)}, f32[3,16]{1,0:T(4,128)}, u32[]{:S(2)}) copy-start(f32[3,16]{1,0:T(4,128)} %project.1) | copy-start | bytes 580
  32.2 16.1 %copy-start.15 = (f32[16,48]{1,0:T(8,128)S(1)}, f32[16,48]{1,0:T(8,128)}, u32[]{:S(2)}) copy-start(f32[16,48]{1,0:T(8,128)} %gain_x.1) | copy-start | bytes 9220
  32.2 18.2 %collective-permute-start.1 = (bf16[17,16,128]{2,1,0:T(8,128)(2,1)S(1)}, bf16[17,16,128]{2,1,0:T(8,128)(2,1)S(1)}, u32[]{:S(2)}, u32[]{:S(2)}) collective-permute-start(bf16[17,16,128]{2,1,0:T(8,128)(2,1)S(1)} %get-tuple-element.34), channel_id=1, source_target_pairs={{0,16},{16,32},{32,48},{48,64},{64,80},{80,96},{96,112},{112,128},... | collective-permute-start | bytes 208904 | tf_op jit(solution)/shard_map/ppermute | solution.py:756
  36.7 13.7 %collective-permute-start.2 = (bf16[10,16,128]{2,1,0:T(8,128)(2,1)S(1)}, bf16[10,16,128]{2,1,0:T(8,128)(2,1)S(1)}, u32[]{:S(2)}, u32[]{:S(2)}) collective-permute-start(bf16[10,16,128]{2,1,0:T(8,128)(2,1)S(1)} %get-tuple-element.35), channel_id=1, source_target_pairs={{16,0},{32,16},{48,32},{64,48},{80,64},{96,80},{112,96},{128,112},... | collective-permute-start | bytes 122888 | tf_op jit(solution)/shard_map/ppermute | solution.py:756
  43.7 6.9 %collective-permute-start = (bf16[128,256]{1,0:T(8,128)(2,1)S(1)}, bf16[128,256]{1,0:T(8,128)(2,1)S(1)}, u32[]{:S(2)}, u32[]{:S(2)}) collective-permute-start(bf16[128,256]{1,0:T(8,128)(2,1)S(1)} %bitcast.16), channel_id=1, source_target_pairs={{0,16},{16,0},{32,48},{48,32},{64,80},{80,64},{96,112},{112,96},{1... | collective-permute-start | bytes 196616 | tf_op jit(solution)/shard_map/ppermute | solution.py:820
  51.4 14.4 %copy-start.10 = (bf16[128,384]{1,0:T(8,128)(2,1)S(1)}, bf16[128,384]{1,0:T(8,128)(2,1)}, u32[]{:S(2)}) copy-start(bf16[128,384]{1,0:T(8,128)(2,1)} %constant.27.clone.inv_y) | copy-start | bytes 294916
  52.8 13.1 %all-to-all-start.2 = ((bf16[4,16,256]{2,1,0:T(8,128)(2,1)}), bf16[4,16,256]{2,1,0:T(8,128)(2,1)S(1)}, u32[]{:S(2)}, u32[]{:S(2)}) async-start(bf16[4,16,256]{2,1,0:T(8,128)(2,1)} %bitcast.8), calls=%async_computation.2 | async-start | bytes 65536 | tf_op jit(solution)/shard_map/all_to_all | solution.py:765
  56.1 9.8 %collective-permute-start.3 = (bf16[17,16,128]{2,1,0:T(8,128)(2,1)S(1)}, bf16[17,16,128]{2,1,0:T(8,128)(2,1)S(1)}, u32[]{:S(2)}, u32[]{:S(2)}) collective-permute-start(bf16[17,16,128]{2,1,0:T(8,128)(2,1)S(1)} %get-tuple-element.36.after), channel_id=1, source_target_pairs={{0,1},{1,2},{2,3},{3,4},{4,5},{5,6},{6,7},{7,8},{8,9},{9,10},{10,1... | collective-permute-start | bytes 208904 | tf_op jit(solution)/shard_map/ppermute | solution.py:756
  60.5 5.3 %collective-permute-start.4 = (bf16[10,16,128]{2,1,0:T(8,128)(2,1)S(1)}, bf16[10,16,128]{2,1,0:T(8,128)(2,1)S(1)}, u32[]{:S(2)}, u32[]{:S(2)}) collective-permute-start(bf16[10,16,128]{2,1,0:T(8,128)(2,1)S(1)} %get-tuple-element.37), channel_id=1, source_target_pairs={{1,0},{2,1},{3,2},{4,3},{5,4},{6,5},{7,6},{8,7},{9,8},{10,9},{11,1... | collective-permute-start | bytes 122888 | tf_op jit(solution)/shard_map/ppermute | solution.py:756
  67.4 11.7 %all-to-all-start.3 = ((bf16[16,8,640]{2,1,0:T(8,128)(2,1)}), bf16[16,8,640]{2,1,0:T(8,128)(2,1)S(1)}, u32[]{:S(2)}, u32[]{:S(2)}) async-start(bf16[16,8,640]{2,1,0:T(8,128)(2,1)} %bitcast.10), calls=%async_computation.3 | async-start | bytes 327680 | tf_op jit(solution)/shard_map/all_to_all | solution.py:877
  (7 other events, 26.2 us)

commit v7 on v6

--- a/solution.py
+++ b/solution.py
@@ -64,15 +64,13 @@
     fwd_y[256:, 128 : 128 + K] = cy[:, y_of].T
     out["fwd_y"] = fwd_y
 
-    fwd_x = np.zeros((HALVES, 2 * LANES, DEPTH * RX), ml_dtypes.bfloat16)
+    fwd_x = np.zeros((2 * LANES, NX), ml_dtypes.bfloat16)
+    fwd_x[:K], fwd_x[64 : 64 + K] = cx, -sx
+    fwd_x[128 : 128 + K], fwd_x[192 : 192 + K] = sx, cx
     inv_x = np.zeros((DEPTH // NEAR, HALVES, NEAR * 16, LANES), ml_dtypes.bfloat16)
     for half in range(HALVES):
         for z in range(DEPTH):
             start = (z * HALVES + half) * RX
-            here, at = slice(start, start + RX), slice(z * RX, (z + 1) * RX)
-            fwd_x[half, :K, at], fwd_x[half, 64 : 64 + K, at] = cx[:, here], -sx[:, here]
-            fwd_x[half, 128 : 128 + K, at] = sx[:, here]
-            fwd_x[half, 192 : 192 + K, at] = cx[:, here]
             x_of = (start + np.array([0, 1, 2, 3, 4, 5, 6, 7, 8, -1])) % NX
             at = slice(z % NEAR * 16, z % NEAR * 16 + 10)
             inv_x[z // NEAR, half, at, :K] = cx[:, x_of].T
@@ -362,9 +360,10 @@
                     value[start : start + 8], at + i * 6, 1
                 )
         rows.append(jnp.concatenate(parts[n], 1))
-    deal = jnp.concatenate(rows, 0).astype(BF16)
+    deal = jnp.concatenate([r for r in rows for _ in range(HALVES)], 0).astype(BF16)
+    size = NEAR * HALVES * 8
     for f in range(DEPTH // NEAR):
-        out[f * NEAR * 8 : (f + 1) * NEAR * 8, :] = deal
+        out[f * size : (f + 1) * size, :] = deal
 
 
 def param_kernel(
@@ -436,15 +435,13 @@
 
 
 def filter_kernel(
-    own, other, coef_a, coef_b, fwd_x, inv_x, phase_x, phase_yz, after, out
+    gathered, coef_a, coef_b, fwd_x, inv_x, phase_x, phase_yz, after, out
 ):
     b, w = own_block()
     half, near = b % HALVES, b // HALVES % NEAR
     lane = iota((1, LANES), 1)
-    mine, theirs = own[...], other[...]
-    both = jnp.dot(fwd_x[half], mine, preferred_element_type=F32) + jnp.dot(
-        fwd_x[1 - half], theirs, preferred_element_type=F32
-    )
+    got = gathered[...]
+    both = jnp.dot(fwd_x[...], got, preferred_element_type=F32)
     full = (both[:LANES, :LANES] + both[LANES:, LANES:]).T
     field = [full[d * SHARE : d * SHARE + PAD] for d in range(3)]
     turned = [pltpu.roll(f, 64, 1) for f in field]
@@ -464,8 +461,7 @@
         preferred_element_type=F32,
     ).reshape(NEAR, 2, 8, 2 * LANES)
 
-    total = mine.astype(F32).reshape(DEPTH, 8, 2 * LANES).sum(0)
-    total = total + theirs.astype(F32).reshape(DEPTH, 8, 2 * LANES).sum(0)
+    total = got.astype(F32).reshape(BULK, 8, 2 * LANES).sum(0)
     total = pltpu.roll(total[:, :LANES] + total[:, LANES:], LANES - 3 * SHARE, 1)
     second = pltpu.roll(total, LANES - 6, 1)
     gap = jnp.zeros((LANES - 16, LANES), F32)
@@ -489,7 +485,7 @@
     out[...] = jnp.concatenate(tiles, 0).astype(BF16)
 
 
-def spread_kernel(shares, inv_y, after_low, after_high, out, rows):
+def spread_kernel(shares, inv_y, out, rows):
     lane = iota((1, LANES), 1)
     got = shares[...].astype(F32).reshape(NEAR, 16, 2 * LANES)
     rows[...] = jnp.zeros((32, 8, LANES), F32)
@@ -767,13 +763,6 @@
     )
 
 
-def dealt_along(block):
-    groups = [[z * HALVES + half for z in range(DEPTH)] for half in range(HALVES)]
-    return lax.all_to_all(
-        block, "bulk", split_axis=0, concat_axis=0, axis_index_groups=groups, tiled=True
-    )
-
-
 def tables_of(name):
     return jnp.asarray(TABLES[name])
 
@@ -814,10 +803,9 @@
     )(source_cells, permittivity, field, seed_magnetic, material)
 
     dealt = call(
-        middle_kernel, shape(DEPTH * 8, 2 * LANES, dtype=BF16), "vvv", (), 20_000_000, 400_000
+        middle_kernel, shape(BULK * 8, 2 * LANES, dtype=BF16), "vvv", (), 20_000_000, 400_000
     )(lines, taken, tables_of("fwd_y"))
-    mine = dealt_along(dealt)
-    theirs = lax.ppermute(mine, "bulk", [(i, i ^ 1) for i in range(BULK)])
+    gathered = lax.all_to_all(dealt, "bulk", split_axis=0, concat_axis=0, tiled=True)
 
     cells = jnp.concatenate([source_cells, source_cells]).reshape(1, LANES)
     coef_a, coef_b, phase_x, phase_yz, injected = call(
@@ -856,9 +844,9 @@
         1_000_000,
     )(field, seed_magnetic, inverse, saved_magnetic, x_low, x_high, coef_a)
     shares = call(
-        filter_kernel, shape(NEAR * 16, 2 * LANES, dtype=BF16), "vvvvvvvva", (), 40_000_000, 600_000
+        filter_kernel, shape(NEAR * 16, 2 * LANES, dtype=BF16), "vvvvvvva", (), 40_000_000, 600_000
     )(
-        mine, theirs, coef_a, coef_b, tables_of("fwd_x"), tables_of("inv_x"), phase_x, phase_yz,
+        gathered, coef_a, coef_b, tables_of("fwd_x"), tables_of("inv_x"), phase_x, phase_yz,
         low_part,
     )
     back = dealt_near(shares)
@@ -869,11 +857,11 @@
     sent = call(
         spread_kernel,
         shape(128, 640, dtype=BF16),
-        "vvaa",
+        "vv",
         [pltpu.VMEM((32, 8, LANES), F32)],
         40_000_000,
         600_000,
-    )(back, tables_of("inv_y"), y_low, y_high)
+    )(back, tables_of("inv_y"))
     returned = lax.all_to_all(sent, "wide", split_axis=0, concat_axis=0, tiled=True)
     early, curled, factor, first_grad, ready = call(
         first_kernel,

time: 80.9 us -> 79.9 us (0.988)
  blocking collectives: 0 us -> 8.57 us
  waiting for transfers between devices: 17.6 us -> 13 us
  starting transfers between devices: 47.1 us -> 43 us
    all_to_all x0 -> x1, blocking collectives: none -> 8.57 us  [dealt_near(): lax.all_to_all(block, 'bulk', split_axis=0, concat_axis=0, axis_index_gro...]
    all_to_all x1, waiting for transfers between devices: 4.69 us -> 0.01 us  [body(): lax.all_to_all(sent, 'wide', split_axis=0, concat_axis=0, tiled=True)]
    ppermute x1 -> x0, starting transfers between devices: 4.48 us -> none  [body(): theirs = lax.ppermute(mine, 'bulk', [(i, i ^ 1) for i in range(BULK)])]
    ppermute x4, waiting for transfers between devices: 3.4 us -> 5.88 us  [passed_along(): return lax.ppermute(block, axis, route)]
    all_to_all x2 -> x1, waiting for transfers between devices: 5.63 us -> 3.28 us  [body(): lax.all_to_all(dealt, 'bulk', split_axis=0, concat_axis=0, tiled=True)]
    all_to_all x1, starting transfers between devices: 5.31 us -> 6.9 us  [body(): lax.all_to_all(sent, 'wide', split_axis=0, concat_axis=0, tiled=True)]
    all_to_all x2 -> x1, starting transfers between devices: 14.8 us -> 14.1 us  [body(): lax.all_to_all(dealt, 'bulk', split_axis=0, concat_axis=0, tiled=True)]
  transfers between devices with their start and end apart: 9 -> 7, of which waited for: 4 -> 4; matrix products, arithmetic and copies ran while one was open for 0% -> 0% of each run, Pallas kernels for 6% -> 6%
where the time goes in v7:
time: 79.9 us; the launch traced here: 79.3 us
  starting transfers between devices  43 us (54%)
  waiting for transfers between devices  13 us (16%)
  Pallas kernels  12.1 us (15%)
  blocking collectives  8.57 us (11%)
  local copies, waits for them, and re-layouts  1.59 us (2%)
  between operations  0.95 us (1%)
    all_to_all x1, starting transfers between devices, body(): lax.all_to_all(dealt, 'bulk', split_axis=0, concat_axis=0, tiled=True)  14.1 us
    ppermute x4, starting transfers between devices, passed_along(): return lax.ppermute(block, axis, route)  11.7 us
    all_to_all x1, starting transfers between devices, body(): lax.all_to_all(payload, 'wide', split_axis=0, concat_axis=0, tiled=True)  10.4 us
    all_to_all x1, blocking collectives, dealt_near(): lax.all_to_all(block, 'bulk', split_axis=0, concat_axis=0, axis_index_gro...  8.57 us
    all_to_all x1, starting transfers between devices, body(): lax.all_to_all(sent, 'wide', split_axis=0, concat_axis=0, tiled=True)  6.9 us
    ppermute x4, waiting for transfers between devices, passed_along(): return lax.ppermute(block, axis, route)  5.88 us
    all_to_all x1, waiting for transfers between devices, body(): lax.all_to_all(payload, 'wide', split_axis=0, concat_axis=0, tiled=True)  3.83 us
    all_to_all x1, waiting for transfers between devices, body(): lax.all_to_all(dealt, 'bulk', split_axis=0, concat_axis=0, tiled=True)  3.28 us
  transfers between devices with their start and end apart: 7, of which 4 were waited for; matrix products, arithmetic and copies ran while one was open for 0% of the time, Pallas kernels for 6%

profile of v7, /device:TPU:1, one launch (start us, length us, event | category | flops | bytes accessed | tf_op | source)
XLA Modules:
  0.0 79.3 jit_solution(9017311932602267808)
XLA Ops:
  0.6 2.3 %shard_map.246 = (bf16[384,128]{1,0:T(8,128)(2,1)}, f32[3,8,16,128]{3,2,1,0:T(8,128)}) custom-call(s32[64]{0:T(128)} %mon.3, f32[3,2,64]{2,1,0:T(2,128)} %bitcast.20, f32[3,8,16,128]{3,2,1,0:T(8,128)} %electric.1, bf16[128,128]{1,0:T(8,128)(2,1)} %constant.20.clone.table_in), custom_call_target="tpu_custom_call" | custom-call | flops 13000000 | bytes 500000 | tf_op jit(solution)/shard_map/pallas_call | solution.py:778
  3.0 10.4 %all-to-all-start = ((bf16[16,24,128]{2,1,0:T(8,128)(2,1)}), bf16[16,24,128]{2,1,0:T(8,128)(2,1)S(1)}, u32[]{:S(2)}, u32[]{:S(2)}) async-start(bf16[16,24,128]{2,1,0:T(8,128)(2,1)} %bitcast.24), calls=%async_computation | async-start | bytes 196608 | tf_op jit(solution)/shard_map/all_to_all | solution.py:790
  13.4 0.9 %copy-done.11 = s32[8,16,128]{2,1,0:T(8,128)S(1)} copy-done((s32[8,16,128]{2,1,0:T(8,128)S(1)}, s32[8,16,128]{2,1,0:T(8,128)}, u32[]{:S(2)}) %copy-start.11) | copy-done | bytes 65560
  14.3 1.1 %shard_map.247 = (f32[8,128]{1,0:T(8,128)S(1)}, f32[8,16,128]{2,1,0:T(8,128)S(1)}) custom-call(s32[64]{0:T(128)S(1)} %copy-done.21, f32[8]{0:T(128)S(1)} %copy-done.20, f32[3,8,16,128]{3,2,1,0:T(8,128)S(1)} %copy-done.1, f32[3,8,16,128]{3,2,1,0:T(8,128)S(1)} %copy-done, s32[8,16,128]{2,1,0:T(8,128)S(1)} %copy-done.11), custom_call_target="tpu_custom_call" | custom-call | flops 3000000 | bytes 1500000 | tf_op jit(solution)/shard_map/pallas_call | solution.py:792
  15.4 3.8 %all-to-all-done = bf16[16,24,128]{2,1,0:T(8,128)(2,1)S(1)} async-done(((bf16[16,24,128]{2,1,0:T(8,128)(2,1)}), bf16[16,24,128]{2,1,0:T(8,128)(2,1)S(1)}, u32[]{:S(2)}, u32[]{:S(2)}) %all-to-all-start) | async-done | bytes 98336 | tf_op jit(solution)/shard_map/all_to_all | solution.py:790
  19.3 1.3 %shard_map.248.after = bf16[256,256]{1,0:T(8,128)(2,1)} custom-call(bf16[384,128]{1,0:T(8,128)(2,1)S(1)} %bitcast.16, f32[8,128]{1,0:T(8,128)S(1)} %get-tuple-element.28.taken, bf16[512,256]{1,0:T(8,128)(2,1)S(1)} %copy-done.3), custom_call_target="tpu_custom_call" | custom-call | flops 20000000 | bytes 400000 | tf_op jit(solution)/shard_map/pallas_call | solution.py:805
  20.6 14.1 %all-to-all-start.1 = ((bf16[32,8,256]{2,1,0:T(8,128)(2,1)}), bf16[32,8,256]{2,1,0:T(8,128)(2,1)S(1)}, u32[]{:S(2)}, u32[]{:S(2)}) async-start(bf16[32,8,256]{2,1,0:T(8,128)(2,1)} %bitcast.3), calls=%async_computation.1 | async-start | bytes 262144 | tf_op jit(solution)/shard_map/all_to_all | solution.py:808
  34.8 4.8 %collective-permute-start = (bf16[17,16,128]{2,1,0:T(8,128)(2,1)S(1)}, bf16[17,16,128]{2,1,0:T(8,128)(2,1)S(1)}, u32[]{:S(2)}, u32[]{:S(2)}) collective-permute-start(bf16[17,16,128]{2,1,0:T(8,128)(2,1)S(1)} %get-tuple-element.34), channel_id=1, source_target_pairs={{0,16},{16,32},{32,48},{48,64},{64,80},{80,96},{96,112},{112,128},... | collective-permute-start | bytes 208904 | tf_op jit(solution)/shard_map/ppermute | solution.py:752
  39.6 1.3 %collective-permute-start.1 = (bf16[10,16,128]{2,1,0:T(8,128)(2,1)S(1)}, bf16[10,16,128]{2,1,0:T(8,128)(2,1)S(1)}, u32[]{:S(2)}, u32[]{:S(2)}) collective-permute-start(bf16[10,16,128]{2,1,0:T(8,128)(2,1)S(1)} %get-tuple-element.35), channel_id=1, source_target_pairs={{16,0},{32,16},{48,32},{64,48},{80,64},{96,80},{112,96},{128,112},... | collective-permute-start | bytes 122888 | tf_op jit(solution)/shard_map/ppermute | solution.py:752
  40.9 0.1 add_bitcast_fusion.cells
  41.1 0.6 copy-done.18
  41.7 2.1 %shard_map.249 = (f32[360,128]{1,0:T(8,128)S(1)}, f32[360,128]{1,0:T(8,128)S(1)}, bf16[128,128]{1,0:T(8,128)(2,1)S(1)}, f32[40,128]{1,0:T(8,128)S(1)}, f32[8,128]{1,0:T(8,128)S(1)}) custom-call(s32[64]{0:T(128)S(1)} %copy-done.17, f32[3,2,64]{2,1,0:T(2,128)S(1)} %bitcast.21, f32[3,16]{1,0:T(4,128)S(1)} %bitcast.23, s32[1,128]{1,0:T(1,128)S(1)} %add_bitcast_fusion.cells, ...), custom_call_target="tpu_custom_call" | custom-call | flops 20000000 | bytes 1000000 | tf_op jit(solution)/shard_map/pallas_call | solution.py:811
  43.8 2.5 %collective-permute-done.1.x_high = bf16[10,16,128]{2,1,0:T(8,128)(2,1)S(1)} collective-permute-done((bf16[10,16,128]{2,1,0:T(8,128)(2,1)S(1)}, bf16[10,16,128]{2,1,0:T(8,128)(2,1)S(1)}, u32[]{:S(2)}, u32[]{:S(2)}) %collective-permute-start.1) | collective-permute-done | bytes 40992 | tf_op jit(solution)/shard_map/ppermute | solution.py:752
  46.3 0.1 shard_map.251
  46.4 3.3 %all-to-all-done.1 = bf16[32,8,256]{2,1,0:T(8,128)(2,1)S(1)} async-done(((bf16[32,8,256]{2,1,0:T(8,128)(2,1)}), bf16[32,8,256]{2,1,0:T(8,128)(2,1)S(1)}, u32[]{:S(2)}, u32[]{:S(2)}) %all-to-all-start.1) | async-done | bytes 131104 | tf_op jit(solution)/shard_map/all_to_all | solution.py:808
  49.7 0.7 shard_map.252
  50.4 8.6 %all_to_all.44 = bf16[4,16,256]{2,1,0:T(8,128)(2,1)S(1)} all-to-all(bf16[4,16,256]{2,1,0:T(8,128)(2,1)S(1)} %bitcast.17), channel_id=1, replica_groups={{0,32,64,96},{16,48,80,112},{128,160,192,224},{144,176,208,240},{256,28..., dimensions={0} | all-to-all | bytes 65536 | tf_op jit(solution)/shard_map/all_to_all | solution.py:761
  59.0 1.5 %shard_map.253.after = bf16[128,640]{1,0:T(8,128)(2,1)} custom-call(bf16[64,256]{1,0:T(8,128)(2,1)S(1)} %bitcast.18, bf16[128,384]{1,0:T(8,128)(2,1)S(1)} %copy-done.10), custom_call_target="tpu_custom_call" | custom-call | flops 40000000 | bytes 600000 | tf_op jit(solution)/shard_map/pallas_call | solution.py:857
  60.5 6.9 %all-to-all-start.3 = ((bf16[16,8,640]{2,1,0:T(8,128)(2,1)}), bf16[16,8,640]{2,1,0:T(8,128)(2,1)S(1)}, u32[]{:S(2)}, u32[]{:S(2)}) async-start(bf16[16,8,640]{2,1,0:T(8,128)(2,1)} %bitcast.10), calls=%async_computation.3 | async-start | bytes 327680 | tf_op jit(solution)/shard_map/all_to_all | solution.py:865
  67.4 3.5 %collective-permute-start.2 = (bf16[17,16,128]{2,1,0:T(8,128)(2,1)S(1)}, bf16[17,16,128]{2,1,0:T(8,128)(2,1)S(1)}, u32[]{:S(2)}, u32[]{:S(2)}) collective-permute-start(bf16[17,16,128]{2,1,0:T(8,128)(2,1)S(1)} %get-tuple-element.36.after), channel_id=1, source_target_pairs={{0,1},{1,2},{2,3},{3,4},{4,5},{5,6},{6,7},{7,8},{8,9},{9,10},{10,1... | collective-permute-start | bytes 208904 | tf_op jit(solution)/shard_map/ppermute | solution.py:752
  70.9 2.1 %collective-permute-start.3 = (bf16[10,16,128]{2,1,0:T(8,128)(2,1)S(1)}, bf16[10,16,128]{2,1,0:T(8,128)(2,1)S(1)}, u32[]{:S(2)}, u32[]{:S(2)}) collective-permute-start(bf16[10,16,128]{2,1,0:T(8,128)(2,1)S(1)} %get-tuple-element.37), channel_id=1, source_target_pairs={{1,0},{2,1},{3,2},{4,3},{5,4},{6,5},{7,6},{8,7},{9,8},{10,9},{11,1... | collective-permute-start | bytes 122888 | tf_op jit(solution)/shard_map/ppermute | solution.py:752
  73.0 3.4 %collective-permute-done.3.y_high = bf16[10,16,128]{2,1,0:T(8,128)(2,1)S(1)} collective-permute-done((bf16[10,16,128]{2,1,0:T(8,128)(2,1)S(1)}, bf16[10,16,128]{2,1,0:T(8,128)(2,1)S(1)}, u32[]{:S(2)}, u32[]{:S(2)}) %collective-permute-start.3) | collective-permute-done | bytes 40992 | tf_op jit(solution)/shard_map/ppermute | solution.py:752
  76.4 1.7 %shard_map.254 = (f32[3,10,24,128]{3,2,1,0:T(8,128)S(1)}, f32[3,10,24,128]{3,2,1,0:T(8,128)S(1)}, f32[10,24,128]{2,1,0:T(8,128)S(1)}, f32[8,16,128]{2,1,0:T(8,128)S(1)}, f32[3,8,16,128]{3,2,1,0:T(8,128)S(1)}) custom-call(s32[64]{0:T(128)S(1)} %copy-done.17, f32[3,2,64]{2,1,0:T(2,128)S(1)} %bitcast.22, f32[3,8,16,128]{3,2,1,0:T(8,128)S(1)} %copy-done.1, ...), custom_call_target="tpu_custom_call" | custom-call | flops 10000000 | bytes 3000000 | tf_op jit(solution)/shard_map/pallas_call | solution.py:866
  78.1 1.2 %shard_map.255 = (f32[3,8,16,128]{3,2,1,0:T(8,128)}, f32[3,8,16,128]{3,2,1,0:T(8,128)}, f32[8,16,128]{2,1,0:T(8,128)}, f32[3,2,64]{2,1,0:T(2,128)}) custom-call(bf16[128,640]{1,0:T(8,128)(2,1)S(1)} %bitcast.14, bf16[128,128]{1,0:T(8,128)(2,1)S(1)} %copy-done.13, bf16[128,256]{1,0:T(8,128)(2,1)S(1)} %copy-done.12, ...), custom_call_target="tpu_custom_call" | custom-call | flops 40000000 | bytes 4000000 | tf_op jit(solution)/shard_map/pallas_call | solution.py:881
  (46 shorter events, 0.1 us)
Async XLA Ops:
  0.6 12.7 %copy-start = (f32[3,8,16,128]{3,2,1,0:T(8,128)S(1)}, f32[3,8,16,128]{3,2,1,0:T(8,128)}, u32[]{:S(2)}) copy-start(f32[3,8,16,128]{3,2,1,0:T(8,128)} %magnetic.5) | copy-start | bytes 589828
  3.0 10.4 %copy-start.1 = (f32[3,8,16,128]{3,2,1,0:T(8,128)S(1)}, f32[3,8,16,128]{3,2,1,0:T(8,128)}, u32[]{:S(2)}) copy-start(f32[3,8,16,128]{3,2,1,0:T(8,128)} %get-tuple-element.27.field.electric) | copy-start | bytes 589828
  3.0 10.4 %copy-start.20 = (f32[8]{0:T(128)S(1)}, f32[8]{0:T(128)}, u32[]{:S(2)}) copy-start(f32[8]{0:T(128)} %perm_in.1) | copy-start | bytes 100
  3.0 10.4 %copy-start.21 = (s32[64]{0:T(128)S(1)}, s32[64]{0:T(128)}, u32[]{:S(2)}) copy-start(s32[64]{0:T(128)} %src_in.1) | copy-start | bytes 772
  3.0 16.3 %all-to-all-start = ((bf16[16,24,128]{2,1,0:T(8,128)(2,1)}), bf16[16,24,128]{2,1,0:T(8,128)(2,1)S(1)}, u32[]{:S(2)}, u32[]{:S(2)}) async-start(bf16[16,24,128]{2,1,0:T(8,128)(2,1)} %bitcast.24), calls=%async_computation | async-start | bytes 196608 | tf_op jit(solution)/shard_map/all_to_all | solution.py:790
  13.4 5.9 %copy-start.3 = (bf16[512,256]{1,0:T(8,128)(2,1)S(1)}, bf16[512,256]{1,0:T(8,128)(2,1)}, u32[]{:S(2)}) copy-start(bf16[512,256]{1,0:T(8,128)(2,1)} %constant.21.clone.table) | copy-start | bytes 786436
  20.6 14.2 %copy-start.2 = (bf16[2,3,8,16,128]{4,3,2,1,0:T(8,128)(2,1)S(1)}, bf16[2,3,8,16,128]{4,3,2,1,0:T(8,128)(2,1)}, u32[]{:S(2)}) copy-start(bf16[2,3,8,16,128]{4,3,2,1,0:T(8,128)(2,1)} %saved.5) | copy-start | bytes 589828
  20.6 29.1 %all-to-all-start.1 = ((bf16[32,8,256]{2,1,0:T(8,128)(2,1)}), bf16[32,8,256]{2,1,0:T(8,128)(2,1)S(1)}, u32[]{:S(2)}, u32[]{:S(2)}) async-start(bf16[32,8,256]{2,1,0:T(8,128)(2,1)} %bitcast.3), calls=%async_computation.1 | async-start | bytes 262144 | tf_op jit(solution)/shard_map/all_to_all | solution.py:808
  34.7 6.3 %copy-start.4 = (bf16[4,2,48,256]{3,2,1,0:T(8,128)(2,1)S(1)}, bf16[4,2,48,256]{3,2,1,0:T(8,128)(2,1)}, u32[]{:S(2)}) copy-start(bf16[4,2,48,256]{3,2,1,0:T(8,128)(2,1)} %constant.23.clone.at_y) | copy-start | bytes 589828
  34.7 6.3 %copy-start.7 = (bf16[2,48,16,16]{1,3,2,0:T(8,128)(2,1)S(1)}, bf16[2,48,16,16]{1,3,2,0:T(8,128)(2,1)}, u32[]{:S(2)}) copy-start(bf16[2,48,16,16]{1,3,2,0:T(8,128)(2,1)} %param.33) | copy-start | bytes 147460
  34.7 6.3 %copy-start.8 = (bf16[2,128,256]{2,1,0:T(8,128)(2,1)S(1)}, bf16[2,128,256]{2,1,0:T(8,128)(2,1)}, u32[]{:S(2)}) copy-start(bf16[2,128,256]{2,1,0:T(8,128)(2,1)} %constant.22.clone.at_x) | copy-start | bytes 393220
  34.8 6.3 %copy-start.9 = (bf16[16,2,16,128]{3,2,1,0:T(8,128)(2,1)S(1)}, bf16[16,2,16,128]{3,2,1,0:T(8,128)(2,1)}, u32[]{:S(2)}) copy-start(bf16[16,2,16,128]{3,2,1,0:T(8,128)(2,1)} %constant.24.clone.at_z) | copy-start | bytes 393220
  34.8 6.3 %copy-start.15 = (f32[16,48]{1,0:T(8,128)S(1)}, f32[16,48]{1,0:T(8,128)}, u32[]{:S(2)}) copy-start(f32[16,48]{1,0:T(8,128)} %gain_x.1) | copy-start | bytes 9220
  34.8 6.3 %copy-start.16 = (f32[16,48]{1,0:T(8,128)S(1)}, f32[16,48]{1,0:T(8,128)}, u32[]{:S(2)}) copy-start(f32[16,48]{1,0:T(8,128)} %gain_y.1) | copy-start | bytes 9220
  34.8 6.3 %copy-start.19 = (f32[3,16]{1,0:T(4,128)S(1)}, f32[3,16]{1,0:T(4,128)}, u32[]{:S(2)}) copy-start(f32[3,16]{1,0:T(4,128)} %project.1) | copy-start | bytes 580
  34.8 11.4 %collective-permute-start = (bf16[17,16,128]{2,1,0:T(8,128)(2,1)S(1)}, bf16[17,16,128]{2,1,0:T(8,128)(2,1)S(1)}, u32[]{:S(2)}, u32[]{:S(2)}) collective-permute-start(bf16[17,16,128]{2,1,0:T(8,128)(2,1)S(1)} %get-tuple-element.34), channel_id=1, source_target_pairs={{0,16},{16,32},{32,48},{48,64},{64,80},{80,96},{96,112},{112,128},... | collective-permute-start | bytes 208904 | tf_op jit(solution)/shard_map/ppermute | solution.py:752
  39.6 6.6 %collective-permute-start.1 = (bf16[10,16,128]{2,1,0:T(8,128)(2,1)S(1)}, bf16[10,16,128]{2,1,0:T(8,128)(2,1)S(1)}, u32[]{:S(2)}, u32[]{:S(2)}) collective-permute-start(bf16[10,16,128]{2,1,0:T(8,128)(2,1)S(1)} %get-tuple-element.35), channel_id=1, source_target_pairs={{16,0},{32,16},{48,32},{64,48},{80,64},{96,80},{112,96},{128,112},... | collective-permute-start | bytes 122888 | tf_op jit(solution)/shard_map/ppermute | solution.py:752
  46.3 3.4 %copy-start.5 = (bf16[256,256]{1,0:T(8,128)(2,1)S(1)}, bf16[256,256]{1,0:T(8,128)(2,1)}, u32[]{:S(2)}) copy-start(bf16[256,256]{1,0:T(8,128)(2,1)} %constant.25.clone.fwd_x) | copy-start | bytes 393220
  46.3 3.4 %copy-start.6 = (bf16[4,2,64,128]{3,2,1,0:T(8,128)(2,1)S(1)}, bf16[4,2,64,128]{3,2,1,0:T(8,128)(2,1)}, u32[]{:S(2)}) copy-start(bf16[4,2,64,128]{3,2,1,0:T(8,128)(2,1)} %constant.26.clone.inv_x) | copy-start | bytes 393220
  49.7 9.3 %copy-start.10 = (bf16[128,384]{1,0:T(8,128)(2,1)S(1)}, bf16[128,384]{1,0:T(8,128)(2,1)}, u32[]{:S(2)}) copy-start(bf16[128,384]{1,0:T(8,128)(2,1)} %constant.27.clone.inv_y) | copy-start | bytes 294916
  60.5 17.6 %all-to-all-start.3 = ((bf16[16,8,640]{2,1,0:T(8,128)(2,1)}), bf16[16,8,640]{2,1,0:T(8,128)(2,1)S(1)}, u32[]{:S(2)}, u32[]{:S(2)}) async-start(bf16[16,8,640]{2,1,0:T(8,128)(2,1)} %bitcast.10), calls=%async_computation.3 | async-start | bytes 327680 | tf_op jit(solution)/shard_map/all_to_all | solution.py:865
  67.4 9.0 %collective-permute-start.2 = (bf16[17,16,128]{2,1,0:T(8,128)(2,1)S(1)}, bf16[17,16,128]{2,1,0:T(8,128)(2,1)S(1)}, u32[]{:S(2)}, u32[]{:S(2)}) collective-permute-start(bf16[17,16,128]{2,1,0:T(8,128)(2,1)S(1)} %get-tuple-element.36.after), channel_id=1, source_target_pairs={{0,1},{1,2},{2,3},{3,4},{4,5},{5,6},{6,7},{7,8},{8,9},{9,10},{10,1... | collective-permute-start | bytes 208904 | tf_op jit(solution)/shard_map/ppermute | solution.py:752
  70.9 7.2 %copy-start.12 = (bf16[128,256]{1,0:T(8,128)(2,1)S(1)}, bf16[128,256]{1,0:T(8,128)(2,1)}, u32[]{:S(2)}) copy-start(bf16[128,256]{1,0:T(8,128)(2,1)} %constant.29.clone.apart) | copy-start | bytes 196612
  70.9 5.5 %collective-permute-start.3 = (bf16[10,16,128]{2,1,0:T(8,128)(2,1)S(1)}, bf16[10,16,128]{2,1,0:T(8,128)(2,1)S(1)}, u32[]{:S(2)}, u32[]{:S(2)}) collective-permute-start(bf16[10,16,128]{2,1,0:T(8,128)(2,1)S(1)} %get-tuple-element.37), channel_id=1, source_target_pairs={{1,0},{2,1},{3,2},{4,3},{5,4},{6,5},{7,6},{8,7},{9,8},{10,9},{11,1... | collective-permute-start | bytes 122888 | tf_op jit(solution)/shard_map/ppermute | solution.py:752
  (5 other events, 5.4 us)

commit v8 on v7

--- a/solution.py
+++ b/solution.py
@@ -407,23 +407,29 @@
     ]
     blank = jnp.zeros((16, 16), F32)
     along = gain_x[...]
+    totals = []
+    for part in range(2):
+        rows = [mix[part, c].astype(F32) for c in range(16)]
+        for d in range(3):
+            total = lift[d, 0] * rows[0]
+            for c in range(1, 16):
+                total = total + lift[d, c] * rows[c]
+            totals.append(total)
+    joined = jnp.dot(
+        jnp.concatenate(totals, 0), hot_k, precision=HIGHEST, preferred_element_type=F32
+    )
+    joined = [joined[i * 16 : (i + 1) * 16] * gains for i in range(6)]
     for part, to in ((0, coef_a), (1, coef_b)):
-        joined = []
-        for d in range(3):
-            total = jnp.zeros((16, K), F32)
-            for c in range(16):
-                total = total + lift[d, c] * mix[part, c].astype(F32)
-            joined.append(
-                gains * jnp.dot(total, hot_k, precision=HIGHEST, preferred_element_type=F32)
-            )
         sign = 1.0 if part == 0 else -1.0
         right = jnp.concatenate([sign * along, blank, along, blank], 1)
+        right = jnp.concatenate([columns[e] * right for e in range(3)], 1)
+        left = jnp.concatenate([j.T for j in joined[part * 3 : part * 3 + 3]], 0)
+        found = jnp.dot(left, right, precision=HIGHEST, preferred_element_type=F32)
         for e in range(3):
             for d in range(3):
-                left = (columns[e] * joined[d]).T
-                to[(e * 3 + d) * PAD : (e * 3 + d + 1) * PAD, :] = jnp.dot(
-                    left, right, precision=HIGHEST, preferred_element_type=F32
-                )
+                to[(e * 3 + d) * PAD : (e * 3 + d + 1) * PAD, :] = found[
+                    d * PAD : (d + 1) * PAD, e * LANES : (e + 1) * LANES
+                ]
     row = iota((8, LANES), 0)
     total = jnp.zeros((8, LANES), F32)
     for i in range(64):
@@ -485,7 +491,7 @@
     out[...] = jnp.concatenate(tiles, 0).astype(BF16)
 
 
-def spread_kernel(shares, inv_y, out, rows):
+def spread_kernel(shares, inv_y, after, out, rows):
     lane = iota((1, LANES), 1)
     got = shares[...].astype(F32).reshape(NEAR, 16, 2 * LANES)
     rows[...] = jnp.zeros((32, 8, LANES), F32)
@@ -857,11 +863,11 @@
     sent = call(
         spread_kernel,
         shape(128, 640, dtype=BF16),
-        "vv",
+        "vva",
         [pltpu.VMEM((32, 8, LANES), F32)],
         40_000_000,
         600_000,
-    )(back, tables_of("inv_y"))
+    )(back, tables_of("inv_y"), y_low)
     returned = lax.all_to_all(sent, "wide", split_axis=0, concat_axis=0, tiled=True)
     early, curled, factor, first_grad, ready = call(
         first_kernel,

time: 79.9 us -> 78.2 us (0.979)
  blocking collectives: 8.57 us -> 0 us
  starting transfers between devices: 43 us -> 47.8 us
  waiting for transfers between devices: 13 us -> 14.9 us
    all_to_all x1 -> x0, blocking collectives: 8.57 us -> none  [dealt_near(): lax.all_to_all(block, 'bulk', split_axis=0, concat_axis=0, axis_index_gro...]
    all_to_all x0 -> x1, starting transfers between devices: none -> 4.27 us  [dealt_near(): lax.all_to_all(block, 'bulk', split_axis=0, concat_axis=0, axis_index_gro...]
    ppermute x4, waiting for transfers between devices: 5.88 us -> 7.75 us  [passed_along(): return lax.ppermute(block, axis, route)]
    ppermute x4, starting transfers between devices: 11.7 us -> 12.8 us  [passed_along(): return lax.ppermute(block, axis, route)]
  transfers between devices with their start and end apart: 7 -> 8, of which waited for: 4 -> 5; matrix products, arithmetic and copies ran while one was open for 0% -> 0% of each run, Pallas kernels for 6% -> 6%
where the time goes in v8:
time: 78.2 us; the launch traced here: 77.5 us
  starting transfers between devices  47.8 us (61%)
  waiting for transfers between devices  14.9 us (19%)
  Pallas kernels  12.3 us (16%)
  local copies, waits for them, and re-layouts  1.58 us (2%)
  between operations  0.95 us (1%)
    all_to_all x1, starting transfers between devices, body(): lax.all_to_all(dealt, 'bulk', split_axis=0, concat_axis=0, tiled=True)  14.1 us
    ppermute x4, starting transfers between devices, passed_along(): return lax.ppermute(block, axis, route)  12.8 us
    all_to_all x1, starting transfers between devices, body(): lax.all_to_all(payload, 'wide', split_axis=0, concat_axis=0, tiled=True)  10.4 us
    ppermute x4, waiting for transfers between devices, passed_along(): return lax.ppermute(block, axis, route)  7.75 us
    all_to_all x1, starting transfers between devices, body(): lax.all_to_all(sent, 'wide', split_axis=0, concat_axis=0, tiled=True)  6.26 us
    all_to_all x1, starting transfers between devices, dealt_near(): lax.all_to_all(block, 'bulk', split_axis=0, concat_axis=0, axis_index_gro...  4.27 us
    all_to_all x1, waiting for transfers between devices, body(): lax.all_to_all(payload, 'wide', split_axis=0, concat_axis=0, tiled=True)  3.83 us
    all_to_all x1, waiting for transfers between devices, body(): lax.all_to_all(dealt, 'bulk', split_axis=0, concat_axis=0, tiled=True)  3.28 us
  transfers between devices with their start and end apart: 8, of which 5 were waited for; matrix products, arithmetic and copies ran while one was open for 0% of the time, Pallas kernels for 6%

profile of v8, /device:TPU:1, one launch (start us, length us, event | category | flops | bytes accessed | tf_op | source)
XLA Modules:
  0.0 77.5 jit_solution(3095483832171827150)
XLA Ops:
  0.6 2.3 %shard_map.246 = (bf16[384,128]{1,0:T(8,128)(2,1)}, f32[3,8,16,128]{3,2,1,0:T(8,128)}) custom-call(s32[64]{0:T(128)} %mon.3, f32[3,2,64]{2,1,0:T(2,128)} %bitcast.19, f32[3,8,16,128]{3,2,1,0:T(8,128)} %electric.1, bf16[128,128]{1,0:T(8,128)(2,1)} %constant.20.clone.table_in), custom_call_target="tpu_custom_call" | custom-call | flops 13000000 | bytes 500000 | tf_op jit(solution)/shard_map/pallas_call | solution.py:784
  3.0 10.4 %all-to-all-start = ((bf16[16,24,128]{2,1,0:T(8,128)(2,1)}), bf16[16,24,128]{2,1,0:T(8,128)(2,1)S(1)}, u32[]{:S(2)}, u32[]{:S(2)}) async-start(bf16[16,24,128]{2,1,0:T(8,128)(2,1)} %bitcast.23), calls=%async_computation | async-start | bytes 196608 | tf_op jit(solution)/shard_map/all_to_all | solution.py:796
  13.4 0.9 %copy-done.11 = s32[8,16,128]{2,1,0:T(8,128)S(1)} copy-done((s32[8,16,128]{2,1,0:T(8,128)S(1)}, s32[8,16,128]{2,1,0:T(8,128)}, u32[]{:S(2)}) %copy-start.11) | copy-done | bytes 65560
  14.3 1.1 %shard_map.247 = (f32[8,128]{1,0:T(8,128)S(1)}, f32[8,16,128]{2,1,0:T(8,128)S(1)}) custom-call(s32[64]{0:T(128)S(1)} %copy-done.21, f32[8]{0:T(128)S(1)} %copy-done.20, f32[3,8,16,128]{3,2,1,0:T(8,128)S(1)} %copy-done.1, f32[3,8,16,128]{3,2,1,0:T(8,128)S(1)} %copy-done, s32[8,16,128]{2,1,0:T(8,128)S(1)} %copy-done.11), custom_call_target="tpu_custom_call" | custom-call | flops 3000000 | bytes 1500000 | tf_op jit(solution)/shard_map/pallas_call | solution.py:798
  15.4 3.8 %all-to-all-done = bf16[16,24,128]{2,1,0:T(8,128)(2,1)S(1)} async-done(((bf16[16,24,128]{2,1,0:T(8,128)(2,1)}), bf16[16,24,128]{2,1,0:T(8,128)(2,1)S(1)}, u32[]{:S(2)}, u32[]{:S(2)}) %all-to-all-start) | async-done | bytes 98336 | tf_op jit(solution)/shard_map/all_to_all | solution.py:796
  19.3 1.3 %shard_map.248.after = bf16[256,256]{1,0:T(8,128)(2,1)} custom-call(bf16[384,128]{1,0:T(8,128)(2,1)S(1)} %bitcast.16, f32[8,128]{1,0:T(8,128)S(1)} %get-tuple-element.28.taken, bf16[512,256]{1,0:T(8,128)(2,1)S(1)} %copy-done.3), custom_call_target="tpu_custom_call" | custom-call | flops 20000000 | bytes 400000 | tf_op jit(solution)/shard_map/pallas_call | solution.py:811
  20.6 14.1 %all-to-all-start.1 = ((bf16[32,8,256]{2,1,0:T(8,128)(2,1)}), bf16[32,8,256]{2,1,0:T(8,128)(2,1)S(1)}, u32[]{:S(2)}, u32[]{:S(2)}) async-start(bf16[32,8,256]{2,1,0:T(8,128)(2,1)} %bitcast.3), calls=%async_computation.1 | async-start | bytes 262144 | tf_op jit(solution)/shard_map/all_to_all | solution.py:814
  34.8 4.8 %collective-permute-start = (bf16[17,16,128]{2,1,0:T(8,128)(2,1)S(1)}, bf16[17,16,128]{2,1,0:T(8,128)(2,1)S(1)}, u32[]{:S(2)}, u32[]{:S(2)}) collective-permute-start(bf16[17,16,128]{2,1,0:T(8,128)(2,1)S(1)} %get-tuple-element.34), channel_id=1, source_target_pairs={{0,16},{16,32},{32,48},{48,64},{64,80},{80,96},{96,112},{112,128},... | collective-permute-start | bytes 208904 | tf_op jit(solution)/shard_map/ppermute | solution.py:758
  39.6 1.3 %collective-permute-start.1 = (bf16[10,16,128]{2,1,0:T(8,128)(2,1)S(1)}, bf16[10,16,128]{2,1,0:T(8,128)(2,1)S(1)}, u32[]{:S(2)}, u32[]{:S(2)}) collective-permute-start(bf16[10,16,128]{2,1,0:T(8,128)(2,1)S(1)} %get-tuple-element.35), channel_id=1, source_target_pairs={{16,0},{32,16},{48,32},{64,48},{80,64},{96,80},{112,96},{128,112},... | collective-permute-start | bytes 122888 | tf_op jit(solution)/shard_map/ppermute | solution.py:758
  41.1 0.6 copy-done.18
  41.7 1.6 %shard_map.249 = (f32[360,128]{1,0:T(8,128)S(1)}, f32[360,128]{1,0:T(8,128)S(1)}, bf16[128,128]{1,0:T(8,128)(2,1)S(1)}, f32[40,128]{1,0:T(8,128)S(1)}, f32[8,128]{1,0:T(8,128)S(1)}) custom-call(s32[64]{0:T(128)S(1)} %copy-done.17, f32[3,2,64]{2,1,0:T(2,128)S(1)} %bitcast.20, f32[3,16]{1,0:T(4,128)S(1)} %bitcast.22, s32[1,128]{1,0:T(1,128)S(1)} %add_bitcast_fusion.cells, ...), custom_call_target="tpu_custom_call" | custom-call | flops 20000000 | bytes 1000000 | tf_op jit(solution)/shard_map/pallas_call | solution.py:817
  43.3 2.9 %collective-permute-done.1.x_high = bf16[10,16,128]{2,1,0:T(8,128)(2,1)S(1)} collective-permute-done((bf16[10,16,128]{2,1,0:T(8,128)(2,1)S(1)}, bf16[10,16,128]{2,1,0:T(8,128)(2,1)S(1)}, u32[]{:S(2)}, u32[]{:S(2)}) %collective-permute-start.1) | collective-permute-done | bytes 40992 | tf_op jit(solution)/shard_map/ppermute | solution.py:758
  46.3 0.1 shard_map.251
  46.4 3.3 %all-to-all-done.1 = bf16[32,8,256]{2,1,0:T(8,128)(2,1)S(1)} async-done(((bf16[32,8,256]{2,1,0:T(8,128)(2,1)}), bf16[32,8,256]{2,1,0:T(8,128)(2,1)S(1)}, u32[]{:S(2)}, u32[]{:S(2)}) %all-to-all-start.1) | async-done | bytes 131104 | tf_op jit(solution)/shard_map/all_to_all | solution.py:814
  49.7 1.4 %shard_map.252 = bf16[64,256]{1,0:T(8,128)(2,1)} custom-call(bf16[256,256]{1,0:T(8,128)(2,1)S(1)} %bitcast.15, f32[360,128]{1,0:T(8,128)S(1)} %get-tuple-element.29.after.coef_a, f32[360,128]{1,0:T(8,128)S(1)} %get-tuple-element.30.coef_b, bf16[256,256]{1,0:T(8,128)(2,1)S(1)} %copy-done.5, bf16[4,2,64,128]{3,2,1,0:T(8,128)(2,1)S(1)} %copy-done.6, ...), custom_call_target="tpu_custom_call" | custom-call | flops 40000000 | bytes 600000 | tf_op jit(solution)/shard_map/pallas_call | solution.py:852
  51.0 4.3 %all-to-all-start.2 = ((bf16[4,16,256]{2,1,0:T(8,128)(2,1)}), bf16[4,16,256]{2,1,0:T(8,128)(2,1)S(1)}, u32[]{:S(2)}, u32[]{:S(2)}) async-start(bf16[4,16,256]{2,1,0:T(8,128)(2,1)} %bitcast.8), calls=%async_computation.2 | async-start | bytes 65536 | tf_op jit(solution)/shard_map/all_to_all | solution.py:767
  55.3 4.5 %collective-permute-start.2 = (bf16[17,16,128]{2,1,0:T(8,128)(2,1)S(1)}, bf16[17,16,128]{2,1,0:T(8,128)(2,1)S(1)}, u32[]{:S(2)}, u32[]{:S(2)}) collective-permute-start(bf16[17,16,128]{2,1,0:T(8,128)(2,1)S(1)} %get-tuple-element.36.after), channel_id=1, source_target_pairs={{0,1},{1,2},{2,3},{3,4},{4,5},{5,6},{6,7},{7,8},{8,9},{9,10},{10,1... | collective-permute-start | bytes 208904 | tf_op jit(solution)/shard_map/ppermute | solution.py:758
  59.8 1.3 %collective-permute-done.2.after.y_low = bf16[17,16,128]{2,1,0:T(8,128)(2,1)S(1)} collective-permute-done((bf16[17,16,128]{2,1,0:T(8,128)(2,1)S(1)}, bf16[17,16,128]{2,1,0:T(8,128)(2,1)S(1)}, u32[]{:S(2)}, u32[]{:S(2)}) %collective-permute-start.2) | collective-permute-done | bytes 69664 | tf_op jit(solution)/shard_map/ppermute | solution.py:758
  61.1 1.5 %shard_map.253.after = bf16[128,640]{1,0:T(8,128)(2,1)} custom-call(bf16[64,256]{1,0:T(8,128)(2,1)S(1)} %bitcast.17, bf16[128,384]{1,0:T(8,128)(2,1)S(1)} %copy-done.10, bf16[17,16,128]{2,1,0:T(8,128)(2,1)S(1)} %collective-permute-done.2.after.y_low), custom_call_target="tpu_custom_call" | custom-call | flops 40000000 | bytes 600000 | tf_op jit(solution)/shard_map/pallas_call | solution.py:863
  62.6 6.3 %all-to-all-start.3 = ((bf16[16,8,640]{2,1,0:T(8,128)(2,1)}), bf16[16,8,640]{2,1,0:T(8,128)(2,1)S(1)}, u32[]{:S(2)}, u32[]{:S(2)}) async-start(bf16[16,8,640]{2,1,0:T(8,128)(2,1)} %bitcast.10), calls=%async_computation.3 | async-start | bytes 327680 | tf_op jit(solution)/shard_map/all_to_all | solution.py:871
  68.9 2.3 %collective-permute-start.3 = (bf16[10,16,128]{2,1,0:T(8,128)(2,1)S(1)}, bf16[10,16,128]{2,1,0:T(8,128)(2,1)S(1)}, u32[]{:S(2)}, u32[]{:S(2)}) collective-permute-start(bf16[10,16,128]{2,1,0:T(8,128)(2,1)S(1)} %get-tuple-element.37), channel_id=1, source_target_pairs={{1,0},{2,1},{3,2},{4,3},{5,4},{6,5},{7,6},{8,7},{9,8},{10,9},{11,1... | collective-permute-start | bytes 122888 | tf_op jit(solution)/shard_map/ppermute | solution.py:758
  71.1 3.5 %collective-permute-done.3.y_high = bf16[10,16,128]{2,1,0:T(8,128)(2,1)S(1)} collective-permute-done((bf16[10,16,128]{2,1,0:T(8,128)(2,1)S(1)}, bf16[10,16,128]{2,1,0:T(8,128)(2,1)S(1)}, u32[]{:S(2)}, u32[]{:S(2)}) %collective-permute-start.3) | collective-permute-done | bytes 40992 | tf_op jit(solution)/shard_map/ppermute | solution.py:758
  74.6 1.7 %shard_map.254 = (f32[3,10,24,128]{3,2,1,0:T(8,128)S(1)}, f32[3,10,24,128]{3,2,1,0:T(8,128)S(1)}, f32[10,24,128]{2,1,0:T(8,128)S(1)}, f32[8,16,128]{2,1,0:T(8,128)S(1)}, f32[3,8,16,128]{3,2,1,0:T(8,128)S(1)}) custom-call(s32[64]{0:T(128)S(1)} %copy-done.17, f32[3,2,64]{2,1,0:T(2,128)S(1)} %bitcast.21, f32[3,8,16,128]{3,2,1,0:T(8,128)S(1)} %copy-done.1, ...), custom_call_target="tpu_custom_call" | custom-call | flops 10000000 | bytes 3000000 | tf_op jit(solution)/shard_map/pallas_call | solution.py:872
  76.4 1.2 %shard_map.255 = (f32[3,8,16,128]{3,2,1,0:T(8,128)}, f32[3,8,16,128]{3,2,1,0:T(8,128)}, f32[8,16,128]{2,1,0:T(8,128)}, f32[3,2,64]{2,1,0:T(2,128)}) custom-call(bf16[128,640]{1,0:T(8,128)(2,1)S(1)} %bitcast.14, bf16[128,128]{1,0:T(8,128)(2,1)S(1)} %copy-done.13, bf16[128,256]{1,0:T(8,128)(2,1)S(1)} %copy-done.12, ...), custom_call_target="tpu_custom_call" | custom-call | flops 40000000 | bytes 4000000 | tf_op jit(solution)/shard_map/pallas_call | solution.py:887
  (47 shorter events, 0.2 us)
Async XLA Ops:
  0.6 12.7 %copy-start = (f32[3,8,16,128]{3,2,1,0:T(8,128)S(1)}, f32[3,8,16,128]{3,2,1,0:T(8,128)}, u32[]{:S(2)}) copy-start(f32[3,8,16,128]{3,2,1,0:T(8,128)} %magnetic.5) | copy-start | bytes 589828
  3.0 10.4 %copy-start.1 = (f32[3,8,16,128]{3,2,1,0:T(8,128)S(1)}, f32[3,8,16,128]{3,2,1,0:T(8,128)}, u32[]{:S(2)}) copy-start(f32[3,8,16,128]{3,2,1,0:T(8,128)} %get-tuple-element.27.field.electric) | copy-start | bytes 589828
  3.0 10.4 %copy-start.20 = (f32[8]{0:T(128)S(1)}, f32[8]{0:T(128)}, u32[]{:S(2)}) copy-start(f32[8]{0:T(128)} %perm_in.1) | copy-start | bytes 100
  3.0 10.4 %copy-start.21 = (s32[64]{0:T(128)S(1)}, s32[64]{0:T(128)}, u32[]{:S(2)}) copy-start(s32[64]{0:T(128)} %src_in.1) | copy-start | bytes 772
  3.0 16.3 %all-to-all-start = ((bf16[16,24,128]{2,1,0:T(8,128)(2,1)}), bf16[16,24,128]{2,1,0:T(8,128)(2,1)S(1)}, u32[]{:S(2)}, u32[]{:S(2)}) async-start(bf16[16,24,128]{2,1,0:T(8,128)(2,1)} %bitcast.23), calls=%async_computation | async-start | bytes 196608 | tf_op jit(solution)/shard_map/all_to_all | solution.py:796
  13.4 5.9 %copy-start.3 = (bf16[512,256]{1,0:T(8,128)(2,1)S(1)}, bf16[512,256]{1,0:T(8,128)(2,1)}, u32[]{:S(2)}) copy-start(bf16[512,256]{1,0:T(8,128)(2,1)} %constant.21.clone.table) | copy-start | bytes 786436
  20.6 14.2 %copy-start.2 = (bf16[2,3,8,16,128]{4,3,2,1,0:T(8,128)(2,1)S(1)}, bf16[2,3,8,16,128]{4,3,2,1,0:T(8,128)(2,1)}, u32[]{:S(2)}) copy-start(bf16[2,3,8,16,128]{4,3,2,1,0:T(8,128)(2,1)} %saved.5) | copy-start | bytes 589828
  20.6 29.1 %all-to-all-start.1 = ((bf16[32,8,256]{2,1,0:T(8,128)(2,1)}), bf16[32,8,256]{2,1,0:T(8,128)(2,1)S(1)}, u32[]{:S(2)}, u32[]{:S(2)}) async-start(bf16[32,8,256]{2,1,0:T(8,128)(2,1)} %bitcast.3), calls=%async_computation.1 | async-start | bytes 262144 | tf_op jit(solution)/shard_map/all_to_all | solution.py:814
  34.7 6.3 %copy-start.4 = (bf16[4,2,48,256]{3,2,1,0:T(8,128)(2,1)S(1)}, bf16[4,2,48,256]{3,2,1,0:T(8,128)(2,1)}, u32[]{:S(2)}) copy-start(bf16[4,2,48,256]{3,2,1,0:T(8,128)(2,1)} %constant.23.clone.at_y) | copy-start | bytes 589828
  34.7 6.3 %copy-start.7 = (bf16[2,48,16,16]{1,3,2,0:T(8,128)(2,1)S(1)}, bf16[2,48,16,16]{1,3,2,0:T(8,128)(2,1)}, u32[]{:S(2)}) copy-start(bf16[2,48,16,16]{1,3,2,0:T(8,128)(2,1)} %param.33) | copy-start | bytes 147460
  34.7 6.3 %copy-start.8 = (bf16[2,128,256]{2,1,0:T(8,128)(2,1)S(1)}, bf16[2,128,256]{2,1,0:T(8,128)(2,1)}, u32[]{:S(2)}) copy-start(bf16[2,128,256]{2,1,0:T(8,128)(2,1)} %constant.22.clone.at_x) | copy-start | bytes 393220
  34.8 6.3 %copy-start.9 = (bf16[16,2,16,128]{3,2,1,0:T(8,128)(2,1)S(1)}, bf16[16,2,16,128]{3,2,1,0:T(8,128)(2,1)}, u32[]{:S(2)}) copy-start(bf16[16,2,16,128]{3,2,1,0:T(8,128)(2,1)} %constant.24.clone.at_z) | copy-start | bytes 393220
  34.8 6.3 %copy-start.15 = (f32[16,48]{1,0:T(8,128)S(1)}, f32[16,48]{1,0:T(8,128)}, u32[]{:S(2)}) copy-start(f32[16,48]{1,0:T(8,128)} %gain_x.1) | copy-start | bytes 9220
  34.8 6.3 %copy-start.16 = (f32[16,48]{1,0:T(8,128)S(1)}, f32[16,48]{1,0:T(8,128)}, u32[]{:S(2)}) copy-start(f32[16,48]{1,0:T(8,128)} %gain_y.1) | copy-start | bytes 9220
  34.8 6.3 %copy-start.19 = (f32[3,16]{1,0:T(4,128)S(1)}, f32[3,16]{1,0:T(4,128)}, u32[]{:S(2)}) copy-start(f32[3,16]{1,0:T(4,128)} %project.1) | copy-start | bytes 580
  34.8 11.4 %collective-permute-start = (bf16[17,16,128]{2,1,0:T(8,128)(2,1)S(1)}, bf16[17,16,128]{2,1,0:T(8,128)(2,1)S(1)}, u32[]{:S(2)}, u32[]{:S(2)}) collective-permute-start(bf16[17,16,128]{2,1,0:T(8,128)(2,1)S(1)} %get-tuple-element.34), channel_id=1, source_target_pairs={{0,16},{16,32},{32,48},{48,64},{64,80},{80,96},{96,112},{112,128},... | collective-permute-start | bytes 208904 | tf_op jit(solution)/shard_map/ppermute | solution.py:758
  39.6 6.6 %collective-permute-start.1 = (bf16[10,16,128]{2,1,0:T(8,128)(2,1)S(1)}, bf16[10,16,128]{2,1,0:T(8,128)(2,1)S(1)}, u32[]{:S(2)}, u32[]{:S(2)}) collective-permute-start(bf16[10,16,128]{2,1,0:T(8,128)(2,1)S(1)} %get-tuple-element.35), channel_id=1, source_target_pairs={{16,0},{32,16},{48,32},{64,48},{80,64},{96,80},{112,96},{128,112},... | collective-permute-start | bytes 122888 | tf_op jit(solution)/shard_map/ppermute | solution.py:758
  46.3 3.4 %copy-start.6 = (bf16[4,2,64,128]{3,2,1,0:T(8,128)(2,1)S(1)}, bf16[4,2,64,128]{3,2,1,0:T(8,128)(2,1)}, u32[]{:S(2)}) copy-start(bf16[4,2,64,128]{3,2,1,0:T(8,128)(2,1)} %constant.26.clone.inv_x) | copy-start | bytes 393220
  49.7 11.5 %copy-start.10 = (bf16[128,384]{1,0:T(8,128)(2,1)S(1)}, bf16[128,384]{1,0:T(8,128)(2,1)}, u32[]{:S(2)}) copy-start(bf16[128,384]{1,0:T(8,128)(2,1)} %constant.27.clone.inv_y) | copy-start | bytes 294916
  51.0 10.1 %all-to-all-start.2 = ((bf16[4,16,256]{2,1,0:T(8,128)(2,1)}), bf16[4,16,256]{2,1,0:T(8,128)(2,1)S(1)}, u32[]{:S(2)}, u32[]{:S(2)}) async-start(bf16[4,16,256]{2,1,0:T(8,128)(2,1)} %bitcast.8), calls=%async_computation.2 | async-start | bytes 65536 | tf_op jit(solution)/shard_map/all_to_all | solution.py:767
  55.3 5.8 %collective-permute-start.2 = (bf16[17,16,128]{2,1,0:T(8,128)(2,1)S(1)}, bf16[17,16,128]{2,1,0:T(8,128)(2,1)S(1)}, u32[]{:S(2)}, u32[]{:S(2)}) collective-permute-start(bf16[17,16,128]{2,1,0:T(8,128)(2,1)S(1)} %get-tuple-element.36.after), channel_id=1, source_target_pairs={{0,1},{1,2},{2,3},{3,4},{4,5},{5,6},{6,7},{7,8},{8,9},{9,10},{10,1... | collective-permute-start | bytes 208904 | tf_op jit(solution)/shard_map/ppermute | solution.py:758
  62.6 13.7 %all-to-all-start.3 = ((bf16[16,8,640]{2,1,0:T(8,128)(2,1)}), bf16[16,8,640]{2,1,0:T(8,128)(2,1)S(1)}, u32[]{:S(2)}, u32[]{:S(2)}) async-start(bf16[16,8,640]{2,1,0:T(8,128)(2,1)} %bitcast.10), calls=%async_computation.3 | async-start | bytes 327680 | tf_op jit(solution)/shard_map/all_to_all | solution.py:871
  68.9 7.5 %copy-start.12 = (bf16[128,256]{1,0:T(8,128)(2,1)S(1)}, bf16[128,256]{1,0:T(8,128)(2,1)}, u32[]{:S(2)}) copy-start(bf16[128,256]{1,0:T(8,128)(2,1)} %constant.29.clone.apart) | copy-start | bytes 196612
  68.9 5.7 %collective-permute-start.3 = (bf16[10,16,128]{2,1,0:T(8,128)(2,1)S(1)}, bf16[10,16,128]{2,1,0:T(8,128)(2,1)S(1)}, u32[]{:S(2)}, u32[]{:S(2)}) collective-permute-start(bf16[10,16,128]{2,1,0:T(8,128)(2,1)S(1)} %get-tuple-element.37), channel_id=1, source_target_pairs={{1,0},{2,1},{3,2},{4,3},{5,4},{6,5},{7,6},{8,7},{9,8},{10,9},{11,1... | collective-permute-start | bytes 122888 | tf_op jit(solution)/shard_map/ppermute | solution.py:758
  (6 other events, 8.8 us)

commit v9 on v5

--- a/solution.py
+++ b/solution.py
@@ -17,6 +17,7 @@
 RX, RY = 8, 16
 NEAR, FAR = 8, 4
 SHARE = OWN * K // NEAR
+PAD = 24
 LANES = 128
 F32, BF16 = jnp.float32, jnp.bfloat16
 PARAMS = pltpu.CompilerParams(vmem_limit_bytes=40 * 1024 * 1024)
@@ -63,9 +64,6 @@
     fwd_y[256:, 128 : 128 + K] = cy[:, y_of].T
     out["fwd_y"] = fwd_y
 
-    fwd_x = np.zeros((2 * LANES, NX), ml_dtypes.bfloat16)
-    fwd_x[:K], fwd_x[64 : 64 + K] = cx, -sx
-    fwd_x[128 : 128 + K], fwd_x[192 : 192 + K] = sx, cx
     inv_x = np.zeros((FAR, LANES, LANES), ml_dtypes.bfloat16)
     for far in range(FAR):
         for n in range(NEAR):
@@ -73,7 +71,7 @@
             x_of = (start + np.array([0, 1, 2, 3, 4, 5, 6, 7, 8, -1])) % NX
             inv_x[far, n * 16 : n * 16 + 10, :K] = cx[:, x_of].T
             inv_x[far, n * 16 : n * 16 + 10, 64 : 64 + K] = -sx[:, x_of].T
-    out["fwd_x"], out["inv_x"] = fwd_x, inv_x
+    out["inv_x"] = inv_x
 
     inv_y = np.zeros((LANES, 384), ml_dtypes.bfloat16)
     inv_y[:K, :256], inv_y[64 : 64 + K, :256] = cy, -sy
@@ -352,11 +350,12 @@
 
 
 def param_kernel(
-    mon, weights, lift, cells, project, gain_x, gain_y, mix, at_x, at_y, at_z, after,
-    coef_a, coef_b, phase_x, phase_yz, injected,
+    mon, weights, lift, cells, project, gain_x, gain_y, mix, at_x, at_y, at_z, inv_x,
+    after, coef_a, coef_b, phase_x, phase_yz, injected, back_x,
 ):
     b, w = own_block()
     n = b % NEAR
+    back_x[...] = inv_x[b // NEAR]
     flat = cells[...]
     x, y, z = place_of(flat)
     first = iota((1, LANES), 1) < 64
@@ -369,21 +368,21 @@
     ).astype(BF16)
     hot_y = jnp.where(iota((NY, LANES), 0) == y, 1.0, 0.0).astype(BF16)
     hot_z = jnp.where(iota((NZ, LANES), 0) == z, 1.0, 0.0).astype(BF16)
-    cy = jnp.dot(at_y[n, 0], hot_y, preferred_element_type=F32)[:24]
-    sy = jnp.dot(at_y[n, 1], hot_y, preferred_element_type=F32)[:24]
+    cy = jnp.dot(at_y[n, 0], hot_y, preferred_element_type=F32)[:PAD]
+    sy = jnp.dot(at_y[n, 1], hot_y, preferred_element_type=F32)[:PAD]
     cz = jnp.dot(at_z[w, 0], hot_z, preferred_element_type=F32)
     sz = jnp.dot(at_z[w, 1], hot_z, preferred_element_type=F32)
-    mode = n * SHARE + iota((24, 1), 0)
+    mode = n * SHARE + iota((PAD, 1), 0)
     ck = jnp.where(mode < K, cz[0:1], jnp.where(mode < 2 * K, cz[1:2], cz[2:3]))
     sk = jnp.where(mode < K, sz[0:1], jnp.where(mode < 2 * K, sz[1:2], sz[2:3]))
     phase_yz[...] = jnp.where(first, cy * ck - sy * sk, -(sy * ck + cy * sk))
 
-    place = iota((K, 24), 1)
+    place = iota((K, PAD), 1)
     mode = n * SHARE + place
     depth = jnp.where(mode < K, 0, jnp.where(mode < 2 * K, 1, 2))
     live = place < SHARE
-    hot_j = jnp.where((iota((K, 24), 0) == mode - depth * K) & live, 1.0, 0.0)
-    hot_k = jnp.where((iota((K, 24), 0) == w * OWN + depth) & live, 1.0, 0.0)
+    hot_j = jnp.where((iota((K, PAD), 0) == mode - depth * K) & live, 1.0, 0.0)
+    hot_k = jnp.where((iota((K, PAD), 0) == w * OWN + depth) & live, 1.0, 0.0)
     gains = jnp.dot(gain_y[...], hot_j, precision=HIGHEST, preferred_element_type=F32)
     diagonal = iota((16, 16), 0) == iota((16, 16), 1)
     columns = [
@@ -392,23 +391,29 @@
     ]
     blank = jnp.zeros((16, 16), F32)
     along = gain_x[...]
+    totals = []
+    for part in range(2):
+        rows = [mix[part, c].astype(F32) for c in range(16)]
+        for d in range(3):
+            total = lift[d, 0] * rows[0]
+            for c in range(1, 16):
+                total = total + lift[d, c] * rows[c]
+            totals.append(total)
+    joined = jnp.dot(
+        jnp.concatenate(totals, 0), hot_k, precision=HIGHEST, preferred_element_type=F32
+    )
+    joined = [joined[i * 16 : (i + 1) * 16] * gains for i in range(6)]
     for part, to in ((0, coef_a), (1, coef_b)):
-        joined = []
-        for d in range(3):
-            total = jnp.zeros((16, K), F32)
-            for c in range(16):
-                total = total + lift[d, c] * mix[part, c].astype(F32)
-            joined.append(
-                gains * jnp.dot(total, hot_k, precision=HIGHEST, preferred_element_type=F32)
-            )
         sign = 1.0 if part == 0 else -1.0
         right = jnp.concatenate([sign * along, blank, along, blank], 1)
+        right = jnp.concatenate([columns[e] * right for e in range(3)], 1)
+        left = jnp.concatenate([j.T for j in joined[part * 3 : part * 3 + 3]], 0)
+        found = jnp.dot(left, right, precision=HIGHEST, preferred_element_type=F32)
         for e in range(3):
             for d in range(3):
-                left = (columns[e] * joined[d]).T
-                to[(e * 3 + d) * 24 : (e * 3 + d + 1) * 24, :] = jnp.dot(
-                    left, right, precision=HIGHEST, preferred_element_type=F32
-                )
+                to[(e * 3 + d) * PAD : (e * 3 + d + 1) * PAD, :] = found[
+                    d * PAD : (d + 1) * PAD, e * LANES : (e + 1) * LANES
+                ]
     row = iota((8, LANES), 0)
     total = jnp.zeros((8, LANES), F32)
     for i in range(64):
@@ -420,19 +425,19 @@
 
 
 def filter_kernel(
-    gathered, coef_a, coef_b, fwd_x, inv_x, phase_x, phase_yz, after, out
+    gathered, coef_a, coef_b, at_x, back_x, phase_x, phase_yz, after, out
 ):
     b, w = own_block()
-    far = b // NEAR
     lane = iota((1, LANES), 1)
     got = gathered[...]
-    both = jnp.dot(fwd_x[...], got, preferred_element_type=F32)
+    real = jnp.dot(at_x[0], got, preferred_element_type=F32)
+    imag = jnp.dot(at_x[1], got, preferred_element_type=F32)
     total = got.astype(F32).reshape(BULK, 8, LANES).sum(0)
     total = total + pltpu.roll(total, 64, 1)
     total = jnp.where(lane < 6, pltpu.roll(total, LANES - 54, 1), 0.0)
     total = jnp.concatenate([total, jnp.zeros((LANES - 8, LANES), F32)], 0).T[:8]
     total = pltpu.roll(total, (b % NEAR) * 8, 1)
-    full = (both[:LANES] + pltpu.roll(both[LANES:], 64, 1)).T
+    full = (real + pltpu.roll(imag, 64, 1)).T
     field = [full[d * SHARE : d * SHARE + 24] for d in range(3)]
     turned = [pltpu.roll(f, 64, 1) for f in field]
     sign = jnp.where(lane < 64, 1.0, -1.0)
@@ -450,7 +455,7 @@
     packed = jnp.concatenate([q[:SHARE] for q in real] + [gap], 0)
     right = jnp.concatenate([packed, pltpu.roll(packed, 64, 1) * sign], 0).astype(BF16)
     back = lax.dot_general(
-        inv_x[far], right, (((1,), (1,)), ((), ())), preferred_element_type=F32
+        back_x[...], right, (((1,), (1,)), ((), ())), preferred_element_type=F32
     ).reshape(NEAR, 2, 8, LANES)
     row = iota((8, LANES), 0)
     for e in range(3):
@@ -465,7 +470,7 @@
     out[...] = jnp.concatenate(tiles, 0).astype(BF16)
 
 
-def spread_kernel(shares, inv_y, after_low, after_high, out, rows):
+def spread_kernel(shares, inv_y, after, out, rows):
     lane = iota((1, LANES), 1)
     got = shares[...].astype(F32).reshape(NEAR, 16, LANES)
     rows[...] = jnp.zeros((32, 8, LANES), F32)
@@ -585,8 +590,8 @@
 
 
 def first_kernel(
-    mon, weights, electric, magnetic, inverse, saved, x_low, x_high, y_low, y_high, after,
-    early, curled, factor, grad, ready, e_ext, h_ext, g_ext,
+    mon, weights, electric, magnetic, inverse, x_low, x_high, y_low, y_high, after,
+    early, curled, factor, e_ext, h_ext, g_ext,
 ):
     b, w = own_block()
     lane = iota((1, NZ), 1)
@@ -640,6 +645,8 @@
     factor[0:9] = half[0:9]
     factor[9:10] = half[11:12]
 
+
+def saved_kernel(electric, inverse, saved, x_low, y_low, after, grad, ready):
     near = inverse[...]
     for step in range(2):
         s = [saved[step, c].astype(F32) for c in range(3)]
@@ -660,7 +667,7 @@
         else:
             total = jnp.zeros((RX, RY, NZ), F32)
             for c in range(3):
-                total = total + a[c][0:8, 0:16] * near * curls[c]
+                total = total + 0.5 * near * electric[c] * near * curls[c]
             grad[...] = -total
 
 
@@ -782,20 +789,20 @@
     gathered = lax.all_to_all(dealt, "bulk", split_axis=0, concat_axis=0, tiled=True)
 
     cells = jnp.concatenate([source_cells, source_cells]).reshape(1, LANES)
-    coef_a, coef_b, phase_x, phase_yz, injected = call(
+    coef_a, coef_b, phase_x, phase_yz, injected, back_x = call(
         param_kernel,
         (
             shape(216, LANES), shape(216, LANES), shape(LANES, LANES, dtype=BF16),
-            shape(24, LANES), shape(8, LANES),
+            shape(PAD, LANES), shape(8, LANES), shape(LANES, LANES, dtype=BF16),
         ),
-        "sssvvvvvvvva",
+        "sssvvvvvvvvva",
         (),
         20_000_000,
         1_000_000,
     )(
         monitor_cells, weights, lift_weight.T, cells, project_weight, gain_first, gain_second,
         mode_mix.transpose(0, 2, 3, 1), tables_of("at_x"), tables_of("at_y"), tables_of("at_z"),
-        dealt,
+        tables_of("inv_x"), dealt,
     )
 
     to_low, to_high = call(
@@ -820,7 +827,7 @@
     shares = call(
         filter_kernel, shape(LANES, LANES, dtype=BF16), "vvvvvvva", (), 40_000_000, 600_000
     )(
-        gathered, coef_a, coef_b, tables_of("fwd_x"), tables_of("inv_x"), phase_x, phase_yz,
+        gathered, coef_a, coef_b, tables_of("at_x"), back_x, phase_x, phase_yz,
         low_part,
     )
     back = dealt_near(shares)
@@ -831,27 +838,26 @@
     sent = call(
         spread_kernel,
         shape(128, 640, dtype=BF16),
-        "vvaa",
+        "vva",
         [pltpu.VMEM((32, 8, LANES), F32)],
         40_000_000,
         600_000,
-    )(back, tables_of("inv_y"), y_low, y_high)
+    )(back, tables_of("inv_y"), y_low)
     returned = lax.all_to_all(sent, "wide", split_axis=0, concat_axis=0, tiled=True)
-    early, curled, factor, first_grad, ready = call(
+    first_grad, ready = call(
+        saved_kernel, (shape(*block), shape(3, *block)), "vvvvva", (), 3_000_000, 1_000_000
+    )(field, inverse, saved_magnetic, x_low, y_low, sent)
+    early, curled, factor = call(
         first_kernel,
-        (
-            shape(3, 10, 24, NZ), shape(3, 10, 24, NZ), shape(10, 24, NZ), shape(*block),
-            shape(3, *block),
-        ),
-        "ssvvvvvvvva",
+        (shape(3, 10, 24, NZ), shape(3, 10, 24, NZ), shape(10, 24, NZ)),
+        "ssvvvvvvva",
         [pltpu.VMEM((3, 12, 24, NZ), F32)] * 2 + [pltpu.VMEM((12, 24, NZ), F32)],
         10_000_000,
         3_000_000,
     )(
-        monitor_cells, weights, field, seed_magnetic, inverse, saved_magnetic,
-        x_low, x_high, y_low, y_high, sent,
-    )
-
+        monitor_cells, weights, field, seed_magnetic, inverse, x_low, x_high, y_low, y_high,
+        sent,
+    )
     grad_e, grad_h, grad_eps, sources = call(
         second_kernel,
         (shape(3, *block), shape(3, *block), shape(*block), shape(3, 2, 64)),

time: 81.6 us -> 80.7 us (0.989)
  waiting for transfers between devices: 17.3 us -> 15.3 us
  starting transfers between devices: 48.6 us -> 50 us
    all_to_all x1, waiting for transfers between devices: 4.7 us -> 0.01 us  [body(): lax.all_to_all(sent, 'wide', split_axis=0, concat_axis=0, tiled=True)]
    all_to_all x1, starting transfers between devices: 5.38 us -> 7.29 us  [body(): lax.all_to_all(sent, 'wide', split_axis=0, concat_axis=0, tiled=True)]
    all_to_all x1, waiting for transfers between devices: 0.01 us -> 1.37 us  [dealt_near(): lax.all_to_all(block, 'bulk', split_axis=0, concat_axis=0, axis_index_gro...]
    ppermute x4, waiting for transfers between devices: 6.31 us -> 7.66 us  [passed_along(): return lax.ppermute(block, axis, route)]
    all_to_all x1, starting transfers between devices: 6.53 us -> 5.68 us  [dealt_near(): lax.all_to_all(block, 'bulk', split_axis=0, concat_axis=0, axis_index_gro...]
    pallas_call x1 -> x2, Pallas kernels: 1.6 us -> 1.76 us  [the longest x1 1.6 us: body(): call(spread_kernel, shape(128, 640, dtype=BF16), 'vva', [pltpu.VMEM((32,...]
  transfers between devices with their start and end apart: 8 -> 8, of which waited for: 5 -> 6; matrix products, arithmetic and copies ran while one was open for 0% -> 0% of each run, Pallas kernels for 6% -> 6%
where the time goes in v9:
time: 80.7 us; the launch traced here: 80.1 us
  starting transfers between devices  50 us (62%)
  waiting for transfers between devices  15.3 us (19%)
  Pallas kernels  12.1 us (15%)
  local copies, waits for them, and re-layouts  1.57 us (2%)
  between operations  0.97 us (1%)
    all_to_all x1, starting transfers between devices, body(): lax.all_to_all(dealt, 'bulk', split_axis=0, concat_axis=0, tiled=True)  14.1 us
    ppermute x4, starting transfers between devices, passed_along(): return lax.ppermute(block, axis, route)  12.5 us
    all_to_all x1, starting transfers between devices, body(): lax.all_to_all(payload, 'wide', split_axis=0, concat_axis=0, tiled=True)  10.4 us
    ppermute x4, waiting for transfers between devices, passed_along(): return lax.ppermute(block, axis, route)  7.66 us
    all_to_all x1, starting transfers between devices, body(): lax.all_to_all(sent, 'wide', split_axis=0, concat_axis=0, tiled=True)  7.29 us
    all_to_all x1, starting transfers between devices, dealt_near(): lax.all_to_all(block, 'bulk', split_axis=0, concat_axis=0, axis_index_gro...  5.68 us
    all_to_all x1, waiting for transfers between devices, body(): lax.all_to_all(payload, 'wide', split_axis=0, concat_axis=0, tiled=True)  3.83 us
    all_to_all x1, waiting for transfers between devices, body(): lax.all_to_all(dealt, 'bulk', split_axis=0, concat_axis=0, tiled=True)  2.48 us
  transfers between devices with their start and end apart: 8, of which 6 were waited for; matrix products, arithmetic and copies ran while one was open for 0% of the time, Pallas kernels for 6%

profile of v9, /device:TPU:1, one launch (start us, length us, event | category | flops | bytes accessed | tf_op | source)
XLA Modules:
  0.0 80.1 jit_solution(419164536986727950)
XLA Ops:
  0.6 2.3 %shard_map.237 = (bf16[384,128]{1,0:T(8,128)(2,1)}, f32[3,8,16,128]{3,2,1,0:T(8,128)}) custom-call(s32[64]{0:T(128)} %mon.3, f32[3,2,64]{2,1,0:T(2,128)} %bitcast.19, f32[3,8,16,128]{3,2,1,0:T(8,128)} %electric.1, bf16[128,128]{1,0:T(8,128)(2,1)} %constant.18.clone.table_in), custom_call_target="tpu_custom_call" | custom-call | flops 13000000 | bytes 500000 | tf_op jit(solution)/shard_map/pallas_call | solution.py:759
  3.0 10.4 %all-to-all-start = ((bf16[16,24,128]{2,1,0:T(8,128)(2,1)}), bf16[16,24,128]{2,1,0:T(8,128)(2,1)S(1)}, u32[]{:S(2)}, u32[]{:S(2)}) async-start(bf16[16,24,128]{2,1,0:T(8,128)(2,1)} %bitcast.23), calls=%async_computation | async-start | bytes 196608 | tf_op jit(solution)/shard_map/all_to_all | solution.py:771
  13.4 0.9 %copy-done.10 = s32[8,16,128]{2,1,0:T(8,128)S(1)} copy-done((s32[8,16,128]{2,1,0:T(8,128)S(1)}, s32[8,16,128]{2,1,0:T(8,128)}, u32[]{:S(2)}) %copy-start.10) | copy-done | bytes 65560
  14.3 1.1 %shard_map.238 = (f32[8,128]{1,0:T(8,128)S(1)}, f32[8,16,128]{2,1,0:T(8,128)S(1)}) custom-call(s32[64]{0:T(128)S(1)} %copy-done.20, f32[8]{0:T(128)S(1)} %copy-done.19, f32[3,8,16,128]{3,2,1,0:T(8,128)S(1)} %copy-done, f32[3,8,16,128]{3,2,1,0:T(8,128)S(1)} %copy-done.1, s32[8,16,128]{2,1,0:T(8,128)S(1)} %copy-done.10), custom_call_target="tpu_custom_call" | custom-call | flops 3000000 | bytes 1500000 | tf_op jit(solution)/shard_map/pallas_call | solution.py:773
  15.4 3.8 %all-to-all-done = bf16[16,24,128]{2,1,0:T(8,128)(2,1)S(1)} async-done(((bf16[16,24,128]{2,1,0:T(8,128)(2,1)}), bf16[16,24,128]{2,1,0:T(8,128)(2,1)S(1)}, u32[]{:S(2)}, u32[]{:S(2)}) %all-to-all-start) | async-done | bytes 98336 | tf_op jit(solution)/shard_map/all_to_all | solution.py:771
  19.3 1.2 %shard_map.239.after = bf16[256,128]{1,0:T(8,128)(2,1)} custom-call(bf16[384,128]{1,0:T(8,128)(2,1)S(1)} %bitcast.15, f32[8,128]{1,0:T(8,128)S(1)} %get-tuple-element.29.taken, bf16[512,256]{1,0:T(8,128)(2,1)S(1)} %copy-done.5), custom_call_target="tpu_custom_call" | custom-call | flops 20000000 | bytes 400000 | tf_op jit(solution)/shard_map/pallas_call | solution.py:786
  20.5 14.1 %all-to-all-start.1 = ((bf16[32,8,128]{2,1,0:T(8,128)(2,1)}), bf16[32,8,128]{2,1,0:T(8,128)(2,1)S(1)}, u32[]{:S(2)}, u32[]{:S(2)}) async-start(bf16[32,8,128]{2,1,0:T(8,128)(2,1)} %bitcast.3), calls=%async_computation.1 | async-start | bytes 131072 | tf_op jit(solution)/shard_map/all_to_all | solution.py:789
  34.8 4.8 %collective-permute-start = (bf16[17,16,128]{2,1,0:T(8,128)(2,1)S(1)}, bf16[17,16,128]{2,1,0:T(8,128)(2,1)S(1)}, u32[]{:S(2)}, u32[]{:S(2)}) collective-permute-start(bf16[17,16,128]{2,1,0:T(8,128)(2,1)S(1)} %get-tuple-element.36), channel_id=1, source_target_pairs={{0,16},{16,32},{32,48},{48,64},{64,80},{80,96},{96,112},{112,128},... | collective-permute-start | bytes 208904 | tf_op jit(solution)/shard_map/ppermute | solution.py:737
  39.5 1.3 %collective-permute-start.1 = (bf16[10,16,128]{2,1,0:T(8,128)(2,1)S(1)}, bf16[10,16,128]{2,1,0:T(8,128)(2,1)S(1)}, u32[]{:S(2)}, u32[]{:S(2)}) collective-permute-start(bf16[10,16,128]{2,1,0:T(8,128)(2,1)S(1)} %get-tuple-element.37), channel_id=1, source_target_pairs={{16,0},{32,16},{48,32},{64,48},{80,64},{96,80},{112,96},{128,112},... | collective-permute-start | bytes 122888 | tf_op jit(solution)/shard_map/ppermute | solution.py:737
  41.0 0.6 copy-done.17
  41.6 1.5 %shard_map.240 = (f32[216,128]{1,0:T(8,128)S(1)}, f32[216,128]{1,0:T(8,128)S(1)}, bf16[128,128]{1,0:T(8,128)(2,1)S(1)}, f32[24,128]{1,0:T(8,128)S(1)}, f32[8,128...) custom-call(s32[64]{0:T(128)S(1)} %copy-done.16, f32[3,2,64]{2,1,0:T(2,128)S(1)} %bitcast.20, f32[3,16]{1,0:T(4,128)S(1)} %bitcast.22, ...), custom_call_target="tpu_custom_call" | custom-call | flops 20000000 | bytes 1000000 | tf_op jit(solution)/shard_map/pallas_call | solution.py:792
  43.1 3.0 %collective-permute-done.1.x_high = bf16[10,16,128]{2,1,0:T(8,128)(2,1)S(1)} collective-permute-done((bf16[10,16,128]{2,1,0:T(8,128)(2,1)S(1)}, bf16[10,16,128]{2,1,0:T(8,128)(2,1)S(1)}, u32[]{:S(2)}, u32[]{:S(2)}) %collective-permute-start.1) | collective-permute-done | bytes 40992 | tf_op jit(solution)/shard_map/ppermute | solution.py:737
  46.2 2.5 %all-to-all-done.1 = bf16[32,8,128]{2,1,0:T(8,128)(2,1)S(1)} async-done(((bf16[32,8,128]{2,1,0:T(8,128)(2,1)}), bf16[32,8,128]{2,1,0:T(8,128)(2,1)S(1)}, u32[]{:S(2)}, u32[]{:S(2)}) %all-to-all-start.1) | async-done | bytes 65568 | tf_op jit(solution)/shard_map/all_to_all | solution.py:789
  48.7 1.3 %shard_map.243 = bf16[128,128]{1,0:T(8,128)(2,1)} custom-call(bf16[256,128]{1,0:T(8,128)(2,1)S(1)} %bitcast.16, f32[216,128]{1,0:T(8,128)S(1)} %get-tuple-element.30.after.coef_a, f32[216,128]{1,0:T(8,128)S(1)} %get-tuple-element.31.coef_b, bf16[2,128,256]{2,1,0:T(8,128)(2,1)S(1)} %copy-done.3, bf16[128,128]{1,0:T(8,128)(2,1)S(1)} %get-tuple-element.32.back_x, ...), custom_call_target="tpu_custom_call" | custom-call | flops 40000000 | bytes 600000 | tf_op jit(solution)/shard_map/pallas_call | solution.py:827
  50.1 5.7 %all-to-all-start.2 = ((bf16[8,16,128]{2,1,0:T(8,128)(2,1)}), bf16[8,16,128]{2,1,0:T(8,128)(2,1)S(1)}, u32[]{:S(2)}, u32[]{:S(2)}) async-start(bf16[8,16,128]{2,1,0:T(8,128)(2,1)} %bitcast.8), calls=%async_computation.2 | async-start | bytes 65536 | tf_op jit(solution)/shard_map/all_to_all | solution.py:742
  55.7 4.3 %collective-permute-start.2 = (bf16[17,16,128]{2,1,0:T(8,128)(2,1)S(1)}, bf16[17,16,128]{2,1,0:T(8,128)(2,1)S(1)}, u32[]{:S(2)}, u32[]{:S(2)}) collective-permute-start(bf16[17,16,128]{2,1,0:T(8,128)(2,1)S(1)} %get-tuple-element.38.after), channel_id=1, source_target_pairs={{0,1},{1,2},{2,3},{3,4},{4,5},{5,6},{6,7},{7,8},{8,9},{9,10},{10,1... | collective-permute-start | bytes 208904 | tf_op jit(solution)/shard_map/ppermute | solution.py:737
  60.1 1.3 %collective-permute-done.2.after.y_low = bf16[17,16,128]{2,1,0:T(8,128)(2,1)S(1)} collective-permute-done((bf16[17,16,128]{2,1,0:T(8,128)(2,1)S(1)}, bf16[17,16,128]{2,1,0:T(8,128)(2,1)S(1)}, u32[]{:S(2)}, u32[]{:S(2)}) %collective-permute-start.2) | collective-permute-done | bytes 69664 | tf_op jit(solution)/shard_map/ppermute | solution.py:737
  61.4 1.4 %all-to-all-done.2 = bf16[8,16,128]{2,1,0:T(8,128)(2,1)S(1)} async-done(((bf16[8,16,128]{2,1,0:T(8,128)(2,1)}), bf16[8,16,128]{2,1,0:T(8,128)(2,1)S(1)}, u32[]{:S(2)}, u32[]{:S(2)}) %all-to-all-start.2) | async-done | bytes 32800 | tf_op jit(solution)/shard_map/all_to_all | solution.py:742
  62.8 1.6 %shard_map.244.after = bf16[128,640]{1,0:T(8,128)(2,1)} custom-call(bf16[128,128]{1,0:T(8,128)(2,1)S(1)} %bitcast.17, bf16[128,384]{1,0:T(8,128)(2,1)S(1)} %copy-done.9, bf16[17,16,128]{2,1,0:T(8,128)(2,1)S(1)} %collective-permute-done.2.after.y_low), custom_call_target="tpu_custom_call" | custom-call | flops 40000000 | bytes 600000 | tf_op jit(solution)/shard_map/pallas_call | solution.py:838
  64.4 7.3 %all-to-all-start.3 = ((bf16[16,8,640]{2,1,0:T(8,128)(2,1)}), bf16[16,8,640]{2,1,0:T(8,128)(2,1)S(1)}, u32[]{:S(2)}, u32[]{:S(2)}) async-start(bf16[16,8,640]{2,1,0:T(8,128)(2,1)} %bitcast.10), calls=%async_computation.3 | async-start | bytes 327680 | tf_op jit(solution)/shard_map/all_to_all | solution.py:846
  71.7 2.1 %collective-permute-start.3 = (bf16[10,16,128]{2,1,0:T(8,128)(2,1)S(1)}, bf16[10,16,128]{2,1,0:T(8,128)(2,1)S(1)}, u32[]{:S(2)}, u32[]{:S(2)}) collective-permute-start(bf16[10,16,128]{2,1,0:T(8,128)(2,1)S(1)} %get-tuple-element.39), channel_id=1, source_target_pairs={{1,0},{2,1},{3,2},{4,3},{5,4},{6,5},{7,6},{8,7},{9,8},{10,9},{11,1... | collective-permute-start | bytes 122888 | tf_op jit(solution)/shard_map/ppermute | solution.py:737
  74.0 3.3 %collective-permute-done.3.y_high = bf16[10,16,128]{2,1,0:T(8,128)(2,1)S(1)} collective-permute-done((bf16[10,16,128]{2,1,0:T(8,128)(2,1)S(1)}, bf16[10,16,128]{2,1,0:T(8,128)(2,1)S(1)}, u32[]{:S(2)}, u32[]{:S(2)}) %collective-permute-start.3) | collective-permute-done | bytes 40992 | tf_op jit(solution)/shard_map/ppermute | solution.py:737
  77.3 1.6 %shard_map.245 = (f32[3,10,24,128]{3,2,1,0:T(8,128)S(1)}, f32[3,10,24,128]{3,2,1,0:T(8,128)S(1)}, f32[10,24,128]{2,1,0:T(8,128)S(1)}) custom-call(s32[64]{0:T(128)S(1)} %copy-done.16, f32[3,2,64]{2,1,0:T(2,128)S(1)} %bitcast.21, f32[3,8,16,128]{3,2,1,0:T(8,128)S(1)} %copy-done, f32[3,8,16,128]{3,2,1,0:T(8,128)S(1)} %copy-done.1, ...), custom_call_target="tpu_custom_call" | custom-call | flops 10000000 | bytes 3000000 | tf_op jit(solution)/shard_map/pallas_call | solution.py:850
  78.9 1.2 %shard_map.247 = (f32[3,8,16,128]{3,2,1,0:T(8,128)}, f32[3,8,16,128]{3,2,1,0:T(8,128)}, f32[8,16,128]{2,1,0:T(8,128)}, f32[3,2,64]{2,1,0:T(2,128)}) custom-call(bf16[128,640]{1,0:T(8,128)(2,1)S(1)} %bitcast.14, bf16[128,128]{1,0:T(8,128)(2,1)S(1)} %copy-done.12, bf16[128,256]{1,0:T(8,128)(2,1)S(1)} %copy-done.11, ...), custom_call_target="tpu_custom_call" | custom-call | flops 40000000 | bytes 4000000 | tf_op jit(solution)/shard_map/pallas_call | solution.py:861
  (46 shorter events, 0.5 us)
Async XLA Ops:
  0.6 12.7 %copy-start.1 = (f32[3,8,16,128]{3,2,1,0:T(8,128)S(1)}, f32[3,8,16,128]{3,2,1,0:T(8,128)}, u32[]{:S(2)}) copy-start(f32[3,8,16,128]{3,2,1,0:T(8,128)} %magnetic.5) | copy-start | bytes 589828
  3.0 10.4 %copy-start = (f32[3,8,16,128]{3,2,1,0:T(8,128)S(1)}, f32[3,8,16,128]{3,2,1,0:T(8,128)}, u32[]{:S(2)}) copy-start(f32[3,8,16,128]{3,2,1,0:T(8,128)} %get-tuple-element.28.field.electric) | copy-start | bytes 589828
  3.0 10.4 %copy-start.19 = (f32[8]{0:T(128)S(1)}, f32[8]{0:T(128)}, u32[]{:S(2)}) copy-start(f32[8]{0:T(128)} %perm_in.1) | copy-start | bytes 100
  3.0 10.4 %copy-start.20 = (s32[64]{0:T(128)S(1)}, s32[64]{0:T(128)}, u32[]{:S(2)}) copy-start(s32[64]{0:T(128)} %src_in.1) | copy-start | bytes 772
  3.0 16.3 %all-to-all-start = ((bf16[16,24,128]{2,1,0:T(8,128)(2,1)}), bf16[16,24,128]{2,1,0:T(8,128)(2,1)S(1)}, u32[]{:S(2)}, u32[]{:S(2)}) async-start(bf16[16,24,128]{2,1,0:T(8,128)(2,1)} %bitcast.23), calls=%async_computation | async-start | bytes 196608 | tf_op jit(solution)/shard_map/all_to_all | solution.py:771
  13.4 5.9 %copy-start.5 = (bf16[512,256]{1,0:T(8,128)(2,1)S(1)}, bf16[512,256]{1,0:T(8,128)(2,1)}, u32[]{:S(2)}) copy-start(bf16[512,256]{1,0:T(8,128)(2,1)} %constant.19.clone.table) | copy-start | bytes 786436
  19.3 15.4 %copy-start.2 = (bf16[2,3,8,16,128]{4,3,2,1,0:T(8,128)(2,1)S(1)}, bf16[2,3,8,16,128]{4,3,2,1,0:T(8,128)(2,1)}, u32[]{:S(2)}) copy-start(bf16[2,3,8,16,128]{4,3,2,1,0:T(8,128)(2,1)} %saved.5) | copy-start | bytes 589828
  20.5 20.4 %copy-start.8 = (bf16[4,128,128]{2,1,0:T(8,128)(2,1)S(1)}, bf16[4,128,128]{2,1,0:T(8,128)(2,1)}, u32[]{:S(2)}) copy-start(bf16[4,128,128]{2,1,0:T(8,128)(2,1)} %constant.23.clone.inv_x) | copy-start | bytes 393220
  20.5 28.2 %all-to-all-start.1 = ((bf16[32,8,128]{2,1,0:T(8,128)(2,1)}), bf16[32,8,128]{2,1,0:T(8,128)(2,1)S(1)}, u32[]{:S(2)}, u32[]{:S(2)}) async-start(bf16[32,8,128]{2,1,0:T(8,128)(2,1)} %bitcast.3), calls=%async_computation.1 | async-start | bytes 131072 | tf_op jit(solution)/shard_map/all_to_all | solution.py:789
  34.6 6.3 %copy-start.3 = (bf16[2,128,256]{2,1,0:T(8,128)(2,1)S(1)}, bf16[2,128,256]{2,1,0:T(8,128)(2,1)}, u32[]{:S(2)}) copy-start(bf16[2,128,256]{2,1,0:T(8,128)(2,1)} %constant.20.clone.at_x) | copy-start | bytes 393220
  34.7 6.3 %copy-start.4 = (bf16[8,2,32,256]{3,2,1,0:T(8,128)(2,1)S(1)}, bf16[8,2,32,256]{3,2,1,0:T(8,128)(2,1)}, u32[]{:S(2)}) copy-start(bf16[8,2,32,256]{3,2,1,0:T(8,128)(2,1)} %constant.21.clone.at_y) | copy-start | bytes 786436
  34.7 6.3 %copy-start.6 = (bf16[2,48,16,16]{1,3,2,0:T(8,128)(2,1)S(1)}, bf16[2,48,16,16]{1,3,2,0:T(8,128)(2,1)}, u32[]{:S(2)}) copy-start(bf16[2,48,16,16]{1,3,2,0:T(8,128)(2,1)} %param.32) | copy-start | bytes 147460
  34.7 6.3 %copy-start.7 = (bf16[16,2,16,128]{3,2,1,0:T(8,128)(2,1)S(1)}, bf16[16,2,16,128]{3,2,1,0:T(8,128)(2,1)}, u32[]{:S(2)}) copy-start(bf16[16,2,16,128]{3,2,1,0:T(8,128)(2,1)} %constant.22.clone.at_z) | copy-start | bytes 393220
  34.7 6.3 %copy-start.14 = (f32[16,48]{1,0:T(8,128)S(1)}, f32[16,48]{1,0:T(8,128)}, u32[]{:S(2)}) copy-start(f32[16,48]{1,0:T(8,128)} %gain_x.1) | copy-start | bytes 9220
  34.7 6.3 %copy-start.15 = (f32[16,48]{1,0:T(8,128)S(1)}, f32[16,48]{1,0:T(8,128)}, u32[]{:S(2)}) copy-start(f32[16,48]{1,0:T(8,128)} %gain_y.1) | copy-start | bytes 9220
  34.7 6.3 %copy-start.18 = (f32[3,16]{1,0:T(4,128)S(1)}, f32[3,16]{1,0:T(4,128)}, u32[]{:S(2)}) copy-start(f32[3,16]{1,0:T(4,128)} %project.1) | copy-start | bytes 580
  34.8 11.4 %collective-permute-start = (bf16[17,16,128]{2,1,0:T(8,128)(2,1)S(1)}, bf16[17,16,128]{2,1,0:T(8,128)(2,1)S(1)}, u32[]{:S(2)}, u32[]{:S(2)}) collective-permute-start(bf16[17,16,128]{2,1,0:T(8,128)(2,1)S(1)} %get-tuple-element.36), channel_id=1, source_target_pairs={{0,16},{16,32},{32,48},{48,64},{64,80},{80,96},{96,112},{112,128},... | collective-permute-start | bytes 208904 | tf_op jit(solution)/shard_map/ppermute | solution.py:737
  39.5 6.6 %collective-permute-start.1 = (bf16[10,16,128]{2,1,0:T(8,128)(2,1)S(1)}, bf16[10,16,128]{2,1,0:T(8,128)(2,1)S(1)}, u32[]{:S(2)}, u32[]{:S(2)}) collective-permute-start(bf16[10,16,128]{2,1,0:T(8,128)(2,1)S(1)} %get-tuple-element.37), channel_id=1, source_target_pairs={{16,0},{32,16},{48,32},{64,48},{80,64},{96,80},{112,96},{128,112},... | collective-permute-start | bytes 122888 | tf_op jit(solution)/shard_map/ppermute | solution.py:737
  48.7 14.1 %copy-start.9 = (bf16[128,384]{1,0:T(8,128)(2,1)S(1)}, bf16[128,384]{1,0:T(8,128)(2,1)}, u32[]{:S(2)}) copy-start(bf16[128,384]{1,0:T(8,128)(2,1)} %constant.24.clone.inv_y) | copy-start | bytes 294916
  50.1 12.7 %all-to-all-start.2 = ((bf16[8,16,128]{2,1,0:T(8,128)(2,1)}), bf16[8,16,128]{2,1,0:T(8,128)(2,1)S(1)}, u32[]{:S(2)}, u32[]{:S(2)}) async-start(bf16[8,16,128]{2,1,0:T(8,128)(2,1)} %bitcast.8), calls=%async_computation.2 | async-start | bytes 65536 | tf_op jit(solution)/shard_map/all_to_all | solution.py:742
  55.7 5.7 %collective-permute-start.2 = (bf16[17,16,128]{2,1,0:T(8,128)(2,1)S(1)}, bf16[17,16,128]{2,1,0:T(8,128)(2,1)S(1)}, u32[]{:S(2)}, u32[]{:S(2)}) collective-permute-start(bf16[17,16,128]{2,1,0:T(8,128)(2,1)S(1)} %get-tuple-element.38.after), channel_id=1, source_target_pairs={{0,1},{1,2},{2,3},{3,4},{4,5},{5,6},{6,7},{7,8},{8,9},{9,10},{10,1... | collective-permute-start | bytes 208904 | tf_op jit(solution)/shard_map/ppermute | solution.py:737
  64.4 14.5 %all-to-all-start.3 = ((bf16[16,8,640]{2,1,0:T(8,128)(2,1)}), bf16[16,8,640]{2,1,0:T(8,128)(2,1)S(1)}, u32[]{:S(2)}, u32[]{:S(2)}) async-start(bf16[16,8,640]{2,1,0:T(8,128)(2,1)} %bitcast.10), calls=%async_computation.3 | async-start | bytes 327680 | tf_op jit(solution)/shard_map/all_to_all | solution.py:846
  71.7 5.6 %collective-permute-start.3 = (bf16[10,16,128]{2,1,0:T(8,128)(2,1)S(1)}, bf16[10,16,128]{2,1,0:T(8,128)(2,1)S(1)}, u32[]{:S(2)}, u32[]{:S(2)}) collective-permute-start(bf16[10,16,128]{2,1,0:T(8,128)(2,1)S(1)} %get-tuple-element.39), channel_id=1, source_target_pairs={{1,0},{2,1},{3,2},{4,3},{5,4},{6,5},{7,6},{8,7},{9,8},{10,9},{11,1... | collective-permute-start | bytes 122888 | tf_op jit(solution)/shard_map/ppermute | solution.py:737
  74.0 4.9 %copy-start.11 = (bf16[128,256]{1,0:T(8,128)(2,1)S(1)}, bf16[128,256]{1,0:T(8,128)(2,1)}, u32[]{:S(2)}) copy-start(bf16[128,256]{1,0:T(8,128)(2,1)} %constant.26.clone.apart) | copy-start | bytes 196612
  (5 other events, 5.3 us)

commit v10 on v8

--- a/solution.py
+++ b/solution.py
@@ -64,9 +64,6 @@
     fwd_y[256:, 128 : 128 + K] = cy[:, y_of].T
     out["fwd_y"] = fwd_y
 
-    fwd_x = np.zeros((2 * LANES, NX), ml_dtypes.bfloat16)
-    fwd_x[:K], fwd_x[64 : 64 + K] = cx, -sx
-    fwd_x[128 : 128 + K], fwd_x[192 : 192 + K] = sx, cx
     inv_x = np.zeros((DEPTH // NEAR, HALVES, NEAR * 16, LANES), ml_dtypes.bfloat16)
     for half in range(HALVES):
         for z in range(DEPTH):
@@ -75,7 +72,7 @@
             at = slice(z % NEAR * 16, z % NEAR * 16 + 10)
             inv_x[z // NEAR, half, at, :K] = cx[:, x_of].T
             inv_x[z // NEAR, half, at, 64 : 64 + K] = -sx[:, x_of].T
-    out["fwd_x"], out["inv_x"] = fwd_x, inv_x
+    out["inv_x"] = inv_x
 
     inv_y = np.zeros((LANES, 384), ml_dtypes.bfloat16)
     inv_y[:K, :256], inv_y[64 : 64 + K, :256] = cy, -sy
@@ -367,11 +364,12 @@
 
 
 def param_kernel(
-    mon, weights, lift, cells, project, gain_x, gain_y, mix, at_x, at_y, at_z, after,
-    coef_a, coef_b, phase_x, phase_yz, injected,
+    mon, weights, lift, cells, project, gain_x, gain_y, mix, at_x, at_y, at_z, inv_x,
+    after, coef_a, coef_b, phase_x, phase_yz, injected, back_x,
 ):
     b, w = own_block()
     n = b // HALVES % NEAR
+    back_x[...] = inv_x[b // (HALVES * NEAR), b % HALVES]
     flat = cells[...]
     x, y, z = place_of(flat)
     first = iota((1, LANES), 1) < 64
@@ -441,14 +439,15 @@
 
 
 def filter_kernel(
-    gathered, coef_a, coef_b, fwd_x, inv_x, phase_x, phase_yz, after, out
+    gathered, coef_a, coef_b, at_x, back_x, phase_x, phase_yz, after, out
 ):
     b, w = own_block()
-    half, near = b % HALVES, b // HALVES % NEAR
+    near = b // HALVES % NEAR
     lane = iota((1, LANES), 1)
     got = gathered[...]
-    both = jnp.dot(fwd_x[...], got, preferred_element_type=F32)
-    full = (both[:LANES, :LANES] + both[LANES:, LANES:]).T
+    real = jnp.dot(at_x[0], got[:, :LANES], preferred_element_type=F32)
+    imag = jnp.dot(at_x[1], got[:, LANES:], preferred_element_type=F32)
+    full = (real + imag).T
     field = [full[d * SHARE : d * SHARE + PAD] for d in range(3)]
     turned = [pltpu.roll(f, 64, 1) for f in field]
     sign = jnp.where(lane < 64, 1.0, -1.0)
@@ -463,7 +462,7 @@
     packed = jnp.concatenate([q[:SHARE] for q in real] + [gap], 0)
     right = jnp.concatenate([packed, pltpu.roll(packed, 64, 1) * sign], 0).astype(BF16)
     back = lax.dot_general(
-        inv_x[b // (HALVES * NEAR), half], right, (((1,), (1,)), ((), ())),
+        back_x[...], right, (((1,), (1,)), ((), ())),
         preferred_element_type=F32,
     ).reshape(NEAR, 2, 8, 2 * LANES)
 
@@ -586,7 +585,7 @@
 
 
 def corner_kernel(
-    electric, magnetic, inverse, saved, x_low, x_high, after, to_low, to_high, low, high
+    electric, magnetic, inverse, saved, x_low, x_high, after, to_first, to_second, low, high
 ):
     x_of = [{}, {}]
     for p, key in enumerate(low_planes(0)):
@@ -608,16 +607,22 @@
     for n in range(2):
         for i, c in enumerate((0, 2)):
             low[13 + 2 * n + i, 0:8, :] = saved[n, c].astype(F32)[:, RY - 1, :]
-    to_low[...] = low[...].astype(BF16)
-    to_high[...] = high[...].astype(BF16)
+    even = jnp.where(lax.axis_index("wide") % 2 == 0, 1.0, 0.0)
+    a, b = low[...], high[...]
+    to_first[...] = (even * a + (1.0 - even) * b).astype(BF16)
+    to_second[...] = (even * b + (1.0 - even) * a).astype(BF16)
 
 
 def first_kernel(
-    mon, weights, electric, magnetic, inverse, saved, x_low, x_high, y_low, y_high, after,
+    mon, weights, electric, magnetic, inverse, saved, x_low, x_high, y_first, y_second, after,
     early, curled, factor, grad, ready, e_ext, h_ext, g_ext,
 ):
     b, w = own_block()
     lane = iota((1, NZ), 1)
+    even = jnp.where(w % 2 == 0, 1.0, 0.0)
+    first, second = y_first[...].astype(F32), y_second[...].astype(F32)
+    y_low = even * second + (1.0 - even) * first
+    y_high = even * first + (1.0 - even) * second
     zero = jnp.zeros((12, 24, NZ), F32)
     for c in range(7):
         to = e_ext.at[c] if c < 3 else (h_ext.at[c - 3] if c < 6 else g_ext)
@@ -631,7 +636,7 @@
         for planes, ref, at in ((high_planes(1), y_high, 16), (low_planes(1), y_low, 22)):
             for p, (f, i) in enumerate(planes):
                 if f == c:
-                    to[:, at + i : at + i + 1, :] = ref[p].astype(F32)[0:12][:, None, :]
+                    to[:, at + i : at + i + 1, :] = ref[p][0:12][:, None, :]
 
     g = g_ext[...]
     half = 0.5 * g
@@ -674,7 +679,7 @@
         before_x = {c: jnp.concatenate([x_low[12 + 2 * step + c].astype(F32)[None], s[c][:-1]], 0) for c in (1, 2)}
         before_y = {}
         for c in (0, 2):
-            edge = y_low[13 + 2 * step + c // 2].astype(F32)[0:8][:, None, :]
+            edge = y_low[13 + 2 * step + c // 2][0:8][:, None, :]
             first = iota((RX, RY, NZ), 1) == 0
             before_y[c] = jnp.where(first, edge, pltpu.roll(s[c], 1, 1))
         curls = (
@@ -814,20 +819,20 @@
     gathered = lax.all_to_all(dealt, "bulk", split_axis=0, concat_axis=0, tiled=True)
 
     cells = jnp.concatenate([source_cells, source_cells]).reshape(1, LANES)
-    coef_a, coef_b, phase_x, phase_yz, injected = call(
+    coef_a, coef_b, phase_x, phase_yz, injected, back_x = call(
         param_kernel,
         (
             shape(9 * PAD, LANES), shape(9 * PAD, LANES), shape(LANES, LANES, dtype=BF16),
-            shape(PAD, LANES), shape(8, LANES),
+            shape(PAD, LANES), shape(8, LANES), shape(NEAR * 16, LANES, dtype=BF16),
         ),
-        "sssvvvvvvvva",
+        "sssvvvvvvvvva",
         (),
         20_000_000,
         1_000_000,
     )(
         monitor_cells, weights, lift_weight.T, cells, project_weight, gain_first, gain_second,
         mode_mix.transpose(0, 2, 3, 1), tables_of("at_x"), tables_of("at_y"), tables_of("at_z"),
-        dealt,
+        tables_of("inv_x"), dealt,
     )
 
     to_low, to_high = call(
@@ -841,24 +846,25 @@
     x_low = passed_along(to_low, "bulk", 1)
     x_high = passed_along(to_high, "bulk", -1)
 
-    low_part, high_part = call(
+    first_part, second_part = call(
         corner_kernel,
-        (shape(17, 16, NZ, dtype=BF16), shape(10, 16, NZ, dtype=BF16)),
+        (shape(17, 16, NZ, dtype=BF16), shape(17, 16, NZ, dtype=BF16)),
         "vvvvvva",
-        [pltpu.VMEM((17, 16, NZ), F32), pltpu.VMEM((10, 16, NZ), F32)],
+        [pltpu.VMEM((17, 16, NZ), F32)] * 2,
         0,
         1_000_000,
     )(field, seed_magnetic, inverse, saved_magnetic, x_low, x_high, coef_a)
     shares = call(
         filter_kernel, shape(NEAR * 16, 2 * LANES, dtype=BF16), "vvvvvvva", (), 40_000_000, 600_000
     )(
-        gathered, coef_a, coef_b, tables_of("fwd_x"), tables_of("inv_x"), phase_x, phase_yz,
-        low_part,
+        gathered, coef_a, coef_b, tables_of("at_x"), back_x, phase_x, phase_yz,
+        first_part,
     )
     back = dealt_near(shares)
 
-    y_low = passed_along(low_part, "wide", 1)
-    y_high = passed_along(high_part, "wide", -1)
+    y_first = lax.ppermute(first_part, "wide", [(i, i ^ 1) for i in range(WIDE)])
+    pairs = [(i, i + 1) for i in range(1, WIDE - 1, 2)]
+    y_second = lax.ppermute(second_part, "wide", pairs + [(j, i) for i, j in pairs])
 
     sent = call(
         spread_kernel,
@@ -867,7 +873,7 @@
         [pltpu.VMEM((32, 8, LANES), F32)],
         40_000_000,
         600_000,
-    )(back, tables_of("inv_y"), y_low)
+    )(back, tables_of("inv_y"), y_second)
     returned = lax.all_to_all(sent, "wide", split_axis=0, concat_axis=0, tiled=True)
     early, curled, factor, first_grad, ready = call(
         first_kernel,
@@ -881,7 +887,7 @@
         3_000_000,
     )(
         monitor_cells, weights, field, seed_magnetic, inverse, saved_magnetic,
-        x_low, x_high, y_low, y_high, sent,
+        x_low, x_high, y_first, y_second, sent,
     )
 
     grad_e, grad_h, grad_eps, sources = call(

time: 78.2 us -> 77 us (0.985)
    ppermute x0 -> x2, starting transfers between devices: none -> 6.73 us  [the longest x1 4.46 us: body(): lax.ppermute(second_part, 'wide', pairs + [(j, i) for i, j in pairs])]
    ppermute x4 -> x2, starting transfers between devices: 12.8 us -> 6.07 us  [passed_along(): return lax.ppermute(block, axis, route)]
    ppermute x4 -> x2, waiting for transfers between devices: 7.75 us -> 2.91 us  [passed_along(): return lax.ppermute(block, axis, route)]
    ppermute x0 -> x2, waiting for transfers between devices: none -> 3.12 us  [the longest x1 2.11 us: body(): lax.ppermute(second_part, 'wide', pairs + [(j, i) for i, j in pairs])]
    all_to_all x1, waiting for transfers between devices: 0.01 us -> 1.43 us  [body(): lax.all_to_all(sent, 'wide', split_axis=0, concat_axis=0, tiled=True)]
    unnamed x44 -> x42, local copies, waits for them, and re-layouts: 1.58 us -> 1.57 us
  transfers between devices with their start and end apart: 8 -> 8, of which waited for: 5 -> 6; matrix products, arithmetic and copies ran while one was open for 0% -> 0% of each run, Pallas kernels for 6% -> 6%
where the time goes in v10:
time: 77 us; the launch traced here: 76.4 us
  starting transfers between devices  47.1 us (61%)
  waiting for transfers between devices  14.5 us (19%)
  Pallas kernels  12.2 us (16%)
  local copies, waits for them, and re-layouts  1.57 us (2%)
  between operations  0.95 us (1%)
    all_to_all x1, starting transfers between devices, body(): lax.all_to_all(dealt, 'bulk', split_axis=0, concat_axis=0, tiled=True)  14.1 us
    all_to_all x1, starting transfers between devices, body(): lax.all_to_all(payload, 'wide', split_axis=0, concat_axis=0, tiled=True)  10.4 us
    ppermute x2, starting transfers between devices, passed_along(): return lax.ppermute(block, axis, route)  6.07 us
    all_to_all x1, starting transfers between devices, body(): lax.all_to_all(sent, 'wide', split_axis=0, concat_axis=0, tiled=True)  5.5 us
    ppermute x1, starting transfers between devices, body(): lax.ppermute(second_part, 'wide', pairs + [(j, i) for i, j in pairs])  4.46 us
    all_to_all x1, starting transfers between devices, dealt_near(): lax.all_to_all(block, 'bulk', split_axis=0, concat_axis=0, axis_index_gro...  4.27 us
    all_to_all x1, waiting for transfers between devices, body(): lax.all_to_all(payload, 'wide', split_axis=0, concat_axis=0, tiled=True)  3.83 us
    all_to_all x1, waiting for transfers between devices, body(): lax.all_to_all(dealt, 'bulk', split_axis=0, concat_axis=0, tiled=True)  3.25 us
  transfers between devices with their start and end apart: 8, of which 6 were waited for; matrix products, arithmetic and copies ran while one was open for 0% of the time, Pallas kernels for 6%

profile of v10, /device:TPU:1, one launch (start us, length us, event | category | flops | bytes accessed | tf_op | source)
XLA Modules:
  0.0 76.4 jit_solution(9626649408177499142)
XLA Ops:
  0.6 2.3 %shard_map.237 = (bf16[384,128]{1,0:T(8,128)(2,1)}, f32[3,8,16,128]{3,2,1,0:T(8,128)}) custom-call(s32[64]{0:T(128)} %mon.3, f32[3,2,64]{2,1,0:T(2,128)} %bitcast.19, f32[3,8,16,128]{3,2,1,0:T(8,128)} %electric.1, bf16[128,128]{1,0:T(8,128)(2,1)} %constant.18.clone.table_in), custom_call_target="tpu_custom_call" | custom-call | flops 13000000 | bytes 500000 | tf_op jit(solution)/shard_map/pallas_call | solution.py:789
  3.0 10.4 %all-to-all-start = ((bf16[16,24,128]{2,1,0:T(8,128)(2,1)}), bf16[16,24,128]{2,1,0:T(8,128)(2,1)S(1)}, u32[]{:S(2)}, u32[]{:S(2)}) async-start(bf16[16,24,128]{2,1,0:T(8,128)(2,1)} %bitcast.23), calls=%async_computation | async-start | bytes 196608 | tf_op jit(solution)/shard_map/all_to_all | solution.py:801
  13.5 0.9 %copy-done.10 = s32[8,16,128]{2,1,0:T(8,128)S(1)} copy-done((s32[8,16,128]{2,1,0:T(8,128)S(1)}, s32[8,16,128]{2,1,0:T(8,128)}, u32[]{:S(2)}) %copy-start.10) | copy-done | bytes 65560
  14.3 1.1 %shard_map.238 = (f32[8,128]{1,0:T(8,128)S(1)}, f32[8,16,128]{2,1,0:T(8,128)S(1)}) custom-call(s32[64]{0:T(128)S(1)} %copy-done.20, f32[8]{0:T(128)S(1)} %copy-done.19, f32[3,8,16,128]{3,2,1,0:T(8,128)S(1)} %copy-done.1, f32[3,8,16,128]{3,2,1,0:T(8,128)S(1)} %copy-done, s32[8,16,128]{2,1,0:T(8,128)S(1)} %copy-done.10), custom_call_target="tpu_custom_call" | custom-call | flops 3000000 | bytes 1500000 | tf_op jit(solution)/shard_map/pallas_call | solution.py:803
  15.5 3.8 %all-to-all-done = bf16[16,24,128]{2,1,0:T(8,128)(2,1)S(1)} async-done(((bf16[16,24,128]{2,1,0:T(8,128)(2,1)}), bf16[16,24,128]{2,1,0:T(8,128)(2,1)S(1)}, u32[]{:S(2)}, u32[]{:S(2)}) %all-to-all-start) | async-done | bytes 98336 | tf_op jit(solution)/shard_map/all_to_all | solution.py:801
  19.3 1.3 %shard_map.239.after = bf16[256,256]{1,0:T(8,128)(2,1)} custom-call(bf16[384,128]{1,0:T(8,128)(2,1)S(1)} %bitcast.16, f32[8,128]{1,0:T(8,128)S(1)} %get-tuple-element.29.taken, bf16[512,256]{1,0:T(8,128)(2,1)S(1)} %copy-done.4), custom_call_target="tpu_custom_call" | custom-call | flops 20000000 | bytes 400000 | tf_op jit(solution)/shard_map/pallas_call | solution.py:816
  20.6 14.1 %all-to-all-start.1 = ((bf16[32,8,256]{2,1,0:T(8,128)(2,1)}), bf16[32,8,256]{2,1,0:T(8,128)(2,1)S(1)}, u32[]{:S(2)}, u32[]{:S(2)}) async-start(bf16[32,8,256]{2,1,0:T(8,128)(2,1)} %bitcast.3), calls=%async_computation.1 | async-start | bytes 262144 | tf_op jit(solution)/shard_map/all_to_all | solution.py:819
  34.8 4.8 %collective-permute-start = (bf16[17,16,128]{2,1,0:T(8,128)(2,1)S(1)}, bf16[17,16,128]{2,1,0:T(8,128)(2,1)S(1)}, u32[]{:S(2)}, u32[]{:S(2)}) collective-permute-start(bf16[17,16,128]{2,1,0:T(8,128)(2,1)S(1)} %get-tuple-element.36), channel_id=1, source_target_pairs={{0,16},{16,32},{32,48},{48,64},{64,80},{80,96},{96,112},{112,128},... | collective-permute-start | bytes 208904 | tf_op jit(solution)/shard_map/ppermute | solution.py:763
  39.6 1.3 %collective-permute-start.1 = (bf16[10,16,128]{2,1,0:T(8,128)(2,1)S(1)}, bf16[10,16,128]{2,1,0:T(8,128)(2,1)S(1)}, u32[]{:S(2)}, u32[]{:S(2)}) collective-permute-start(bf16[10,16,128]{2,1,0:T(8,128)(2,1)S(1)} %get-tuple-element.37), channel_id=1, source_target_pairs={{16,0},{32,16},{48,32},{64,48},{80,64},{96,80},{112,96},{128,112},... | collective-permute-start | bytes 122888 | tf_op jit(solution)/shard_map/ppermute | solution.py:763
  41.1 0.6 copy-done.17
  41.7 1.7 %shard_map.240 = (f32[360,128]{1,0:T(8,128)S(1)}, f32[360,128]{1,0:T(8,128)S(1)}, bf16[128,128]{1,0:T(8,128)(2,1)S(1)}, f32[40,128]{1,0:T(8,128)S(1)}, f32[8,128...) custom-call(s32[64]{0:T(128)S(1)} %copy-done.16, f32[3,2,64]{2,1,0:T(2,128)S(1)} %bitcast.20, f32[3,16]{1,0:T(4,128)S(1)} %bitcast.22, ...), custom_call_target="tpu_custom_call" | custom-call | flops 20000000 | bytes 1000000 | tf_op jit(solution)/shard_map/pallas_call | solution.py:822
  43.4 2.9 %collective-permute-done.1.x_high = bf16[10,16,128]{2,1,0:T(8,128)(2,1)S(1)} collective-permute-done((bf16[10,16,128]{2,1,0:T(8,128)(2,1)S(1)}, bf16[10,16,128]{2,1,0:T(8,128)(2,1)S(1)}, u32[]{:S(2)}, u32[]{:S(2)}) %collective-permute-start.1) | collective-permute-done | bytes 40992 | tf_op jit(solution)/shard_map/ppermute | solution.py:763
  46.4 3.2 %all-to-all-done.1 = bf16[32,8,256]{2,1,0:T(8,128)(2,1)S(1)} async-done(((bf16[32,8,256]{2,1,0:T(8,128)(2,1)}), bf16[32,8,256]{2,1,0:T(8,128)(2,1)S(1)}, u32[]{:S(2)}, u32[]{:S(2)}) %all-to-all-start.1) | async-done | bytes 131104 | tf_op jit(solution)/shard_map/all_to_all | solution.py:819
  49.7 1.3 %shard_map.243 = bf16[64,256]{1,0:T(8,128)(2,1)} custom-call(bf16[256,256]{1,0:T(8,128)(2,1)S(1)} %bitcast.15, f32[360,128]{1,0:T(8,128)S(1)} %get-tuple-element.30.after.coef_a, f32[360,128]{1,0:T(8,128)S(1)} %get-tuple-element.31.coef_b, bf16[2,128,256]{2,1,0:T(8,128)(2,1)S(1)} %copy-done.3, bf16[64,128]{1,0:T(8,128)(2,1)S(1)} %get-tuple-element.32.back_x, ...), custom_call_target="tpu_custom_call" | custom-call | flops 40000000 | bytes 600000 | tf_op jit(solution)/shard_map/pallas_call | solution.py:857
  50.9 4.3 %all-to-all-start.2 = ((bf16[4,16,256]{2,1,0:T(8,128)(2,1)}), bf16[4,16,256]{2,1,0:T(8,128)(2,1)S(1)}, u32[]{:S(2)}, u32[]{:S(2)}) async-start(bf16[4,16,256]{2,1,0:T(8,128)(2,1)} %bitcast.8), calls=%async_computation.2 | async-start | bytes 65536 | tf_op jit(solution)/shard_map/all_to_all | solution.py:772
  55.2 4.5 %collective-permute-start.2 = (bf16[17,16,128]{2,1,0:T(8,128)(2,1)S(1)}, bf16[17,16,128]{2,1,0:T(8,128)(2,1)S(1)}, u32[]{:S(2)}, u32[]{:S(2)}) collective-permute-start(bf16[17,16,128]{2,1,0:T(8,128)(2,1)S(1)} %get-tuple-element.39), channel_id=1, source_target_pairs={{1,2},{3,4},{5,6},{7,8},{9,10},{11,12},{13,14},{2,1},{4,3},{6,5},{... | collective-permute-start | bytes 208904 | tf_op jit(solution)/shard_map/ppermute | solution.py:867
  59.7 2.1 %collective-permute-done.2.after.y_second = bf16[17,16,128]{2,1,0:T(8,128)(2,1)S(1)} collective-permute-done((bf16[17,16,128]{2,1,0:T(8,128)(2,1)S(1)}, bf16[17,16,128]{2,1,0:T(8,128)(2,1)S(1)}, u32[]{:S(2)}, u32[]{:S(2)}) %collective-permute-start.2) | collective-permute-done | bytes 69664 | tf_op jit(solution)/shard_map/ppermute | solution.py:867
  61.8 1.5 %shard_map.244.after = bf16[128,640]{1,0:T(8,128)(2,1)} custom-call(bf16[64,256]{1,0:T(8,128)(2,1)S(1)} %bitcast.17, bf16[128,384]{1,0:T(8,128)(2,1)S(1)} %copy-done.9, bf16[17,16,128]{2,1,0:T(8,128)(2,1)S(1)} %collective-permute-done.2.after.y_second), custom_call_target="tpu_custom_call" | custom-call | flops 40000000 | bytes 600000 | tf_op jit(solution)/shard_map/pallas_call | solution.py:869
  63.3 5.5 %all-to-all-start.3 = ((bf16[16,8,640]{2,1,0:T(8,128)(2,1)}), bf16[16,8,640]{2,1,0:T(8,128)(2,1)S(1)}, u32[]{:S(2)}, u32[]{:S(2)}) async-start(bf16[16,8,640]{2,1,0:T(8,128)(2,1)} %bitcast.10), calls=%async_computation.3 | async-start | bytes 327680 | tf_op jit(solution)/shard_map/all_to_all | solution.py:877
  68.8 2.3 %collective-permute-start.3 = (bf16[17,16,128]{2,1,0:T(8,128)(2,1)S(1)}, bf16[17,16,128]{2,1,0:T(8,128)(2,1)S(1)}, u32[]{:S(2)}, u32[]{:S(2)}) collective-permute-start(bf16[17,16,128]{2,1,0:T(8,128)(2,1)S(1)} %get-tuple-element.38.after), channel_id=1, source_target_pairs={{0,1},{1,0},{2,3},{3,2},{4,5},{5,4},{6,7},{7,6},{8,9},{9,8},{10,11... | collective-permute-start | bytes 208904 | tf_op jit(solution)/shard_map/ppermute | solution.py:865
  71.0 1.0 %collective-permute-done.3.y_first = bf16[17,16,128]{2,1,0:T(8,128)(2,1)S(1)} collective-permute-done((bf16[17,16,128]{2,1,0:T(8,128)(2,1)S(1)}, bf16[17,16,128]{2,1,0:T(8,128)(2,1)S(1)}, u32[]{:S(2)}, u32[]{:S(2)}) %collective-permute-start.3) | collective-permute-done | bytes 69664 | tf_op jit(solution)/shard_map/ppermute | solution.py:865
  72.1 1.7 %shard_map.245 = (f32[3,10,24,128]{3,2,1,0:T(8,128)S(1)}, f32[3,10,24,128]{3,2,1,0:T(8,128)S(1)}, f32[10,24,128]{2,1,0:T(8,128)S(1)}, f32[8,16,128]{2,1,0:T(8,128)S(1)}, f32[3,8,16,128]{3,2,1,0:T(8,128)S(1)}) custom-call(s32[64]{0:T(128)S(1)} %copy-done.16, f32[3,2,64]{2,1,0:T(2,128)S(1)} %bitcast.21, f32[3,8,16,128]{3,2,1,0:T(8,128)S(1)} %copy-done.1, ...), custom_call_target="tpu_custom_call" | custom-call | flops 10000000 | bytes 3000000 | tf_op jit(solution)/shard_map/pallas_call | solution.py:878
  73.8 1.4 %all-to-all-done.3 = bf16[16,8,640]{2,1,0:T(8,128)(2,1)S(1)} async-done(((bf16[16,8,640]{2,1,0:T(8,128)(2,1)}), bf16[16,8,640]{2,1,0:T(8,128)(2,1)S(1)}, u32[]{:S(2)}, u32[]{:S(2)}) %all-to-all-start.3) | async-done | bytes 163872 | tf_op jit(solution)/shard_map/all_to_all | solution.py:877
  75.2 1.2 %shard_map.246 = (f32[3,8,16,128]{3,2,1,0:T(8,128)}, f32[3,8,16,128]{3,2,1,0:T(8,128)}, f32[8,16,128]{2,1,0:T(8,128)}, f32[3,2,64]{2,1,0:T(2,128)}) custom-call(bf16[128,640]{1,0:T(8,128)(2,1)S(1)} %bitcast.14, bf16[128,128]{1,0:T(8,128)(2,1)S(1)} %copy-done.12, bf16[128,256]{1,0:T(8,128)(2,1)S(1)} %copy-done.11, ...), custom_call_target="tpu_custom_call" | custom-call | flops 40000000 | bytes 4000000 | tf_op jit(solution)/shard_map/pallas_call | solution.py:893
  (45 shorter events, 0.3 us)
Async XLA Ops:
  0.6 12.8 %copy-start = (f32[3,8,16,128]{3,2,1,0:T(8,128)S(1)}, f32[3,8,16,128]{3,2,1,0:T(8,128)}, u32[]{:S(2)}) copy-start(f32[3,8,16,128]{3,2,1,0:T(8,128)} %magnetic.5) | copy-start | bytes 589828
  3.0 10.5 %copy-start.1 = (f32[3,8,16,128]{3,2,1,0:T(8,128)S(1)}, f32[3,8,16,128]{3,2,1,0:T(8,128)}, u32[]{:S(2)}) copy-start(f32[3,8,16,128]{3,2,1,0:T(8,128)} %get-tuple-element.28.field.electric) | copy-start | bytes 589828
  3.0 10.5 %copy-start.19 = (f32[8]{0:T(128)S(1)}, f32[8]{0:T(128)}, u32[]{:S(2)}) copy-start(f32[8]{0:T(128)} %perm_in.1) | copy-start | bytes 100
  3.0 10.5 %copy-start.20 = (s32[64]{0:T(128)S(1)}, s32[64]{0:T(128)}, u32[]{:S(2)}) copy-start(s32[64]{0:T(128)} %src_in.1) | copy-start | bytes 772
  3.0 16.3 %all-to-all-start = ((bf16[16,24,128]{2,1,0:T(8,128)(2,1)}), bf16[16,24,128]{2,1,0:T(8,128)(2,1)S(1)}, u32[]{:S(2)}, u32[]{:S(2)}) async-start(bf16[16,24,128]{2,1,0:T(8,128)(2,1)} %bitcast.23), calls=%async_computation | async-start | bytes 196608 | tf_op jit(solution)/shard_map/all_to_all | solution.py:801
  13.4 5.9 %copy-start.4 = (bf16[512,256]{1,0:T(8,128)(2,1)S(1)}, bf16[512,256]{1,0:T(8,128)(2,1)}, u32[]{:S(2)}) copy-start(bf16[512,256]{1,0:T(8,128)(2,1)} %constant.19.clone.table) | copy-start | bytes 786436
  20.6 14.1 %copy-start.2 = (bf16[2,3,8,16,128]{4,3,2,1,0:T(8,128)(2,1)S(1)}, bf16[2,3,8,16,128]{4,3,2,1,0:T(8,128)(2,1)}, u32[]{:S(2)}) copy-start(bf16[2,3,8,16,128]{4,3,2,1,0:T(8,128)(2,1)} %saved.5) | copy-start | bytes 589828
  20.6 29.0 %all-to-all-start.1 = ((bf16[32,8,256]{2,1,0:T(8,128)(2,1)}), bf16[32,8,256]{2,1,0:T(8,128)(2,1)S(1)}, u32[]{:S(2)}, u32[]{:S(2)}) async-start(bf16[32,8,256]{2,1,0:T(8,128)(2,1)} %bitcast.3), calls=%async_computation.1 | async-start | bytes 262144 | tf_op jit(solution)/shard_map/all_to_all | solution.py:819
  34.7 6.3 %copy-start.3 = (bf16[2,128,256]{2,1,0:T(8,128)(2,1)S(1)}, bf16[2,128,256]{2,1,0:T(8,128)(2,1)}, u32[]{:S(2)}) copy-start(bf16[2,128,256]{2,1,0:T(8,128)(2,1)} %constant.20.clone.at_x) | copy-start | bytes 393220
  34.7 6.3 %copy-start.5 = (bf16[4,2,48,256]{3,2,1,0:T(8,128)(2,1)S(1)}, bf16[4,2,48,256]{3,2,1,0:T(8,128)(2,1)}, u32[]{:S(2)}) copy-start(bf16[4,2,48,256]{3,2,1,0:T(8,128)(2,1)} %constant.21.clone.at_y) | copy-start | bytes 589828
  34.7 6.3 %copy-start.6 = (bf16[2,48,16,16]{1,3,2,0:T(8,128)(2,1)S(1)}, bf16[2,48,16,16]{1,3,2,0:T(8,128)(2,1)}, u32[]{:S(2)}) copy-start(bf16[2,48,16,16]{1,3,2,0:T(8,128)(2,1)} %param.32) | copy-start | bytes 147460
  34.8 6.3 %copy-start.7 = (bf16[16,2,16,128]{3,2,1,0:T(8,128)(2,1)S(1)}, bf16[16,2,16,128]{3,2,1,0:T(8,128)(2,1)}, u32[]{:S(2)}) copy-start(bf16[16,2,16,128]{3,2,1,0:T(8,128)(2,1)} %constant.22.clone.at_z) | copy-start | bytes 393220
  34.8 6.3 %copy-start.8 = (bf16[4,2,64,128]{3,2,1,0:T(8,128)(2,1)S(1)}, bf16[4,2,64,128]{3,2,1,0:T(8,128)(2,1)}, u32[]{:S(2)}) copy-start(bf16[4,2,64,128]{3,2,1,0:T(8,128)(2,1)} %constant.23.clone.inv_x) | copy-start | bytes 393220
  34.8 6.3 %copy-start.14 = (f32[16,48]{1,0:T(8,128)S(1)}, f32[16,48]{1,0:T(8,128)}, u32[]{:S(2)}) copy-start(f32[16,48]{1,0:T(8,128)} %gain_x.1) | copy-start | bytes 9220
  34.8 6.3 %copy-start.15 = (f32[16,48]{1,0:T(8,128)S(1)}, f32[16,48]{1,0:T(8,128)}, u32[]{:S(2)}) copy-start(f32[16,48]{1,0:T(8,128)} %gain_y.1) | copy-start | bytes 9220
  34.8 6.3 %copy-start.18 = (f32[3,16]{1,0:T(4,128)S(1)}, f32[3,16]{1,0:T(4,128)}, u32[]{:S(2)}) copy-start(f32[3,16]{1,0:T(4,128)} %project.1) | copy-start | bytes 580
  34.8 11.4 %collective-permute-start = (bf16[17,16,128]{2,1,0:T(8,128)(2,1)S(1)}, bf16[17,16,128]{2,1,0:T(8,128)(2,1)S(1)}, u32[]{:S(2)}, u32[]{:S(2)}) collective-permute-start(bf16[17,16,128]{2,1,0:T(8,128)(2,1)S(1)} %get-tuple-element.36), channel_id=1, source_target_pairs={{0,16},{16,32},{32,48},{48,64},{64,80},{80,96},{96,112},{112,128},... | collective-permute-start | bytes 208904 | tf_op jit(solution)/shard_map/ppermute | solution.py:763
  39.6 6.6 %collective-permute-start.1 = (bf16[10,16,128]{2,1,0:T(8,128)(2,1)S(1)}, bf16[10,16,128]{2,1,0:T(8,128)(2,1)S(1)}, u32[]{:S(2)}, u32[]{:S(2)}) collective-permute-start(bf16[10,16,128]{2,1,0:T(8,128)(2,1)S(1)} %get-tuple-element.37), channel_id=1, source_target_pairs={{16,0},{32,16},{48,32},{64,48},{80,64},{96,80},{112,96},{128,112},... | collective-permute-start | bytes 122888 | tf_op jit(solution)/shard_map/ppermute | solution.py:763
  49.6 12.1 %copy-start.9 = (bf16[128,384]{1,0:T(8,128)(2,1)S(1)}, bf16[128,384]{1,0:T(8,128)(2,1)}, u32[]{:S(2)}) copy-start(bf16[128,384]{1,0:T(8,128)(2,1)} %constant.24.clone.inv_y) | copy-start | bytes 294916
  50.9 10.9 %all-to-all-start.2 = ((bf16[4,16,256]{2,1,0:T(8,128)(2,1)}), bf16[4,16,256]{2,1,0:T(8,128)(2,1)S(1)}, u32[]{:S(2)}, u32[]{:S(2)}) async-start(bf16[4,16,256]{2,1,0:T(8,128)(2,1)} %bitcast.8), calls=%async_computation.2 | async-start | bytes 65536 | tf_op jit(solution)/shard_map/all_to_all | solution.py:772
  55.2 6.6 %collective-permute-start.2 = (bf16[17,16,128]{2,1,0:T(8,128)(2,1)S(1)}, bf16[17,16,128]{2,1,0:T(8,128)(2,1)S(1)}, u32[]{:S(2)}, u32[]{:S(2)}) collective-permute-start(bf16[17,16,128]{2,1,0:T(8,128)(2,1)S(1)} %get-tuple-element.39), channel_id=1, source_target_pairs={{1,2},{3,4},{5,6},{7,8},{9,10},{11,12},{13,14},{2,1},{4,3},{6,5},{... | collective-permute-start | bytes 208904 | tf_op jit(solution)/shard_map/ppermute | solution.py:867
  63.3 12.0 %all-to-all-start.3 = ((bf16[16,8,640]{2,1,0:T(8,128)(2,1)}), bf16[16,8,640]{2,1,0:T(8,128)(2,1)S(1)}, u32[]{:S(2)}, u32[]{:S(2)}) async-start(bf16[16,8,640]{2,1,0:T(8,128)(2,1)} %bitcast.10), calls=%async_computation.3 | async-start | bytes 327680 | tf_op jit(solution)/shard_map/all_to_all | solution.py:877
  68.8 6.5 %copy-start.11 = (bf16[128,256]{1,0:T(8,128)(2,1)S(1)}, bf16[128,256]{1,0:T(8,128)(2,1)}, u32[]{:S(2)}) copy-start(bf16[128,256]{1,0:T(8,128)(2,1)} %constant.26.clone.apart) | copy-start | bytes 196612
  68.8 3.3 %collective-permute-start.3 = (bf16[17,16,128]{2,1,0:T(8,128)(2,1)S(1)}, bf16[17,16,128]{2,1,0:T(8,128)(2,1)S(1)}, u32[]{:S(2)}, u32[]{:S(2)}) collective-permute-start(bf16[17,16,128]{2,1,0:T(8,128)(2,1)S(1)} %get-tuple-element.38.after), channel_id=1, source_target_pairs={{0,1},{1,0},{2,3},{3,2},{4,5},{5,4},{6,7},{7,6},{8,9},{9,8},{10,11... | collective-permute-start | bytes 208904 | tf_op jit(solution)/shard_map/ppermute | solution.py:865
  (5 other events, 6.9 us)

commit v11 on v10

--- a/solution.py
+++ b/solution.py
@@ -490,7 +490,7 @@
     out[...] = jnp.concatenate(tiles, 0).astype(BF16)
 
 
-def spread_kernel(shares, inv_y, after, out, rows):
+def spread_kernel(shares, inv_y, after_first, after_second, out, rows):
     lane = iota((1, LANES), 1)
     got = shares[...].astype(F32).reshape(NEAR, 16, 2 * LANES)
     rows[...] = jnp.zeros((32, 8, LANES), F32)
@@ -571,27 +571,37 @@
     return planes + [(3 + first, 0), (3 + second, 0)] + [(3 + c, 1) for c in range(3)]
 
 
-def edge_kernel(electric, magnetic, inverse, saved, after, to_low, to_high):
+def swapped(axis, for_next, for_previous):
+    even = jnp.where(lax.axis_index(axis) % 2 == 0, 1.0, 0.0)
+    first = even * for_next + (1.0 - even) * for_previous
+    return first, even * for_previous + (1.0 - even) * for_next
+
+
+def edge_kernel(electric, magnetic, inverse, saved, after, to_first, to_second, to_low, to_high):
     def own(f):
         return electric.at[f] if f < 3 else (magnetic.at[f - 3] if f < 6 else inverse)
 
     for p, (f, i) in enumerate(low_planes(0)):
-        to_low[p] = own(f)[6 + i].astype(BF16)
+        to_low[p] = own(f)[6 + i]
     for n in range(2):
         for c in range(2):
-            to_low[13 + 2 * n + c] = saved[n, 1 + c, 7]
+            to_low[13 + 2 * n + c] = saved[n, 1 + c, 7].astype(F32)
+    to_high[...] = jnp.zeros(to_high.shape, F32)
     for p, (f, i) in enumerate(high_planes(0)):
-        to_high[p] = own(f)[i].astype(BF16)
+        to_high[p] = own(f)[i]
+    first, second = swapped("bulk", to_low[...], to_high[...])
+    to_first[...], to_second[...] = first.astype(BF16), second.astype(BF16)
 
 
 def corner_kernel(
-    electric, magnetic, inverse, saved, x_low, x_high, after, to_first, to_second, low, high
+    electric, magnetic, inverse, saved, x_first, x_second, after, to_first, to_second, low, high
 ):
+    x_high, x_low = swapped("bulk", x_first[...].astype(F32), x_second[...].astype(F32))
     x_of = [{}, {}]
     for p, key in enumerate(low_planes(0)):
-        x_of[0][key] = x_low[p].astype(F32)
+        x_of[0][key] = x_low[p]
     for p, key in enumerate(high_planes(0)):
-        x_of[1][key] = x_high[p].astype(F32)
+        x_of[1][key] = x_high[p]
     low[...] = jnp.zeros(low.shape, F32)
     high[...] = jnp.zeros(high.shape, F32)
     for to, planes, start in ((low, low_planes(1), 14), (high, high_planes(1), 0)):
@@ -607,22 +617,18 @@
     for n in range(2):
         for i, c in enumerate((0, 2)):
             low[13 + 2 * n + i, 0:8, :] = saved[n, c].astype(F32)[:, RY - 1, :]
-    even = jnp.where(lax.axis_index("wide") % 2 == 0, 1.0, 0.0)
-    a, b = low[...], high[...]
-    to_first[...] = (even * a + (1.0 - even) * b).astype(BF16)
-    to_second[...] = (even * b + (1.0 - even) * a).astype(BF16)
+    first, second = swapped("wide", low[...], high[...])
+    to_first[...], to_second[...] = first.astype(BF16), second.astype(BF16)
 
 
 def first_kernel(
-    mon, weights, electric, magnetic, inverse, saved, x_low, x_high, y_first, y_second, after,
+    mon, weights, electric, magnetic, inverse, saved, x_first, x_second, y_first, y_second, after,
     early, curled, factor, grad, ready, e_ext, h_ext, g_ext,
 ):
     b, w = own_block()
     lane = iota((1, NZ), 1)
-    even = jnp.where(w % 2 == 0, 1.0, 0.0)
-    first, second = y_first[...].astype(F32), y_second[...].astype(F32)
-    y_low = even * second + (1.0 - even) * first
-    y_high = even * first + (1.0 - even) * second
+    x_high, x_low = swapped("bulk", x_first[...].astype(F32), x_second[...].astype(F32))
+    y_high, y_low = swapped("wide", y_first[...].astype(F32), y_second[...].astype(F32))
     zero = jnp.zeros((12, 24, NZ), F32)
     for c in range(7):
         to = e_ext.at[c] if c < 3 else (h_ext.at[c - 3] if c < 6 else g_ext)
@@ -632,7 +638,7 @@
         for planes, ref, at in ((high_planes(0), x_high, 8), (low_planes(0), x_low, 10)):
             for p, (f, i) in enumerate(planes):
                 if f == c:
-                    to[at + i, 0:16, :] = ref[p].astype(F32)
+                    to[at + i, 0:16, :] = ref[p]
         for planes, ref, at in ((high_planes(1), y_high, 16), (low_planes(1), y_low, 22)):
             for p, (f, i) in enumerate(planes):
                 if f == c:
@@ -676,7 +682,7 @@
     near = inverse[...]
     for step in range(2):
         s = [saved[step, c].astype(F32) for c in range(3)]
-        before_x = {c: jnp.concatenate([x_low[12 + 2 * step + c].astype(F32)[None], s[c][:-1]], 0) for c in (1, 2)}
+        before_x = {c: jnp.concatenate([x_low[12 + 2 * step + c][None], s[c][:-1]], 0) for c in (1, 2)}
         before_y = {}
         for c in (0, 2):
             edge = y_low[13 + 2 * step + c // 2][0:8][:, None, :]
@@ -757,10 +763,13 @@
     return jax.ShapeDtypeStruct(dims, dtype)
 
 
-def passed_along(block, axis, distance):
-    devices = range(lax.axis_size(axis))
-    route = [(i - distance, i) for i in devices if i - distance in devices]
-    return lax.ppermute(block, axis, route)
+def swaps(first, second, axis):
+    size = lax.axis_size(axis)
+    pairs = [(i, i + 1) for i in range(1, size - 1, 2)]
+    return (
+        lax.ppermute(first, axis, [(i, i ^ 1) for i in range(size)]),
+        lax.ppermute(second, axis, pairs + [(j, i) for i, j in pairs]),
+    )
 
 
 def dealt_near(block):
@@ -835,16 +844,15 @@
         tables_of("inv_x"), dealt,
     )
 
-    to_low, to_high = call(
+    x_first_part, x_second_part = call(
         edge_kernel,
-        (shape(17, RY, NZ, dtype=BF16), shape(10, RY, NZ, dtype=BF16)),
+        (shape(17, RY, NZ, dtype=BF16), shape(17, RY, NZ, dtype=BF16)),
         "vvvva",
-        (),
+        [pltpu.VMEM((17, RY, NZ), F32)] * 2,
         0,
         500_000,
     )(field, seed_magnetic, inverse, saved_magnetic, dealt)
-    x_low = passed_along(to_low, "bulk", 1)
-    x_high = passed_along(to_high, "bulk", -1)
+    x_first, x_second = swaps(x_first_part, x_second_part, "bulk")
 
     first_part, second_part = call(
         corner_kernel,
@@ -853,7 +861,7 @@
         [pltpu.VMEM((17, 16, NZ), F32)] * 2,
         0,
         1_000_000,
-    )(field, seed_magnetic, inverse, saved_magnetic, x_low, x_high, coef_a)
+    )(field, seed_magnetic, inverse, saved_magnetic, x_first, x_second, coef_a)
     shares = call(
         filter_kernel, shape(NEAR * 16, 2 * LANES, dtype=BF16), "vvvvvvva", (), 40_000_000, 600_000
     )(
@@ -862,18 +870,16 @@
     )
     back = dealt_near(shares)
 
-    y_first = lax.ppermute(first_part, "wide", [(i, i ^ 1) for i in range(WIDE)])
-    pairs = [(i, i + 1) for i in range(1, WIDE - 1, 2)]
-    y_second = lax.ppermute(second_part, "wide", pairs + [(j, i) for i, j in pairs])
+    y_first, y_second = swaps(first_part, second_part, "wide")
 
     sent = call(
         spread_kernel,
         shape(128, 640, dtype=BF16),
-        "vva",
+        "vvaa",
         [pltpu.VMEM((32, 8, LANES), F32)],
         40_000_000,
         600_000,
-    )(back, tables_of("inv_y"), y_second)
+    )(back, tables_of("inv_y"), y_first, y_second)
     returned = lax.all_to_all(sent, "wide", split_axis=0, concat_axis=0, tiled=True)
     early, curled, factor, first_grad, ready = call(
         first_kernel,
@@ -887,7 +893,7 @@
         3_000_000,
     )(
         monitor_cells, weights, field, seed_magnetic, inverse, saved_magnetic,
-        x_low, x_high, y_first, y_second, sent,
+        x_first, x_second, y_first, y_second, sent,
     )
 
     grad_e, grad_h, grad_eps, sources = call(

time: 77 us -> 78.8 us (1.023)
  waiting for transfers between devices: 14.5 us -> 18.9 us
  starting transfers between devices: 47.1 us -> 44.4 us
    all_to_all x1, waiting for transfers between devices: 3.25 us -> 6.7 us  [body(): lax.all_to_all(dealt, 'bulk', split_axis=0, concat_axis=0, tiled=True)]
    all_to_all x1, waiting for transfers between devices: 1.43 us -> 4.65 us  [body(): lax.all_to_all(sent, 'wide', split_axis=0, concat_axis=0, tiled=True)]
    ppermute x4, waiting for transfers between devices: 6.04 us -> 3.7 us  [the longest x2 3.69 us: swaps(): lax.ppermute(second, axis, pairs + [(j, i) for i, j in pairs])]
    all_to_all x1, starting transfers between devices: 5.5 us -> 3.84 us  [body(): lax.all_to_all(sent, 'wide', split_axis=0, concat_axis=0, tiled=True)]
    ppermute x4, starting transfers between devices: 12.8 us -> 11.8 us  [the longest x2 9.18 us: swaps(): lax.ppermute(first, axis, [(i, i ^ 1) for i in range(size)])]
  transfers between devices with their start and end apart: 8 -> 8, of which waited for: 6 -> 4; matrix products, arithmetic and copies ran while one was open for 0% -> 0% of each run, Pallas kernels for 6% -> 6%
where the time goes in v11:
time: 78.8 us; the launch traced here: 78.2 us
  starting transfers between devices  44.4 us (56%)
  waiting for transfers between devices  18.9 us (24%)
  Pallas kernels  12.3 us (16%)
  local copies, waits for them, and re-layouts  1.58 us (2%)
  between operations  0.98 us (1%)
    all_to_all x1, starting transfers between devices, body(): lax.all_to_all(dealt, 'bulk', split_axis=0, concat_axis=0, tiled=True)  14 us
    all_to_all x1, starting transfers between devices, body(): lax.all_to_all(payload, 'wide', split_axis=0, concat_axis=0, tiled=True)  10.5 us
    ppermute x2, starting transfers between devices, swaps(): lax.ppermute(first, axis, [(i, i ^ 1) for i in range(size)])  9.18 us
    all_to_all x1, waiting for transfers between devices, body(): lax.all_to_all(dealt, 'bulk', split_axis=0, concat_axis=0, tiled=True)  6.7 us
    all_to_all x1, waiting for transfers between devices, body(): lax.all_to_all(sent, 'wide', split_axis=0, concat_axis=0, tiled=True)  4.65 us
    all_to_all x1, starting transfers between devices, dealt_near(): lax.all_to_all(block, 'bulk', split_axis=0, concat_axis=0, axis_index_gro...  4.27 us
    all_to_all x1, starting transfers between devices, body(): lax.all_to_all(sent, 'wide', split_axis=0, concat_axis=0, tiled=True)  3.84 us
    all_to_all x1, waiting for transfers between devices, body(): lax.all_to_all(payload, 'wide', split_axis=0, concat_axis=0, tiled=True)  3.83 us
  transfers between devices with their start and end apart: 8, of which 4 were waited for; matrix products, arithmetic and copies ran while one was open for 0% of the time, Pallas kernels for 6%

profile of v11, /device:TPU:1, one launch (start us, length us, event | category | flops | bytes accessed | tf_op | source)
XLA Modules:
  0.0 78.2 jit_solution(3939862299943639472)
XLA Ops:
  0.6 2.3 %shard_map.237 = (bf16[384,128]{1,0:T(8,128)(2,1)}, f32[3,8,16,128]{3,2,1,0:T(8,128)}) custom-call(s32[64]{0:T(128)} %mon.3, f32[3,2,64]{2,1,0:T(2,128)} %bitcast.19, f32[3,8,16,128]{3,2,1,0:T(8,128)} %electric.1, bf16[128,128]{1,0:T(8,128)(2,1)} %constant.18.clone.table_in), custom_call_target="tpu_custom_call" | custom-call | flops 13000000 | bytes 500000 | tf_op jit(solution)/shard_map/pallas_call | solution.py:798
  3.0 10.5 %all-to-all-start = ((bf16[16,24,128]{2,1,0:T(8,128)(2,1)}), bf16[16,24,128]{2,1,0:T(8,128)(2,1)S(1)}, u32[]{:S(2)}, u32[]{:S(2)}) async-start(bf16[16,24,128]{2,1,0:T(8,128)(2,1)} %bitcast.23), calls=%async_computation | async-start | bytes 196608 | tf_op jit(solution)/shard_map/all_to_all | solution.py:810
  13.5 0.9 %copy-done.10 = s32[8,16,128]{2,1,0:T(8,128)S(1)} copy-done((s32[8,16,128]{2,1,0:T(8,128)S(1)}, s32[8,16,128]{2,1,0:T(8,128)}, u32[]{:S(2)}) %copy-start.10) | copy-done | bytes 65560
  14.4 1.1 %shard_map.238 = (f32[8,128]{1,0:T(8,128)S(1)}, f32[8,16,128]{2,1,0:T(8,128)S(1)}) custom-call(s32[64]{0:T(128)S(1)} %copy-done.20, f32[8]{0:T(128)S(1)} %copy-done.19, f32[3,8,16,128]{3,2,1,0:T(8,128)S(1)} %copy-done.1, f32[3,8,16,128]{3,2,1,0:T(8,128)S(1)} %copy-done, s32[8,16,128]{2,1,0:T(8,128)S(1)} %copy-done.10), custom_call_target="tpu_custom_call" | custom-call | flops 3000000 | bytes 1500000 | tf_op jit(solution)/shard_map/pallas_call | solution.py:812
  15.5 3.8 %all-to-all-done = bf16[16,24,128]{2,1,0:T(8,128)(2,1)S(1)} async-done(((bf16[16,24,128]{2,1,0:T(8,128)(2,1)}), bf16[16,24,128]{2,1,0:T(8,128)(2,1)S(1)}, u32[]{:S(2)}, u32[]{:S(2)}) %all-to-all-start) | async-done | bytes 98336 | tf_op jit(solution)/shard_map/all_to_all | solution.py:810
  19.4 1.3 %shard_map.239.after = bf16[256,256]{1,0:T(8,128)(2,1)} custom-call(bf16[384,128]{1,0:T(8,128)(2,1)S(1)} %bitcast.16, f32[8,128]{1,0:T(8,128)S(1)} %get-tuple-element.29.taken, bf16[512,256]{1,0:T(8,128)(2,1)S(1)} %copy-done.4), custom_call_target="tpu_custom_call" | custom-call | flops 20000000 | bytes 400000 | tf_op jit(solution)/shard_map/pallas_call | solution.py:825
  20.7 14.0 %all-to-all-start.1 = ((bf16[32,8,256]{2,1,0:T(8,128)(2,1)}), bf16[32,8,256]{2,1,0:T(8,128)(2,1)S(1)}, u32[]{:S(2)}, u32[]{:S(2)}) async-start(bf16[32,8,256]{2,1,0:T(8,128)(2,1)} %bitcast.3), calls=%async_computation.1 | async-start | bytes 262144 | tf_op jit(solution)/shard_map/all_to_all | solution.py:828
  34.9 4.8 %collective-permute-start = (bf16[17,16,128]{2,1,0:T(8,128)(2,1)S(1)}, bf16[17,16,128]{2,1,0:T(8,128)(2,1)S(1)}, u32[]{:S(2)}, u32[]{:S(2)}) collective-permute-start(bf16[17,16,128]{2,1,0:T(8,128)(2,1)S(1)} %get-tuple-element.36), channel_id=1, source_target_pairs={{0,16},{16,0},{32,48},{48,32},{64,80},{80,64},{96,112},{112,96},{1... | collective-permute-start | bytes 208904 | tf_op jit(solution)/shard_map/ppermute | solution.py:770
  39.7 0.7 collective-permute-start.1
  40.3 0.1 add_bitcast_fusion.cells
  40.5 0.6 copy-done.17
  41.1 1.7 %shard_map.240 = (f32[360,128]{1,0:T(8,128)S(1)}, f32[360,128]{1,0:T(8,128)S(1)}, bf16[128,128]{1,0:T(8,128)(2,1)S(1)}, f32[40,128]{1,0:T(8,128)S(1)}, f32[8,128...) custom-call(s32[64]{0:T(128)S(1)} %copy-done.16, f32[3,2,64]{2,1,0:T(2,128)S(1)} %bitcast.20, f32[3,16]{1,0:T(4,128)S(1)} %bitcast.22, ...), custom_call_target="tpu_custom_call" | custom-call | flops 20000000 | bytes 1000000 | tf_op jit(solution)/shard_map/pallas_call | solution.py:831
  42.8 0.1 shard_map.242
  42.9 6.7 %all-to-all-done.1 = bf16[32,8,256]{2,1,0:T(8,128)(2,1)S(1)} async-done(((bf16[32,8,256]{2,1,0:T(8,128)(2,1)}), bf16[32,8,256]{2,1,0:T(8,128)(2,1)S(1)}, u32[]{:S(2)}, u32[]{:S(2)}) %all-to-all-start.1) | async-done | bytes 131104 | tf_op jit(solution)/shard_map/all_to_all | solution.py:828
  49.6 1.3 %shard_map.243 = bf16[64,256]{1,0:T(8,128)(2,1)} custom-call(bf16[256,256]{1,0:T(8,128)(2,1)S(1)} %bitcast.15, f32[360,128]{1,0:T(8,128)S(1)} %get-tuple-element.30.after.coef_a, f32[360,128]{1,0:T(8,128)S(1)} %get-tuple-element.31.coef_b, bf16[2,128,256]{2,1,0:T(8,128)(2,1)S(1)} %copy-done.3, bf16[64,128]{1,0:T(8,128)(2,1)S(1)} %get-tuple-element.32.back_x, ...), custom_call_target="tpu_custom_call" | custom-call | flops 40000000 | bytes 600000 | tf_op jit(solution)/shard_map/pallas_call | solution.py:865
  50.9 4.3 %all-to-all-start.2 = ((bf16[4,16,256]{2,1,0:T(8,128)(2,1)}), bf16[4,16,256]{2,1,0:T(8,128)(2,1)S(1)}, u32[]{:S(2)}, u32[]{:S(2)}) async-start(bf16[4,16,256]{2,1,0:T(8,128)(2,1)} %bitcast.8), calls=%async_computation.2 | async-start | bytes 65536 | tf_op jit(solution)/shard_map/all_to_all | solution.py:781
  55.2 4.4 %collective-permute-start.2 = (bf16[17,16,128]{2,1,0:T(8,128)(2,1)S(1)}, bf16[17,16,128]{2,1,0:T(8,128)(2,1)S(1)}, u32[]{:S(2)}, u32[]{:S(2)}) collective-permute-start(bf16[17,16,128]{2,1,0:T(8,128)(2,1)S(1)} %get-tuple-element.38.after), channel_id=1, source_target_pairs={{0,1},{1,0},{2,3},{3,2},{4,5},{5,4},{6,7},{7,6},{8,9},{9,8},{10,11... | collective-permute-start | bytes 208904 | tf_op jit(solution)/shard_map/ppermute | solution.py:770
  59.6 1.9 %collective-permute-start.3 = (bf16[17,16,128]{2,1,0:T(8,128)(2,1)S(1)}, bf16[17,16,128]{2,1,0:T(8,128)(2,1)S(1)}, u32[]{:S(2)}, u32[]{:S(2)}) collective-permute-start(bf16[17,16,128]{2,1,0:T(8,128)(2,1)S(1)} %get-tuple-element.39), channel_id=1, source_target_pairs={{1,2},{3,4},{5,6},{7,8},{9,10},{11,12},{13,14},{2,1},{4,3},{6,5},{... | collective-permute-start | bytes 208904 | tf_op jit(solution)/shard_map/ppermute | solution.py:771
  61.6 3.7 %collective-permute-done.3.after_second.y_second = bf16[17,16,128]{2,1,0:T(8,128)(2,1)S(1)} collective-permute-done((bf16[17,16,128]{2,1,0:T(8,128)(2,1)S(1)}, bf16[17,16,128]{2,1,0:T(8,128)(2,1)S(1)}, u32[]{:S(2)}, u32[]{:S(2)}) %collective-permute-start.3) | collective-permute-done | bytes 69664 | tf_op jit(solution)/shard_map/ppermute | solution.py:771
  65.2 1.5 %shard_map.244.after = bf16[128,640]{1,0:T(8,128)(2,1)} custom-call(bf16[64,256]{1,0:T(8,128)(2,1)S(1)} %bitcast.18, bf16[128,384]{1,0:T(8,128)(2,1)S(1)} %copy-done.9, bf16[17,16,128]{2,1,0:T(8,128)(2,1)S(1)} %collective-permute-done.2.after_first.y_first, bf16[17,16,128]{2,1,0:T(8,128)(2,1)S(1)} %collective-permute-done.3.after_second.y_second), custom_call_target="tpu_custom_call" | custom-call | flops 40000000 | bytes 600000 | tf_op jit(solution)/shard_map/pallas_call | solution.py:875
  66.7 3.8 %all-to-all-start.3 = ((bf16[16,8,640]{2,1,0:T(8,128)(2,1)}), bf16[16,8,640]{2,1,0:T(8,128)(2,1)S(1)}, u32[]{:S(2)}, u32[]{:S(2)}) async-start(bf16[16,8,640]{2,1,0:T(8,128)(2,1)} %bitcast.10), calls=%async_computation.3 | async-start | bytes 327680 | tf_op jit(solution)/shard_map/all_to_all | solution.py:883
  70.6 1.8 %shard_map.245 = (f32[3,10,24,128]{3,2,1,0:T(8,128)S(1)}, f32[3,10,24,128]{3,2,1,0:T(8,128)S(1)}, f32[10,24,128]{2,1,0:T(8,128)S(1)}, f32[8,16,128]{2,1,0:T(8,128)S(1)}, f32[3,8,16,128]{3,2,1,0:T(8,128)S(1)}) custom-call(s32[64]{0:T(128)S(1)} %copy-done.16, f32[3,2,64]{2,1,0:T(2,128)S(1)} %bitcast.21, f32[3,8,16,128]{3,2,1,0:T(8,128)S(1)} %copy-done.1, ...), custom_call_target="tpu_custom_call" | custom-call | flops 10000000 | bytes 3000000 | tf_op jit(solution)/shard_map/pallas_call | solution.py:884
  72.4 4.7 %all-to-all-done.3 = bf16[16,8,640]{2,1,0:T(8,128)(2,1)S(1)} async-done(((bf16[16,8,640]{2,1,0:T(8,128)(2,1)}), bf16[16,8,640]{2,1,0:T(8,128)(2,1)S(1)}, u32[]{:S(2)}, u32[]{:S(2)}) %all-to-all-start.3) | async-done | bytes 163872 | tf_op jit(solution)/shard_map/all_to_all | solution.py:883
  77.0 1.2 %shard_map.246 = (f32[3,8,16,128]{3,2,1,0:T(8,128)}, f32[3,8,16,128]{3,2,1,0:T(8,128)}, f32[8,16,128]{2,1,0:T(8,128)}, f32[3,2,64]{2,1,0:T(2,128)}) custom-call(bf16[128,640]{1,0:T(8,128)(2,1)S(1)} %bitcast.14, bf16[128,128]{1,0:T(8,128)(2,1)S(1)} %copy-done.12, bf16[128,256]{1,0:T(8,128)(2,1)S(1)} %copy-done.11, ...), custom_call_target="tpu_custom_call" | custom-call | flops 40000000 | bytes 4000000 | tf_op jit(solution)/shard_map/pallas_call | solution.py:899
  (45 shorter events, 0.2 us)
Async XLA Ops:
  0.6 12.8 %copy-start = (f32[3,8,16,128]{3,2,1,0:T(8,128)S(1)}, f32[3,8,16,128]{3,2,1,0:T(8,128)}, u32[]{:S(2)}) copy-start(f32[3,8,16,128]{3,2,1,0:T(8,128)} %magnetic.5) | copy-start | bytes 589828
  3.0 10.5 %copy-start.1 = (f32[3,8,16,128]{3,2,1,0:T(8,128)S(1)}, f32[3,8,16,128]{3,2,1,0:T(8,128)}, u32[]{:S(2)}) copy-start(f32[3,8,16,128]{3,2,1,0:T(8,128)} %get-tuple-element.28.field.electric) | copy-start | bytes 589828
  3.0 10.5 %copy-start.19 = (f32[8]{0:T(128)S(1)}, f32[8]{0:T(128)}, u32[]{:S(2)}) copy-start(f32[8]{0:T(128)} %perm_in.1) | copy-start | bytes 100
  3.0 10.5 %copy-start.20 = (s32[64]{0:T(128)S(1)}, s32[64]{0:T(128)}, u32[]{:S(2)}) copy-start(s32[64]{0:T(128)} %src_in.1) | copy-start | bytes 772
  3.0 16.4 %all-to-all-start = ((bf16[16,24,128]{2,1,0:T(8,128)(2,1)}), bf16[16,24,128]{2,1,0:T(8,128)(2,1)S(1)}, u32[]{:S(2)}, u32[]{:S(2)}) async-start(bf16[16,24,128]{2,1,0:T(8,128)(2,1)} %bitcast.23), calls=%async_computation | async-start | bytes 196608 | tf_op jit(solution)/shard_map/all_to_all | solution.py:810
  13.5 5.9 %copy-start.4 = (bf16[512,256]{1,0:T(8,128)(2,1)S(1)}, bf16[512,256]{1,0:T(8,128)(2,1)}, u32[]{:S(2)}) copy-start(bf16[512,256]{1,0:T(8,128)(2,1)} %constant.19.clone.table) | copy-start | bytes 786436
  20.7 14.0 %copy-start.2 = (bf16[2,3,8,16,128]{4,3,2,1,0:T(8,128)(2,1)S(1)}, bf16[2,3,8,16,128]{4,3,2,1,0:T(8,128)(2,1)}, u32[]{:S(2)}) copy-start(bf16[2,3,8,16,128]{4,3,2,1,0:T(8,128)(2,1)} %saved.5) | copy-start | bytes 589828
  20.7 29.0 %all-to-all-start.1 = ((bf16[32,8,256]{2,1,0:T(8,128)(2,1)}), bf16[32,8,256]{2,1,0:T(8,128)(2,1)S(1)}, u32[]{:S(2)}, u32[]{:S(2)}) async-start(bf16[32,8,256]{2,1,0:T(8,128)(2,1)} %bitcast.3), calls=%async_computation.1 | async-start | bytes 262144 | tf_op jit(solution)/shard_map/all_to_all | solution.py:828
  34.7 5.7 %copy-start.3 = (bf16[2,128,256]{2,1,0:T(8,128)(2,1)S(1)}, bf16[2,128,256]{2,1,0:T(8,128)(2,1)}, u32[]{:S(2)}) copy-start(bf16[2,128,256]{2,1,0:T(8,128)(2,1)} %constant.20.clone.at_x) | copy-start | bytes 393220
  34.7 5.7 %copy-start.5 = (bf16[4,2,48,256]{3,2,1,0:T(8,128)(2,1)S(1)}, bf16[4,2,48,256]{3,2,1,0:T(8,128)(2,1)}, u32[]{:S(2)}) copy-start(bf16[4,2,48,256]{3,2,1,0:T(8,128)(2,1)} %constant.21.clone.at_y) | copy-start | bytes 589828
  34.7 5.7 %copy-start.6 = (bf16[2,48,16,16]{1,3,2,0:T(8,128)(2,1)S(1)}, bf16[2,48,16,16]{1,3,2,0:T(8,128)(2,1)}, u32[]{:S(2)}) copy-start(bf16[2,48,16,16]{1,3,2,0:T(8,128)(2,1)} %param.32) | copy-start | bytes 147460
  34.8 5.7 %copy-start.7 = (bf16[16,2,16,128]{3,2,1,0:T(8,128)(2,1)S(1)}, bf16[16,2,16,128]{3,2,1,0:T(8,128)(2,1)}, u32[]{:S(2)}) copy-start(bf16[16,2,16,128]{3,2,1,0:T(8,128)(2,1)} %constant.22.clone.at_z) | copy-start | bytes 393220
  34.8 5.7 %copy-start.8 = (bf16[4,2,64,128]{3,2,1,0:T(8,128)(2,1)S(1)}, bf16[4,2,64,128]{3,2,1,0:T(8,128)(2,1)}, u32[]{:S(2)}) copy-start(bf16[4,2,64,128]{3,2,1,0:T(8,128)(2,1)} %constant.23.clone.inv_x) | copy-start | bytes 393220
  34.8 5.7 %copy-start.14 = (f32[16,48]{1,0:T(8,128)S(1)}, f32[16,48]{1,0:T(8,128)}, u32[]{:S(2)}) copy-start(f32[16,48]{1,0:T(8,128)} %gain_x.1) | copy-start | bytes 9220
  34.8 5.7 %copy-start.15 = (f32[16,48]{1,0:T(8,128)S(1)}, f32[16,48]{1,0:T(8,128)}, u32[]{:S(2)}) copy-start(f32[16,48]{1,0:T(8,128)} %gain_y.1) | copy-start | bytes 9220
  34.9 7.9 %collective-permute-start = (bf16[17,16,128]{2,1,0:T(8,128)(2,1)S(1)}, bf16[17,16,128]{2,1,0:T(8,128)(2,1)S(1)}, u32[]{:S(2)}, u32[]{:S(2)}) collective-permute-start(bf16[17,16,128]{2,1,0:T(8,128)(2,1)S(1)} %get-tuple-element.36), channel_id=1, source_target_pairs={{0,16},{16,0},{32,48},{48,32},{64,80},{80,64},{96,112},{112,96},{1... | collective-permute-start | bytes 208904 | tf_op jit(solution)/shard_map/ppermute | solution.py:770
  39.7 3.1 %collective-permute-start.1 = (bf16[17,16,128]{2,1,0:T(8,128)(2,1)S(1)}, bf16[17,16,128]{2,1,0:T(8,128)(2,1)S(1)}, u32[]{:S(2)}, u32[]{:S(2)}) collective-permute-start(bf16[17,16,128]{2,1,0:T(8,128)(2,1)S(1)} %get-tuple-element.37), channel_id=1, source_target_pairs={{16,32},{48,64},{80,96},{112,128},{144,160},{176,192},{208,224},{2... | collective-permute-start | bytes 208904 | tf_op jit(solution)/shard_map/ppermute | solution.py:771
  49.6 15.6 %copy-start.9 = (bf16[128,384]{1,0:T(8,128)(2,1)S(1)}, bf16[128,384]{1,0:T(8,128)(2,1)}, u32[]{:S(2)}) copy-start(bf16[128,384]{1,0:T(8,128)(2,1)} %constant.24.clone.inv_y) | copy-start | bytes 294916
  50.9 14.3 %all-to-all-start.2 = ((bf16[4,16,256]{2,1,0:T(8,128)(2,1)}), bf16[4,16,256]{2,1,0:T(8,128)(2,1)S(1)}, u32[]{:S(2)}, u32[]{:S(2)}) async-start(bf16[4,16,256]{2,1,0:T(8,128)(2,1)} %bitcast.8), calls=%async_computation.2 | async-start | bytes 65536 | tf_op jit(solution)/shard_map/all_to_all | solution.py:781
  55.2 6.3 %collective-permute-start.2 = (bf16[17,16,128]{2,1,0:T(8,128)(2,1)S(1)}, bf16[17,16,128]{2,1,0:T(8,128)(2,1)S(1)}, u32[]{:S(2)}, u32[]{:S(2)}) collective-permute-start(bf16[17,16,128]{2,1,0:T(8,128)(2,1)S(1)} %get-tuple-element.38.after), channel_id=1, source_target_pairs={{0,1},{1,0},{2,3},{3,2},{4,5},{5,4},{6,7},{7,6},{8,9},{9,8},{10,11... | collective-permute-start | bytes 208904 | tf_op jit(solution)/shard_map/ppermute | solution.py:770
  59.6 5.6 %collective-permute-start.3 = (bf16[17,16,128]{2,1,0:T(8,128)(2,1)S(1)}, bf16[17,16,128]{2,1,0:T(8,128)(2,1)S(1)}, u32[]{:S(2)}, u32[]{:S(2)}) collective-permute-start(bf16[17,16,128]{2,1,0:T(8,128)(2,1)S(1)} %get-tuple-element.39), channel_id=1, source_target_pairs={{1,2},{3,4},{5,6},{7,8},{9,10},{11,12},{13,14},{2,1},{4,3},{6,5},{... | collective-permute-start | bytes 208904 | tf_op jit(solution)/shard_map/ppermute | solution.py:771
  66.7 10.3 %all-to-all-start.3 = ((bf16[16,8,640]{2,1,0:T(8,128)(2,1)}), bf16[16,8,640]{2,1,0:T(8,128)(2,1)S(1)}, u32[]{:S(2)}, u32[]{:S(2)}) async-start(bf16[16,8,640]{2,1,0:T(8,128)(2,1)} %bitcast.10), calls=%async_computation.3 | async-start | bytes 327680 | tf_op jit(solution)/shard_map/all_to_all | solution.py:883
  70.6 6.4 %copy-start.11 = (bf16[128,256]{1,0:T(8,128)(2,1)S(1)}, bf16[128,256]{1,0:T(8,128)(2,1)}, u32[]{:S(2)}) copy-start(bf16[128,256]{1,0:T(8,128)(2,1)} %constant.26.clone.apart) | copy-start | bytes 196612
  70.6 6.4 %copy-start.12 = (bf16[128,128]{1,0:T(8,128)(2,1)S(1)}, bf16[128,128]{1,0:T(8,128)(2,1)}, u32[]{:S(2)}) copy-start(bf16[128,128]{1,0:T(8,128)(2,1)} %constant.25.clone.table) | copy-start | bytes 98308
  (5 other events, 8.8 us)

commit v12 on v10

--- a/solution.py
+++ b/solution.py
@@ -884,7 +884,7 @@
         "ssvvvvvvvva",
         [pltpu.VMEM((3, 12, 24, NZ), F32)] * 2 + [pltpu.VMEM((12, 24, NZ), F32)],
         10_000_000,
-        3_000_000,
+        60_000_000,
     )(
         monitor_cells, weights, field, seed_magnetic, inverse, saved_magnetic,
         x_low, x_high, y_first, y_second, sent,

time: 77 us -> 77.1 us (level)
  no operation moved by 1% of the time
where the time goes in v12:
time: 77.1 us; the launch traced here: 76.6 us
  starting transfers between devices  47.2 us (61%)
  waiting for transfers between devices  14.5 us (19%)
  Pallas kernels  12.2 us (16%)
  local copies, waits for them, and re-layouts  1.57 us (2%)
  between operations  0.95 us (1%)
    all_to_all x1, starting transfers between devices, body(): lax.all_to_all(dealt, 'bulk', split_axis=0, concat_axis=0, tiled=True)  14.3 us
    all_to_all x1, starting transfers between devices, body(): lax.all_to_all(payload, 'wide', split_axis=0, concat_axis=0, tiled=True)  10.4 us
    ppermute x2, starting transfers between devices, passed_along(): return lax.ppermute(block, axis, route)  6.07 us
    all_to_all x1, starting transfers between devices, body(): lax.all_to_all(sent, 'wide', split_axis=0, concat_axis=0, tiled=True)  5.5 us
    ppermute x1, starting transfers between devices, body(): lax.ppermute(second_part, 'wide', pairs + [(j, i) for i, j in pairs])  4.46 us
    all_to_all x1, starting transfers between devices, dealt_near(): lax.all_to_all(block, 'bulk', split_axis=0, concat_axis=0, axis_index_gro...  4.27 us
    all_to_all x1, waiting for transfers between devices, body(): lax.all_to_all(payload, 'wide', split_axis=0, concat_axis=0, tiled=True)  3.83 us
    all_to_all x1, waiting for transfers between devices, body(): lax.all_to_all(dealt, 'bulk', split_axis=0, concat_axis=0, tiled=True)  3.25 us
  transfers between devices with their start and end apart: 8, of which 6 were waited for; matrix products, arithmetic and copies ran while one was open for 0% of the time, Pallas kernels for 6%

profile of v12, /device:TPU:1, one launch (start us, length us, event | category | flops | bytes accessed | tf_op | source)
XLA Modules:
  0.0 76.6 jit_solution(9626649408177499142)
XLA Ops:
  0.6 2.3 %shard_map.237 = (bf16[384,128]{1,0:T(8,128)(2,1)}, f32[3,8,16,128]{3,2,1,0:T(8,128)}) custom-call(s32[64]{0:T(128)} %mon.3, f32[3,2,64]{2,1,0:T(2,128)} %bitcast.19, f32[3,8,16,128]{3,2,1,0:T(8,128)} %electric.1, bf16[128,128]{1,0:T(8,128)(2,1)} %constant.18.clone.table_in), custom_call_target="tpu_custom_call" | custom-call | flops 13000000 | bytes 500000 | tf_op jit(solution)/shard_map/pallas_call | solution.py:789
  3.0 10.4 %all-to-all-start = ((bf16[16,24,128]{2,1,0:T(8,128)(2,1)}), bf16[16,24,128]{2,1,0:T(8,128)(2,1)S(1)}, u32[]{:S(2)}, u32[]{:S(2)}) async-start(bf16[16,24,128]{2,1,0:T(8,128)(2,1)} %bitcast.23), calls=%async_computation | async-start | bytes 196608 | tf_op jit(solution)/shard_map/all_to_all | solution.py:801
  13.4 0.9 %copy-done.10 = s32[8,16,128]{2,1,0:T(8,128)S(1)} copy-done((s32[8,16,128]{2,1,0:T(8,128)S(1)}, s32[8,16,128]{2,1,0:T(8,128)}, u32[]{:S(2)}) %copy-start.10) | copy-done | bytes 65560
  14.3 1.1 %shard_map.238 = (f32[8,128]{1,0:T(8,128)S(1)}, f32[8,16,128]{2,1,0:T(8,128)S(1)}) custom-call(s32[64]{0:T(128)S(1)} %copy-done.20, f32[8]{0:T(128)S(1)} %copy-done.19, f32[3,8,16,128]{3,2,1,0:T(8,128)S(1)} %copy-done.1, f32[3,8,16,128]{3,2,1,0:T(8,128)S(1)} %copy-done, s32[8,16,128]{2,1,0:T(8,128)S(1)} %copy-done.10), custom_call_target="tpu_custom_call" | custom-call | flops 3000000 | bytes 1500000 | tf_op jit(solution)/shard_map/pallas_call | solution.py:803
  15.4 3.8 %all-to-all-done = bf16[16,24,128]{2,1,0:T(8,128)(2,1)S(1)} async-done(((bf16[16,24,128]{2,1,0:T(8,128)(2,1)}), bf16[16,24,128]{2,1,0:T(8,128)(2,1)S(1)}, u32[]{:S(2)}, u32[]{:S(2)}) %all-to-all-start) | async-done | bytes 98336 | tf_op jit(solution)/shard_map/all_to_all | solution.py:801
  19.3 1.3 %shard_map.239.after = bf16[256,256]{1,0:T(8,128)(2,1)} custom-call(bf16[384,128]{1,0:T(8,128)(2,1)S(1)} %bitcast.16, f32[8,128]{1,0:T(8,128)S(1)} %get-tuple-element.29.taken, bf16[512,256]{1,0:T(8,128)(2,1)S(1)} %copy-done.4), custom_call_target="tpu_custom_call" | custom-call | flops 20000000 | bytes 400000 | tf_op jit(solution)/shard_map/pallas_call | solution.py:816
  20.6 14.3 %all-to-all-start.1 = ((bf16[32,8,256]{2,1,0:T(8,128)(2,1)}), bf16[32,8,256]{2,1,0:T(8,128)(2,1)S(1)}, u32[]{:S(2)}, u32[]{:S(2)}) async-start(bf16[32,8,256]{2,1,0:T(8,128)(2,1)} %bitcast.3), calls=%async_computation.1 | async-start | bytes 262144 | tf_op jit(solution)/shard_map/all_to_all | solution.py:819
  35.0 4.8 %collective-permute-start = (bf16[17,16,128]{2,1,0:T(8,128)(2,1)S(1)}, bf16[17,16,128]{2,1,0:T(8,128)(2,1)S(1)}, u32[]{:S(2)}, u32[]{:S(2)}) collective-permute-start(bf16[17,16,128]{2,1,0:T(8,128)(2,1)S(1)} %get-tuple-element.36), channel_id=1, source_target_pairs={{0,16},{16,32},{32,48},{48,64},{64,80},{80,96},{96,112},{112,128},... | collective-permute-start | bytes 208904 | tf_op jit(solution)/shard_map/ppermute | solution.py:763
  39.8 1.3 %collective-permute-start.1 = (bf16[10,16,128]{2,1,0:T(8,128)(2,1)S(1)}, bf16[10,16,128]{2,1,0:T(8,128)(2,1)S(1)}, u32[]{:S(2)}, u32[]{:S(2)}) collective-permute-start(bf16[10,16,128]{2,1,0:T(8,128)(2,1)S(1)} %get-tuple-element.37), channel_id=1, source_target_pairs={{16,0},{32,16},{48,32},{64,48},{80,64},{96,80},{112,96},{128,112},... | collective-permute-start | bytes 122888 | tf_op jit(solution)/shard_map/ppermute | solution.py:763
  41.3 0.6 copy-done.17
  41.9 1.7 %shard_map.240 = (f32[360,128]{1,0:T(8,128)S(1)}, f32[360,128]{1,0:T(8,128)S(1)}, bf16[128,128]{1,0:T(8,128)(2,1)S(1)}, f32[40,128]{1,0:T(8,128)S(1)}, f32[8,128...) custom-call(s32[64]{0:T(128)S(1)} %copy-done.16, f32[3,2,64]{2,1,0:T(2,128)S(1)} %bitcast.20, f32[3,16]{1,0:T(4,128)S(1)} %bitcast.22, ...), custom_call_target="tpu_custom_call" | custom-call | flops 20000000 | bytes 1000000 | tf_op jit(solution)/shard_map/pallas_call | solution.py:822
  43.5 2.9 %collective-permute-done.1.x_high = bf16[10,16,128]{2,1,0:T(8,128)(2,1)S(1)} collective-permute-done((bf16[10,16,128]{2,1,0:T(8,128)(2,1)S(1)}, bf16[10,16,128]{2,1,0:T(8,128)(2,1)S(1)}, u32[]{:S(2)}, u32[]{:S(2)}) %collective-permute-start.1) | collective-permute-done | bytes 40992 | tf_op jit(solution)/shard_map/ppermute | solution.py:763
  46.6 3.2 %all-to-all-done.1 = bf16[32,8,256]{2,1,0:T(8,128)(2,1)S(1)} async-done(((bf16[32,8,256]{2,1,0:T(8,128)(2,1)}), bf16[32,8,256]{2,1,0:T(8,128)(2,1)S(1)}, u32[]{:S(2)}, u32[]{:S(2)}) %all-to-all-start.1) | async-done | bytes 131104 | tf_op jit(solution)/shard_map/all_to_all | solution.py:819
  49.8 1.3 %shard_map.243 = bf16[64,256]{1,0:T(8,128)(2,1)} custom-call(bf16[256,256]{1,0:T(8,128)(2,1)S(1)} %bitcast.15, f32[360,128]{1,0:T(8,128)S(1)} %get-tuple-element.30.after.coef_a, f32[360,128]{1,0:T(8,128)S(1)} %get-tuple-element.31.coef_b, bf16[2,128,256]{2,1,0:T(8,128)(2,1)S(1)} %copy-done.3, bf16[64,128]{1,0:T(8,128)(2,1)S(1)} %get-tuple-element.32.back_x, ...), custom_call_target="tpu_custom_call" | custom-call | flops 40000000 | bytes 600000 | tf_op jit(solution)/shard_map/pallas_call | solution.py:857
  51.1 4.3 %all-to-all-start.2 = ((bf16[4,16,256]{2,1,0:T(8,128)(2,1)}), bf16[4,16,256]{2,1,0:T(8,128)(2,1)S(1)}, u32[]{:S(2)}, u32[]{:S(2)}) async-start(bf16[4,16,256]{2,1,0:T(8,128)(2,1)} %bitcast.8), calls=%async_computation.2 | async-start | bytes 65536 | tf_op jit(solution)/shard_map/all_to_all | solution.py:772
  55.4 4.5 %collective-permute-start.2 = (bf16[17,16,128]{2,1,0:T(8,128)(2,1)S(1)}, bf16[17,16,128]{2,1,0:T(8,128)(2,1)S(1)}, u32[]{:S(2)}, u32[]{:S(2)}) collective-permute-start(bf16[17,16,128]{2,1,0:T(8,128)(2,1)S(1)} %get-tuple-element.39), channel_id=1, source_target_pairs={{1,2},{3,4},{5,6},{7,8},{9,10},{11,12},{13,14},{2,1},{4,3},{6,5},{... | collective-permute-start | bytes 208904 | tf_op jit(solution)/shard_map/ppermute | solution.py:867
  59.8 2.1 %collective-permute-done.2.after.y_second = bf16[17,16,128]{2,1,0:T(8,128)(2,1)S(1)} collective-permute-done((bf16[17,16,128]{2,1,0:T(8,128)(2,1)S(1)}, bf16[17,16,128]{2,1,0:T(8,128)(2,1)S(1)}, u32[]{:S(2)}, u32[]{:S(2)}) %collective-permute-start.2) | collective-permute-done | bytes 69664 | tf_op jit(solution)/shard_map/ppermute | solution.py:867
  61.9 1.5 %shard_map.244.after = bf16[128,640]{1,0:T(8,128)(2,1)} custom-call(bf16[64,256]{1,0:T(8,128)(2,1)S(1)} %bitcast.17, bf16[128,384]{1,0:T(8,128)(2,1)S(1)} %copy-done.9, bf16[17,16,128]{2,1,0:T(8,128)(2,1)S(1)} %collective-permute-done.2.after.y_second), custom_call_target="tpu_custom_call" | custom-call | flops 40000000 | bytes 600000 | tf_op jit(solution)/shard_map/pallas_call | solution.py:869
  63.4 5.5 %all-to-all-start.3 = ((bf16[16,8,640]{2,1,0:T(8,128)(2,1)}), bf16[16,8,640]{2,1,0:T(8,128)(2,1)S(1)}, u32[]{:S(2)}, u32[]{:S(2)}) async-start(bf16[16,8,640]{2,1,0:T(8,128)(2,1)} %bitcast.10), calls=%async_computation.3 | async-start | bytes 327680 | tf_op jit(solution)/shard_map/all_to_all | solution.py:877
  68.9 2.3 %collective-permute-start.3 = (bf16[17,16,128]{2,1,0:T(8,128)(2,1)S(1)}, bf16[17,16,128]{2,1,0:T(8,128)(2,1)S(1)}, u32[]{:S(2)}, u32[]{:S(2)}) collective-permute-start(bf16[17,16,128]{2,1,0:T(8,128)(2,1)S(1)} %get-tuple-element.38.after), channel_id=1, source_target_pairs={{0,1},{1,0},{2,3},{3,2},{4,5},{5,4},{6,7},{7,6},{8,9},{9,8},{10,11... | collective-permute-start | bytes 208904 | tf_op jit(solution)/shard_map/ppermute | solution.py:865
  71.2 1.0 %collective-permute-done.3.y_first = bf16[17,16,128]{2,1,0:T(8,128)(2,1)S(1)} collective-permute-done((bf16[17,16,128]{2,1,0:T(8,128)(2,1)S(1)}, bf16[17,16,128]{2,1,0:T(8,128)(2,1)S(1)}, u32[]{:S(2)}, u32[]{:S(2)}) %collective-permute-start.3) | collective-permute-done | bytes 69664 | tf_op jit(solution)/shard_map/ppermute | solution.py:865
  72.2 1.7 %shard_map.245 = (f32[3,10,24,128]{3,2,1,0:T(8,128)S(1)}, f32[3,10,24,128]{3,2,1,0:T(8,128)S(1)}, f32[10,24,128]{2,1,0:T(8,128)S(1)}, f32[8,16,128]{2,1,0:T(8,128)S(1)}, f32[3,8,16,128]{3,2,1,0:T(8,128)S(1)}) custom-call(s32[64]{0:T(128)S(1)} %copy-done.16, f32[3,2,64]{2,1,0:T(2,128)S(1)} %bitcast.21, f32[3,8,16,128]{3,2,1,0:T(8,128)S(1)} %copy-done.1, ...), custom_call_target="tpu_custom_call" | custom-call | flops 10000000 | bytes 60000000 | tf_op jit(solution)/shard_map/pallas_call | solution.py:878
  74.0 1.4 %all-to-all-done.3 = bf16[16,8,640]{2,1,0:T(8,128)(2,1)S(1)} async-done(((bf16[16,8,640]{2,1,0:T(8,128)(2,1)}), bf16[16,8,640]{2,1,0:T(8,128)(2,1)S(1)}, u32[]{:S(2)}, u32[]{:S(2)}) %all-to-all-start.3) | async-done | bytes 163872 | tf_op jit(solution)/shard_map/all_to_all | solution.py:877
  75.4 1.2 %shard_map.246 = (f32[3,8,16,128]{3,2,1,0:T(8,128)}, f32[3,8,16,128]{3,2,1,0:T(8,128)}, f32[8,16,128]{2,1,0:T(8,128)}, f32[3,2,64]{2,1,0:T(2,128)}) custom-call(bf16[128,640]{1,0:T(8,128)(2,1)S(1)} %bitcast.14, bf16[128,128]{1,0:T(8,128)(2,1)S(1)} %copy-done.12, bf16[128,256]{1,0:T(8,128)(2,1)S(1)} %copy-done.11, ...), custom_call_target="tpu_custom_call" | custom-call | flops 40000000 | bytes 4000000 | tf_op jit(solution)/shard_map/pallas_call | solution.py:893
  (45 shorter events, 0.3 us)
Async XLA Ops:
  0.6 12.7 %copy-start = (f32[3,8,16,128]{3,2,1,0:T(8,128)S(1)}, f32[3,8,16,128]{3,2,1,0:T(8,128)}, u32[]{:S(2)}) copy-start(f32[3,8,16,128]{3,2,1,0:T(8,128)} %magnetic.5) | copy-start | bytes 589828
  3.0 10.4 %copy-start.1 = (f32[3,8,16,128]{3,2,1,0:T(8,128)S(1)}, f32[3,8,16,128]{3,2,1,0:T(8,128)}, u32[]{:S(2)}) copy-start(f32[3,8,16,128]{3,2,1,0:T(8,128)} %get-tuple-element.28.field.electric) | copy-start | bytes 589828
  3.0 10.4 %copy-start.19 = (f32[8]{0:T(128)S(1)}, f32[8]{0:T(128)}, u32[]{:S(2)}) copy-start(f32[8]{0:T(128)} %perm_in.1) | copy-start | bytes 100
  3.0 10.4 %copy-start.20 = (s32[64]{0:T(128)S(1)}, s32[64]{0:T(128)}, u32[]{:S(2)}) copy-start(s32[64]{0:T(128)} %src_in.1) | copy-start | bytes 772
  3.0 16.3 %all-to-all-start = ((bf16[16,24,128]{2,1,0:T(8,128)(2,1)}), bf16[16,24,128]{2,1,0:T(8,128)(2,1)S(1)}, u32[]{:S(2)}, u32[]{:S(2)}) async-start(bf16[16,24,128]{2,1,0:T(8,128)(2,1)} %bitcast.23), calls=%async_computation | async-start | bytes 196608 | tf_op jit(solution)/shard_map/all_to_all | solution.py:801
  13.4 5.9 %copy-start.4 = (bf16[512,256]{1,0:T(8,128)(2,1)S(1)}, bf16[512,256]{1,0:T(8,128)(2,1)}, u32[]{:S(2)}) copy-start(bf16[512,256]{1,0:T(8,128)(2,1)} %constant.19.clone.table) | copy-start | bytes 786436
  20.6 14.3 %copy-start.2 = (bf16[2,3,8,16,128]{4,3,2,1,0:T(8,128)(2,1)S(1)}, bf16[2,3,8,16,128]{4,3,2,1,0:T(8,128)(2,1)}, u32[]{:S(2)}) copy-start(bf16[2,3,8,16,128]{4,3,2,1,0:T(8,128)(2,1)} %saved.5) | copy-start | bytes 589828
  20.6 29.2 %all-to-all-start.1 = ((bf16[32,8,256]{2,1,0:T(8,128)(2,1)}), bf16[32,8,256]{2,1,0:T(8,128)(2,1)S(1)}, u32[]{:S(2)}, u32[]{:S(2)}) async-start(bf16[32,8,256]{2,1,0:T(8,128)(2,1)} %bitcast.3), calls=%async_computation.1 | async-start | bytes 262144 | tf_op jit(solution)/shard_map/all_to_all | solution.py:819
  34.9 6.3 %copy-start.3 = (bf16[2,128,256]{2,1,0:T(8,128)(2,1)S(1)}, bf16[2,128,256]{2,1,0:T(8,128)(2,1)}, u32[]{:S(2)}) copy-start(bf16[2,128,256]{2,1,0:T(8,128)(2,1)} %constant.20.clone.at_x) | copy-start | bytes 393220
  34.9 6.3 %copy-start.5 = (bf16[4,2,48,256]{3,2,1,0:T(8,128)(2,1)S(1)}, bf16[4,2,48,256]{3,2,1,0:T(8,128)(2,1)}, u32[]{:S(2)}) copy-start(bf16[4,2,48,256]{3,2,1,0:T(8,128)(2,1)} %constant.21.clone.at_y) | copy-start | bytes 589828
  34.9 6.3 %copy-start.6 = (bf16[2,48,16,16]{1,3,2,0:T(8,128)(2,1)S(1)}, bf16[2,48,16,16]{1,3,2,0:T(8,128)(2,1)}, u32[]{:S(2)}) copy-start(bf16[2,48,16,16]{1,3,2,0:T(8,128)(2,1)} %param.32) | copy-start | bytes 147460
  34.9 6.3 %copy-start.7 = (bf16[16,2,16,128]{3,2,1,0:T(8,128)(2,1)S(1)}, bf16[16,2,16,128]{3,2,1,0:T(8,128)(2,1)}, u32[]{:S(2)}) copy-start(bf16[16,2,16,128]{3,2,1,0:T(8,128)(2,1)} %constant.22.clone.at_z) | copy-start | bytes 393220
  34.9 6.3 %copy-start.8 = (bf16[4,2,64,128]{3,2,1,0:T(8,128)(2,1)S(1)}, bf16[4,2,64,128]{3,2,1,0:T(8,128)(2,1)}, u32[]{:S(2)}) copy-start(bf16[4,2,64,128]{3,2,1,0:T(8,128)(2,1)} %constant.23.clone.inv_x) | copy-start | bytes 393220
  34.9 6.3 %copy-start.14 = (f32[16,48]{1,0:T(8,128)S(1)}, f32[16,48]{1,0:T(8,128)}, u32[]{:S(2)}) copy-start(f32[16,48]{1,0:T(8,128)} %gain_x.1) | copy-start | bytes 9220
  35.0 6.3 %copy-start.15 = (f32[16,48]{1,0:T(8,128)S(1)}, f32[16,48]{1,0:T(8,128)}, u32[]{:S(2)}) copy-start(f32[16,48]{1,0:T(8,128)} %gain_y.1) | copy-start | bytes 9220
  35.0 6.3 %copy-start.18 = (f32[3,16]{1,0:T(4,128)S(1)}, f32[3,16]{1,0:T(4,128)}, u32[]{:S(2)}) copy-start(f32[3,16]{1,0:T(4,128)} %project.1) | copy-start | bytes 580
  35.0 11.4 %collective-permute-start = (bf16[17,16,128]{2,1,0:T(8,128)(2,1)S(1)}, bf16[17,16,128]{2,1,0:T(8,128)(2,1)S(1)}, u32[]{:S(2)}, u32[]{:S(2)}) collective-permute-start(bf16[17,16,128]{2,1,0:T(8,128)(2,1)S(1)} %get-tuple-element.36), channel_id=1, source_target_pairs={{0,16},{16,32},{32,48},{48,64},{64,80},{80,96},{96,112},{112,128},... | collective-permute-start | bytes 208904 | tf_op jit(solution)/shard_map/ppermute | solution.py:763
  39.8 6.6 %collective-permute-start.1 = (bf16[10,16,128]{2,1,0:T(8,128)(2,1)S(1)}, bf16[10,16,128]{2,1,0:T(8,128)(2,1)S(1)}, u32[]{:S(2)}, u32[]{:S(2)}) collective-permute-start(bf16[10,16,128]{2,1,0:T(8,128)(2,1)S(1)} %get-tuple-element.37), channel_id=1, source_target_pairs={{16,0},{32,16},{48,32},{64,48},{80,64},{96,80},{112,96},{128,112},... | collective-permute-start | bytes 122888 | tf_op jit(solution)/shard_map/ppermute | solution.py:763
  49.8 12.1 %copy-start.9 = (bf16[128,384]{1,0:T(8,128)(2,1)S(1)}, bf16[128,384]{1,0:T(8,128)(2,1)}, u32[]{:S(2)}) copy-start(bf16[128,384]{1,0:T(8,128)(2,1)} %constant.24.clone.inv_y) | copy-start | bytes 294916
  51.1 10.9 %all-to-all-start.2 = ((bf16[4,16,256]{2,1,0:T(8,128)(2,1)}), bf16[4,16,256]{2,1,0:T(8,128)(2,1)S(1)}, u32[]{:S(2)}, u32[]{:S(2)}) async-start(bf16[4,16,256]{2,1,0:T(8,128)(2,1)} %bitcast.8), calls=%async_computation.2 | async-start | bytes 65536 | tf_op jit(solution)/shard_map/all_to_all | solution.py:772
  55.4 6.6 %collective-permute-start.2 = (bf16[17,16,128]{2,1,0:T(8,128)(2,1)S(1)}, bf16[17,16,128]{2,1,0:T(8,128)(2,1)S(1)}, u32[]{:S(2)}, u32[]{:S(2)}) collective-permute-start(bf16[17,16,128]{2,1,0:T(8,128)(2,1)S(1)} %get-tuple-element.39), channel_id=1, source_target_pairs={{1,2},{3,4},{5,6},{7,8},{9,10},{11,12},{13,14},{2,1},{4,3},{6,5},{... | collective-permute-start | bytes 208904 | tf_op jit(solution)/shard_map/ppermute | solution.py:867
  63.4 12.0 %all-to-all-start.3 = ((bf16[16,8,640]{2,1,0:T(8,128)(2,1)}), bf16[16,8,640]{2,1,0:T(8,128)(2,1)S(1)}, u32[]{:S(2)}, u32[]{:S(2)}) async-start(bf16[16,8,640]{2,1,0:T(8,128)(2,1)} %bitcast.10), calls=%async_computation.3 | async-start | bytes 327680 | tf_op jit(solution)/shard_map/all_to_all | solution.py:877
  68.9 6.5 %copy-start.11 = (bf16[128,256]{1,0:T(8,128)(2,1)S(1)}, bf16[128,256]{1,0:T(8,128)(2,1)}, u32[]{:S(2)}) copy-start(bf16[128,256]{1,0:T(8,128)(2,1)} %constant.26.clone.apart) | copy-start | bytes 196612
  68.9 3.3 %collective-permute-start.3 = (bf16[17,16,128]{2,1,0:T(8,128)(2,1)S(1)}, bf16[17,16,128]{2,1,0:T(8,128)(2,1)S(1)}, u32[]{:S(2)}, u32[]{:S(2)}) collective-permute-start(bf16[17,16,128]{2,1,0:T(8,128)(2,1)S(1)} %get-tuple-element.38.after), channel_id=1, source_target_pairs={{0,1},{1,0},{2,3},{3,2},{4,5},{5,4},{6,7},{7,6},{8,9},{9,8},{10,11... | collective-permute-start | bytes 208904 | tf_op jit(solution)/shard_map/ppermute | solution.py:865
  (5 other events, 6.9 us)

commit v13 on v10

--- a/solution.py
+++ b/solution.py
@@ -854,15 +854,15 @@
         0,
         1_000_000,
     )(field, seed_magnetic, inverse, saved_magnetic, x_low, x_high, coef_a)
+    y_first = lax.ppermute(first_part, "wide", [(i, i ^ 1) for i in range(WIDE)])
     shares = call(
         filter_kernel, shape(NEAR * 16, 2 * LANES, dtype=BF16), "vvvvvvva", (), 40_000_000, 600_000
     )(
         gathered, coef_a, coef_b, tables_of("at_x"), back_x, phase_x, phase_yz,
-        first_part,
+        y_first,
     )
     back = dealt_near(shares)
 
-    y_first = lax.ppermute(first_part, "wide", [(i, i ^ 1) for i in range(WIDE)])
     pairs = [(i, i + 1) for i in range(1, WIDE - 1, 2)]
     y_second = lax.ppermute(second_part, "wide", pairs + [(j, i) for i, j in pairs])
 

time: 77 us -> 77.9 us (1.012); the launches traced: 76.4 us -> 76.5 us
  waiting for transfers between devices: 14.5 us -> 16 us
  starting transfers between devices: 47.1 us -> 45.7 us
    all_to_all x1, waiting for transfers between devices: 1.43 us -> 4.7 us  [body(): lax.all_to_all(sent, 'wide', split_axis=0, concat_axis=0, tiled=True)]
    all_to_all x1, waiting for transfers between devices: 3.25 us -> 0.01 us  [body(): lax.all_to_all(dealt, 'bulk', split_axis=0, concat_axis=0, tiled=True)]
    ppermute x1, starting transfers between devices: 2.26 us -> 4.29 us  [body(): lax.ppermute(first_part, 'wide', [(i, i ^ 1) for i in range(WIDE)])]
    ppermute x1, starting transfers between devices: 4.46 us -> 2.68 us  [body(): lax.ppermute(second_part, 'wide', pairs + [(j, i) for i, j in pairs])]
    all_to_all x1, starting transfers between devices: 5.5 us -> 3.97 us  [body(): lax.all_to_all(sent, 'wide', split_axis=0, concat_axis=0, tiled=True)]
    ppermute x1, waiting for transfers between devices: 2.11 us -> 3.64 us  [body(): lax.ppermute(second_part, 'wide', pairs + [(j, i) for i, j in pairs])]
  transfers between devices with their start and end apart: 8 -> 8, of which waited for: 6 -> 5; matrix products, arithmetic and copies ran while one was open for 0% -> 0% of each run, Pallas kernels for 6% -> 6%
where the time goes in v13:
time: 77.9 us; the launch traced here: 76.5 us
  starting transfers between devices  45.7 us (59%)
  waiting for transfers between devices  16 us (21%)
  Pallas kernels  12.2 us (16%)
  local copies, waits for them, and re-layouts  1.58 us (2%)
  between operations  0.96 us (1%)
    all_to_all x1, starting transfers between devices, body(): lax.all_to_all(dealt, 'bulk', split_axis=0, concat_axis=0, tiled=True)  14.3 us
    all_to_all x1, starting transfers between devices, body(): lax.all_to_all(payload, 'wide', split_axis=0, concat_axis=0, tiled=True)  10.4 us
    ppermute x2, starting transfers between devices, passed_along(): return lax.ppermute(block, axis, route)  6.07 us
    all_to_all x1, waiting for transfers between devices, body(): lax.all_to_all(sent, 'wide', split_axis=0, concat_axis=0, tiled=True)  4.7 us
    ppermute x1, starting transfers between devices, body(): lax.ppermute(first_part, 'wide', [(i, i ^ 1) for i in range(WIDE)])  4.29 us
    all_to_all x1, starting transfers between devices, dealt_near(): lax.all_to_all(block, 'bulk', split_axis=0, concat_axis=0, axis_index_gro...  4.12 us
    all_to_all x1, starting transfers between devices, body(): lax.all_to_all(sent, 'wide', split_axis=0, concat_axis=0, tiled=True)  3.97 us
    all_to_all x1, waiting for transfers between devices, body(): lax.all_to_all(payload, 'wide', split_axis=0, concat_axis=0, tiled=True)  3.83 us
  transfers between devices with their start and end apart: 8, of which 5 were waited for; matrix products, arithmetic and copies ran while one was open for 0% of the time, Pallas kernels for 6%

profile of v13, /device:TPU:1, one launch (start us, length us, event | category | flops | bytes accessed | tf_op | source)
XLA Modules:
  0.0 76.5 jit_solution(18018905355607238190)
XLA Ops:
  0.6 2.3 %shard_map.237 = (bf16[384,128]{1,0:T(8,128)(2,1)}, f32[3,8,16,128]{3,2,1,0:T(8,128)}) custom-call(s32[64]{0:T(128)} %mon.3, f32[3,2,64]{2,1,0:T(2,128)} %bitcast.19, f32[3,8,16,128]{3,2,1,0:T(8,128)} %electric.1, bf16[128,128]{1,0:T(8,128)(2,1)} %constant.18.clone.table_in), custom_call_target="tpu_custom_call" | custom-call | flops 13000000 | bytes 500000 | tf_op jit(solution)/shard_map/pallas_call | solution.py:789
  3.0 10.4 %all-to-all-start = ((bf16[16,24,128]{2,1,0:T(8,128)(2,1)}), bf16[16,24,128]{2,1,0:T(8,128)(2,1)S(1)}, u32[]{:S(2)}, u32[]{:S(2)}) async-start(bf16[16,24,128]{2,1,0:T(8,128)(2,1)} %bitcast.23), calls=%async_computation | async-start | bytes 196608 | tf_op jit(solution)/shard_map/all_to_all | solution.py:801
  13.4 0.9 %copy-done.10 = s32[8,16,128]{2,1,0:T(8,128)S(1)} copy-done((s32[8,16,128]{2,1,0:T(8,128)S(1)}, s32[8,16,128]{2,1,0:T(8,128)}, u32[]{:S(2)}) %copy-start.10) | copy-done | bytes 65560
  14.3 1.1 %shard_map.238 = (f32[8,128]{1,0:T(8,128)S(1)}, f32[8,16,128]{2,1,0:T(8,128)S(1)}) custom-call(s32[64]{0:T(128)S(1)} %copy-done.20, f32[8]{0:T(128)S(1)} %copy-done.19, f32[3,8,16,128]{3,2,1,0:T(8,128)S(1)} %copy-done.1, f32[3,8,16,128]{3,2,1,0:T(8,128)S(1)} %copy-done, s32[8,16,128]{2,1,0:T(8,128)S(1)} %copy-done.10), custom_call_target="tpu_custom_call" | custom-call | flops 3000000 | bytes 1500000 | tf_op jit(solution)/shard_map/pallas_call | solution.py:803
  15.4 3.8 %all-to-all-done = bf16[16,24,128]{2,1,0:T(8,128)(2,1)S(1)} async-done(((bf16[16,24,128]{2,1,0:T(8,128)(2,1)}), bf16[16,24,128]{2,1,0:T(8,128)(2,1)S(1)}, u32[]{:S(2)}, u32[]{:S(2)}) %all-to-all-start) | async-done | bytes 98336 | tf_op jit(solution)/shard_map/all_to_all | solution.py:801
  19.3 1.3 %shard_map.239.after = bf16[256,256]{1,0:T(8,128)(2,1)} custom-call(bf16[384,128]{1,0:T(8,128)(2,1)S(1)} %bitcast.16, f32[8,128]{1,0:T(8,128)S(1)} %get-tuple-element.29.taken, bf16[512,256]{1,0:T(8,128)(2,1)S(1)} %copy-done.4), custom_call_target="tpu_custom_call" | custom-call | flops 20000000 | bytes 400000 | tf_op jit(solution)/shard_map/pallas_call | solution.py:816
  20.6 14.3 %all-to-all-start.1 = ((bf16[32,8,256]{2,1,0:T(8,128)(2,1)}), bf16[32,8,256]{2,1,0:T(8,128)(2,1)S(1)}, u32[]{:S(2)}, u32[]{:S(2)}) async-start(bf16[32,8,256]{2,1,0:T(8,128)(2,1)} %bitcast.3), calls=%async_computation.1 | async-start | bytes 262144 | tf_op jit(solution)/shard_map/all_to_all | solution.py:819
  35.0 4.8 %collective-permute-start = (bf16[17,16,128]{2,1,0:T(8,128)(2,1)S(1)}, bf16[17,16,128]{2,1,0:T(8,128)(2,1)S(1)}, u32[]{:S(2)}, u32[]{:S(2)}) collective-permute-start(bf16[17,16,128]{2,1,0:T(8,128)(2,1)S(1)} %get-tuple-element.36), channel_id=1, source_target_pairs={{0,16},{16,32},{32,48},{48,64},{64,80},{80,96},{96,112},{112,128},... | collective-permute-start | bytes 208904 | tf_op jit(solution)/shard_map/ppermute | solution.py:763
  39.8 1.3 %collective-permute-start.1 = (bf16[10,16,128]{2,1,0:T(8,128)(2,1)S(1)}, bf16[10,16,128]{2,1,0:T(8,128)(2,1)S(1)}, u32[]{:S(2)}, u32[]{:S(2)}) collective-permute-start(bf16[10,16,128]{2,1,0:T(8,128)(2,1)S(1)} %get-tuple-element.37), channel_id=1, source_target_pairs={{16,0},{32,16},{48,32},{64,48},{80,64},{96,80},{112,96},{128,112},... | collective-permute-start | bytes 122888 | tf_op jit(solution)/shard_map/ppermute | solution.py:763
  41.2 0.6 copy-done.17
  41.8 1.7 %shard_map.240 = (f32[360,128]{1,0:T(8,128)S(1)}, f32[360,128]{1,0:T(8,128)S(1)}, bf16[128,128]{1,0:T(8,128)(2,1)S(1)}, f32[40,128]{1,0:T(8,128)S(1)}, f32[8,128...) custom-call(s32[64]{0:T(128)S(1)} %copy-done.16, f32[3,2,64]{2,1,0:T(2,128)S(1)} %bitcast.20, f32[3,16]{1,0:T(4,128)S(1)} %bitcast.22, ...), custom_call_target="tpu_custom_call" | custom-call | flops 20000000 | bytes 1000000 | tf_op jit(solution)/shard_map/pallas_call | solution.py:822
  43.5 2.9 %collective-permute-done.1.x_high = bf16[10,16,128]{2,1,0:T(8,128)(2,1)S(1)} collective-permute-done((bf16[10,16,128]{2,1,0:T(8,128)(2,1)S(1)}, bf16[10,16,128]{2,1,0:T(8,128)(2,1)S(1)}, u32[]{:S(2)}, u32[]{:S(2)}) %collective-permute-start.1) | collective-permute-done | bytes 40992 | tf_op jit(solution)/shard_map/ppermute | solution.py:763
  46.4 0.1 shard_map.242
  46.5 4.3 %collective-permute-start.2 = (bf16[17,16,128]{2,1,0:T(8,128)(2,1)S(1)}, bf16[17,16,128]{2,1,0:T(8,128)(2,1)S(1)}, u32[]{:S(2)}, u32[]{:S(2)}) collective-permute-start(bf16[17,16,128]{2,1,0:T(8,128)(2,1)S(1)} %get-tuple-element.38), channel_id=1, source_target_pairs={{0,1},{1,0},{2,3},{3,2},{4,5},{5,4},{6,7},{7,6},{8,9},{9,8},{10,11... | collective-permute-start | bytes 208904 | tf_op jit(solution)/shard_map/ppermute | solution.py:857
  50.8 0.9 %collective-permute-done.2.after.y_first = bf16[17,16,128]{2,1,0:T(8,128)(2,1)S(1)} collective-permute-done((bf16[17,16,128]{2,1,0:T(8,128)(2,1)S(1)}, bf16[17,16,128]{2,1,0:T(8,128)(2,1)S(1)}, u32[]{:S(2)}, u32[]{:S(2)}) %collective-permute-start.2) | collective-permute-done | bytes 69664 | tf_op jit(solution)/shard_map/ppermute | solution.py:857
  51.7 1.3 %shard_map.243 = bf16[64,256]{1,0:T(8,128)(2,1)} custom-call(bf16[256,256]{1,0:T(8,128)(2,1)S(1)} %bitcast.15, f32[360,128]{1,0:T(8,128)S(1)} %get-tuple-element.30.after.coef_a, f32[360,128]{1,0:T(8,128)S(1)} %get-tuple-element.31.coef_b, bf16[2,128,256]{2,1,0:T(8,128)(2,1)S(1)} %copy-done.3, bf16[64,128]{1,0:T(8,128)(2,1)S(1)} %get-tuple-element.32.back_x, ...), custom_call_target="tpu_custom_call" | custom-call | flops 40000000 | bytes 600000 | tf_op jit(solution)/shard_map/pallas_call | solution.py:858
  53.0 4.1 %all-to-all-start.2 = ((bf16[4,16,256]{2,1,0:T(8,128)(2,1)}), bf16[4,16,256]{2,1,0:T(8,128)(2,1)S(1)}, u32[]{:S(2)}, u32[]{:S(2)}) async-start(bf16[4,16,256]{2,1,0:T(8,128)(2,1)} %bitcast.8), calls=%async_computation.2 | async-start | bytes 65536 | tf_op jit(solution)/shard_map/all_to_all | solution.py:772
  57.1 2.7 %collective-permute-start.3 = (bf16[17,16,128]{2,1,0:T(8,128)(2,1)S(1)}, bf16[17,16,128]{2,1,0:T(8,128)(2,1)S(1)}, u32[]{:S(2)}, u32[]{:S(2)}) collective-permute-start(bf16[17,16,128]{2,1,0:T(8,128)(2,1)S(1)} %get-tuple-element.39), channel_id=1, source_target_pairs={{1,2},{3,4},{5,6},{7,8},{9,10},{11,12},{13,14},{2,1},{4,3},{6,5},{... | collective-permute-start | bytes 208904 | tf_op jit(solution)/shard_map/ppermute | solution.py:867
  59.8 3.6 %collective-permute-done.3.after.y_second = bf16[17,16,128]{2,1,0:T(8,128)(2,1)S(1)} collective-permute-done((bf16[17,16,128]{2,1,0:T(8,128)(2,1)S(1)}, bf16[17,16,128]{2,1,0:T(8,128)(2,1)S(1)}, u32[]{:S(2)}, u32[]{:S(2)}) %collective-permute-start.3) | collective-permute-done | bytes 69664 | tf_op jit(solution)/shard_map/ppermute | solution.py:867
  63.4 1.5 %shard_map.244.after = bf16[128,640]{1,0:T(8,128)(2,1)} custom-call(bf16[64,256]{1,0:T(8,128)(2,1)S(1)} %bitcast.17, bf16[128,384]{1,0:T(8,128)(2,1)S(1)} %copy-done.9, bf16[17,16,128]{2,1,0:T(8,128)(2,1)S(1)} %collective-permute-done.3.after.y_second), custom_call_target="tpu_custom_call" | custom-call | flops 40000000 | bytes 600000 | tf_op jit(solution)/shard_map/pallas_call | solution.py:869
  64.9 4.0 %all-to-all-start.3 = ((bf16[16,8,640]{2,1,0:T(8,128)(2,1)}), bf16[16,8,640]{2,1,0:T(8,128)(2,1)S(1)}, u32[]{:S(2)}, u32[]{:S(2)}) async-start(bf16[16,8,640]{2,1,0:T(8,128)(2,1)} %bitcast.10), calls=%async_computation.3 | async-start | bytes 327680 | tf_op jit(solution)/shard_map/all_to_all | solution.py:877
  68.9 1.7 %shard_map.245 = (f32[3,10,24,128]{3,2,1,0:T(8,128)S(1)}, f32[3,10,24,128]{3,2,1,0:T(8,128)S(1)}, f32[10,24,128]{2,1,0:T(8,128)S(1)}, f32[8,16,128]{2,1,0:T(8,128)S(1)}, f32[3,8,16,128]{3,2,1,0:T(8,128)S(1)}) custom-call(s32[64]{0:T(128)S(1)} %copy-done.16, f32[3,2,64]{2,1,0:T(2,128)S(1)} %bitcast.21, f32[3,8,16,128]{3,2,1,0:T(8,128)S(1)} %copy-done.1, ...), custom_call_target="tpu_custom_call" | custom-call | flops 10000000 | bytes 3000000 | tf_op jit(solution)/shard_map/pallas_call | solution.py:878
  70.7 4.7 %all-to-all-done.3 = bf16[16,8,640]{2,1,0:T(8,128)(2,1)S(1)} async-done(((bf16[16,8,640]{2,1,0:T(8,128)(2,1)}), bf16[16,8,640]{2,1,0:T(8,128)(2,1)S(1)}, u32[]{:S(2)}, u32[]{:S(2)}) %all-to-all-start.3) | async-done | bytes 163872 | tf_op jit(solution)/shard_map/all_to_all | solution.py:877
  75.4 1.2 %shard_map.246 = (f32[3,8,16,128]{3,2,1,0:T(8,128)}, f32[3,8,16,128]{3,2,1,0:T(8,128)}, f32[8,16,128]{2,1,0:T(8,128)}, f32[3,2,64]{2,1,0:T(2,128)}) custom-call(bf16[128,640]{1,0:T(8,128)(2,1)S(1)} %bitcast.14, bf16[128,128]{1,0:T(8,128)(2,1)S(1)} %copy-done.12, bf16[128,256]{1,0:T(8,128)(2,1)S(1)} %copy-done.11, ...), custom_call_target="tpu_custom_call" | custom-call | flops 40000000 | bytes 4000000 | tf_op jit(solution)/shard_map/pallas_call | solution.py:893
  (45 shorter events, 0.2 us)
Async XLA Ops:
  0.6 12.7 %copy-start = (f32[3,8,16,128]{3,2,1,0:T(8,128)S(1)}, f32[3,8,16,128]{3,2,1,0:T(8,128)}, u32[]{:S(2)}) copy-start(f32[3,8,16,128]{3,2,1,0:T(8,128)} %magnetic.5) | copy-start | bytes 589828
  3.0 10.4 %copy-start.1 = (f32[3,8,16,128]{3,2,1,0:T(8,128)S(1)}, f32[3,8,16,128]{3,2,1,0:T(8,128)}, u32[]{:S(2)}) copy-start(f32[3,8,16,128]{3,2,1,0:T(8,128)} %get-tuple-element.28.field.electric) | copy-start | bytes 589828
  3.0 10.4 %copy-start.19 = (f32[8]{0:T(128)S(1)}, f32[8]{0:T(128)}, u32[]{:S(2)}) copy-start(f32[8]{0:T(128)} %perm_in.1) | copy-start | bytes 100
  3.0 10.4 %copy-start.20 = (s32[64]{0:T(128)S(1)}, s32[64]{0:T(128)}, u32[]{:S(2)}) copy-start(s32[64]{0:T(128)} %src_in.1) | copy-start | bytes 772
  3.0 16.3 %all-to-all-start = ((bf16[16,24,128]{2,1,0:T(8,128)(2,1)}), bf16[16,24,128]{2,1,0:T(8,128)(2,1)S(1)}, u32[]{:S(2)}, u32[]{:S(2)}) async-start(bf16[16,24,128]{2,1,0:T(8,128)(2,1)} %bitcast.23), calls=%async_computation | async-start | bytes 196608 | tf_op jit(solution)/shard_map/all_to_all | solution.py:801
  20.6 14.3 %copy-start.2 = (bf16[2,3,8,16,128]{4,3,2,1,0:T(8,128)(2,1)S(1)}, bf16[2,3,8,16,128]{4,3,2,1,0:T(8,128)(2,1)}, u32[]{:S(2)}) copy-start(bf16[2,3,8,16,128]{4,3,2,1,0:T(8,128)(2,1)} %saved.5) | copy-start | bytes 589828
  20.6 31.1 %all-to-all-start.1 = ((bf16[32,8,256]{2,1,0:T(8,128)(2,1)}), bf16[32,8,256]{2,1,0:T(8,128)(2,1)S(1)}, u32[]{:S(2)}, u32[]{:S(2)}) async-start(bf16[32,8,256]{2,1,0:T(8,128)(2,1)} %bitcast.3), calls=%async_computation.1 | async-start | bytes 262144 | tf_op jit(solution)/shard_map/all_to_all | solution.py:819
  34.8 6.3 %copy-start.3 = (bf16[2,128,256]{2,1,0:T(8,128)(2,1)S(1)}, bf16[2,128,256]{2,1,0:T(8,128)(2,1)}, u32[]{:S(2)}) copy-start(bf16[2,128,256]{2,1,0:T(8,128)(2,1)} %constant.20.clone.at_x) | copy-start | bytes 393220
  34.9 6.3 %copy-start.5 = (bf16[4,2,48,256]{3,2,1,0:T(8,128)(2,1)S(1)}, bf16[4,2,48,256]{3,2,1,0:T(8,128)(2,1)}, u32[]{:S(2)}) copy-start(bf16[4,2,48,256]{3,2,1,0:T(8,128)(2,1)} %constant.21.clone.at_y) | copy-start | bytes 589828
  34.9 6.3 %copy-start.6 = (bf16[2,48,16,16]{1,3,2,0:T(8,128)(2,1)S(1)}, bf16[2,48,16,16]{1,3,2,0:T(8,128)(2,1)}, u32[]{:S(2)}) copy-start(bf16[2,48,16,16]{1,3,2,0:T(8,128)(2,1)} %param.32) | copy-start | bytes 147460
  34.9 6.3 %copy-start.7 = (bf16[16,2,16,128]{3,2,1,0:T(8,128)(2,1)S(1)}, bf16[16,2,16,128]{3,2,1,0:T(8,128)(2,1)}, u32[]{:S(2)}) copy-start(bf16[16,2,16,128]{3,2,1,0:T(8,128)(2,1)} %constant.22.clone.at_z) | copy-start | bytes 393220
  34.9 6.3 %copy-start.8 = (bf16[4,2,64,128]{3,2,1,0:T(8,128)(2,1)S(1)}, bf16[4,2,64,128]{3,2,1,0:T(8,128)(2,1)}, u32[]{:S(2)}) copy-start(bf16[4,2,64,128]{3,2,1,0:T(8,128)(2,1)} %constant.23.clone.inv_x) | copy-start | bytes 393220
  34.9 6.3 %copy-start.14 = (f32[16,48]{1,0:T(8,128)S(1)}, f32[16,48]{1,0:T(8,128)}, u32[]{:S(2)}) copy-start(f32[16,48]{1,0:T(8,128)} %gain_x.1) | copy-start | bytes 9220
  34.9 6.3 %copy-start.15 = (f32[16,48]{1,0:T(8,128)S(1)}, f32[16,48]{1,0:T(8,128)}, u32[]{:S(2)}) copy-start(f32[16,48]{1,0:T(8,128)} %gain_y.1) | copy-start | bytes 9220
  34.9 6.3 %copy-start.18 = (f32[3,16]{1,0:T(4,128)S(1)}, f32[3,16]{1,0:T(4,128)}, u32[]{:S(2)}) copy-start(f32[3,16]{1,0:T(4,128)} %project.1) | copy-start | bytes 580
  35.0 11.4 %collective-permute-start = (bf16[17,16,128]{2,1,0:T(8,128)(2,1)S(1)}, bf16[17,16,128]{2,1,0:T(8,128)(2,1)S(1)}, u32[]{:S(2)}, u32[]{:S(2)}) collective-permute-start(bf16[17,16,128]{2,1,0:T(8,128)(2,1)S(1)} %get-tuple-element.36), channel_id=1, source_target_pairs={{0,16},{16,32},{32,48},{48,64},{64,80},{80,96},{96,112},{112,128},... | collective-permute-start | bytes 208904 | tf_op jit(solution)/shard_map/ppermute | solution.py:763
  39.8 6.6 %collective-permute-start.1 = (bf16[10,16,128]{2,1,0:T(8,128)(2,1)S(1)}, bf16[10,16,128]{2,1,0:T(8,128)(2,1)S(1)}, u32[]{:S(2)}, u32[]{:S(2)}) collective-permute-start(bf16[10,16,128]{2,1,0:T(8,128)(2,1)S(1)} %get-tuple-element.37), channel_id=1, source_target_pairs={{16,0},{32,16},{48,32},{64,48},{80,64},{96,80},{112,96},{128,112},... | collective-permute-start | bytes 122888 | tf_op jit(solution)/shard_map/ppermute | solution.py:763
  46.5 5.2 %collective-permute-start.2 = (bf16[17,16,128]{2,1,0:T(8,128)(2,1)S(1)}, bf16[17,16,128]{2,1,0:T(8,128)(2,1)S(1)}, u32[]{:S(2)}, u32[]{:S(2)}) collective-permute-start(bf16[17,16,128]{2,1,0:T(8,128)(2,1)S(1)} %get-tuple-element.38), channel_id=1, source_target_pairs={{0,1},{1,0},{2,3},{3,2},{4,5},{5,4},{6,7},{7,6},{8,9},{9,8},{10,11... | collective-permute-start | bytes 208904 | tf_op jit(solution)/shard_map/ppermute | solution.py:857
  51.7 11.7 %copy-start.9 = (bf16[128,384]{1,0:T(8,128)(2,1)S(1)}, bf16[128,384]{1,0:T(8,128)(2,1)}, u32[]{:S(2)}) copy-start(bf16[128,384]{1,0:T(8,128)(2,1)} %constant.24.clone.inv_y) | copy-start | bytes 294916
  53.0 10.4 %all-to-all-start.2 = ((bf16[4,16,256]{2,1,0:T(8,128)(2,1)}), bf16[4,16,256]{2,1,0:T(8,128)(2,1)S(1)}, u32[]{:S(2)}, u32[]{:S(2)}) async-start(bf16[4,16,256]{2,1,0:T(8,128)(2,1)} %bitcast.8), calls=%async_computation.2 | async-start | bytes 65536 | tf_op jit(solution)/shard_map/all_to_all | solution.py:772
  57.1 6.3 %collective-permute-start.3 = (bf16[17,16,128]{2,1,0:T(8,128)(2,1)S(1)}, bf16[17,16,128]{2,1,0:T(8,128)(2,1)S(1)}, u32[]{:S(2)}, u32[]{:S(2)}) collective-permute-start(bf16[17,16,128]{2,1,0:T(8,128)(2,1)S(1)} %get-tuple-element.39), channel_id=1, source_target_pairs={{1,2},{3,4},{5,6},{7,8},{9,10},{11,12},{13,14},{2,1},{4,3},{6,5},{... | collective-permute-start | bytes 208904 | tf_op jit(solution)/shard_map/ppermute | solution.py:867
  64.9 10.4 %all-to-all-start.3 = ((bf16[16,8,640]{2,1,0:T(8,128)(2,1)}), bf16[16,8,640]{2,1,0:T(8,128)(2,1)S(1)}, u32[]{:S(2)}, u32[]{:S(2)}) async-start(bf16[16,8,640]{2,1,0:T(8,128)(2,1)} %bitcast.10), calls=%async_computation.3 | async-start | bytes 327680 | tf_op jit(solution)/shard_map/all_to_all | solution.py:877
  68.9 6.5 %copy-start.11 = (bf16[128,256]{1,0:T(8,128)(2,1)S(1)}, bf16[128,256]{1,0:T(8,128)(2,1)}, u32[]{:S(2)}) copy-start(bf16[128,256]{1,0:T(8,128)(2,1)} %constant.26.clone.apart) | copy-start | bytes 196612
  68.9 6.5 %copy-start.12 = (bf16[128,128]{1,0:T(8,128)(2,1)S(1)}, bf16[128,128]{1,0:T(8,128)(2,1)}, u32[]{:S(2)}) copy-start(bf16[128,128]{1,0:T(8,128)(2,1)} %constant.25.clone.table) | copy-start | bytes 98308
  (5 other events, 9.6 us)
